TPU v7x, 128 devices: a whole 4x4x4 slice. The times are simulated.
128 devices in a mesh: rep: 8 (over x_lo, z), shard: 16 (over y, x_hi, core).
Axes of the slice: x: 4 (x_hi: 2, x_lo: 2; x = x_hi * 2 + x_lo), y: 4, z: 4, core: 2. Of those that a mesh axis runs over, the one named last changes fastest.
Arguments:
- hidden_in: bfloat16 [32768, 2048], P(('rep', 'shard')), may hold values from -6 to 6
- cotangent: bfloat16 [32768, 2048], P(('rep', 'shard')), may hold values from -6 to 6
- segment_ids: int32 [32768], P('rep'), may hold values from 0 to 2, as said below
- positions: int32 [32768], P('rep'), may hold values from 0 to 3583, as said below
- attn_gain: float32 [2048], P('shard'), may hold values from 0.25 to 1.75
- query_gain: float32 [128], replicated, may hold values from 0.25 to 1.75
- key_gain: float32 [128], replicated, may hold values from 0.25 to 1.75
- query_weight: float32 [2048, 2048], P('shard'), may hold values from -0.125 to 0.125
- key_weight: float32 [2048, 1024], P('shard'), may hold values from -0.125 to 0.125
- value_weight: float32 [2048, 1024], P('shard'), may hold values from -0.125 to 0.125
- out_weight: float32 [2048, 2048], P('shard'), may hold values from -3 to 3
- mlp_gain: float32 [2048], P('shard'), may hold values from 0.25 to 1.75
- gate_weight: float32 [2048, 6144], P('shard'), may hold values from -0.125 to 0.125
- up_weight: float32 [2048, 6144], P('shard'), may hold values from -0.125 to 0.125
- down_weight: float32 [2048, 6144], P('shard'), may hold values from -0.078125 to 0.078125
Outputs:
- output: bfloat16 [32768, 2048], P(('rep', 'shard'))
- hidden_grad: bfloat16 [32768, 2048], P(('rep', 'shard'))
- attn_gain_grad: float32 [2048], P('shard')
- query_gain_grad: float32 [128], replicated
- key_gain_grad: float32 [128], replicated
- query_weight_grad: float32 [2048, 2048], P('shard')
- key_weight_grad: float32 [2048, 1024], P('shard')
- value_weight_grad: float32 [2048, 1024], P('shard')
- out_weight_grad: float32 [2048, 2048], P('shard')
- mlp_gain_grad: float32 [2048], P('shard')
- gate_weight_grad: float32 [2048, 6144], P('shard')
- up_weight_grad: float32 [2048, 6144], P('shard')
- down_weight_grad: float32 [2048, 6144], P('shard')
Inputs may be any that keep to these rules, and one draw needn't show every extreme that they name: `segment_ids`: within the 4096 rows of each index of rep, one prompt of 3072 rows (segment 0) and 2 continuations of 512 rows (segments 1 to 2) are laid out; each index of shard holds 256 consecutive rows of the order prompt, continuation 1, ..., and these runs are placed on the devices in a drawn order. Prompt rows have positions 0 to 3071 in order; continuation rows have positions 3072 to 3583 in order, in the layout of segment_ids.
All inputs are finite; a program needn't handle non-finite values.
Results may differ from a plain program's by a relative error of at most 0.025.
Values may be sent and summed in bfloat16 or wider, within the bound.
No kernel may reach another device: no remote copies, remote signals or barrier semaphores. Data moves between devices by JAX's collectives and lax.ppermute only.
A program may use at most 384 MiB of HBM per device.

v0:
```python
import jax
import jax.numpy as jnp
from jax import lax
from jax.sharding import PartitionSpec as P

HEADS = 16
KV_HEADS = 8
HEAD_DIM = 128
Q_DIM = 2048
KV_DIM = 1024


norm_eps = 1e-06
rope_base = 1000000.0
masked_score = -1e30
contract_first = (((0,), (0,)), ((), ()))
contract_last = (((1,), (1,)), ((), ()))


def normalize(values):
    return values * lax.rsqrt(jnp.mean(values * values, axis=-1, keepdims=True) + norm_eps)


def scaled_norm(values, scale):
    return normalize(values) * scale


def rotate(values, places):
    half_dim = values.shape[-1] // 2
    frequency = rope_base ** (-2.0 * jnp.arange(half_dim, dtype=jnp.float32) / values.shape[-1])
    angles = places.astype(jnp.float32)[:, None] * frequency[None, :]
    cosine = jnp.cos(angles)[:, None, :]
    sine_part = jnp.sin(angles)[:, None, :]
    first_half = values[..., :half_dim]
    second_half = values[..., half_dim:]
    return jnp.concatenate(
        [
            first_half * cosine - second_half * sine_part,
            second_half * cosine + first_half * sine_part,
        ],
        axis=-1,
    )


def swiglu(gate_in, upper_in):
    return jax.nn.silu(gate_in) * upper_in


def owner_share(left, right):
    term = lax.dot_general(left, right, contract_first, preferred_element_type=jnp.float32)
    return lax.psum_scatter(
        term.astype(jnp.bfloat16), "shard", scatter_dimension=0, tiled=True
    ).astype(jnp.float32)


def local(
    hidden_in,
    cotangent,
    segment_ids,
    positions,
    attn_gain,
    query_gain,
    key_gain,
    query_weight,
    key_weight,
    value_weight,
    out_weight,
    mlp_gain,
    gate_weight,
    up_weight,
    down_weight,
):
    row_count = hidden_in.shape[0]
    own_rows = attn_gain.shape[0]
    my_index = lax.axis_index("shard")
    group_rows = segment_ids.shape[0]
    group_size = HEADS // KV_HEADS
    score_scale = HEAD_DIM ** (-0.5)
    own_segments = lax.dynamic_slice_in_dim(segment_ids, my_index * row_count, row_count)
    own_places = lax.dynamic_slice_in_dim(positions, my_index * row_count, row_count)
    hidden = hidden_in.astype(jnp.float32)
    gain_low, query_low, key_low, value_low, out_low = (
        lax.all_gather(attn_gain.astype(jnp.bfloat16), "shard", axis=0, tiled=True),
        lax.all_gather(query_weight.astype(jnp.bfloat16), "shard", axis=0, tiled=True),
        lax.all_gather(key_weight.astype(jnp.bfloat16), "shard", axis=0, tiled=True),
        lax.all_gather(value_weight.astype(jnp.bfloat16), "shard", axis=0, tiled=True),
        lax.all_gather(out_weight.astype(jnp.bfloat16), "shard", axis=0, tiled=True),
    )
    attn_scale = gain_low.astype(jnp.float32)
    first_in = scaled_norm(hidden, attn_scale).astype(jnp.bfloat16)
    query_pre = jnp.dot(first_in, query_low, preferred_element_type=jnp.float32)
    key_pre = jnp.dot(first_in, key_low, preferred_element_type=jnp.float32)
    value_pre = jnp.dot(first_in, value_low, preferred_element_type=jnp.float32)

    def head_prep(query_part, key_part, query_scale, key_scale):
        query_out = rotate(
            normalize(query_part.reshape(row_count, HEADS, HEAD_DIM)) * query_scale, own_places
        )
        key_out = rotate(
            normalize(key_part.reshape(row_count, KV_HEADS, HEAD_DIM)) * key_scale, own_places
        )
        return (query_out, key_out)

    (queries, key_act), prep_back = jax.vjp(head_prep, query_pre, key_pre, query_gain, key_gain)
    key_send = key_act.astype(jnp.bfloat16).reshape(row_count, KV_DIM)
    value_send = value_pre.astype(jnp.bfloat16)
    key_all, value_all = (
        lax.all_gather(key_send, "shard", axis=0, tiled=True),
        lax.all_gather(value_send, "shard", axis=0, tiled=True),
    )
    visible = (positions[None, :] <= own_places[:, None]) & (
        (segment_ids[None, :] == 0) | (segment_ids[None, :] == own_segments[:, None])
    )
    tiled_mask = jnp.tile(visible, (group_size, 1))
    query_heads = (
        queries.astype(jnp.bfloat16)
        .reshape(row_count, KV_HEADS, group_size, HEAD_DIM)
        .transpose(1, 2, 0, 3)
        .reshape(KV_HEADS, group_size * row_count, HEAD_DIM)
    )

    def head_scores(head_index):
        head_keys = lax.dynamic_slice_in_dim(key_all, head_index * HEAD_DIM, HEAD_DIM, 1)
        raw_scores = (
            lax.dot_general(
                query_heads[head_index],
                head_keys,
                contract_last,
                preferred_element_type=jnp.float32,
            )
            * score_scale
        )
        return (jnp.where(tiled_mask, raw_scores, masked_score), head_keys)

    def forward_head(head_index):
        scores, head_keys = head_scores(head_index)
        row_max = jnp.max(scores, axis=-1, keepdims=True)
        unscaled = jnp.exp(scores - row_max)
        row_total = jnp.sum(unscaled, axis=-1, keepdims=True)
        probabilities = unscaled / row_total
        head_values = lax.dynamic_slice_in_dim(value_all, head_index * HEAD_DIM, HEAD_DIM, 1)
        head_mixed = jnp.dot(
            probabilities.astype(jnp.bfloat16), head_values, preferred_element_type=jnp.float32
        )
        return (head_mixed, row_max + jnp.log(row_total))

    mixed_heads, log_totals = lax.map(forward_head, jnp.arange(KV_HEADS))
    mixed_out = (
        mixed_heads.reshape(KV_HEADS, group_size, row_count, HEAD_DIM)
        .transpose(2, 0, 1, 3)
        .reshape(row_count, Q_DIM)
    )
    mixed_low = mixed_out.astype(jnp.bfloat16)
    attn_out = lax.dot_general(
        mixed_low, out_low, contract_last, preferred_element_type=jnp.float32
    )
    middle = hidden + attn_out
    second_norm = normalize(middle)
    gate_cast = gate_weight.astype(jnp.bfloat16)
    up_cast = up_weight.astype(jnp.bfloat16)
    down_cast = down_weight.astype(jnp.bfloat16)
    gain_piece = lax.all_gather(mlp_gain.astype(jnp.bfloat16), "shard", axis=0, tiled=True)
    gate_piece = lax.all_gather(gate_cast, "shard", axis=0, tiled=True)
    up_piece = lax.all_gather(up_cast, "shard", axis=0, tiled=True)
    columns = second_norm
    piece_in = (columns * gain_piece.astype(jnp.float32)).astype(jnp.bfloat16)
    gate_act = jnp.dot(piece_in, gate_piece, preferred_element_type=jnp.float32)
    up_act = jnp.dot(piece_in, up_piece, preferred_element_type=jnp.float32)
    mlp_scale = gain_piece.astype(jnp.float32)
    activated, swiglu_back = jax.vjp(swiglu, gate_act, up_act)
    inner_low = activated.astype(jnp.bfloat16)
    mlp_out = lax.dot_general(
        inner_low,
        lax.all_gather(down_cast, "shard", axis=0, tiled=True),
        contract_last,
        preferred_element_type=jnp.float32,
    )
    output = (middle + mlp_out).astype(jnp.bfloat16)
    cot_float = cotangent.astype(jnp.float32)
    columns = cotangent
    inner_grad = jnp.dot(
        columns,
        lax.all_gather(down_cast, "shard", axis=0, tiled=True),
        preferred_element_type=jnp.float32,
    )
    gate_grad, upper_grad = swiglu_back(inner_grad)
    gate_grad_low = gate_grad.astype(jnp.bfloat16)
    upper_grad_low = upper_grad.astype(jnp.bfloat16)
    block = lax.dot_general(
        gate_grad_low,
        lax.all_gather(gate_cast, "shard", axis=0, tiled=True),
        contract_last,
        preferred_element_type=jnp.float32,
    ) + lax.dot_general(
        upper_grad_low,
        lax.all_gather(up_cast, "shard", axis=0, tiled=True),
        contract_last,
        preferred_element_type=jnp.float32,
    )
    _, second_back = jax.vjp(scaled_norm, middle, mlp_scale)
    middle_part, mlp_gain_part = second_back(block)
    middle_grad = cot_float + middle_part
    middle_low = middle_grad.astype(jnp.bfloat16)
    mixed_grad_low = jnp.dot(middle_low, out_low, preferred_element_type=jnp.float32).astype(
        jnp.bfloat16
    )
    mixed_grad_heads = (
        mixed_grad_low.reshape(row_count, KV_HEADS, group_size, HEAD_DIM)
        .transpose(1, 2, 0, 3)
        .reshape(KV_HEADS, group_size * row_count, HEAD_DIM)
    )

    def backward_head(head_index, running):
        query_grads, key_grads, value_grads = running
        scores, head_keys = head_scores(head_index)
        probabilities = jnp.exp(scores - log_totals[head_index])
        head_values = lax.dynamic_slice_in_dim(value_all, head_index * HEAD_DIM, HEAD_DIM, 1)
        head_out_grad = mixed_grad_heads[head_index]
        prob_grad = lax.dot_general(
            head_out_grad, head_values, contract_last, preferred_element_type=jnp.float32
        )
        score_grad = probabilities * (
            prob_grad - jnp.sum(probabilities * prob_grad, axis=-1, keepdims=True)
        )
        score_low = score_grad.astype(jnp.bfloat16)
        query_part = jnp.dot(score_low, head_keys, preferred_element_type=jnp.float32) * score_scale
        key_part = (
            lax.dot_general(
                score_low,
                query_heads[head_index],
                contract_first,
                preferred_element_type=jnp.float32,
            )
            * score_scale
        )
        value_part = lax.dot_general(
            probabilities.astype(jnp.bfloat16),
            head_out_grad,
            contract_first,
            preferred_element_type=jnp.float32,
        )
        return (
            lax.dynamic_update_index_in_dim(query_grads, query_part, head_index, 0),
            lax.dynamic_update_slice_in_dim(key_grads, key_part, head_index * HEAD_DIM, 1),
            lax.dynamic_update_slice_in_dim(value_grads, value_part, head_index * HEAD_DIM, 1),
        )

    start_grads = (
        jnp.zeros((KV_HEADS, group_size * row_count, HEAD_DIM), jnp.float32),
        jnp.zeros((group_rows, KV_DIM), jnp.float32),
        jnp.zeros((group_rows, KV_DIM), jnp.float32),
    )
    query_grads, key_grads, value_grads = lax.fori_loop(0, KV_HEADS, backward_head, start_grads)
    key_grad_own, value_grad_own = (
        lax.psum_scatter(
            key_grads.astype(jnp.bfloat16), "shard", scatter_dimension=0, tiled=True
        ).astype(jnp.float32),
        lax.psum_scatter(
            value_grads.astype(jnp.bfloat16), "shard", scatter_dimension=0, tiled=True
        ).astype(jnp.float32),
    )
    query_grad = (
        query_grads.reshape(KV_HEADS, group_size, row_count, HEAD_DIM)
        .transpose(2, 0, 1, 3)
        .reshape(row_count, HEADS, HEAD_DIM)
    )
    query_pre_grad, key_pre_grad, query_gain_part, key_gain_part = prep_back(
        (query_grad, key_grad_own.reshape(row_count, KV_HEADS, HEAD_DIM))
    )
    query_pre_low = query_pre_grad.astype(jnp.bfloat16)
    key_pre_low = key_pre_grad.astype(jnp.bfloat16)
    value_pre_low = value_grad_own.astype(jnp.bfloat16)
    first_grad = (
        lax.dot_general(query_pre_low, query_low, contract_last, preferred_element_type=jnp.float32)
        + lax.dot_general(key_pre_low, key_low, contract_last, preferred_element_type=jnp.float32)
        + lax.dot_general(
            value_pre_low, value_low, contract_last, preferred_element_type=jnp.float32
        )
    )
    _, first_back = jax.vjp(scaled_norm, hidden, attn_scale)
    hidden_part, attn_gain_part = first_back(first_grad)
    hidden_grad = (middle_grad + hidden_part).astype(jnp.bfloat16)
    query_share = owner_share(first_in, query_pre_low)
    key_share = owner_share(first_in, key_pre_low)
    value_share = owner_share(first_in, value_pre_low)
    out_share = owner_share(middle_low, mixed_low)
    gate_share, up_share, down_share = (
        owner_share(piece_in, gate_grad_low),
        owner_share(piece_in, upper_grad_low),
        owner_share(cotangent, inner_low),
    )
    gain_totals = lax.psum(
        (attn_gain_part, mlp_gain_part, query_gain_part, key_gain_part), ("rep", "shard")
    )
    attn_gain_out = lax.dynamic_slice_in_dim(gain_totals[0], my_index * own_rows, own_rows)
    mlp_gain_out = lax.dynamic_slice_in_dim(gain_totals[1], my_index * own_rows, own_rows)
    totals = (
        lax.psum(query_share.astype(jnp.bfloat16), "rep").astype(jnp.float32),
        lax.psum(key_share.astype(jnp.bfloat16), "rep").astype(jnp.float32),
        lax.psum(value_share.astype(jnp.bfloat16), "rep").astype(jnp.float32),
        lax.psum(out_share.astype(jnp.bfloat16), "rep").astype(jnp.float32),
        lax.psum(gate_share.astype(jnp.bfloat16), "rep").astype(jnp.float32),
        lax.psum(up_share.astype(jnp.bfloat16), "rep").astype(jnp.float32),
        lax.psum(down_share.astype(jnp.bfloat16), "rep").astype(jnp.float32),
    )
    return (
        output,
        hidden_grad,
        attn_gain_out,
        gain_totals[2],
        gain_totals[3],
        totals[0],
        totals[1],
        totals[2],
        totals[3],
        mlp_gain_out,
        totals[4],
        totals[5],
        totals[6],
    )


def solution(mesh):
    in_specs = (
        P(("rep", "shard"), None),
        P(("rep", "shard"), None),
        P("rep"),
        P("rep"),
        P("shard"),
        P(),
        P(),
        P("shard", None),
        P("shard", None),
        P("shard", None),
        P("shard", None),
        P("shard"),
        P("shard", None),
        P("shard", None),
        P("shard", None),
    )
    out_specs = (
        P(("rep", "shard"), None),
        P(("rep", "shard"), None),
        P("shard"),
        P(),
        P(),
        P("shard", None),
        P("shard", None),
        P("shard", None),
        P("shard", None),
        P("shard"),
        P("shard", None),
        P("shard", None),
        P("shard", None),
    )
    return jax.shard_map(local, mesh=mesh, in_specs=in_specs, out_specs=out_specs, check_vma=False)
```

profile of v0, /device:TPU:4, one launch (start us, length us, event | category | flops | bytes accessed | tf_op | source)
XLA Modules:
  0.0 2545.6 jit_solution(4251775933046974446)
XLA Ops:
  13.2 19.7 all-gather
  34.4 31.6 %all-gather.14.cloned.1.call-done = bf16[2048,1024]{1,0:T(8,128)(2,1)} async-done(((bf16[128,1024]{1,0:T(8,128)(2,1)}), bf16[2048,1024]{1,0:T(8,128)(2,1)}) %all-gather.14.cloned.1.call-update) | async-done | bytes 4194320 | tf_op jit(solution)/shard_map/all_gather | solution.py:85
  72.5 49.7 %all-gather.18.cloned.1.call-done = bf16[2048,1024]{1,0:T(8,128)(2,1)} async-done(((bf16[128,1024]{1,0:T(8,128)(2,1)}), bf16[2048,1024]{1,0:T(8,128)(2,1)}) %all-gather.18.cloned.1.call-update) | async-done | bytes 4194320 | tf_op jit(solution)/shard_map/all_gather | solution.py:86
  137.7 21.6 all-gather.1
  161.7 34.3 %all-gather.12.cloned.1.call-done = bf16[2048,2048]{1,0:T(8,128)(2,1)} async-done(((bf16[128,2048]{1,0:T(8,128)(2,1)}), bf16[2048,2048]{1,0:T(8,128)(2,1)}) %all-gather.12.cloned.1.call-update) | async-done | bytes 8388624 | tf_op jit(solution)/shard_map/all_gather | solution.py:84
  211.1 58.5 %all-gather.16.cloned.1.call-done = bf16[4096,1024]{1,0:T(8,128)(2,1)} async-done(((bf16[256,1024]{1,0:T(8,128)(2,1)}), bf16[4096,1024]{1,0:T(8,128)(2,1)}) %all-gather.16.cloned.1.call-update) | async-done | bytes 8388624 | tf_op jit(solution)/shard_map/all_gather | solution.py:108
  269.7 73.6 %all-gather.20.cloned.1.call-done = bf16[4096,1024]{1,0:T(8,128)(2,1)} async-done(((bf16[256,1024]{1,0:T(8,128)(2,1)}), bf16[4096,1024]{1,0:T(8,128)(2,1)}) %all-gather.20.cloned.1.call-update) | async-done | bytes 8388624 | tf_op jit(solution)/shard_map/all_gather | solution.py:109
  343.3 118.4 %while.33 = (s32[]{:T(128)}, bf16[8,512,128]{2,1,0:T(8,128)(2,1)}, f32[8,512,1]{1,2,0:T(1,128)S(1)}, s32[8]{0:T(128)S(1)}, bf16[8,512,128]{2,1,0:T(8,128)(2,1)},...) while((s32[]{:T(128)}, bf16[8,512,128]{2,1,0:T(8,128)(2,1)}, ...), condition=%wide.region_6.7_spmd.clone.clone, body=%wide.region_3.6_spmd.clone.sunk.clone | while | flops 1098907136 | bytes 39211712 | solution.py:147
  471.8 93.0 %all-gather.24.cloned.1.call-done = bf16[2048,6144]{1,0:T(8,128)(2,1)} async-done(((bf16[128,6144]{1,0:T(8,128)(2,1)}), bf16[2048,6144]{1,0:T(8,128)(2,1)}) %all-gather.24.cloned.1.call-update) | async-done | bytes 25165840 | tf_op jit(solution)/shard_map/all_gather | solution.py:163
  579.8 133.2 %all-gather.26.cloned.1.call-done = bf16[2048,6144]{1,0:T(8,128)(2,1)} async-done(((bf16[128,6144]{1,0:T(8,128)(2,1)}), bf16[2048,6144]{1,0:T(8,128)(2,1)}) %all-gather.26.cloned.1.call-update) | async-done | bytes 25165840 | tf_op jit(solution)/shard_map/all_gather | solution.py:164
  727.8 133.5 %all-gather.28.cloned.1.call-done = bf16[2048,6144]{1,0:T(8,128)(2,1)} async-done(((bf16[128,6144]{1,0:T(8,128)(2,1)}), bf16[2048,6144]{1,0:T(8,128)(2,1)}) %all-gather.28.cloned.1.call-update) | async-done | bytes 25165840 | tf_op jit(solution)/shard_map/all_gather | solution.py:174
  930.9 252.0 %while.34 = (s32[]{:T(128)}, f32[8,512,128]{2,1,0:T(8,128)}, bf16[4096,1024]{1,0:T(8,128)(2,1)}, bf16[4096,1024]{1,0:T(8,128)(2,1)}, bf16[8,512,128]{2,1,0:T(8,1...) while((s32[]{:T(128)}, f32[8,512,128]{2,1,0:T(8,128)}, ...), condition=%wide.region_11.12_spmd.clone.clone, body=%wide.region_9.11_spmd.clone.sunk.clone | while | flops 2703818240 | bytes 105657016 | solution.py:253
  1200.4 31.9 %copy.74 = bf16[2048,6144]{1,0:T(8,128)(2,1)} copy(bf16[2048,6144]{0,1:T(8,128)(2,1)} %convert_bitcast_fusion) | data formatting | bytes 50331648
  1261.8 21.2 reduce-scatter.12.cloned.1.call-done
  1293.5 95.0 %reduce-scatter.14.cloned.1.call-done = bf16[256,1024]{1,0:T(8,128)(2,1)} async-done(((bf16[4096,1024]{1,0:T(8,128)(2,1)}), bf16[256,1024]{1,0:T(8,128)(2,1)}) %reduce-scatter.14.cloned.1.call-update) | async-done | bytes 524304 | tf_op jit(solution)/shard_map/reduce_scatter | solution.py:258
  1412.5 19.0 convolution_convert_fusion
  1431.5 150.2 %reduce-scatter.28.cloned.1.call-done = bf16[128,6144]{1,0:T(8,128)(2,1)} async-done(((bf16[2048,6144]{1,0:T(8,128)(2,1)}), bf16[128,6144]{1,0:T(8,128)(2,1)}) %reduce-scatter.28.cloned.1.call-update) | async-done | bytes 1572880
  1584.3 101.9 %reduce-scatter.16.cloned.1.call-done = bf16[128,2048]{1,0:T(8,128)(2,1)} async-done(((bf16[2048,2048]{1,0:T(8,128)(2,1)}), bf16[128,2048]{1,0:T(8,128)(2,1)}) %reduce-scatter.16.cloned.1.call-update) | async-done | bytes 524304 | tf_op jit(solution)/shard_map/reduce_scatter | solution.py:51
  1686.2 105.3 %reduce-scatter.22.cloned.1.call-done = bf16[128,2048]{1,0:T(8,128)(2,1)} async-done(((bf16[2048,2048]{1,0:T(8,128)(2,1)}), bf16[128,2048]{1,0:T(8,128)(2,1)}) %reduce-scatter.22.cloned.1.call-update) | async-done | bytes 524304 | tf_op jit(solution)/shard_map/reduce_scatter | solution.py:51
  1791.5 84.5 %reduce-scatter.18.cloned.1.call-done = bf16[128,1024]{1,0:T(8,128)(2,1)} async-done(((bf16[2048,1024]{1,0:T(8,128)(2,1)}), bf16[128,1024]{1,0:T(8,128)(2,1)}) %reduce-scatter.18.cloned.1.call-update) | async-done | bytes 262160 | tf_op jit(solution)/shard_map/reduce_scatter | solution.py:51
  1876.0 83.7 %reduce-scatter.20.cloned.1.call-done = bf16[128,1024]{1,0:T(8,128)(2,1)} async-done(((bf16[2048,1024]{1,0:T(8,128)(2,1)}), bf16[128,1024]{1,0:T(8,128)(2,1)}) %reduce-scatter.20.cloned.1.call-update) | async-done | bytes 262160 | tf_op jit(solution)/shard_map/reduce_scatter | solution.py:51
  1959.7 192.1 %reduce-scatter.24.cloned.1.call-done = bf16[128,6144]{1,0:T(8,128)(2,1)} async-done(((bf16[2048,6144]{1,0:T(8,128)(2,1)}), bf16[128,6144]{1,0:T(8,128)(2,1)}) %reduce-scatter.24.cloned.1.call-update) | async-done | bytes 1572880 | tf_op jit(solution)/shard_map/reduce_scatter | solution.py:51
  2151.8 192.4 %reduce-scatter.26.cloned.1.call-done = bf16[128,6144]{1,0:T(8,128)(2,1)} async-done(((bf16[2048,6144]{1,0:T(8,128)(2,1)}), bf16[128,6144]{1,0:T(8,128)(2,1)}) %reduce-scatter.26.cloned.1.call-update) | async-done | bytes 1572880 | tf_op jit(solution)/shard_map/reduce_scatter | solution.py:51
  2373.3 149.5 %all-reduce.4 = (f32[2048]{0:T(1024)S(1)}, f32[128]{0:T(128)}, f32[128]{0:T(128)}, f32[2048]{0:T(1024)S(1)}) all-reduce(f32[2048]{0:T(1024)S(1)} %get-tuple-element.356, f32[128]{0:T(128)S(1)} %copy-done.52, f32[128]{0:T(128)S(1)} %get-tuple-element.358, f32[2048]{0:T(1024)S(1)} %copy-done.47), channel_id=1, replica_groups=mesh['rep'=8,'shard'=16] {'rep','shard'}, use_global_device_ids=true, to_apply=%region_18.19 | all-reduce | flops 4352 | bytes 34816 | tf_op jit(solution)/shard_map/psum | solution.py:292
  (374 shorter events, 633.6 us)
Async XLA Ops:
  7.2 58.8 %all-gather.14.cloned.1.call-start = ((), (), s32[]{:S(2)}) async-start(), calls=%async_computation.10 | async-start | bytes 4456448 | tf_op jit(solution)/shard_map/all_gather | solution.py:85
  9.1 113.0 %all-gather.18.cloned.1.call-start = ((), (), s32[]{:S(2)}) async-start(), calls=%async_computation.12 | async-start | bytes 4456448 | tf_op jit(solution)/shard_map/all_gather | solution.py:86
  11.0 185.0 %all-gather.12.cloned.1.call-start = ((), (), s32[]{:S(2)}) async-start(), calls=%async_computation.9 | async-start | bytes 8912896 | tf_op jit(solution)/shard_map/all_gather | solution.py:84
  13.2 256.5 %all-gather.16.cloned.1.call-start = ((), (), s32[]{:S(2)}) async-start(), calls=%async_computation.11 | async-start | bytes 8912896 | tf_op jit(solution)/shard_map/all_gather | solution.py:108
  32.9 163.1 %copy-start.30 = (f32[16,1,128]{2,1,0:T(1,128)}, f32[16,1,128]{2,1,0:T(1,128)S(1)}, u32[]{:S(2)}) copy-start(f32[16,1,128]{2,1,0:T(1,128)S(1)} %convert_element_type.240) | copy-start | bytes 24580
  33.9 162.2 %copy-start.39 = (f32[256]{0:T(256)}, f32[256]{0:T(256)S(1)}, u32[]{:S(2)}) copy-start(f32[256]{0:T(256)S(1)} %fusion.64) | copy-start | bytes 3076
  34.4 173.7 %copy-start.19 = (f32[256,64]{1,0:T(8,128)}, f32[256,64]{1,0:T(8,128)S(1)}, u32[]{:S(2)}) copy-start(f32[256,64]{1,0:T(8,128)S(1)} %get-tuple-element.424) | copy-start | bytes 196612
  34.4 173.7 %copy-start.21 = (f32[256,64]{1,0:T(8,128)}, f32[256,64]{1,0:T(8,128)S(1)}, u32[]{:S(2)}) copy-start(f32[256,64]{1,0:T(8,128)S(1)} %get-tuple-element.425) | copy-start | bytes 196612
  72.5 270.8 %all-gather.20.cloned.1.call-start = ((), (), s32[]{:S(2)}) async-start(), calls=%async_computation.13 | async-start | bytes 8912896 | tf_op jit(solution)/shard_map/all_gather | solution.py:109
  126.5 337.4 %all-gather.22.cloned.1.call-start = ((), (), s32[]{:S(2)}) async-start(), calls=%async_computation.14 | async-start | bytes 8912896 | tf_op jit(solution)/shard_map/all_gather | solution.py:87
  127.4 437.3 %all-gather.24.cloned.1.call-start = ((), (), s32[]{:S(2)}) async-start(), calls=%async_computation.15 | async-start | bytes 26738688 | tf_op jit(solution)/shard_map/all_gather | solution.py:163
  130.7 582.3 %all-gather.26.cloned.1.call-start = ((), (), s32[]{:S(2)}) async-start(), calls=%async_computation.16 | async-start | bytes 26738688 | tf_op jit(solution)/shard_map/all_gather | solution.py:164
  134.1 727.2 %all-gather.28.cloned.1.call-start = ((), (), s32[]{:S(2)}) async-start(), calls=%async_computation.17 | async-start | bytes 26738688 | tf_op jit(solution)/shard_map/all_gather | solution.py:174
  137.6 1145.4 %reduce-scatter.12.cloned.1.call-start = ((), (), s32[]{:S(2)}) async-start(), calls=%async_computation.18 | async-start | bytes 8912896 | tf_op jit(solution)/shard_map/reduce_scatter | solution.py:255
  471.8 241.2 %copy-start.9 = (bf16[256,2048]{1,0:T(8,128)(2,1)}, bf16[256,2048]{1,0:T(8,128)(2,1)S(1)}, u32[]{:S(2)}) copy-start(bf16[256,2048]{1,0:T(8,128)(2,1)S(1)} %multiply_convert_fusion.3) | copy-start | bytes 3145732
  1182.9 205.5 %reduce-scatter.14.cloned.1.call-start = ((), (), s32[]{:S(2)}) async-start(), calls=%async_computation.19 | async-start | bytes 8912896 | tf_op jit(solution)/shard_map/reduce_scatter | solution.py:258
  1183.7 398.1 %reduce-scatter.28.cloned.1.call-start = ((), (), s32[]{:S(2)}) async-start(), calls=%async_computation.26 | async-start | bytes 26738688
  1232.3 453.9 %reduce-scatter.16.cloned.1.call-start = ((), (), s32[]{:S(2)}) async-start(), calls=%async_computation.20 | async-start | bytes 8912896 | tf_op jit(solution)/shard_map/reduce_scatter | solution.py:51
  1253.2 538.3 %reduce-scatter.22.cloned.1.call-start = ((), (), s32[]{:S(2)}) async-start(), calls=%async_computation.23 | async-start | bytes 8912896 | tf_op jit(solution)/shard_map/reduce_scatter | solution.py:51
  1261.7 614.2 %reduce-scatter.18.cloned.1.call-start = ((), (), s32[]{:S(2)}) async-start(), calls=%async_computation.21 | async-start | bytes 4456448 | tf_op jit(solution)/shard_map/reduce_scatter | solution.py:51
  1293.4 666.3 %reduce-scatter.20.cloned.1.call-start = ((), (), s32[]{:S(2)}) async-start(), calls=%async_computation.22 | async-start | bytes 4456448 | tf_op jit(solution)/shard_map/reduce_scatter | solution.py:51
  1392.8 759.0 %reduce-scatter.24.cloned.1.call-start = ((), (), s32[]{:S(2)}) async-start(), calls=%async_computation.24 | async-start | bytes 26738688 | tf_op jit(solution)/shard_map/reduce_scatter | solution.py:51
  1412.2 932.0 %reduce-scatter.26.cloned.1.call-start = ((), (), s32[]{:S(2)}) async-start(), calls=%async_computation.25 | async-start | bytes 26738688 | tf_op jit(solution)/shard_map/reduce_scatter | solution.py:51
  1431.5 1095.7 %all-reduce.8.cloned.1.call-start = ((), (), s32[]{:S(2)}) async-start(), calls=%async_computation.27 | async-start | bytes 12582912 | tf_op jit(solution)/shard_map/psum | solution.py:304
  (57 other events, 620.2 us)
Sparse Core Ops, SparseCore 0:
  11.1 54.9 all-gather.13
  69.1 53.0 all-gather.17
  125.2 70.7 all-gather.11
  198.9 70.6 all-gather.15
  272.6 70.6 all-gather.19
  345.6 70.6 all-gather.21
  419.4 145.3 all-gather.23
  567.8 145.1 all-gather.25
  716.1 145.1 all-gather.27
  1183.1 99.8 reduce-scatter.11
  1287.3 101.0 reduce-scatter.13
  1392.6 189.0 reduce-scatter.27
  1586.0 100.1 reduce-scatter.15
  1690.3 101.1 reduce-scatter.21
  1795.3 80.5 reduce-scatter.17
  1880.3 79.2 reduce-scatter.19
  1963.9 187.8 reduce-scatter.23
  2156.0 188.1 reduce-scatter.25
  2347.8 148.0 all-reduce.7
where the time goes:
time: 2560 us; the launch traced here: 2550 us
  waiting for transfers between devices  1630 us (64%)
  matrix products  445 us (17%)
  blocking collectives  191 us (7%)
  other arithmetic  162 us (6%)
  local copies, waits for them, and re-layouts  74.8 us (3%)
    reduce_scatter x6, waiting for transfers between devices, owner_share(): lax.psum_scatter(term.astype(jnp.bfloat16), 'shard', scatter_dimension=0,...  760 us
    unnamed x20, waiting for transfers between devices  151 us
    psum x1, blocking collectives, local(): lax.psum((attn_gain_part, mlp_gain_part, query_gain_part, key_gain_part),...  150 us
    all_gather x1, waiting for transfers between devices, local(): lax.all_gather(down_cast, 'shard', axis=0, tiled=True)  133 us
    all_gather x1, waiting for transfers between devices, local(): up_piece = lax.all_gather(up_cast, 'shard', axis=0, tiled=True)  133 us
    dot_general x16, matrix products, head_scores(): lax.dot_general(query_heads[head_index], head_keys, contract_last, prefer...  96.6 us
    reduce_scatter x1, waiting for transfers between devices, local(): lax.psum_scatter(value_grads.astype(jnp.bfloat16), 'shard', scatter_dimen...  95 us
    all_gather x1, waiting for transfers between devices, local(): gate_piece = lax.all_gather(gate_cast, 'shard', axis=0, tiled=True)  93 us
  transfers between devices with their start and end apart: 19, of which 17 were waited for; matrix products, arithmetic and copies ran while one was open for 13% of the time, Pallas kernels for 0%

commit v1 on v0

v1 whole, which is shorter than its diff:
```python
import jax
import jax.numpy as jnp
from jax import lax
from jax.experimental import pallas as pl
from jax.experimental.pallas import tpu as pltpu
from jax.sharding import Mesh
from jax.sharding import PartitionSpec as P

HEAD_DIM = 128
RING = 4
BLOCK = 256
BLOCKS = 16
TILE = 512
TILES = 8
PROMPT_TILES = 6

norm_eps = 1e-06
rope_base = 1000000.0
score_scale = HEAD_DIM ** (-0.5)
score_scale_log2 = score_scale * 1.4426950408889634
contract_first = (((0,), (0,)), ((), ()))
contract_last = (((1,), (1,)), ((), ()))
GROUP_AXES = ("y", "x_hi", "core")
ALL_AXES = ("x_lo", "z", "y", "x_hi", "core")
low = jnp.bfloat16


def inverse_rms(values):
    return lax.rsqrt(jnp.mean(values * values, axis=-1, keepdims=True) + norm_eps)


def normalize(values):
    return values * inverse_rms(values)


def shift(values, axis, by, size=RING):
    return lax.ppermute(values, axis, [(i, (i + by) % size) for i in range(size)])


def gather_z(values):
    return jnp.concatenate(
        [values, shift(values, "z", 1), shift(values, "z", 2), shift(values, "z", 3)], axis=0
    )


def scatter_z(partial):
    rows = partial.shape[0] // RING
    blocks = [partial[r * rows : (r + 1) * rows] for r in range(RING)]
    total = blocks[0].astype(jnp.float32)
    for r in range(1, RING):
        total = total + shift(blocks[r].astype(low), "z", -r).astype(jnp.float32)
    return total


def forward_kernel(order, q_ref, k_ref, v_ref, mixed_ref, mixed_t_ref, log_ref, k_all, v_t, acc, total):
    tile = pl.program_id(0)

    @pl.when(tile == 0)
    def _():
        for at in range(BLOCKS):
            k_all[at * BLOCK : (at + 1) * BLOCK, :] = k_ref[order[at]]
            v_t[at // 2, :, (at % 2) * BLOCK : (at % 2 + 1) * BLOCK] = (
                v_ref[order[at]].astype(jnp.float32).T.astype(low)
            )

    queries = jnp.concatenate([q_ref[order[2 * tile]], q_ref[order[2 * tile + 1]]], axis=0)
    acc[...] = jnp.zeros_like(acc)
    total[...] = jnp.zeros_like(total)

    def chunk(at, masked):
        keys = k_all[pl.ds(pl.multiple_of(at * TILE, TILE), TILE), :]
        scores = lax.dot_general(keys, queries, contract_last, preferred_element_type=jnp.float32)
        weights = jnp.exp2(scores * score_scale_log2)
        if masked:
            key_row = lax.broadcasted_iota(jnp.int32, (TILE, TILE), 0)
            query_row = lax.broadcasted_iota(jnp.int32, (TILE, TILE), 1)
            weights = jnp.where(key_row <= query_row, weights, 0.0)
        total[...] += jnp.sum(weights, axis=0, keepdims=True)
        acc[...] += jnp.dot(v_t[at], weights.astype(low), preferred_element_type=jnp.float32)

    @pl.loop(0, jnp.minimum(tile, PROMPT_TILES))
    def _(at):
        chunk(at, False)

    chunk(tile, True)
    mixed_t = acc[...] / total[...]
    mixed_t_ref[tile] = mixed_t
    log_ref[tile] = jnp.log2(total[...])
    mixed = mixed_t.T.astype(low)
    mixed_ref[order[2 * tile]] = mixed[:BLOCK]
    mixed_ref[order[2 * tile + 1]] = mixed[BLOCK:]


def attention_forward(order, queries, keys, values):
    whole = pl.BlockSpec(memory_space=pltpu.VMEM)
    return pl.pallas_call(
        forward_kernel,
        out_shape=(
            jax.ShapeDtypeStruct((BLOCKS, BLOCK, HEAD_DIM), low),
            jax.ShapeDtypeStruct((TILES, HEAD_DIM, TILE), jnp.float32),
            jax.ShapeDtypeStruct((TILES, 1, TILE), jnp.float32),
        ),
        grid_spec=pltpu.PrefetchScalarGridSpec(
            num_scalar_prefetch=1,
            grid=(TILES,),
            in_specs=[whole] * 3,
            out_specs=(whole, whole, whole),
            scratch_shapes=[
                pltpu.VMEM((BLOCKS * BLOCK, HEAD_DIM), low),
                pltpu.VMEM((TILES, HEAD_DIM, TILE), low),
                pltpu.VMEM((HEAD_DIM, TILE), jnp.float32),
                pltpu.VMEM((1, TILE), jnp.float32),
            ],
        ),
        compiler_params=pltpu.CompilerParams(vmem_limit_bytes=40 * 1024 * 1024),
        cost_estimate=pl.CostEstimate(
            flops=1024, bytes_accessed=1024, transcendentals=0
        ),
    )(order, queries, keys, values)


def backward_kernel(
    order,
    q_ref,
    k_ref,
    v_ref,
    g_ref,
    mixed_t_ref,
    log_ref,
    q_out,
    k_out,
    v_out,
    k_all,
    v_all,
    k_t,
    q_acc,
    k_acc,
    v_acc,
):
    tile = pl.program_id(0)

    @pl.when(tile == 0)
    def _():
        for at in range(BLOCKS):
            rows = slice(at * BLOCK, (at + 1) * BLOCK)
            keys = k_ref[order[at]]
            k_all[rows, :] = keys
            v_all[rows, :] = v_ref[order[at]]
            k_t[at // 2, :, (at % 2) * BLOCK : (at % 2 + 1) * BLOCK] = (
                keys.astype(jnp.float32).T.astype(low)
            )
        k_acc[...] = jnp.zeros_like(k_acc)
        v_acc[...] = jnp.zeros_like(v_acc)

    queries = jnp.concatenate([q_ref[order[2 * tile]], q_ref[order[2 * tile + 1]]], axis=0)
    grads = jnp.concatenate([g_ref[order[2 * tile]], g_ref[order[2 * tile + 1]]], axis=0)
    grads_t = grads.astype(jnp.float32).T
    shared = jnp.sum(grads_t * mixed_t_ref[tile], axis=0, keepdims=True)
    logs = log_ref[tile]
    q_acc[...] = jnp.zeros_like(q_acc)

    def chunk(at, masked):
        rows = pl.ds(pl.multiple_of(at * TILE, TILE), TILE)
        scores = lax.dot_general(
            k_all[rows, :], queries, contract_last, preferred_element_type=jnp.float32
        )
        probs = jnp.exp2(scores * score_scale_log2 - logs)
        if masked:
            key_row = lax.broadcasted_iota(jnp.int32, (TILE, TILE), 0)
            query_row = lax.broadcasted_iota(jnp.int32, (TILE, TILE), 1)
            probs = jnp.where(key_row <= query_row, probs, 0.0)
        prob_grads = lax.dot_general(
            v_all[rows, :], grads, contract_last, preferred_element_type=jnp.float32
        )
        score_grads = (probs * (prob_grads - shared)).astype(low)
        v_acc[rows, :] += jnp.dot(probs.astype(low), grads, preferred_element_type=jnp.float32)
        k_acc[rows, :] += jnp.dot(score_grads, queries, preferred_element_type=jnp.float32)
        q_acc[...] += jnp.dot(k_t[at], score_grads, preferred_element_type=jnp.float32)

    @pl.loop(0, jnp.minimum(tile, PROMPT_TILES))
    def _(at):
        chunk(at, False)

    chunk(tile, True)
    query_grad = (q_acc[...] * score_scale).T.astype(low)
    q_out[order[2 * tile]] = query_grad[:BLOCK]
    q_out[order[2 * tile + 1]] = query_grad[BLOCK:]

    @pl.when(tile == TILES - 1)
    def _():
        for at in range(BLOCKS):
            rows = slice(at * BLOCK, (at + 1) * BLOCK)
            k_out[order[at]] = (k_acc[rows, :] * score_scale).astype(low)
            v_out[order[at]] = v_acc[rows, :].astype(low)


def attention_backward(order, queries, keys, values, grads, mixed_t, logs):
    whole = pl.BlockSpec(memory_space=pltpu.VMEM)
    rows = BLOCKS * BLOCK
    return pl.pallas_call(
        backward_kernel,
        out_shape=(jax.ShapeDtypeStruct((BLOCKS, BLOCK, HEAD_DIM), low),) * 3,
        grid_spec=pltpu.PrefetchScalarGridSpec(
            num_scalar_prefetch=1,
            grid=(TILES,),
            in_specs=[whole] * 6,
            out_specs=(whole, whole, whole),
            scratch_shapes=[
                pltpu.VMEM((rows, HEAD_DIM), low),
                pltpu.VMEM((rows, HEAD_DIM), low),
                pltpu.VMEM((TILES, HEAD_DIM, TILE), low),
                pltpu.VMEM((HEAD_DIM, TILE), jnp.float32),
                pltpu.VMEM((rows, HEAD_DIM), jnp.float32),
                pltpu.VMEM((rows, HEAD_DIM), jnp.float32),
            ],
        ),
        compiler_params=pltpu.CompilerParams(vmem_limit_bytes=48 * 1024 * 1024),
        cost_estimate=pl.CostEstimate(
            flops=1024, bytes_accessed=1024, transcendentals=0
        ),
    )(order, queries, keys, values, grads, mixed_t, logs)


def mlp_kernel(second_ref, cot_ref, gate_ref, up_ref, down_ref, *refs):
    inner_ref, both_ref, grad_ref, acc = refs[-4:]
    at = pl.program_id(0)
    step = gate_ref.shape[1]
    second = second_ref[...]
    gate_weight = gate_ref[...]
    up_weight = up_ref[...]
    gate_act = jnp.dot(second, gate_weight, preferred_element_type=jnp.float32)
    up_act = jnp.dot(second, up_weight, preferred_element_type=jnp.float32)
    inner_grad = jnp.dot(cot_ref[...], down_ref[...], preferred_element_type=jnp.float32)
    sigmoid = 1.0 / (1.0 + jnp.exp(-gate_act))
    silu = gate_act * sigmoid
    inner_ref[0] = (silu * up_act).astype(low)
    gate_grad = (inner_grad * up_act * (sigmoid * (1.0 + gate_act * (1.0 - sigmoid)))).astype(low)
    up_grad = (inner_grad * silu).astype(low)
    both_ref[0, :, pl.ds(pl.multiple_of(at * step, step), step)] = gate_grad
    up_at = (pl.num_programs(0) + at) * step
    both_ref[0, :, pl.ds(pl.multiple_of(up_at, step), step)] = up_grad
    part = lax.dot_general(
        gate_grad, gate_weight, contract_last, preferred_element_type=jnp.float32
    ) + lax.dot_general(up_grad, up_weight, contract_last, preferred_element_type=jnp.float32)

    @pl.when(at == 0)
    def _():
        acc[...] = part

    @pl.when(at > 0)
    def _():
        acc[...] += part

    @pl.when(at == pl.num_programs(0) - 1)
    def _():
        grad_ref[...] = acc[...].astype(low)


def mlp_block(block, second, cot, weights, held):
    rows, width = second.shape
    hidden_width = weights.shape[1] // 3
    step = 256
    steps = hidden_width // step
    whole = pl.BlockSpec((rows, width), lambda c: (0, 0))
    kept = pl.BlockSpec((1, rows, step), lambda c: (block, 0, c))
    kept_both = pl.BlockSpec((1, rows, 2 * hidden_width), lambda c: (block, 0, 0))
    return pl.pallas_call(
        mlp_kernel,
        grid=(steps,),
        in_specs=[
            whole,
            whole,
            pl.BlockSpec((width, step), lambda c: (0, c)),
            pl.BlockSpec((width, step), lambda c: (0, steps + c)),
            pl.BlockSpec((width, step), lambda c: (0, 2 * steps + c)),
        ]
        + [pl.BlockSpec(memory_space=pl.ANY)] * len(held),
        out_specs=(kept, kept_both, whole),
        out_shape=(
            jax.ShapeDtypeStruct((RING, rows, hidden_width), low),
            jax.ShapeDtypeStruct((RING, rows, 2 * hidden_width), low),
            jax.ShapeDtypeStruct((rows, width), low),
        ),
        scratch_shapes=[pltpu.VMEM((rows, width), jnp.float32)],
        input_output_aliases={5 + i: i for i in range(len(held))},
        compiler_params=pltpu.CompilerParams(vmem_limit_bytes=40 * 1024 * 1024),
        cost_estimate=pl.CostEstimate(
            flops=2 * 5 * rows * width * hidden_width,
            bytes_accessed=2 * 3 * width * hidden_width,
            transcendentals=rows * hidden_width,
        ),
    )(second, cot, weights, weights, weights, *held)


def first_kernel(
    hidden_ref, gain_ref, weight_ref, cos_ref, sin_ref, query_gain, key_gain, first_ref, pre_ref, send_ref
):
    first = (normalize(hidden_ref[0].astype(jnp.float32)) * gain_ref[...]).astype(low)
    first_ref[0] = first
    pre = jnp.dot(first, weight_ref[...], preferred_element_type=jnp.float32)
    pre_ref[0] = pre
    cosine = cos_ref[0]
    sine = sin_ref[0]

    def turned(head, gain):
        values = normalize(pre[:, head * HEAD_DIM : (head + 1) * HEAD_DIM]) * gain
        return (values * cosine + pltpu.roll(values, HEAD_DIM // 2, 1) * sine).astype(low)

    for head in range(4):
        send_ref[head, 0] = turned(head, query_gain[...])
    for head in range(2):
        send_ref[2 * head, 1] = turned(4 + head, key_gain[...])
        send_ref[2 * head + 1, 1] = pre[:, (6 + head) * HEAD_DIM : (7 + head) * HEAD_DIM].astype(low)


def first_part(hidden_all, gain, weights, cosine, sine, query_gain, key_gain):
    _, rows, width = hidden_all.shape
    row = pl.BlockSpec((1, HEAD_DIM), lambda r: (0, 0))
    turn = pl.BlockSpec((1, rows, HEAD_DIM), lambda r: (r, 0, 0))
    return pl.pallas_call(
        first_kernel,
        grid=(RING,),
        in_specs=[
            pl.BlockSpec((1, rows, width), lambda r: (r, 0, 0)),
            pl.BlockSpec((1, width), lambda r: (0, 0)),
            pl.BlockSpec((width, 1024), lambda r: (0, 0)),
            turn,
            turn,
            row,
            row,
        ],
        out_specs=(
            pl.BlockSpec((1, rows, width), lambda r: (r, 0, 0)),
            pl.BlockSpec((1, rows, 1024), lambda r: (r, 0, 0)),
            pl.BlockSpec((4, 2, rows, HEAD_DIM), lambda r: (r, 0, 0, 0)),
        ),
        out_shape=(
            jax.ShapeDtypeStruct((RING, rows, width), low),
            jax.ShapeDtypeStruct((RING, rows, 1024), jnp.float32),
            jax.ShapeDtypeStruct((BLOCKS, 2, rows, HEAD_DIM), low),
        ),
        compiler_params=pltpu.CompilerParams(vmem_limit_bytes=40 * 1024 * 1024),
        cost_estimate=pl.CostEstimate(
            flops=2 * RING * rows * width * 1024,
            bytes_accessed=20 * 1024 * 1024,
            transcendentals=0,
        ),
    )(hidden_all, gain, weights, cosine, sine, query_gain, key_gain)


def first_back_kernel(
    back_ref, pre_ref, cos_ref, sin_ref, query_gain, key_gain, grad_ref, query_sum, key_sum
):
    cosine = cos_ref[0]
    sine = sin_ref[0]

    @pl.when(pl.program_id(0) == 0)
    def _():
        query_sum[...] = jnp.zeros_like(query_sum)
        key_sum[...] = jnp.zeros_like(key_sum)

    def back(grads, head, gain, sums):
        columns = slice(head * HEAD_DIM, (head + 1) * HEAD_DIM)
        values = pre_ref[0, :, columns]
        grads = grads.astype(jnp.float32)
        grads = grads * cosine - pltpu.roll(grads, HEAD_DIM // 2, 1) * sine
        scale = inverse_rms(values)
        normed = values * scale
        sums[...] += jnp.sum(grads * normed, axis=0, keepdims=True)
        scaled = grads * gain
        out = scale * (scaled - normed * jnp.mean(scaled * normed, axis=-1, keepdims=True))
        grad_ref[0, :, columns] = out.astype(low)

    for head in range(4):
        back(back_ref[head, 0], head, query_gain[...], query_sum)
    for head in range(2):
        back(back_ref[2 * head, 1], 4 + head, key_gain[...], key_sum)
        grad_ref[0, :, (6 + head) * HEAD_DIM : (7 + head) * HEAD_DIM] = back_ref[2 * head + 1, 1]


def first_back(returned, pre, cosine, sine, query_gain, key_gain):
    _, rows, _ = pre.shape
    row = pl.BlockSpec((1, HEAD_DIM), lambda r: (0, 0))
    turn = pl.BlockSpec((1, rows, HEAD_DIM), lambda r: (r, 0, 0))
    wide = pl.BlockSpec((1, rows, 1024), lambda r: (r, 0, 0))
    return pl.pallas_call(
        first_back_kernel,
        grid=(RING,),
        in_specs=[
            pl.BlockSpec((4, 2, rows, HEAD_DIM), lambda r: (r, 0, 0, 0)),
            wide,
            turn,
            turn,
            row,
            row,
        ],
        out_specs=(wide, row, row),
        out_shape=(
            jax.ShapeDtypeStruct((RING, rows, 1024), low),
            jax.ShapeDtypeStruct((1, HEAD_DIM), jnp.float32),
            jax.ShapeDtypeStruct((1, HEAD_DIM), jnp.float32),
        ),
        compiler_params=pltpu.CompilerParams(vmem_limit_bytes=40 * 1024 * 1024),
        cost_estimate=pl.CostEstimate(
            flops=1024, bytes_accessed=1024, transcendentals=0
        ),
    )(returned, pre, cosine, sine, query_gain, key_gain)


def to_heads(send):
    return lax.all_to_all(send, GROUP_AXES, 0, 0, tiled=True)


def after(value, *others):
    return lax.optimization_barrier((value, others))[0]


def ring_blocks(values):
    half = values.shape[0] // 2
    left = shift(values, "z", 1)
    right = shift(values, "z", 3)
    opposite = jnp.concatenate(
        [shift(left[:half], "z", 1), shift(right[half:], "z", 3)], axis=0
    )
    return [values, left, opposite, right]


def together(*values):
    return lax.optimization_barrier(values)


def place_kernel(z_ref, *refs):
    blocks, outs = refs[:RING], refs[RING:]
    for r in range(RING):
        slot = lax.rem(z_ref[0] - r + RING, RING)
        start = 0
        for out in outs:
            part = out.shape[1] // RING
            at = pl.multiple_of(slot * part, part)
            out[:, pl.ds(at, part)] = blocks[r][:, start : start + part].astype(jnp.float32)
            start += part


def place(z_at, blocks, widths):
    rows = blocks[0].shape[0]
    whole = pl.BlockSpec(memory_space=pltpu.VMEM)
    return pl.pallas_call(
        place_kernel,
        in_specs=[pl.BlockSpec(memory_space=pltpu.SMEM)] + [whole] * RING,
        out_specs=tuple(whole for _ in widths),
        out_shape=tuple(jax.ShapeDtypeStruct((rows, RING * part), jnp.float32) for part in widths),
        compiler_params=pltpu.CompilerParams(vmem_limit_bytes=24 * 1024 * 1024),
        cost_estimate=pl.CostEstimate(
            flops=0, bytes_accessed=rows * sum(widths) * 24, transcendentals=0
        ),
    )(z_at[None], *blocks)


def send_back(block, r):
    return shift(block, "z", -r)


def local(
    hidden_in,
    cotangent,
    segment_ids,
    positions,
    attn_gain,
    query_gain,
    key_gain,
    query_weight,
    key_weight,
    value_weight,
    out_weight,
    mlp_gain,
    gate_weight,
    up_weight,
    down_weight,
):
    f32 = jnp.float32
    rows, width = hidden_in.shape
    ring_rows = RING * rows
    z_at = lax.axis_index("z")
    y_at = lax.axis_index("y")
    core_at = lax.axis_index("core")
    my_index = (y_at * 2 + lax.axis_index("x_hi")) * 2 + core_at

    def columns(weight):
        part = weight.shape[1] // RING
        return lax.dynamic_slice_in_dim(weight, z_at * part, part, 1).astype(low)

    def gather(block):
        return lax.all_gather(block, GROUP_AXES, axis=0, tiled=True)

    own_places = lax.dynamic_slice_in_dim(positions, my_index * rows, rows)
    firsts = positions.reshape(BLOCKS, BLOCK)[:, 0]
    segments = segment_ids.reshape(BLOCKS, BLOCK)[:, 0]
    logical = firsts // BLOCK + jnp.maximum(segments - 1, 0) * 2
    numbers = jnp.arange(BLOCKS, dtype=jnp.int32)
    order = jnp.sum(jnp.where(logical[:, None] == numbers[None, :], numbers[:, None], 0), axis=0)
    notes = gather_z(jnp.concatenate([own_places, order, jnp.zeros((112,), jnp.int32)])[None])
    places = notes[:, :rows]
    order = lax.dynamic_index_in_dim(notes, y_at, 0, keepdims=False)[rows : rows + BLOCKS]

    gains = jnp.pad(
        jnp.stack([attn_gain, mlp_gain], axis=1).astype(low), ((0, 0), (0, HEAD_DIM - 2))
    )
    first_weights = gather(
        jnp.concatenate(
            [
                columns(query_weight),
                columns(key_weight),
                columns(value_weight),
                columns(out_weight),
                gains,
            ],
            axis=1,
        )
    )
    out_full = first_weights[:, 1024:1536]
    attn_scale = first_weights[:, 1536].astype(f32)[None]
    mlp_scale = first_weights[:, 1537].astype(f32)[None]
    mlp_weights = gather(
        jnp.concatenate([columns(gate_weight), columns(up_weight), columns(down_weight)], axis=1)
    )
    down_full = mlp_weights[:, 3072:]

    hidden_blocks = ring_blocks(hidden_in)
    cot_blocks = ring_blocks(after(cotangent, *hidden_blocks))
    frequency = rope_base ** (-2.0 * jnp.arange(HEAD_DIM // 2, dtype=f32) / HEAD_DIM)
    angles = places.astype(f32)[:, :, None] * frequency[None, None, :]
    cosine = jnp.cos(angles)
    sine = jnp.sin(angles)
    cosine = jnp.concatenate([cosine, cosine], axis=-1)
    sine = jnp.concatenate([-sine, sine], axis=-1)
    query_row = query_gain[None]
    key_row = key_gain[None]

    first_in, qkv_pre, send = first_part(
        jnp.stack(hidden_blocks), attn_scale, first_weights, cosine, sine, query_row, key_row
    )
    arrived = to_heads(send)
    head_queries = arrived[:, 0]
    own_pair = arrived[:, 1]
    other_pair = shift(own_pair, "core", 1, 2)
    head_keys = jnp.where(core_at == 0, own_pair, other_pair)
    head_values = jnp.where(core_at == 0, other_pair, own_pair)
    head_mixed, head_mixed_t, head_logs = attention_forward(
        order, head_queries, head_keys, head_values
    )
    head_mixed = after(head_mixed, *cot_blocks)

    def from_heads(values):
        return values.reshape(RING, 4, rows, HEAD_DIM).transpose(0, 2, 1, 3).reshape(ring_rows, 512)

    mixed = from_heads(to_heads(head_mixed))
    attn_out = lax.dot_general(mixed, out_full, contract_last, preferred_element_type=f32)
    hidden = hidden_in.astype(f32)
    middle = hidden + scatter_z(attn_out)
    middle_rms = inverse_rms(middle)
    second_norm = middle * middle_rms
    second_in = (second_norm * mlp_scale).astype(low)
    left = shift(second_in, "z", 1)
    right = shift(second_in, "z", 3)
    *held, own_part = mlp_block(0, second_in, cot_blocks[0], mlp_weights, ())
    held, own_part, left, right = together(held, own_part, left, right)
    half = rows // 2
    top = shift(left[:half], "z", 1)
    bottom = shift(right[half:], "z", 3)
    *held, left_part = mlp_block(1, left, cot_blocks[1], mlp_weights, held)
    left_back = send_back(left_part, 1)
    *held, right_part = mlp_block(3, right, cot_blocks[3], mlp_weights, held)
    right_back = send_back(right_part, 3)
    held, top, bottom = together(held, top, bottom)
    opposite = jnp.concatenate([top, bottom], axis=0)
    *held, opposite_part = mlp_block(2, opposite, cot_blocks[2], mlp_weights, held)
    opposite_back = send_back(opposite_part, 2)
    inner = held[0].reshape(ring_rows, 1536)
    both_grad = held[1].reshape(ring_rows, 3072)

    def weight_grad(left, right):
        return lax.dot_general(left, right, contract_first, preferred_element_type=f32).astype(low)

    def pair_start(term):
        term = term.reshape(8, 2, 128, term.shape[1])
        keep = lax.dynamic_index_in_dim(term, core_at, 1, keepdims=False)
        give = lax.dynamic_index_in_dim(term, 1 - core_at, 1, keepdims=False)
        return keep, shift(give, "core", 1, 2)

    def pair_sum(keep, come):
        return (keep.astype(f32) + come.astype(f32)).astype(low)

    def to_owners(pair):
        terms = lax.all_to_all(pair, ("y", "x_hi"), 0, 0, tiled=True)
        return jnp.sum(terms.astype(f32), axis=0).astype(low)

    def over_x(share):
        return share, shift(share, "x_lo", 1, 2)

    def over_z(pair):
        share = pair_sum(*pair)
        return [share] + [shift(share, "z", r) for r in range(1, RING)]

    second_all = jnp.concatenate([second_in, left, opposite, right], axis=0)
    cot_all = jnp.concatenate(cot_blocks, axis=0)
    down_term = weight_grad(cot_all, inner)
    left_back, right_back, opposite_back, down_term, both_grad = together(
        left_back, right_back, opposite_back, down_term, both_grad
    )
    down_pair = pair_start(down_term)

    second_grad = (
        own_part.astype(f32)
        + left_back.astype(f32)
        + right_back.astype(f32)
        + opposite_back.astype(f32)
    )
    mlp_gain_part = jnp.sum(second_grad * second_norm, axis=0)
    scaled_grad = second_grad * mlp_scale
    middle_grad = cotangent.astype(f32) + middle_rms * (
        scaled_grad - second_norm * jnp.mean(scaled_grad * second_norm, axis=-1, keepdims=True)
    )
    own_low = middle_grad.astype(low)
    left_low = shift(own_low, "z", 1)
    right_low = shift(own_low, "z", 3)
    down_sum = pair_sum(*down_pair)
    gate_term = weight_grad(second_all, both_grad[:, :1536])
    left_low, right_low, gate_term, down_sum, both_grad = together(
        left_low, right_low, gate_term, down_sum, both_grad
    )
    down_share = to_owners(down_sum)
    gate_pair = pair_start(gate_term)
    top_low = shift(left_low[:half], "z", 1)
    bottom_low = shift(right_low[half:], "z", 3)
    up_term = weight_grad(second_all, both_grad[:, 1536:])
    mlp_out = lax.dot_general(
        inner, down_full, contract_last, preferred_element_type=f32
    ).reshape(RING, rows, width)
    mlp_own = mlp_out[0].astype(low)
    mlp_rest = mlp_out[1:].astype(low)
    top_low, bottom_low, up_term, mlp_own, mlp_rest = together(
        top_low, bottom_low, up_term, mlp_own, mlp_rest
    )
    up_pair = pair_start(up_term)
    middle_low = jnp.concatenate([own_low, left_low, top_low, bottom_low, right_low], axis=0)
    mixed_grad = jnp.dot(middle_low, out_full, preferred_element_type=f32).astype(low)
    mixed_grad = mixed_grad.reshape(RING, rows, 4, HEAD_DIM).transpose(0, 2, 1, 3)
    mixed_grad, down_share = together(mixed_grad, down_share)
    head_grads = to_heads(mixed_grad.reshape(BLOCKS, rows, HEAD_DIM))
    down_pair = over_x(down_share)
    mlp_left = send_back(mlp_rest[0], 1)
    mlp_right = send_back(mlp_rest[2], 3)
    out_term = weight_grad(middle_low, mixed)
    gate_sum = pair_sum(*gate_pair)
    head_grads, out_term, gate_sum, down_pair, mlp_left, mlp_right, mlp_opposite = together(
        head_grads, out_term, gate_sum, down_pair, mlp_left, mlp_right, mlp_rest[1]
    )
    gate_share = to_owners(gate_sum)
    down_blocks = over_z(down_pair)
    out_pair = pair_start(out_term)

    query_grad, key_grad, value_grad = attention_backward(
        order, head_queries, head_keys, head_values, head_grads, head_mixed_t, head_logs
    )
    up_sum = pair_sum(*up_pair)
    out_sum = pair_sum(*out_pair)
    query_grad, gate_share, up_sum, out_sum = together(query_grad, gate_share, up_sum, out_sum)
    gate_pair = over_x(gate_share)
    mlp_opposite = send_back(mlp_opposite, 2)
    keep = jnp.where(core_at == 0, key_grad, value_grad)
    give = jnp.where(core_at == 0, value_grad, key_grad)
    pair_grad = (keep.astype(f32) + shift(give, "core", 1, 2).astype(f32)).astype(low)
    returned = to_heads(jnp.stack([query_grad, pair_grad], axis=1))
    returned, up_sum, gate_pair, down_blocks, mlp_opposite = together(
        returned, up_sum, gate_pair, down_blocks, mlp_opposite
    )
    up_share = to_owners(up_sum)
    gate_blocks = over_z(gate_pair)
    output = (
        middle
        + mlp_own.astype(f32)
        + mlp_left.astype(f32)
        + mlp_right.astype(f32)
        + mlp_opposite.astype(f32)
    ).astype(low)
    qkv_grad, query_gain_part, key_gain_part = first_back(
        returned, qkv_pre, cosine, sine, query_row, key_row
    )
    qkv_grad = qkv_grad.reshape(ring_rows, 1024)
    qkv_term = weight_grad(first_in.reshape(ring_rows, width), qkv_grad)
    qkv_pair = pair_start(qkv_term)
    first_partial = lax.dot_general(
        after(qkv_grad, qkv_term),
        first_weights[:, :1024],
        contract_last,
        preferred_element_type=f32,
    )
    qkv_pair, first_partial, up_share, gate_blocks = together(
        qkv_pair, first_partial.astype(low), up_share, gate_blocks
    )
    up_pair = over_x(up_share)
    qkv_share = to_owners(jnp.concatenate([pair_sum(*qkv_pair), out_sum], axis=2))
    first_blocks = [first_partial[r * rows : (r + 1) * rows] for r in range(RING)]
    first_blocks = [first_blocks[0]] + [send_back(first_blocks[r], r) for r in range(1, RING)]
    first_blocks, qkv_share, up_pair = together(first_blocks, qkv_share, up_pair)
    first_grad = sum(block.astype(f32) for block in first_blocks)
    hidden_rms = inverse_rms(hidden)
    own_norm = hidden * hidden_rms
    attn_gain_part = jnp.sum(first_grad * own_norm, axis=0)
    scaled_first = first_grad * attn_scale
    hidden_grad = (
        middle_grad
        + hidden_rms
        * (scaled_first - own_norm * jnp.mean(scaled_first * own_norm, axis=-1, keepdims=True))
    ).astype(low)

    (down_grad_out,) = place(z_at, down_blocks, (1536,))
    (gate_grad_out,) = place(z_at, gate_blocks, (1536,))
    (up_grad_out,) = place(z_at, over_z(up_pair), (1536,))
    query_grad_out, key_grad_out, value_grad_out, out_grad_out = place(
        z_at, over_z(over_x(qkv_share)), (512, 256, 256, 512)
    )

    gain_send = jnp.stack(
        [
            attn_gain_part.reshape(BLOCKS, HEAD_DIM),
            mlp_gain_part.reshape(BLOCKS, HEAD_DIM),
            jnp.broadcast_to(query_gain_part, (BLOCKS, HEAD_DIM)),
            jnp.broadcast_to(key_gain_part, (BLOCKS, HEAD_DIM)),
        ],
        axis=1,
    )
    gain_sum = jnp.sum(to_heads(gain_send), axis=0)
    gain_sum = gain_sum + shift(gain_sum, "x_lo", 1, 2)
    pair_sum = gain_sum + shift(gain_sum, "z", 2)
    gain_sum = pair_sum + shift(pair_sum, "z", 1)

    return (
        output,
        hidden_grad,
        gain_sum[0],
        gain_sum[2],
        gain_sum[3],
        query_grad_out,
        key_grad_out,
        value_grad_out,
        out_grad_out,
        gain_sum[1],
        gate_grad_out,
        up_grad_out,
        down_grad_out,
    )


def solution(mesh):
    fine = Mesh(mesh.devices.reshape(2, 4, 4, 2, 2), ALL_AXES)
    rep = ("x_lo", "z")
    row = P(ALL_AXES, None)
    part = P(GROUP_AXES)
    weight = P(GROUP_AXES, None)
    in_specs = (
        row,
        row,
        P(rep),
        P(rep),
        part,
        P(),
        P(),
        weight,
        weight,
        weight,
        weight,
        part,
        weight,
        weight,
        weight,
    )
    out_specs = (
        row,
        row,
        part,
        P(),
        P(),
        weight,
        weight,
        weight,
        weight,
        part,
        weight,
        weight,
        weight,
    )
    return jax.shard_map(local, mesh=fine, in_specs=in_specs, out_specs=out_specs, check_vma=False)
```

time: 2560 us -> 822 us (0.32)
  waiting for transfers between devices: 1630 us -> 280 us
  matrix products: 445 us -> 67.1 us
  blocking collectives: 191 us -> 29.4 us
  Pallas kernels: 0 us -> 153 us
  starting transfers between devices: 1.17 us -> 123 us
  other arithmetic: 162 us -> 73.2 us
    reduce_scatter x8 -> x0, waiting for transfers between devices: 876 us -> none  [the longest x6 760 us: owner_share(): lax.psum_scatter(term.astype(jnp.bfloat16), 'shard', scatter_dimension=0,...]
    all_gather x9 -> x2, waiting for transfers between devices: 607 us -> 18.7 us  [gather(): return lax.all_gather(block, GROUP_AXES, axis=0, tiled=True)]
    dot_general x77 -> x9, matrix products: 445 us -> 67.1 us  [the longest x5 40.7 us: weight_grad(): lax.dot_general(left, right, contract_first, preferred_element_type=f32)]
    ppermute x0 -> x57, waiting for transfers between devices: none -> 213 us  [shift(): lax.ppermute(values, axis, [(i, (i + by) % size) for i in range(size)])]
    pallas_call x0 -> x12, Pallas kernels: none -> 153 us  [the longest x4 79.7 us: mlp_block(): pl.pallas_call(mlp_kernel, grid=(steps,), in_specs=[whole, whole, pl.Bloc...]
    unnamed x20 -> x2, waiting for transfers between devices: 151 us -> 0.03 us
    psum x1 -> x0, blocking collectives: 150 us -> none  [local(): lax.psum((attn_gain_part, mlp_gain_part, query_gain_part, key_gain_part),...]
    convert_element_type x36 -> x13, other arithmetic: 119 us -> 31.1 us  [the longest x9 19.6 us: pair_sum(): return (keep.astype(f32) + come.astype(f32)).astype(low)]
  transfers between devices with their start and end apart: 19 -> 67, of which waited for: 17 -> 29; matrix products, arithmetic and copies ran while one was open for 13% -> 21% of each run, Pallas kernels for 0% -> 19%
where the time goes in v1:
time: 822 us; the launch traced here: 812 us
  waiting for transfers between devices  280 us (34%)
  Pallas kernels  153 us (19%)
  starting transfers between devices  123 us (15%)
  other arithmetic  73.2 us (9%)
  local copies, waits for them, and re-layouts  70 us (9%)
  matrix products  67.1 us (8%)
  blocking collectives  29.4 us (4%)
  between operations  15.4 us (2%)
    ppermute x57, waiting for transfers between devices, shift(): lax.ppermute(values, axis, [(i, (i + by) % size) for i in range(size)])  213 us
    pallas_call x4, Pallas kernels, mlp_block(): pl.pallas_call(mlp_kernel, grid=(steps,), in_specs=[whole, whole, pl.Bloc...  79.7 us
    ppermute x57, starting transfers between devices, shift(): lax.ppermute(values, axis, [(i, (i + by) % size) for i in range(size)])  64.6 us
    dot_general x5, matrix products, weight_grad(): lax.dot_general(left, right, contract_first, preferred_element_type=f32)  40.7 us
    all_to_all x4, waiting for transfers between devices, to_owners(): terms = lax.all_to_all(pair, ('y', 'x_hi'), 0, 0, tiled=True)  39.5 us
    pallas_call x1, Pallas kernels, attention_backward(): pl.pallas_call(backward_kernel, out_shape=(jax.ShapeDtypeStruct((BLOCKS,...  33.3 us
    unnamed x151, local copies, waits for them, and re-layouts  30.1 us
    all_to_all x4, starting transfers between devices, to_owners(): terms = lax.all_to_all(pair, ('y', 'x_hi'), 0, 0, tiled=True)  29.4 us
  transfers between devices with their start and end apart: 67, of which 29 were waited for; matrix products, arithmetic and copies ran while one was open for 21% of the time, Pallas kernels for 19%

profile of v1, /device:TPU:4, one launch (start us, length us, event | category | flops | bytes accessed | tf_op | source)
XLA Modules:
  0.0 811.6 jit_solution(3935196527034720817)
XLA Ops:
  25.8 19.0 %collective-permute-done.2 = s32[1,384]{1,0:T(1,128)S(1)} collective-permute-done((s32[1,384]{1,0:T(1,128)S(1)}, s32[1,384]{1,0:T(1,128)S(1)}, u32[]{:S(2)}, u32[]{:S(2)}) %collective-permute-start.2) | collective-permute-done | bytes 1568 | tf_op jit(solution)/shard_map/ppermute | solution.py:37
  62.8 18.7 %all-gather.3.cloned.1.call-done.weight_ref = bf16[2048,1664]{1,0:T(8,128)(2,1)} async-done(((bf16[128,1664]{1,0:T(8,128)(2,1)}), bf16[2048,1664]{1,0:T(8,128)(2,1)}) %all-gather.3.cloned.1.call-update) | async-done | bytes 6815760 | tf_op jit(solution)/shard_map/all_gather | solution.py:493
  83.3 10.2 %shard_map.246 = (bf16[4,256,2048]{2,1,0:T(8,128)(2,1)S(1)}, f32[4,256,1024]{2,1,0:T(8,128)S(1)}, bf16[16,2,256,128]{3,2,1,0:T(8,128)(2,1)}) custom-call(bf16[4,256,2048]{2,1,0:T(8,128)(2,1)} %pad_maximum_fusion.hidden_ref, f32[1,2048]{1,0:T(1,128)S(1)} %bitcast.112, bf16[2048,1664]{1,0:T(8,128)(2,1)} %all-gather.3.cloned.1.call-done.weight_ref, ...), custom_call_target="tpu_custom_call" | custom-call | flops 4294967296 | bytes 20971520 | tf_op jit(solution)/shard_map/pallas_call | solution.py:320
  108.1 23.2 %collective-permute-done.8.cot_ref = bf16[256,2048]{1,0:T(8,128)(2,1)S(1)} collective-permute-done((bf16[256,2048]{1,0:T(8,128)(2,1)S(1)}, bf16[256,2048]{1,0:T(8,128)(2,1)S(1)}, u32[]{:S(2)}, u32[]{:S(2)}) %collective-permute-start.8) | collective-permute-done | bytes 1048608 | tf_op jit(solution)/shard_map/ppermute | solution.py:37
  132.5 8.9 %all-to-all-done = bf16[16,2,256,128]{3,2,1,0:T(8,128)(2,1)} async-done(((bf16[16,2,256,128]{3,2,1,0:T(8,128)(2,1)}), bf16[16,2,256,128]{3,2,1,0:T(8,128)(2,1)}, u32[]{:S(2)}, u32[]{:S(2)}) %all-to-all-start) | async-done | bytes 2097184 | tf_op jit(solution)/shard_map/all_to_all | solution.py:411
  148.1 10.4 %collective-permute-done.11 = bf16[128,2048]{1,0:T(8,128)(2,1)S(1)} collective-permute-done((bf16[128,2048]{1,0:T(8,128)(2,1)S(1)}, bf16[128,2048]{1,0:T(8,128)(2,1)S(1)}, u32[]{:S(2)}, u32[]{:S(2)}) %collective-permute-start.11) | collective-permute-done | bytes 524320 | tf_op jit(solution)/shard_map/ppermute | solution.py:37
  161.9 18.4 %shard_map.247 = (bf16[16,256,128]{2,1,0:T(8,128)(2,1)S(1)}, f32[8,128,512]{2,1,0:T(8,128)S(1)}, f32[8,1,512]{2,1,0:T(1,128)S(1)}) custom-call(s32[16]{0:T(128)S(1)} %dynamic-slice_bitcast_fusion.6.order, bf16[16,256,128]{2,1,0:T(8,128)(2,1)S(1)} %get-tuple-element.227.q_ref, bf16[16,256,128]{2,1,0:T(8,128)(2,1)S(1)} %get-tuple-element.225.k_ref, ...), custom_call_target="tpu_custom_call" | custom-call | flops 1024 | bytes 1024 | tf_op jit(solution)/shard_map/pallas_call | solution.py:96
  180.3 29.4 %all_to_all.45 = bf16[16,256,128]{2,1,0:T(8,128)(2,1)S(1)} all-to-all(bf16[16,256,128]{2,1,0:T(8,128)(2,1)S(1)} %get-tuple-element.109), channel_id=1, replica_groups=mesh['x_lo'=2,'z'=4,'y'=4,'x_hi'=2,'core'=2] {'y','x_hi','core'}, dimensions={0} | all-to-all | bytes 2097152 | tf_op jit(solution)/shard_map/all_to_all | solution.py:411
  220.6 43.6 %collective-permute-done.12 = bf16[256,2048]{1,0:T(8,128)(2,1)S(1)} collective-permute-done((bf16[256,2048]{1,0:T(8,128)(2,1)S(1)}, bf16[256,2048]{1,0:T(8,128)(2,1)S(1)}, u32[]{:S(2)}, u32[]{:S(2)}) %collective-permute-start.12) | collective-permute-done | bytes 1048608 | tf_op jit(solution)/shard_map/ppermute | solution.py:37
  276.4 20.1 %shard_map.248 = (bf16[4,256,1536]{2,1,0:T(8,128)(2,1)S(1)}, bf16[4,256,3072]{2,1,0:T(8,128)(2,1)S(1)}, bf16[256,2048]{1,0:T(8,128)(2,1)S(1)}) custom-call(bf16[256,2048]{1,0:T(8,128)(2,1)} %get-tuple-element.206.second_ref, bf16[256,2048]{1,0:T(8,128)(2,1)S(1)} %copy-done.4, bf16[2048,4608]{1,0:T(8,128)(2,1)} %all-gather.5.cloned.1.call-done.gate_ref.up_ref.down_ref, ...), custom_call_target="tpu_custom_call" | custom-call | flops 8053063680 | bytes 18874368 | tf_op jit(solution)/shard_map/pallas_call | solution.py:267
  303.6 20.0 %shard_map.249 = (bf16[4,256,1536]{2,1,0:T(8,128)(2,1)S(1)}, bf16[4,256,3072]{2,1,0:T(8,128)(2,1)S(1)}, bf16[256,2048]{1,0:T(8,128)(2,1)S(1)}) custom-call(bf16[256,2048]{1,0:T(8,128)(2,1)} %collective-permute-done.15.second_ref, bf16[256,2048]{1,0:T(8,128)(2,1)S(1)} %collective-permute-done.8.cot_ref, ...), custom_call_target="tpu_custom_call", output_to_operand_aliasing={{0}: (5, {}), {1}: (6, {})} | custom-call | flops 8053063680 | bytes 18874368 | tf_op jit(solution)/shard_map/pallas_call | solution.py:267
  325.2 20.1 %shard_map.250 = (bf16[4,256,1536]{2,1,0:T(8,128)(2,1)S(1)}, bf16[4,256,3072]{2,1,0:T(8,128)(2,1)S(1)}, bf16[256,2048]{1,0:T(8,128)(2,1)S(1)}) custom-call(bf16[256,2048]{1,0:T(8,128)(2,1)} %collective-permute-done.16.second_ref, bf16[256,2048]{1,0:T(8,128)(2,1)S(1)} %collective-permute-done.10.cot_ref, ...), custom_call_target="tpu_custom_call", output_to_operand_aliasing={{0}: (5, {}), {1}: (6, {})} | custom-call | flops 8053063680 | bytes 18874368 | tf_op jit(solution)/shard_map/pallas_call | solution.py:267
  349.1 19.5 %shard_map.251 = (bf16[4,256,1536]{2,1,0:T(8,128)(2,1)S(1)}, bf16[4,256,3072]{2,1,0:T(8,128)(2,1)S(1)}, bf16[256,2048]{1,0:T(8,128)(2,1)S(1)}) custom-call(bf16[256,2048]{1,0:T(8,128)(2,1)S(1)} %pad_maximum_fusion.4.second_ref, bf16[256,2048]{1,0:T(8,128)(2,1)S(1)} %copy-done.13, ...), custom_call_target="tpu_custom_call", output_to_operand_aliasing={{0}: (5, {}), {1}: (6, {})} | custom-call | flops 8053063680 | bytes 18874368 | tf_op jit(solution)/shard_map/pallas_call | solution.py:267
  377.3 8.8 %fusion.7 = bf16[1024,2048]{1,0:T(8,128)(2,1)S(1)} fusion(bf16[1024,1536]{1,0:T(8,128)(2,1)S(1)} %bitcast.110, bf16[2048,4608]{1,0:T(8,128)(2,1)} %all-gather.5.cloned.1.call-done.gate_ref.up_ref.down_ref), kind=kOutput, calls=%fused_computation.16 | convolution fusion | flops 6444548096 | bytes 13631488 | tf_op jit(solution)/shard_map/dot_general | solution.py:636
  403.9 11.1 %convolution_convert_fusion.1 = bf16[2048,1536]{1,0:T(8,128)(2,1)} fusion(bf16[1024,2048]{1,0:T(8,128)(2,1)} %constant_dynamic-update-slice_fusion.10, bf16[1024,3072]{1,0:T(8,128)(2,1)S(1)} %bitcast.107), kind=kOutput, calls=%fused_computation.2 | convolution fusion | flops 6445596672 | bytes 13631488 | tf_op jit(solution)/shard_map/dot_general | solution.py:582
  417.6 9.9 %collective-permute-done.23 = bf16[256,2048]{1,0:T(8,128)(2,1)} collective-permute-done((bf16[256,2048]{1,0:T(8,128)(2,1)S(1)}, bf16[256,2048]{1,0:T(8,128)(2,1)}, u32[]{:S(2)}, u32[]{:S(2)}) %collective-permute-start.23) | collective-permute-done | bytes 1048608 | tf_op jit(solution)/shard_map/ppermute | solution.py:37
  447.5 11.2 %convolution_convert_fusion = bf16[2048,1536]{1,0:T(8,128)(2,1)} fusion(bf16[1024,2048]{1,0:T(8,128)(2,1)} %constant_dynamic-update-slice_fusion.10, bf16[1024,3072]{1,0:T(8,128)(2,1)S(1)} %bitcast.108), kind=kOutput, calls=%fused_computation.1 | convolution fusion | flops 6445596672 | bytes 13631488 | tf_op jit(solution)/shard_map/dot_general | solution.py:582
  522.3 33.3 %shard_map.252 = (bf16[16,256,128]{2,1,0:T(8,128)(2,1)S(1)}, bf16[16,256,128]{2,1,0:T(8,128)(2,1)S(1)}, bf16[16,256,128]{2,1,0:T(8,128)(2,1)S(1)}) custom-call(s32[16]{0:T(128)S(1)} %copy-done.28, bf16[16,256,128]{2,1,0:T(8,128)(2,1)S(1)} %copy-done.9, bf16[16,256,128]{2,1,0:T(8,128)(2,1)S(1)} %copy-done.7, bf16[16,256,128]{2,1,0:T(8,128)(2,1)} %copy-done.5, ...), custom_call_target="tpu_custom_call" | custom-call | flops 1024 | bytes 1024 | tf_op jit(solution)/shard_map/pallas_call | solution.py:200
  581.9 26.5 %collective-permute-done.37.refs_3_ = bf16[128,1536]{1,0:T(8,128)(2,1)S(1)} collective-permute-done((bf16[128,1536]{1,0:T(8,128)(2,1)S(1)}, bf16[128,1536]{1,0:T(8,128)(2,1)S(1)}, u32[]{:S(2)}, u32[]{:S(2)}) %collective-permute-start.37) | collective-permute-done | bytes 393248 | tf_op jit(solution)/shard_map/ppermute | solution.py:37
  644.7 8.3 %fusion.10 = bf16[1024,2048]{1,0:T(8,128)(2,1)} fusion(bf16[1024,1024]{1,0:T(8,128)(2,1)S(1)} %bitcast.119, bf16[2048,1664]{1,0:T(8,128)(2,1)} %all-gather.3.cloned.1.call-done.weight_ref), kind=kOutput, calls=%fused_computation.17 | convolution fusion | flops 4297064448 | bytes 10485760 | tf_op jit(solution)/shard_map/dot_general | solution.py:692
  653.0 11.8 %all-to-all-done.6 = bf16[8,128,1536]{2,1,0:T(8,128)(2,1)} async-done(((bf16[8,128,1536]{2,1,0:T(8,128)(2,1)}), bf16[8,128,1536]{2,1,0:T(8,128)(2,1)}, u32[]{:S(2)}, u32[]{:S(2)}) %all-to-all-start.6) | async-done | bytes 3145760 | tf_op jit(solution)/shard_map/all_to_all | solution.py:594
  689.0 27.7 %all-to-all-done.7 = bf16[8,128,1536]{2,1,0:T(8,128)(2,1)} async-done(((bf16[8,128,1536]{2,1,0:T(8,128)(2,1)}), bf16[8,128,1536]{2,1,0:T(8,128)(2,1)}, u32[]{:S(2)}, u32[]{:S(2)}) %all-to-all-start.7) | async-done | bytes 3145760 | tf_op jit(solution)/shard_map/all_to_all | solution.py:594
  724.0 8.3 %collective-permute-done.45 = bf16[256,2048]{1,0:T(8,128)(2,1)} collective-permute-done((bf16[256,2048]{1,0:T(8,128)(2,1)}, bf16[256,2048]{1,0:T(8,128)(2,1)}, u32[]{:S(2)}, u32[]{:S(2)}) %collective-permute-start.45) | collective-permute-done | bytes 1048608 | tf_op jit(solution)/shard_map/ppermute | solution.py:37
  765.2 15.0 %collective-permute-done.48 = f32[4,128]{1,0:T(4,128)S(1)} collective-permute-done((f32[4,128]{1,0:T(4,128)S(1)}, f32[4,128]{1,0:T(4,128)S(1)}, u32[]{:S(2)}, u32[]{:S(2)}) %collective-permute-start.48) | collective-permute-done | bytes 2080 | tf_op jit(solution)/shard_map/ppermute | solution.py:37
  (375 shorter events, 362.8 us)
Async XLA Ops:
  7.2 74.3 %all-gather.3.cloned.1.call-start = ((), (), s32[]{:S(2)}) async-start(), calls=%async_computation.9 | async-start | bytes 7241728 | tf_op jit(solution)/shard_map/all_gather | solution.py:493
  15.2 261.2 %all-gather.5.cloned.1.call-start = ((), (), s32[]{:S(2)}) async-start(), calls=%async_computation.10 | async-start | bytes 20054016 | tf_op jit(solution)/shard_map/all_gather | solution.py:493
  97.5 43.9 %all-to-all-start = ((bf16[16,2,256,128]{3,2,1,0:T(8,128)(2,1)}), bf16[16,2,256,128]{3,2,1,0:T(8,128)(2,1)}, u32[]{:S(2)}, u32[]{:S(2)}) async-start(bf16[16,2,256,128]{3,2,1,0:T(8,128)(2,1)} %get-tuple-element.106), calls=%async_computation | async-start | bytes 4194304 | tf_op jit(solution)/shard_map/all_to_all | solution.py:411
  215.3 48.9 %collective-permute-start.12 = (bf16[256,2048]{1,0:T(8,128)(2,1)S(1)}, bf16[256,2048]{1,0:T(8,128)(2,1)S(1)}, u32[]{:S(2)}, u32[]{:S(2)}) collective-permute-start(bf16[256,2048]{1,0:T(8,128)(2,1)S(1)} %get-tuple-element.218), channel_id=1, source_target_pairs={{0,48},{16,0},{32,16},{48,32},{1,49},{17,1},{33,17},{49,33},{2,50}... | collective-permute-start | bytes 3145736 | tf_op jit(solution)/shard_map/ppermute | solution.py:37
  219.0 48.5 %collective-permute-start.14 = (bf16[256,2048]{1,0:T(8,128)(2,1)S(1)}, bf16[256,2048]{1,0:T(8,128)(2,1)S(1)}, u32[]{:S(2)}, u32[]{:S(2)}) collective-permute-start(bf16[256,2048]{1,0:T(8,128)(2,1)S(1)} %get-tuple-element.219), channel_id=1, source_target_pairs={{0,16},{16,32},{32,48},{48,0},{1,17},{17,33},{33,49},{49,1},{2,18}... | collective-permute-start | bytes 3145736 | tf_op jit(solution)/shard_map/ppermute | solution.py:37
  219.0 48.5 %collective-permute-start.13 = (bf16[256,2048]{1,0:T(8,128)(2,1)S(1)}, bf16[256,2048]{1,0:T(8,128)(2,1)S(1)}, u32[]{:S(2)}, u32[]{:S(2)}) collective-permute-start(bf16[256,2048]{1,0:T(8,128)(2,1)S(1)} %get-tuple-element.220), channel_id=1, source_target_pairs={{0,32},{16,48},{32,0},{48,16},{1,33},{17,49},{33,1},{49,17},{2,34}... | collective-permute-start | bytes 3145736 | tf_op jit(solution)/shard_map/ppermute | solution.py:37
  301.3 46.9 %collective-permute-start.20 = (bf16[128,2048]{1,0:T(8,128)(2,1)S(1)}, bf16[128,2048]{1,0:T(8,128)(2,1)S(1)}, u32[]{:S(2)}, u32[]{:S(2)}) collective-permute-start(bf16[128,2048]{1,0:T(8,128)(2,1)S(1)} %slice.143), channel_id=1, source_target_pairs={{0,48},{16,0},{32,16},{48,32},{1,49},{17,1},{33,17},{49,33},{2,50}... | collective-permute-start | bytes 1572872 | tf_op jit(solution)/shard_map/ppermute | solution.py:37
  301.7 46.5 %collective-permute-start.19 = (bf16[128,2048]{1,0:T(8,128)(2,1)S(1)}, bf16[128,2048]{1,0:T(8,128)(2,1)S(1)}, u32[]{:S(2)}, u32[]{:S(2)}) collective-permute-start(bf16[128,2048]{1,0:T(8,128)(2,1)S(1)} %slice.142), channel_id=1, source_target_pairs={{0,16},{16,32},{32,48},{48,0},{1,17},{17,33},{33,49},{49,1},{2,18}... | collective-permute-start | bytes 1572872 | tf_op jit(solution)/shard_map/ppermute | solution.py:37
  323.6 69.2 %collective-permute-start.17 = (bf16[256,2048]{1,0:T(8,128)(2,1)S(1)}, bf16[256,2048]{1,0:T(8,128)(2,1)S(1)}, u32[]{:S(2)}, u32[]{:S(2)}) collective-permute-start(bf16[256,2048]{1,0:T(8,128)(2,1)S(1)} %get-tuple-element.117), channel_id=1, source_target_pairs={{0,48},{16,0},{32,16},{48,32},{1,49},{17,1},{33,17},{49,33},{2,50}... | collective-permute-start | bytes 3145736 | tf_op jit(solution)/shard_map/ppermute | solution.py:37
  345.3 47.5 %collective-permute-start.18 = (bf16[256,2048]{1,0:T(8,128)(2,1)S(1)}, bf16[256,2048]{1,0:T(8,128)(2,1)S(1)}, u32[]{:S(2)}, u32[]{:S(2)}) collective-permute-start(bf16[256,2048]{1,0:T(8,128)(2,1)S(1)} %get-tuple-element.121), channel_id=1, source_target_pairs={{0,16},{16,32},{32,48},{48,0},{1,17},{17,33},{33,49},{49,1},{2,18}... | collective-permute-start | bytes 3145736 | tf_op jit(solution)/shard_map/ppermute | solution.py:37
  430.5 51.8 %all-to-all-start.2 = ((bf16[8,128,1536]{2,1,0:T(8,128)(2,1)}), bf16[8,128,1536]{2,1,0:T(8,128)(2,1)S(1)}, u32[]{:S(2)}, u32[]{:S(2)}) async-start(bf16[8,128,1536]{2,1,0:T(8,128)(2,1)} %fusion.4), calls=%async_computation.2 | async-start | bytes 6291456 | tf_op jit(solution)/shard_map/all_to_all | solution.py:594
  446.5 51.3 %collective-permute-start.27 = (bf16[8,128,1536]{2,1,0:T(8,128)(2,1)}, bf16[8,128,1536]{2,1,0:T(8,128)(2,1)}, u32[]{:S(2)}, u32[]{:S(2)}) collective-permute-start(bf16[8,128,1536]{2,1,0:T(8,128)(2,1)} %dynamic-slice_bitcast_fusion.1), channel_id=1, source_target_pairs={{0,1},{1,0},{2,3},{3,2},{4,5},{5,4},{6,7},{7,6},{8,9},{9,8},{10,11... | collective-permute-start | bytes 9437192 | tf_op jit(solution)/shard_map/ppermute | solution.py:37
  476.8 79.5 %collective-permute-start.31 = (bf16[8,128,1536]{2,1,0:T(8,128)(2,1)}, bf16[8,128,1536]{2,1,0:T(8,128)(2,1)}, u32[]{:S(2)}, u32[]{:S(2)}) collective-permute-start(bf16[8,128,1536]{2,1,0:T(8,128)(2,1)} %dynamic-slice_bitcast_fusion), channel_id=1, source_target_pairs={{0,1},{1,0},{2,3},{3,2},{4,5},{5,4},{6,7},{7,6},{8,9},{9,8},{10,11... | collective-permute-start | bytes 9437192 | tf_op jit(solution)/shard_map/ppermute | solution.py:37
  513.4 49.2 %all-to-all-start.4 = ((bf16[8,128,1536]{2,1,0:T(8,128)(2,1)}), bf16[8,128,1536]{2,1,0:T(8,128)(2,1)}, u32[]{:S(2)}, u32[]{:S(2)}) async-start(bf16[8,128,1536]{2,1,0:T(8,128)(2,1)} %fusion.3), calls=%async_computation.4 | async-start | bytes 6291456 | tf_op jit(solution)/shard_map/all_to_all | solution.py:594
  522.2 38.7 %collective-permute-start.32 = (bf16[8,128,512]{2,1,0:T(8,128)(2,1)S(1)}, bf16[8,128,512]{2,1,0:T(8,128)(2,1)S(1)}, u32[]{:S(2)}, u32[]{:S(2)}) collective-permute-start(bf16[8,128,512]{2,1,0:T(8,128)(2,1)S(1)} %dynamic-slice_bitcast_fusion.5), channel_id=1, source_target_pairs={{0,1},{1,0},{2,3},{3,2},{4,5},{5,4},{6,7},{7,6},{8,9},{9,8},{10,11... | collective-permute-start | bytes 3145736 | tf_op jit(solution)/shard_map/ppermute | solution.py:37
  567.3 53.0 %all-to-all-start.5 = ((bf16[16,2,256,128]{3,2,1,0:T(8,128)(2,1)}), bf16[16,2,256,128]{3,2,1,0:T(8,128)(2,1)S(1)}, u32[]{:S(2)}, u32[]{:S(2)}) async-start(bf16[16,2,256,128]{3,2,1,0:T(8,128)(2,1)} %pad_maximum_fusion.2), calls=%async_computation.5 | async-start | bytes 4194304 | tf_op jit(solution)/shard_map/all_to_all | solution.py:411
  574.7 44.7 %collective-permute-start.38 = (bf16[256,2048]{1,0:T(8,128)(2,1)}, bf16[256,2048]{1,0:T(8,128)(2,1)S(1)}, u32[]{:S(2)}, u32[]{:S(2)}) collective-permute-start(bf16[256,2048]{1,0:T(8,128)(2,1)} %get-tuple-element.163), channel_id=1, source_target_pairs={{0,32},{16,48},{32,0},{48,16},{1,33},{17,49},{33,1},{49,17},{2,34}... | collective-permute-start | bytes 3145736 | tf_op jit(solution)/shard_map/ppermute | solution.py:37
  579.7 38.9 %collective-permute-start.35 = (bf16[128,1536]{1,0:T(8,128)(2,1)S(1)}, bf16[128,1536]{1,0:T(8,128)(2,1)S(1)}, u32[]{:S(2)}, u32[]{:S(2)}) collective-permute-start(bf16[128,1536]{1,0:T(8,128)(2,1)S(1)} %add_convert_fusion.6.refs_0_), channel_id=1, source_target_pairs={{0,16},{16,32},{32,48},{48,0},{1,17},{17,33},{33,49},{49,1},{2,18}... | collective-permute-start | bytes 1179656 | tf_op jit(solution)/shard_map/ppermute | solution.py:37
  581.0 39.3 %collective-permute-start.34 = (bf16[128,1536]{1,0:T(8,128)(2,1)}, bf16[128,1536]{1,0:T(8,128)(2,1)}, u32[]{:S(2)}, u32[]{:S(2)}) collective-permute-start(bf16[128,1536]{1,0:T(8,128)(2,1)} %reduce_sum.124), channel_id=1, source_target_pairs={{0,64},{64,0},{1,65},{65,1},{2,66},{66,2},{3,67},{67,3},{4,68},{68... | collective-permute-start | bytes 1179656 | tf_op jit(solution)/shard_map/ppermute | solution.py:37
  620.3 44.5 %all-to-all-start.6 = ((bf16[8,128,1536]{2,1,0:T(8,128)(2,1)}), bf16[8,128,1536]{2,1,0:T(8,128)(2,1)}, u32[]{:S(2)}, u32[]{:S(2)}) async-start(bf16[8,128,1536]{2,1,0:T(8,128)(2,1)} %fusion.2), calls=%async_computation.6 | async-start | bytes 6291456 | tf_op jit(solution)/shard_map/all_to_all | solution.py:594
  673.3 43.4 %all-to-all-start.7 = ((bf16[8,128,1536]{2,1,0:T(8,128)(2,1)}), bf16[8,128,1536]{2,1,0:T(8,128)(2,1)}, u32[]{:S(2)}, u32[]{:S(2)}) async-start(bf16[8,128,1536]{2,1,0:T(8,128)(2,1)} %pad_maximum_fusion.1), calls=%async_computation.7 | async-start | bytes 6291456 | tf_op jit(solution)/shard_map/all_to_all | solution.py:594
  684.7 47.6 %collective-permute-start.45 = (bf16[256,2048]{1,0:T(8,128)(2,1)}, bf16[256,2048]{1,0:T(8,128)(2,1)}, u32[]{:S(2)}, u32[]{:S(2)}) collective-permute-start(bf16[256,2048]{1,0:T(8,128)(2,1)} %get-tuple-element.212), channel_id=1, source_target_pairs={{0,16},{16,32},{32,48},{48,0},{1,17},{17,33},{33,49},{49,1},{2,18}... | collective-permute-start | bytes 3145736 | tf_op jit(solution)/shard_map/ppermute | solution.py:37
  684.7 47.6 %collective-permute-start.44 = (bf16[256,2048]{1,0:T(8,128)(2,1)}, bf16[256,2048]{1,0:T(8,128)(2,1)}, u32[]{:S(2)}, u32[]{:S(2)}) collective-permute-start(bf16[256,2048]{1,0:T(8,128)(2,1)} %get-tuple-element.213), channel_id=1, source_target_pairs={{0,32},{16,48},{32,0},{48,16},{1,33},{17,49},{33,1},{49,17},{2,34}... | collective-permute-start | bytes 3145736 | tf_op jit(solution)/shard_map/ppermute | solution.py:37
  686.4 46.5 %collective-permute-start.43 = (bf16[256,2048]{1,0:T(8,128)(2,1)}, bf16[256,2048]{1,0:T(8,128)(2,1)}, u32[]{:S(2)}, u32[]{:S(2)}) collective-permute-start(bf16[256,2048]{1,0:T(8,128)(2,1)} %get-tuple-element.214), channel_id=1, source_target_pairs={{0,48},{16,0},{32,16},{48,32},{1,49},{17,1},{33,17},{49,33},{2,50}... | collective-permute-start | bytes 3145736 | tf_op jit(solution)/shard_map/ppermute | solution.py:37
  (112 other events, 2104.8 us)
Sparse Core Ops, SparseCore 0:
  15.3 66.1 all-gather.2
  84.5 147.2 all-gather.4

commit v2 on v1

--- a/solution.py
+++ b/solution.py
@@ -222,10 +222,16 @@
 
 
 def mlp_kernel(second_ref, cot_ref, gate_ref, up_ref, down_ref, *refs):
-    inner_ref, both_ref, grad_ref, acc = refs[-4:]
+    inner_ref, both_ref, second_out, cot_out, grad_ref, acc = refs[-6:]
     at = pl.program_id(0)
     step = gate_ref.shape[1]
     second = second_ref[...]
+
+    @pl.when(at == 0)
+    def _():
+        second_out[0] = second
+        cot_out[0] = cot_ref[...]
+
     gate_weight = gate_ref[...]
     up_weight = up_ref[...]
     gate_act = jnp.dot(second, gate_weight, preferred_element_type=jnp.float32)
@@ -259,11 +265,13 @@
 def mlp_block(block, second, cot, weights, held):
     rows, width = second.shape
     hidden_width = weights.shape[1] // 3
-    step = 256
+    step = 512
     steps = hidden_width // step
     whole = pl.BlockSpec((rows, width), lambda c: (0, 0))
     kept = pl.BlockSpec((1, rows, step), lambda c: (block, 0, c))
     kept_both = pl.BlockSpec((1, rows, 2 * hidden_width), lambda c: (block, 0, 0))
+    kept_rows = pl.BlockSpec((1, rows, width), lambda c: (block, 0, 0))
+    rows_shape = jax.ShapeDtypeStruct((RING, rows, width), low)
     return pl.pallas_call(
         mlp_kernel,
         grid=(steps,),
@@ -275,15 +283,17 @@
             pl.BlockSpec((width, step), lambda c: (0, 2 * steps + c)),
         ]
         + [pl.BlockSpec(memory_space=pl.ANY)] * len(held),
-        out_specs=(kept, kept_both, whole),
+        out_specs=(kept, kept_both, kept_rows, kept_rows, whole),
         out_shape=(
             jax.ShapeDtypeStruct((RING, rows, hidden_width), low),
             jax.ShapeDtypeStruct((RING, rows, 2 * hidden_width), low),
+            rows_shape,
+            rows_shape,
             jax.ShapeDtypeStruct((rows, width), low),
         ),
         scratch_shapes=[pltpu.VMEM((rows, width), jnp.float32)],
         input_output_aliases={5 + i: i for i in range(len(held))},
-        compiler_params=pltpu.CompilerParams(vmem_limit_bytes=40 * 1024 * 1024),
+        compiler_params=pltpu.CompilerParams(vmem_limit_bytes=48 * 1024 * 1024),
         cost_estimate=pl.CostEstimate(
             flops=2 * 5 * rows * width * hidden_width,
             bytes_accessed=2 * 3 * width * hidden_width,
@@ -407,6 +417,44 @@
     )(returned, pre, cosine, sine, query_gain, key_gain)
 
 
+def last_kernel(grad_ref, weight_ref, hidden_ref, part_ref, gain_ref):
+    part = lax.dot_general(
+        grad_ref[0], weight_ref[...], contract_last, preferred_element_type=jnp.float32
+    )
+    part_ref[0] = part.astype(low)
+    normed = normalize(hidden_ref[0].astype(jnp.float32))
+    gain = jnp.sum(part * normed, axis=0, keepdims=True)
+
+    @pl.when(pl.program_id(0) == 0)
+    def _():
+        gain_ref[...] = gain
+
+    @pl.when(pl.program_id(0) > 0)
+    def _():
+        gain_ref[...] += gain
+
+
+def last_part(grads, weights, hidden_all):
+    _, rows, width = hidden_all.shape
+    wide = pl.BlockSpec((1, rows, width), lambda r: (r, 0, 0))
+    return pl.pallas_call(
+        last_kernel,
+        grid=(RING,),
+        in_specs=[
+            pl.BlockSpec((1, rows, 1024), lambda r: (r, 0, 0)),
+            pl.BlockSpec((width, 1024), lambda r: (0, 0)),
+            wide,
+        ],
+        out_specs=(wide, pl.BlockSpec((1, width), lambda r: (0, 0))),
+        out_shape=(
+            jax.ShapeDtypeStruct((RING, rows, width), low),
+            jax.ShapeDtypeStruct((1, width), jnp.float32),
+        ),
+        compiler_params=pltpu.CompilerParams(vmem_limit_bytes=40 * 1024 * 1024),
+        cost_estimate=pl.CostEstimate(flops=1024, bytes_accessed=1024, transcendentals=0),
+    )(grads, weights, hidden_all)
+
+
 def to_heads(send):
     return lax.all_to_all(send, GROUP_AXES, 0, 0, tiled=True)
 
@@ -435,25 +483,42 @@
         slot = lax.rem(z_ref[0] - r + RING, RING)
         start = 0
         for out in outs:
+            if out.shape[1] == HEAD_DIM:
+                columns = blocks[r][:, start : start + HEAD_DIM].astype(jnp.float32)
+                out[...] = columns if r == 0 else out[...] + columns
+                continue
             part = out.shape[1] // RING
             at = pl.multiple_of(slot * part, part)
             out[:, pl.ds(at, part)] = blocks[r][:, start : start + part].astype(jnp.float32)
             start += part
 
 
-def place(z_at, blocks, widths):
+def place(z_at, blocks, widths, summed=False):
+    shapes = [RING * part for part in widths] + [HEAD_DIM] * summed
     rows = blocks[0].shape[0]
     whole = pl.BlockSpec(memory_space=pltpu.VMEM)
     return pl.pallas_call(
         place_kernel,
         in_specs=[pl.BlockSpec(memory_space=pltpu.SMEM)] + [whole] * RING,
-        out_specs=tuple(whole for _ in widths),
-        out_shape=tuple(jax.ShapeDtypeStruct((rows, RING * part), jnp.float32) for part in widths),
+        out_specs=tuple(whole for _ in shapes),
+        out_shape=tuple(jax.ShapeDtypeStruct((rows, part), jnp.float32) for part in shapes),
         compiler_params=pltpu.CompilerParams(vmem_limit_bytes=24 * 1024 * 1024),
         cost_estimate=pl.CostEstimate(
             flops=0, bytes_accessed=rows * sum(widths) * 24, transcendentals=0
         ),
     )(z_at[None], *blocks)
+
+
+def ring_sum(own, left, opposite, right):
+    half = left.shape[0] // 2
+    f32 = jnp.float32
+    top = shift(opposite[:half], "z", 3)
+    bottom = shift(opposite[half:], "z", 1)
+    left_top = (left[:half].astype(f32) + top.astype(f32)).astype(low)
+    right_bottom = (right[half:].astype(f32) + bottom.astype(f32)).astype(low)
+    left = shift(jnp.concatenate([left_top, left[half:]], axis=0), "z", 3)
+    right = shift(jnp.concatenate([right[:half], right_bottom], axis=0), "z", 1)
+    return own, left, right
 
 
 def send_back(block, r):
@@ -524,9 +589,12 @@
         jnp.concatenate([columns(gate_weight), columns(up_weight), columns(down_weight)], axis=1)
     )
     down_full = mlp_weights[:, 3072:]
+    out_all = gather(out_weight.astype(low))
 
     hidden_blocks = ring_blocks(hidden_in)
-    cot_blocks = ring_blocks(after(cotangent, *hidden_blocks))
+    cot_own = after(cotangent, *hidden_blocks)
+    cot_left = shift(cot_own, "z", 1)
+    cot_right = shift(cot_own, "z", 3)
     frequency = rope_base ** (-2.0 * jnp.arange(HEAD_DIM // 2, dtype=f32) / HEAD_DIM)
     angles = places.astype(f32)[:, :, None] * frequency[None, None, :]
     cosine = jnp.cos(angles)
@@ -536,10 +604,14 @@
     query_row = query_gain[None]
     key_row = key_gain[None]
 
+    hidden_all = jnp.stack(hidden_blocks)
     first_in, qkv_pre, send = first_part(
-        jnp.stack(hidden_blocks), attn_scale, first_weights, cosine, sine, query_row, key_row
-    )
-    arrived = to_heads(send)
+        hidden_all, attn_scale, first_weights, cosine, sine, query_row, key_row
+    )
+    arrived, cot_left, cot_right, cot_own = together(
+        to_heads(send), cot_left, cot_right, cot_own
+    )
+    cot_opposite = shift(cot_own, "z", 2)
     head_queries = arrived[:, 0]
     own_pair = arrived[:, 1]
     other_pair = shift(own_pair, "core", 1, 2)
@@ -548,12 +620,12 @@
     head_mixed, head_mixed_t, head_logs = attention_forward(
         order, head_queries, head_keys, head_values
     )
-    head_mixed = after(head_mixed, *cot_blocks)
 
     def from_heads(values):
         return values.reshape(RING, 4, rows, HEAD_DIM).transpose(0, 2, 1, 3).reshape(ring_rows, 512)
 
-    mixed = from_heads(to_heads(head_mixed))
+    mixed_arrived, cot_opposite = together(to_heads(head_mixed), cot_opposite)
+    mixed = from_heads(mixed_arrived)
     attn_out = lax.dot_general(mixed, out_full, contract_last, preferred_element_type=f32)
     hidden = hidden_in.astype(f32)
     middle = hidden + scatter_z(attn_out)
@@ -562,21 +634,23 @@
     second_in = (second_norm * mlp_scale).astype(low)
     left = shift(second_in, "z", 1)
     right = shift(second_in, "z", 3)
-    *held, own_part = mlp_block(0, second_in, cot_blocks[0], mlp_weights, ())
+    *held, own_part = mlp_block(0, second_in, cot_own, mlp_weights, ())
     held, own_part, left, right = together(held, own_part, left, right)
     half = rows // 2
     top = shift(left[:half], "z", 1)
     bottom = shift(right[half:], "z", 3)
-    *held, left_part = mlp_block(1, left, cot_blocks[1], mlp_weights, held)
+    *held, left_part = mlp_block(1, left, cot_left, mlp_weights, held)
     left_back = send_back(left_part, 1)
-    *held, right_part = mlp_block(3, right, cot_blocks[3], mlp_weights, held)
+    *held, right_part = mlp_block(3, right, cot_right, mlp_weights, held)
     right_back = send_back(right_part, 3)
     held, top, bottom = together(held, top, bottom)
     opposite = jnp.concatenate([top, bottom], axis=0)
-    *held, opposite_part = mlp_block(2, opposite, cot_blocks[2], mlp_weights, held)
+    *held, opposite_part = mlp_block(2, opposite, cot_opposite, mlp_weights, held)
     opposite_back = send_back(opposite_part, 2)
     inner = held[0].reshape(ring_rows, 1536)
     both_grad = held[1].reshape(ring_rows, 3072)
+    second_all = held[2].reshape(ring_rows, width)
+    cot_all = held[3].reshape(ring_rows, width)
 
     def weight_grad(left, right):
         return lax.dot_general(left, right, contract_first, preferred_element_type=f32).astype(low)
@@ -601,13 +675,16 @@
         share = pair_sum(*pair)
         return [share] + [shift(share, "z", r) for r in range(1, RING)]
 
-    second_all = jnp.concatenate([second_in, left, opposite, right], axis=0)
-    cot_all = jnp.concatenate(cot_blocks, axis=0)
-    down_term = weight_grad(cot_all, inner)
-    left_back, right_back, opposite_back, down_term, both_grad = together(
-        left_back, right_back, opposite_back, down_term, both_grad
-    )
-    down_pair = pair_start(down_term)
+    both_term = weight_grad(second_all, both_grad)
+    mlp_out = lax.dot_general(
+        inner, down_full, contract_last, preferred_element_type=f32
+    ).reshape(RING, rows, width)
+    mlp_own = mlp_out[0].astype(low)
+    mlp_rest = mlp_out[1:].astype(low)
+    left_back, right_back, opposite_back, both_term, mlp_own, mlp_rest, inner = together(
+        left_back, right_back, opposite_back, both_term, mlp_own, mlp_rest, inner
+    )
+    both_share = lax.psum_scatter(both_term, GROUP_AXES, scatter_dimension=0, tiled=True)
 
     second_grad = (
         own_part.astype(f32)
@@ -621,92 +698,96 @@
         scaled_grad - second_norm * jnp.mean(scaled_grad * second_norm, axis=-1, keepdims=True)
     )
     own_low = middle_grad.astype(low)
-    left_low = shift(own_low, "z", 1)
-    right_low = shift(own_low, "z", 3)
+    mixed_grad = jnp.dot(own_low, out_all, preferred_element_type=f32).astype(low)
+
+    def heads_of(r):
+        return lax.dynamic_slice_in_dim(mixed_grad, ((z_at + r) & (RING - 1)) * 512, 512, 1)
+
+    grad_blocks = [heads_of(0)] + [shift(heads_of(r), "z", r) for r in range(1, RING)]
+    down_term = weight_grad(cot_all, inner)
+    grad_blocks, down_term, own_low, mlp_rest = together(grad_blocks, down_term, own_low, mlp_rest)
+    down_pair = pair_start(down_term)
+    mixed_grad = jnp.stack(grad_blocks).reshape(RING, rows, 4, HEAD_DIM).transpose(0, 2, 1, 3)
+    head_grads = to_heads(mixed_grad.reshape(BLOCKS, rows, HEAD_DIM))
     down_sum = pair_sum(*down_pair)
-    gate_term = weight_grad(second_all, both_grad[:, :1536])
-    left_low, right_low, gate_term, down_sum, both_grad = together(
-        left_low, right_low, gate_term, down_sum, both_grad
-    )
+    low_left = shift(own_low, "z", 1)
+    low_right = shift(own_low, "z", 3)
+    head_grads, down_sum, low_left, low_right, own_low, mlp_rest = together(
+        head_grads, down_sum, low_left, low_right, own_low, mlp_rest
+    )
+    low_opposite = shift(own_low, "z", 2)
     down_share = to_owners(down_sum)
-    gate_pair = pair_start(gate_term)
-    top_low = shift(left_low[:half], "z", 1)
-    bottom_low = shift(right_low[half:], "z", 3)
-    up_term = weight_grad(second_all, both_grad[:, 1536:])
-    mlp_out = lax.dot_general(
-        inner, down_full, contract_last, preferred_element_type=f32
-    ).reshape(RING, rows, width)
-    mlp_own = mlp_out[0].astype(low)
-    mlp_rest = mlp_out[1:].astype(low)
-    top_low, bottom_low, up_term, mlp_own, mlp_rest = together(
-        top_low, bottom_low, up_term, mlp_own, mlp_rest
-    )
-    up_pair = pair_start(up_term)
-    middle_low = jnp.concatenate([own_low, left_low, top_low, bottom_low, right_low], axis=0)
-    mixed_grad = jnp.dot(middle_low, out_full, preferred_element_type=f32).astype(low)
-    mixed_grad = mixed_grad.reshape(RING, rows, 4, HEAD_DIM).transpose(0, 2, 1, 3)
-    mixed_grad, down_share = together(mixed_grad, down_share)
-    head_grads = to_heads(mixed_grad.reshape(BLOCKS, rows, HEAD_DIM))
-    down_pair = over_x(down_share)
-    mlp_left = send_back(mlp_rest[0], 1)
-    mlp_right = send_back(mlp_rest[2], 3)
-    out_term = weight_grad(middle_low, mixed)
-    gate_sum = pair_sum(*gate_pair)
-    head_grads, out_term, gate_sum, down_pair, mlp_left, mlp_right, mlp_opposite = together(
-        head_grads, out_term, gate_sum, down_pair, mlp_left, mlp_right, mlp_rest[1]
-    )
-    gate_share = to_owners(gate_sum)
-    down_blocks = over_z(down_pair)
-    out_pair = pair_start(out_term)
 
     query_grad, key_grad, value_grad = attention_backward(
         order, head_queries, head_keys, head_values, head_grads, head_mixed_t, head_logs
     )
-    up_sum = pair_sum(*up_pair)
-    out_sum = pair_sum(*out_pair)
-    query_grad, gate_share, up_sum, out_sum = together(query_grad, gate_share, up_sum, out_sum)
-    gate_pair = over_x(gate_share)
-    mlp_opposite = send_back(mlp_opposite, 2)
+    query_grad, key_grad, value_grad, low_opposite, mlp_rest = together(
+        query_grad, key_grad, value_grad, low_opposite, mlp_rest
+    )
     keep = jnp.where(core_at == 0, key_grad, value_grad)
     give = jnp.where(core_at == 0, value_grad, key_grad)
     pair_grad = (keep.astype(f32) + shift(give, "core", 1, 2).astype(f32)).astype(low)
     returned = to_heads(jnp.stack([query_grad, pair_grad], axis=1))
-    returned, up_sum, gate_pair, down_blocks, mlp_opposite = together(
-        returned, up_sum, gate_pair, down_blocks, mlp_opposite
-    )
-    up_share = to_owners(up_sum)
-    gate_blocks = over_z(gate_pair)
-    output = (
-        middle
-        + mlp_own.astype(f32)
-        + mlp_left.astype(f32)
-        + mlp_right.astype(f32)
-        + mlp_opposite.astype(f32)
-    ).astype(low)
+    down_pair = over_x(down_share)
+    middle_low = jnp.concatenate([own_low, low_left, low_opposite, low_right], axis=0)
+    out_sum = pair_sum(*pair_start(weight_grad(middle_low, mixed)))
+    mlp_top = shift(mlp_rest[1][:half], "z", 3)
+    mlp_bottom = shift(mlp_rest[1][half:], "z", 1)
+    returned, down_pair, out_sum, mlp_top, mlp_bottom = together(
+        returned, down_pair, out_sum, mlp_top, mlp_bottom
+    )
+    out_share = to_owners(out_sum)
+    mlp_left = jnp.concatenate(
+        [(mlp_rest[0][:half].astype(f32) + mlp_top.astype(f32)).astype(low), mlp_rest[0][half:]],
+        axis=0,
+    )
+    mlp_right = jnp.concatenate(
+        [mlp_rest[2][:half], (mlp_rest[2][half:].astype(f32) + mlp_bottom.astype(f32)).astype(low)],
+        axis=0,
+    )
+    mlp_left = shift(mlp_left, "z", 3)
+    mlp_right = shift(mlp_right, "z", 1)
     qkv_grad, query_gain_part, key_gain_part = first_back(
         returned, qkv_pre, cosine, sine, query_row, key_row
     )
-    qkv_grad = qkv_grad.reshape(ring_rows, 1024)
-    qkv_term = weight_grad(first_in.reshape(ring_rows, width), qkv_grad)
+    qkv_term = weight_grad(
+        first_in.reshape(ring_rows, width), qkv_grad.reshape(ring_rows, 1024)
+    )
     qkv_pair = pair_start(qkv_term)
-    first_partial = lax.dot_general(
-        after(qkv_grad, qkv_term),
-        first_weights[:, :1024],
-        contract_last,
-        preferred_element_type=f32,
-    )
-    qkv_pair, first_partial, up_share, gate_blocks = together(
-        qkv_pair, first_partial.astype(low), up_share, gate_blocks
-    )
-    up_pair = over_x(up_share)
-    qkv_share = to_owners(jnp.concatenate([pair_sum(*qkv_pair), out_sum], axis=2))
-    first_blocks = [first_partial[r * rows : (r + 1) * rows] for r in range(RING)]
-    first_blocks = [first_blocks[0]] + [send_back(first_blocks[r], r) for r in range(1, RING)]
-    first_blocks, qkv_share, up_pair = together(first_blocks, qkv_share, up_pair)
+    first_partial, attn_gain_part = last_part(
+        after(qkv_grad, qkv_term), first_weights, hidden_all
+    )
+    first_partial, attn_gain_part, out_share = together(first_partial, attn_gain_part, out_share)
+    gains_part = jnp.stack(
+        [
+            attn_gain_part[0],
+            mlp_gain_part,
+            jnp.tile(query_gain_part[0], BLOCKS),
+            jnp.tile(key_gain_part[0], BLOCKS),
+        ],
+        axis=1,
+    )
+    gains_part = jnp.pad(gains_part.astype(low), ((0, 0), (0, HEAD_DIM - 4)))
+    gains_pair = pair_start(gains_part)
+    down_blocks = over_z(down_pair)
+    qkv_pair, gains_pair, first_partial = together(qkv_pair, gains_pair, first_partial)
+    qkv_share = to_owners(
+        jnp.concatenate([pair_sum(*qkv_pair), pair_sum(*gains_pair)], axis=2)
+    )
+    out_pair = over_x(out_share)
+    first_blocks = ring_sum(*[first_partial[r] for r in range(RING)])
+    both_pair = over_x(both_share)
+    first_blocks, qkv_share, out_pair, both_pair, down_blocks, mlp_left, mlp_right = together(
+        first_blocks, qkv_share, out_pair, both_pair, down_blocks, mlp_left, mlp_right
+    )
+    qkv_pair = over_x(qkv_share)
+    both_blocks = over_z(both_pair)
+    output = (
+        middle + mlp_own.astype(f32) + mlp_left.astype(f32) + mlp_right.astype(f32)
+    ).astype(low)
     first_grad = sum(block.astype(f32) for block in first_blocks)
     hidden_rms = inverse_rms(hidden)
     own_norm = hidden * hidden_rms
-    attn_gain_part = jnp.sum(first_grad * own_norm, axis=0)
     scaled_first = first_grad * attn_scale
     hidden_grad = (
         middle_grad
@@ -715,25 +796,12 @@
     ).astype(low)
 
     (down_grad_out,) = place(z_at, down_blocks, (1536,))
-    (gate_grad_out,) = place(z_at, gate_blocks, (1536,))
-    (up_grad_out,) = place(z_at, over_z(up_pair), (1536,))
-    query_grad_out, key_grad_out, value_grad_out, out_grad_out = place(
-        z_at, over_z(over_x(qkv_share)), (512, 256, 256, 512)
-    )
-
-    gain_send = jnp.stack(
-        [
-            attn_gain_part.reshape(BLOCKS, HEAD_DIM),
-            mlp_gain_part.reshape(BLOCKS, HEAD_DIM),
-            jnp.broadcast_to(query_gain_part, (BLOCKS, HEAD_DIM)),
-            jnp.broadcast_to(key_gain_part, (BLOCKS, HEAD_DIM)),
-        ],
-        axis=1,
-    )
-    gain_sum = jnp.sum(to_heads(gain_send), axis=0)
-    gain_sum = gain_sum + shift(gain_sum, "x_lo", 1, 2)
-    pair_sum = gain_sum + shift(gain_sum, "z", 2)
-    gain_sum = pair_sum + shift(pair_sum, "z", 1)
+    gate_grad_out, up_grad_out = place(z_at, both_blocks, (1536, 1536))
+    (out_grad_out,) = place(z_at, over_z(out_pair), (512,))
+    query_grad_out, key_grad_out, value_grad_out, gain_sum = place(
+        z_at, over_z(qkv_pair), (512, 256, 256), True
+    )
+    gain_sum = gain_sum[:, :4].T
 
     return (
         output,

time: 822 us -> 752 us (0.915)
  blocking collectives: 29.4 us -> 0 us
  local copies, waits for them, and re-layouts: 70 us -> 50.7 us
  matrix products: 67.1 us -> 57.3 us
    all_to_all x4, waiting for transfers between devices: 8.96 us -> 44.2 us  [to_heads(): return lax.all_to_all(send, GROUP_AXES, 0, 0, tiled=True)]
    all_to_all x4 -> x3, waiting for transfers between devices: 39.5 us -> 9.8 us  [to_owners(): terms = lax.all_to_all(pair, ('y', 'x_hi'), 0, 0, tiled=True)]
    all_to_all x1 -> x0, blocking collectives: 29.4 us -> none  [to_heads(): return lax.all_to_all(send, GROUP_AXES, 0, 0, tiled=True)]
    pallas_call x4, Pallas kernels: 79.7 us -> 65.6 us  [mlp_block(): pl.pallas_call(mlp_kernel, grid=(steps,), in_specs=[whole, whole, pl.Bloc...]
    convert_element_type x0 -> x5, other arithmetic: none -> 11.8 us  [the longest x1 4.64 us: local(): own_low = middle_grad.astype(low)]
    ppermute x57 -> x56, starting transfers between devices: 64.6 us -> 75.8 us  [shift(): lax.ppermute(values, axis, [(i, (i + by) % size) for i in range(size)])]
    ppermute x57 -> x56, waiting for transfers between devices: 213 us -> 205 us  [shift(): lax.ppermute(values, axis, [(i, (i + by) % size) for i in range(size)])]
    convert_element_type x9 -> x8, other arithmetic: 19.6 us -> 13.8 us  [pair_sum(): return (keep.astype(f32) + come.astype(f32)).astype(low)]
  transfers between devices with their start and end apart: 67 -> 67, of which waited for: 29 -> 24; matrix products, arithmetic and copies ran while one was open for 21% -> 19% of each run, Pallas kernels for 19% -> 19%
where the time goes in v2:
time: 752 us; the launch traced here: 742 us
  waiting for transfers between devices  277 us (37%)
  Pallas kernels  147 us (20%)
  starting transfers between devices  127 us (17%)
  other arithmetic  66.9 us (9%)
  matrix products  57.3 us (8%)
  local copies, waits for them, and re-layouts  50.7 us (7%)
  between operations  15.4 us (2%)
    ppermute x56, waiting for transfers between devices, shift(): lax.ppermute(values, axis, [(i, (i + by) % size) for i in range(size)])  205 us
    ppermute x56, starting transfers between devices, shift(): lax.ppermute(values, axis, [(i, (i + by) % size) for i in range(size)])  75.8 us
    pallas_call x4, Pallas kernels, mlp_block(): pl.pallas_call(mlp_kernel, grid=(steps,), in_specs=[whole, whole, pl.Bloc...  65.6 us
    all_to_all x4, waiting for transfers between devices, to_heads(): return lax.all_to_all(send, GROUP_AXES, 0, 0, tiled=True)  44.2 us
    dot_general x4, matrix products, weight_grad(): lax.dot_general(left, right, contract_first, preferred_element_type=f32)  36.6 us
    pallas_call x1, Pallas kernels, attention_backward(): pl.pallas_call(backward_kernel, out_shape=(jax.ShapeDtypeStruct((BLOCKS,...  33.3 us
    unnamed x134, local copies, waits for them, and re-layouts  30.7 us
    all_to_all x4, starting transfers between devices, to_heads(): return lax.all_to_all(send, GROUP_AXES, 0, 0, tiled=True)  26.9 us
  transfers between devices with their start and end apart: 67, of which 24 were waited for; matrix products, arithmetic and copies ran while one was open for 19% of the time, Pallas kernels for 19%

profile of v2, /device:TPU:4, one launch (start us, length us, event | category | flops | bytes accessed | tf_op | source)
XLA Modules:
  0.0 742.2 jit_solution(4283425785561125582)
XLA Ops:
  27.4 18.3 %collective-permute-done = s32[1,384]{1,0:T(1,128)S(1)} collective-permute-done((s32[1,384]{1,0:T(1,128)S(1)}, s32[1,384]{1,0:T(1,128)S(1)}, u32[]{:S(2)}, u32[]{:S(2)}) %collective-permute-start) | collective-permute-done | bytes 1568 | tf_op jit(solution)/shard_map/ppermute | solution.py:37
  63.1 18.3 %all-gather.4.cloned.1.call-done.weight_ref = bf16[2048,1664]{1,0:T(8,128)(2,1)} async-done(((bf16[128,1664]{1,0:T(8,128)(2,1)}), bf16[2048,1664]{1,0:T(8,128)(2,1)}) %all-gather.4.cloned.1.call-update) | async-done | bytes 6815760 | tf_op jit(solution)/shard_map/all_gather | solution.py:558
  83.3 9.3 %shard_map.246 = (bf16[4,256,2048]{2,1,0:T(8,128)(2,1)S(1)}, f32[4,256,1024]{2,1,0:T(8,128)S(1)}, bf16[16,2,256,128]{3,2,1,0:T(8,128)(2,1)S(1)}) custom-call(bf16[4,256,2048]{2,1,0:T(8,128)(2,1)} %pad_maximum_fusion.hidden_ref, f32[1,2048]{1,0:T(1,128)S(1)} %bitcast.132, bf16[2048,1664]{1,0:T(8,128)(2,1)} %all-gather.4.cloned.1.call-done.weight_ref, ...), custom_call_target="tpu_custom_call" | custom-call | flops 4294967296 | bytes 20971520 | tf_op jit(solution)/shard_map/pallas_call | solution.py:330
  110.6 21.1 %collective-permute-done.7.cot_ref = bf16[256,2048]{1,0:T(8,128)(2,1)S(1)} collective-permute-done((bf16[256,2048]{1,0:T(8,128)(2,1)S(1)}, bf16[256,2048]{1,0:T(8,128)(2,1)S(1)}, u32[]{:S(2)}, u32[]{:S(2)}) %collective-permute-start.7) | collective-permute-done | bytes 1048608 | tf_op jit(solution)/shard_map/ppermute | solution.py:37
  148.8 18.4 %shard_map.247 = (bf16[16,256,128]{2,1,0:T(8,128)(2,1)S(1)}, f32[8,128,512]{2,1,0:T(8,128)S(1)}, f32[8,1,512]{2,1,0:T(1,128)S(1)}) custom-call(s32[16]{0:T(128)S(1)} %dynamic-slice_bitcast_fusion.6.order, bf16[16,256,128]{2,1,0:T(8,128)(2,1)S(1)} %get-tuple-element.273.q_ref, bf16[16,256,128]{2,1,0:T(8,128)(2,1)S(1)} %get-tuple-element.271.k_ref, ...), custom_call_target="tpu_custom_call" | custom-call | flops 1024 | bytes 1024 | tf_op jit(solution)/shard_map/pallas_call | solution.py:96
  176.4 24.1 %all-to-all-done.1 = bf16[16,256,128]{2,1,0:T(8,128)(2,1)S(1)} async-done(((bf16[16,256,128]{2,1,0:T(8,128)(2,1)}), bf16[16,256,128]{2,1,0:T(8,128)(2,1)S(1)}, u32[]{:S(2)}, u32[]{:S(2)}) %all-to-all-start.1) | async-done | bytes 1048608 | tf_op jit(solution)/shard_map/all_to_all | solution.py:459
  209.7 43.5 %collective-permute-done.11 = bf16[256,2048]{1,0:T(8,128)(2,1)S(1)} collective-permute-done((bf16[256,2048]{1,0:T(8,128)(2,1)S(1)}, bf16[256,2048]{1,0:T(8,128)(2,1)S(1)}, u32[]{:S(2)}, u32[]{:S(2)}) %collective-permute-start.11) | collective-permute-done | bytes 1048608 | tf_op jit(solution)/shard_map/ppermute | solution.py:37
  263.2 15.8 %shard_map.248 = (bf16[4,256,1536]{2,1,0:T(8,128)(2,1)}, bf16[4,256,3072]{2,1,0:T(8,128)(2,1)}, bf16[4,256,2048]{2,1,0:T(8,128)(2,1)}, bf16[4,256,2048]{2,1,0:T(8,128)(2,1)}, bf16[256,2048]{1,0:T(8,128)(2,1)S(1)}) custom-call(bf16[256,2048]{1,0:T(8,128)(2,1)S(1)} %multiply_convert_fusion.second_ref, bf16[256,2048]{1,0:T(8,128)(2,1)S(1)} %copy-done.8, ...), custom_call_target="tpu_custom_call" | custom-call | flops 8053063680 | bytes 18874368 | tf_op jit(solution)/shard_map/pallas_call | solution.py:275
  292.1 16.8 %shard_map.249 = (bf16[4,256,1536]{2,1,0:T(8,128)(2,1)}, bf16[4,256,3072]{2,1,0:T(8,128)(2,1)}, bf16[4,256,2048]{2,1,0:T(8,128)(2,1)}, bf16[4,256,2048]{2,1,0:T(8,128)(2,1)}, bf16[256,2048]{1,0:T(8,128)(2,1)}) custom-call(bf16[256,2048]{1,0:T(8,128)(2,1)} %collective-permute-done.14.second_re, ...), custom_call_target="tpu_custom_call", output_to_operand_aliasing={{0}: (5, {}), {1}: (6, {}), {2}: (7, {}), {3}: (8, {})} | custom-call | flops 8053063680 | bytes 18874368 | tf_op jit(solution)/shard_map/pallas_call | solution.py:275
  308.9 16.5 %shard_map.250 = (bf16[4,256,1536]{2,1,0:T(8,128)(2,1)}, bf16[4,256,3072]{2,1,0:T(8,128)(2,1)}, bf16[4,256,2048]{2,1,0:T(8,128)(2,1)}, bf16[4,256,2048]{2,1,0:T(8,128)(2,1)}, bf16[256,2048]{1,0:T(8,128)(2,1)}) custom-call(bf16[256,2048]{1,0:T(8,128)(2,1)} %collective-permute-done.15.second_re, ...), custom_call_target="tpu_custom_call", output_to_operand_aliasing={{0}: (5, {}), {1}: (6, {}), {2}: (7, {}), {3}: (8, {})} | custom-call | flops 8053063680 | bytes 18874368 | tf_op jit(solution)/shard_map/pallas_call | solution.py:275
  328.7 16.5 %shard_map.251 = (bf16[4,256,1536]{2,1,0:T(8,128)(2,1)}, bf16[4,256,3072]{2,1,0:T(8,128)(2,1)}, bf16[4,256,2048]{2,1,0:T(8,128)(2,1)}, bf16[4,256,2048]{2,1,0:T(8,128)(2,1)}, bf16[256,2048]{1,0:T(8,128)(2,1)}) custom-call(bf16[256,2048]{1,0:T(8,128)(2,1)S(1)} %pad_maximum_fusion.4.second_ref,, ...), custom_call_target="tpu_custom_call", output_to_operand_aliasing={{0}: (5, {}), {1}: (6, {}), {2}: (7, {}), {3}: (8, {})} | custom-call | flops 8053063680 | bytes 18874368 | tf_op jit(solution)/shard_map/pallas_call | solution.py:275
  345.4 19.4 %bitcast_convert_fusion = bf16[2048,3072]{1,0:T(8,128)(2,1)} fusion(bf16[4,256,2048]{2,1,0:T(8,128)(2,1)} %get-tuple-element.164, bf16[4,256,3072]{2,1,0:T(8,128)(2,1)} %get-tuple-element.165), kind=kOutput, calls=%fused_computation | convolution fusion | flops 12891193344 | bytes 23068672 | tf_op jit(solution)/shard_map/dot_general | solution.py:656
  364.8 10.2 %fusion.11 = bf16[1024,2048]{1,0:T(8,128)(2,1)S(1)} fusion(bf16[1024,1536]{1,0:T(8,128)(2,1)} %bitcast.138, bf16[2048,4608]{1,0:T(8,128)(2,1)} %all-gather.6.cloned.1.call-done.gate_ref.up_ref.down_ref), kind=kOutput, calls=%fused_computation.17 | convolution fusion | flops 6444548096 | bytes 13631488 | tf_op jit(solution)/shard_map/dot_general | solution.py:679
  415.8 8.4 %all-to-all-start.2 = ((bf16[16,256,128]{2,1,0:T(8,128)(2,1)}), bf16[16,256,128]{2,1,0:T(8,128)(2,1)S(1)}, u32[]{:S(2)}, u32[]{:S(2)}) async-start(bf16[16,256,128]{2,1,0:T(8,128)(2,1)} %bitcast.21), calls=%async_computation.2 | async-start | bytes 2097152 | tf_op jit(solution)/shard_map/all_to_all | solution.py:459
  429.7 12.4 %all-to-all-done.2.g_ref = bf16[16,256,128]{2,1,0:T(8,128)(2,1)S(1)} async-done(((bf16[16,256,128]{2,1,0:T(8,128)(2,1)}), bf16[16,256,128]{2,1,0:T(8,128)(2,1)S(1)}, u32[]{:S(2)}, u32[]{:S(2)}) %all-to-all-start.2) | async-done | bytes 1048608 | tf_op jit(solution)/shard_map/all_to_all | solution.py:459
  443.1 9.9 %all-to-all-start.4 = ((bf16[8,128,1536]{2,1,0:T(8,128)(2,1)}), bf16[8,128,1536]{2,1,0:T(8,128)(2,1)}, u32[]{:S(2)}, u32[]{:S(2)}) async-start(bf16[8,128,1536]{2,1,0:T(8,128)(2,1)} %fusion.2), calls=%async_computation.4 | async-start | bytes 6291456 | tf_op jit(solution)/shard_map/all_to_all | solution.py:668
  453.0 33.3 %shard_map.252 = (bf16[16,256,128]{2,1,0:T(8,128)(2,1)S(1)}, bf16[16,256,128]{2,1,0:T(8,128)(2,1)S(1)}, bf16[16,256,128]{2,1,0:T(8,128)(2,1)S(1)}) custom-call(s32[16]{0:T(128)S(1)} %copy-done.27, bf16[16,256,128]{2,1,0:T(8,128)(2,1)S(1)} %copy-done.7, bf16[16,256,128]{2,1,0:T(8,128)(2,1)S(1)} %copy-done.5, bf16[16,256,128]{2,1,0:T(8,128)(2,1)} %copy-done.3, ...), custom_call_target="tpu_custom_call" | custom-call | flops 1024 | bytes 1024 | tf_op jit(solution)/shard_map/pallas_call | solution.py:200
  491.2 9.8 %all-to-all-done.4 = bf16[8,128,1536]{2,1,0:T(8,128)(2,1)} async-done(((bf16[8,128,1536]{2,1,0:T(8,128)(2,1)}), bf16[8,128,1536]{2,1,0:T(8,128)(2,1)}, u32[]{:S(2)}, u32[]{:S(2)}) %all-to-all-start.4) | async-done | bytes 3145760 | tf_op jit(solution)/shard_map/all_to_all | solution.py:668
  528.9 20.5 %collective-permute-done.29 = bf16[128,1536]{1,0:T(8,128)(2,1)} collective-permute-done((bf16[128,1536]{1,0:T(8,128)(2,1)S(1)}, bf16[128,1536]{1,0:T(8,128)(2,1)}, u32[]{:S(2)}, u32[]{:S(2)}) %collective-permute-start.29) | collective-permute-done | bytes 393248 | tf_op jit(solution)/shard_map/ppermute | solution.py:37
  625.3 17.3 %collective-permute-done.39 = bf16[128,512]{1,0:T(8,128)(2,1)S(1)} collective-permute-done((bf16[128,512]{1,0:T(8,128)(2,1)S(1)}, bf16[128,512]{1,0:T(8,128)(2,1)S(1)}, u32[]{:S(2)}, u32[]{:S(2)}) %collective-permute-start.39) | collective-permute-done | bytes 131104 | tf_op jit(solution)/shard_map/ppermute | solution.py:37
  649.1 14.4 %collective-permute-done.38 = bf16[256,2048]{1,0:T(8,128)(2,1)} collective-permute-done((bf16[256,2048]{1,0:T(8,128)(2,1)}, bf16[256,2048]{1,0:T(8,128)(2,1)}, u32[]{:S(2)}, u32[]{:S(2)}) %collective-permute-start.38) | collective-permute-done | bytes 1048608 | tf_op jit(solution)/shard_map/ppermute | solution.py:37
  688.8 9.7 %collective-permute-done.47.refs_1_ = bf16[128,1152]{1,0:T(8,128)(2,1)S(1)} collective-permute-done((bf16[128,1152]{1,0:T(8,128)(2,1)S(1)}, bf16[128,1152]{1,0:T(8,128)(2,1)S(1)}, u32[]{:S(2)}, u32[]{:S(2)}) %collective-permute-start.47) | collective-permute-done | bytes 294944 | tf_op jit(solution)/shard_map/ppermute | solution.py:37
  706.3 12.8 %collective-permute-done.48.refs_2_ = bf16[128,1152]{1,0:T(8,128)(2,1)S(1)} collective-permute-done((bf16[128,1152]{1,0:T(8,128)(2,1)S(1)}, bf16[128,1152]{1,0:T(8,128)(2,1)S(1)}, u32[]{:S(2)}, u32[]{:S(2)}) %collective-permute-start.48) | collective-permute-done | bytes 294944 | tf_op jit(solution)/shard_map/ppermute | solution.py:37
  719.2 10.8 %collective-permute-done.49.refs_3_ = bf16[128,1152]{1,0:T(8,128)(2,1)S(1)} collective-permute-done((bf16[128,1152]{1,0:T(8,128)(2,1)S(1)}, bf16[128,1152]{1,0:T(8,128)(2,1)S(1)}, u32[]{:S(2)}, u32[]{:S(2)}) %collective-permute-start.49) | collective-permute-done | bytes 294944 | tf_op jit(solution)/shard_map/ppermute | solution.py:37
  (356 shorter events, 319.4 us)
Async XLA Ops:
  7.2 74.3 %all-gather.4.cloned.1.call-start = ((), (), s32[]{:S(2)}) async-start(), calls=%async_computation.8 | async-start | bytes 7241728 | tf_op jit(solution)/shard_map/all_gather | solution.py:558
  15.2 248.0 %all-gather.6.cloned.1.call-start = ((), (), s32[]{:S(2)}) async-start(), calls=%async_computation.9 | async-start | bytes 20054016 | tf_op jit(solution)/shard_map/all_gather | solution.py:558
  97.9 43.5 %all-to-all-start = ((bf16[16,2,256,128]{3,2,1,0:T(8,128)(2,1)}), bf16[16,2,256,128]{3,2,1,0:T(8,128)(2,1)}, u32[]{:S(2)}, u32[]{:S(2)}) async-start(bf16[16,2,256,128]{3,2,1,0:T(8,128)(2,1)} %copy-done.14), calls=%async_computation | async-start | bytes 4194304 | tf_op jit(solution)/shard_map/all_to_all | solution.py:459
  105.2 281.6 %all-gather.8.cloned.1.call-start = ((), (), s32[]{:S(2)}) async-start(), calls=%async_computation.10 | async-start | bytes 8912896 | tf_op jit(solution)/shard_map/all_gather | solution.py:558
  176.3 466.3 %reduce-scatter.2.cloned.1.call-start = ((), (), s32[]{:S(2)}) async-start(), calls=%async_computation.11 | async-start | bytes 13369344 | tf_op jit(solution)/shard_map/reduce_scatter | solution.py:687
  205.9 47.4 %collective-permute-start.11 = (bf16[256,2048]{1,0:T(8,128)(2,1)S(1)}, bf16[256,2048]{1,0:T(8,128)(2,1)S(1)}, u32[]{:S(2)}, u32[]{:S(2)}) collective-permute-start(bf16[256,2048]{1,0:T(8,128)(2,1)S(1)} %get-tuple-element.261), channel_id=1, source_target_pairs={{0,48},{16,0},{32,16},{48,32},{1,49},{17,1},{33,17},{49,33},{2,50}... | collective-permute-start | bytes 3145736 | tf_op jit(solution)/shard_map/ppermute | solution.py:37
  208.1 45.1 %collective-permute-start.12 = (bf16[256,2048]{1,0:T(8,128)(2,1)S(1)}, bf16[256,2048]{1,0:T(8,128)(2,1)S(1)}, u32[]{:S(2)}, u32[]{:S(2)}) collective-permute-start(bf16[256,2048]{1,0:T(8,128)(2,1)S(1)} %get-tuple-element.263), channel_id=1, source_target_pairs={{0,32},{16,48},{32,0},{48,16},{1,33},{17,49},{33,1},{49,17},{2,34}... | collective-permute-start | bytes 3145736 | tf_op jit(solution)/shard_map/ppermute | solution.py:37
  208.8 48.1 %collective-permute-start.13 = (bf16[256,2048]{1,0:T(8,128)(2,1)S(1)}, bf16[256,2048]{1,0:T(8,128)(2,1)S(1)}, u32[]{:S(2)}, u32[]{:S(2)}) collective-permute-start(bf16[256,2048]{1,0:T(8,128)(2,1)S(1)} %get-tuple-element.262), channel_id=1, source_target_pairs={{0,16},{16,32},{32,48},{48,0},{1,17},{17,33},{33,49},{49,1},{2,18}... | collective-permute-start | bytes 3145736 | tf_op jit(solution)/shard_map/ppermute | solution.py:37
  287.4 41.2 %collective-permute-start.18 = (bf16[128,2048]{1,0:T(8,128)(2,1)S(1)}, bf16[128,2048]{1,0:T(8,128)(2,1)S(1)}, u32[]{:S(2)}, u32[]{:S(2)}) collective-permute-start(bf16[128,2048]{1,0:T(8,128)(2,1)S(1)} %slice.201), channel_id=1, source_target_pairs={{0,16},{16,32},{32,48},{48,0},{1,17},{17,33},{33,49},{49,1},{2,18}... | collective-permute-start | bytes 1572872 | tf_op jit(solution)/shard_map/ppermute | solution.py:37
  288.6 40.0 %collective-permute-start.19 = (bf16[128,2048]{1,0:T(8,128)(2,1)S(1)}, bf16[128,2048]{1,0:T(8,128)(2,1)S(1)}, u32[]{:S(2)}, u32[]{:S(2)}) collective-permute-start(bf16[128,2048]{1,0:T(8,128)(2,1)S(1)} %slice.202), channel_id=1, source_target_pairs={{0,48},{16,0},{32,16},{48,32},{1,49},{17,1},{33,17},{49,33},{2,50}... | collective-permute-start | bytes 1572872 | tf_op jit(solution)/shard_map/ppermute | solution.py:37
  325.4 52.5 %collective-permute-start.17 = (bf16[256,2048]{1,0:T(8,128)(2,1)}, bf16[256,2048]{1,0:T(8,128)(2,1)}, u32[]{:S(2)}, u32[]{:S(2)}) collective-permute-start(bf16[256,2048]{1,0:T(8,128)(2,1)} %get-tuple-element.151), channel_id=1, source_target_pairs={{0,16},{16,32},{32,48},{48,0},{1,17},{17,33},{33,49},{49,1},{2,18}... | collective-permute-start | bytes 3145736 | tf_op jit(solution)/shard_map/ppermute | solution.py:37
  325.4 52.5 %collective-permute-start.16 = (bf16[256,2048]{1,0:T(8,128)(2,1)}, bf16[256,2048]{1,0:T(8,128)(2,1)}, u32[]{:S(2)}, u32[]{:S(2)}) collective-permute-start(bf16[256,2048]{1,0:T(8,128)(2,1)} %get-tuple-element.144), channel_id=1, source_target_pairs={{0,48},{16,0},{32,16},{48,32},{1,49},{17,1},{33,17},{49,33},{2,50}... | collective-permute-start | bytes 3145736 | tf_op jit(solution)/shard_map/ppermute | solution.py:37
  442.1 44.2 %collective-permute-start.27 = (bf16[256,2048]{1,0:T(8,128)(2,1)}, bf16[256,2048]{1,0:T(8,128)(2,1)}, u32[]{:S(2)}, u32[]{:S(2)}) collective-permute-start(bf16[256,2048]{1,0:T(8,128)(2,1)} %get-tuple-element.189), channel_id=1, source_target_pairs={{0,32},{16,48},{32,0},{48,16},{1,33},{17,49},{33,1},{49,17},{2,34}... | collective-permute-start | bytes 3145736 | tf_op jit(solution)/shard_map/ppermute | solution.py:37
  443.1 57.9 %all-to-all-start.4 = ((bf16[8,128,1536]{2,1,0:T(8,128)(2,1)}), bf16[8,128,1536]{2,1,0:T(8,128)(2,1)}, u32[]{:S(2)}, u32[]{:S(2)}) async-start(bf16[8,128,1536]{2,1,0:T(8,128)(2,1)} %fusion.2), calls=%async_computation.4 | async-start | bytes 6291456 | tf_op jit(solution)/shard_map/all_to_all | solution.py:668
  501.0 48.4 %all-to-all-start.3 = ((bf16[16,2,256,128]{3,2,1,0:T(8,128)(2,1)}), bf16[16,2,256,128]{3,2,1,0:T(8,128)(2,1)S(1)}, u32[]{:S(2)}, u32[]{:S(2)}) async-start(bf16[16,2,256,128]{3,2,1,0:T(8,128)(2,1)} %pad_maximum_fusion.2), calls=%async_computation.3 | async-start | bytes 4194304 | tf_op jit(solution)/shard_map/all_to_all | solution.py:459
  550.7 71.4 %collective-permute-start.41 = (bf16[128,1536]{1,0:T(8,128)(2,1)S(1)}, bf16[128,1536]{1,0:T(8,128)(2,1)}, u32[]{:S(2)}, u32[]{:S(2)}) collective-permute-start(bf16[128,1536]{1,0:T(8,128)(2,1)S(1)} %add_convert_fusion.4.refs_0_), channel_id=1, source_target_pairs={{0,16},{16,32},{32,48},{48,0},{1,17},{17,33},{33,49},{49,1},{2,18}... | collective-permute-start | bytes 1179656 | tf_op jit(solution)/shard_map/ppermute | solution.py:37
  550.7 71.3 %collective-permute-start.42 = (bf16[128,1536]{1,0:T(8,128)(2,1)S(1)}, bf16[128,1536]{1,0:T(8,128)(2,1)}, u32[]{:S(2)}, u32[]{:S(2)}) collective-permute-start(bf16[128,1536]{1,0:T(8,128)(2,1)S(1)} %add_convert_fusion.4.refs_0_), channel_id=1, source_target_pairs={{0,32},{16,48},{32,0},{48,16},{1,33},{17,49},{33,1},{49,17},{2,34}... | collective-permute-start | bytes 1179656 | tf_op jit(solution)/shard_map/ppermute | solution.py:37
  554.5 70.8 %collective-permute-start.43 = (bf16[128,1536]{1,0:T(8,128)(2,1)S(1)}, bf16[128,1536]{1,0:T(8,128)(2,1)}, u32[]{:S(2)}, u32[]{:S(2)}) collective-permute-start(bf16[128,1536]{1,0:T(8,128)(2,1)S(1)} %add_convert_fusion.4.refs_0_), channel_id=1, source_target_pairs={{0,48},{16,0},{32,16},{48,32},{1,49},{17,1},{33,17},{49,33},{2,50}... | collective-permute-start | bytes 1179656 | tf_op jit(solution)/shard_map/ppermute | solution.py:37
  606.5 40.2 %all-to-all-start.6 = ((bf16[8,128,1152]{2,1,0:T(8,128)(2,1)}), bf16[8,128,1152]{2,1,0:T(8,128)(2,1)}, u32[]{:S(2)}, u32[]{:S(2)}) async-start(bf16[8,128,1152]{2,1,0:T(8,128)(2,1)} %pad_maximum_fusion.1), calls=%async_computation.6 | async-start | bytes 4718592 | tf_op jit(solution)/shard_map/all_to_all | solution.py:668
  622.1 41.4 %collective-permute-start.38 = (bf16[256,2048]{1,0:T(8,128)(2,1)}, bf16[256,2048]{1,0:T(8,128)(2,1)}, u32[]{:S(2)}, u32[]{:S(2)}) collective-permute-start(bf16[256,2048]{1,0:T(8,128)(2,1)} %pad_maximum_fusion.8), channel_id=1, source_target_pairs={{0,16},{16,32},{32,48},{48,0},{1,17},{17,33},{33,49},{49,1},{2,18}... | collective-permute-start | bytes 3145736 | tf_op jit(solution)/shard_map/ppermute | solution.py:37
  622.1 41.4 %collective-permute-start.36 = (bf16[256,2048]{1,0:T(8,128)(2,1)}, bf16[256,2048]{1,0:T(8,128)(2,1)}, u32[]{:S(2)}, u32[]{:S(2)}) collective-permute-start(bf16[256,2048]{1,0:T(8,128)(2,1)} %pad_maximum_fusion.7), channel_id=1, source_target_pairs={{0,48},{16,0},{32,16},{48,32},{1,49},{17,1},{33,17},{49,33},{2,50}... | collective-permute-start | bytes 3145736 | tf_op jit(solution)/shard_map/ppermute | solution.py:37
  669.6 62.5 %collective-permute-start.53 = (bf16[128,3072]{1,0:T(8,128)(2,1)S(1)}, bf16[128,3072]{1,0:T(8,128)(2,1)S(1)}, u32[]{:S(2)}, u32[]{:S(2)}) collective-permute-start(bf16[128,3072]{1,0:T(8,128)(2,1)S(1)} %add_convert_fusion.3.refs_0_), channel_id=1, source_target_pairs={{0,16},{16,32},{32,48},{48,0},{1,17},{17,33},{33,49},{49,1},{2,18}... | collective-permute-start | bytes 2359304 | tf_op jit(solution)/shard_map/ppermute | solution.py:37
  682.7 49.4 %collective-permute-start.54 = (bf16[128,3072]{1,0:T(8,128)(2,1)S(1)}, bf16[128,3072]{1,0:T(8,128)(2,1)S(1)}, u32[]{:S(2)}, u32[]{:S(2)}) collective-permute-start(bf16[128,3072]{1,0:T(8,128)(2,1)S(1)} %add_convert_fusion.3.refs_0_), channel_id=1, source_target_pairs={{0,32},{16,48},{32,0},{48,16},{1,33},{17,49},{33,1},{49,17},{2,34}... | collective-permute-start | bytes 2359304 | tf_op jit(solution)/shard_map/ppermute | solution.py:37
  685.3 46.8 %collective-permute-start.55 = (bf16[128,3072]{1,0:T(8,128)(2,1)S(1)}, bf16[128,3072]{1,0:T(8,128)(2,1)S(1)}, u32[]{:S(2)}, u32[]{:S(2)}) collective-permute-start(bf16[128,3072]{1,0:T(8,128)(2,1)S(1)} %add_convert_fusion.3.refs_0_), channel_id=1, source_target_pairs={{0,48},{16,0},{32,16},{48,32},{1,49},{17,1},{33,17},{49,33},{2,50}... | collective-permute-start | bytes 2359304 | tf_op jit(solution)/shard_map/ppermute | solution.py:37
  (106 other events, 1743.3 us)
Sparse Core Ops, SparseCore 0:
  15.3 66.0 all-gather.3
  84.5 147.2 all-gather.5
  234.9 70.6 all-gather.7
  386.8 160.3 reduce-scatter.1

commit v3 on v2

--- a/solution.py
+++ b/solution.py
@@ -13,6 +13,7 @@
 TILE = 512
 TILES = 8
 PROMPT_TILES = 6
+FF_STEP = 512
 
 norm_eps = 1e-06
 rope_base = 1000000.0
@@ -41,15 +42,6 @@
     return jnp.concatenate(
         [values, shift(values, "z", 1), shift(values, "z", 2), shift(values, "z", 3)], axis=0
     )
-
-
-def scatter_z(partial):
-    rows = partial.shape[0] // RING
-    blocks = [partial[r * rows : (r + 1) * rows] for r in range(RING)]
-    total = blocks[0].astype(jnp.float32)
-    for r in range(1, RING):
-        total = total + shift(blocks[r].astype(low), "z", -r).astype(jnp.float32)
-    return total
 
 
 def forward_kernel(order, q_ref, k_ref, v_ref, mixed_ref, mixed_t_ref, log_ref, k_all, v_t, acc, total):
@@ -221,10 +213,10 @@
     )(order, queries, keys, values, grads, mixed_t, logs)
 
 
-def mlp_kernel(second_ref, cot_ref, gate_ref, up_ref, down_ref, *refs):
+def mlp_kernel(second_ref, cot_ref, both_weight_ref, down_ref, *refs):
     inner_ref, both_ref, second_out, cot_out, grad_ref, acc = refs[-6:]
     at = pl.program_id(0)
-    step = gate_ref.shape[1]
+    step = down_ref.shape[1]
     second = second_ref[...]
 
     @pl.when(at == 0)
@@ -232,40 +224,38 @@
         second_out[0] = second
         cot_out[0] = cot_ref[...]
 
-    gate_weight = gate_ref[...]
-    up_weight = up_ref[...]
-    gate_act = jnp.dot(second, gate_weight, preferred_element_type=jnp.float32)
-    up_act = jnp.dot(second, up_weight, preferred_element_type=jnp.float32)
+    both_act = jnp.dot(second, both_weight_ref[...], preferred_element_type=jnp.float32)
     inner_grad = jnp.dot(cot_ref[...], down_ref[...], preferred_element_type=jnp.float32)
+    gate_act = both_act[:, :step]
+    up_act = both_act[:, step:]
     sigmoid = 1.0 / (1.0 + jnp.exp(-gate_act))
     silu = gate_act * sigmoid
     inner_ref[0] = (silu * up_act).astype(low)
     gate_grad = (inner_grad * up_act * (sigmoid * (1.0 + gate_act * (1.0 - sigmoid)))).astype(low)
-    up_grad = (inner_grad * silu).astype(low)
-    both_ref[0, :, pl.ds(pl.multiple_of(at * step, step), step)] = gate_grad
-    up_at = (pl.num_programs(0) + at) * step
-    both_ref[0, :, pl.ds(pl.multiple_of(up_at, step), step)] = up_grad
+    both_grad = jnp.concatenate([gate_grad, (inner_grad * silu).astype(low)], axis=1)
+    both_ref[0, :, pl.ds(pl.multiple_of(at * 2 * step, 2 * step), 2 * step)] = both_grad
     part = lax.dot_general(
-        gate_grad, gate_weight, contract_last, preferred_element_type=jnp.float32
-    ) + lax.dot_general(up_grad, up_weight, contract_last, preferred_element_type=jnp.float32)
+        both_grad, both_weight_ref[...], contract_last, preferred_element_type=jnp.float32
+    )
+    last = pl.num_programs(0) - 1
 
     @pl.when(at == 0)
     def _():
         acc[...] = part
 
-    @pl.when(at > 0)
+    @pl.when((at > 0) & (at < last))
     def _():
         acc[...] += part
 
-    @pl.when(at == pl.num_programs(0) - 1)
-    def _():
-        grad_ref[...] = acc[...].astype(low)
+    @pl.when(at == last)
+    def _():
+        grad_ref[...] = (acc[...] + part).astype(low)
 
 
 def mlp_block(block, second, cot, weights, held):
     rows, width = second.shape
     hidden_width = weights.shape[1] // 3
-    step = 512
+    step = FF_STEP
     steps = hidden_width // step
     whole = pl.BlockSpec((rows, width), lambda c: (0, 0))
     kept = pl.BlockSpec((1, rows, step), lambda c: (block, 0, c))
@@ -278,8 +268,7 @@
         in_specs=[
             whole,
             whole,
-            pl.BlockSpec((width, step), lambda c: (0, c)),
-            pl.BlockSpec((width, step), lambda c: (0, steps + c)),
+            pl.BlockSpec((width, 2 * step), lambda c: (0, c)),
             pl.BlockSpec((width, step), lambda c: (0, 2 * steps + c)),
         ]
         + [pl.BlockSpec(memory_space=pl.ANY)] * len(held),
@@ -292,14 +281,112 @@
             jax.ShapeDtypeStruct((rows, width), low),
         ),
         scratch_shapes=[pltpu.VMEM((rows, width), jnp.float32)],
-        input_output_aliases={5 + i: i for i in range(len(held))},
+        input_output_aliases={4 + i: i for i in range(len(held))},
         compiler_params=pltpu.CompilerParams(vmem_limit_bytes=48 * 1024 * 1024),
         cost_estimate=pl.CostEstimate(
             flops=2 * 5 * rows * width * hidden_width,
             bytes_accessed=2 * 3 * width * hidden_width,
             transcendentals=rows * hidden_width,
         ),
-    )(second, cot, weights, weights, weights, *held)
+    )(second, cot, weights, weights, *held)
+
+
+def middle_kernel(*refs):
+    mixed_refs, weight_refs = refs[:RING], refs[RING : 2 * RING]
+    hidden_ref, gain_ref, middle_ref, second_ref = refs[2 * RING :]
+    at = pl.program_id(0)
+    step = weight_refs[0].shape[0]
+    columns = pl.ds(pl.multiple_of(at * step, step), step)
+    total = hidden_ref[:, columns].astype(jnp.float32)
+    for mixed, weight in zip(mixed_refs, weight_refs):
+        rows = jnp.concatenate([mixed[head] for head in range(4)], axis=1)
+        total += lax.dot_general(
+            rows, weight[...], contract_last, preferred_element_type=jnp.float32
+        )
+    middle_ref[:, columns] = total
+
+    @pl.when(at == pl.num_programs(0) - 1)
+    def _():
+        second_ref[...] = (normalize(middle_ref[...]) * gain_ref[...]).astype(low)
+
+
+def middle_part(mixed_blocks, weights, hidden, gain):
+    rows, width = hidden.shape
+    steps = 4
+    whole = pl.BlockSpec((rows, width), lambda d: (0, 0))
+    return pl.pallas_call(
+        middle_kernel,
+        grid=(steps,),
+        in_specs=[pl.BlockSpec((4, rows, HEAD_DIM), lambda d: (0, 0, 0))] * RING
+        + [pl.BlockSpec((width // steps, 512), lambda d: (d, 0))] * RING
+        + [whole, pl.BlockSpec((1, width), lambda d: (0, 0))],
+        out_specs=(whole, whole),
+        out_shape=(
+            jax.ShapeDtypeStruct((rows, width), jnp.float32),
+            jax.ShapeDtypeStruct((rows, width), low),
+        ),
+        compiler_params=pltpu.CompilerParams(vmem_limit_bytes=32 * 1024 * 1024),
+        cost_estimate=pl.CostEstimate(flops=1024, bytes_accessed=1024, transcendentals=0),
+    )(*mixed_blocks, *weights, hidden, gain)
+
+
+def middle_back_kernel(*refs):
+    parts, weight_refs = refs[:RING], refs[RING : 2 * RING]
+    middle_ref, cot_ref, gain_ref, grad_ref, low_ref, gain_out, *rest = refs[2 * RING :]
+    outs, accs = rest[:RING], rest[RING:]
+    at = pl.program_id(0)
+    step = weight_refs[0].shape[0]
+
+    @pl.when(at == 0)
+    def _():
+        second_grad = sum(part[...].astype(jnp.float32) for part in parts)
+        middle = middle_ref[...]
+        scale = inverse_rms(middle)
+        normed = middle * scale
+        gain_out[...] = jnp.sum(second_grad * normed, axis=0, keepdims=True)
+        scaled = second_grad * gain_ref[...]
+        grad = cot_ref[...].astype(jnp.float32) + scale * (
+            scaled - normed * jnp.mean(scaled * normed, axis=-1, keepdims=True)
+        )
+        grad_ref[...] = grad
+        low_ref[...] = grad.astype(low)
+        for acc in accs:
+            acc[...] = jnp.zeros_like(acc)
+
+    rows = low_ref[:, pl.ds(pl.multiple_of(at * step, step), step)]
+    for weight, acc in zip(weight_refs, accs):
+        acc[...] += jnp.dot(rows, weight[...], preferred_element_type=jnp.float32)
+
+    @pl.when(at == pl.num_programs(0) - 1)
+    def _():
+        for out, acc in zip(outs, accs):
+            for head in range(4):
+                out[head] = acc[:, head * HEAD_DIM : (head + 1) * HEAD_DIM].astype(low)
+
+
+def middle_back(parts, weights, middle, cot, gain):
+    rows, width = middle.shape
+    steps = 4
+    whole = pl.BlockSpec((rows, width), lambda d: (0, 0))
+    row = pl.BlockSpec((1, width), lambda d: (0, 0))
+    heads = pl.BlockSpec((4, rows, HEAD_DIM), lambda d: (0, 0, 0))
+    return pl.pallas_call(
+        middle_back_kernel,
+        grid=(steps,),
+        in_specs=[whole] * RING
+        + [pl.BlockSpec((width // steps, 512), lambda d: (d, 0))] * RING
+        + [whole, whole, row],
+        out_specs=(whole, whole, row) + (heads,) * RING,
+        out_shape=(
+            jax.ShapeDtypeStruct((rows, width), jnp.float32),
+            jax.ShapeDtypeStruct((rows, width), low),
+            jax.ShapeDtypeStruct((1, width), jnp.float32),
+        )
+        + (jax.ShapeDtypeStruct((4, rows, HEAD_DIM), low),) * RING,
+        scratch_shapes=[pltpu.VMEM((rows, 512), jnp.float32)] * RING,
+        compiler_params=pltpu.CompilerParams(vmem_limit_bytes=40 * 1024 * 1024),
+        cost_estimate=pl.CostEstimate(flops=1024, bytes_accessed=1024, transcendentals=0),
+    )(*parts, *weights, middle, cot, gain)
 
 
 def first_kernel(
@@ -359,12 +446,15 @@
 
 
 def first_back_kernel(
-    back_ref, pre_ref, cos_ref, sin_ref, query_gain, key_gain, grad_ref, query_sum, key_sum
+    core_ref, back_ref, pre_ref, cos_ref, sin_ref, query_gain, key_gain, first_ref,
+    grad_ref, keep_ref, give_ref, query_sum, key_sum, all_grads,
 ):
+    at = pl.program_id(0)
+    rows = grad_ref.shape[1]
     cosine = cos_ref[0]
     sine = sin_ref[0]
 
-    @pl.when(pl.program_id(0) == 0)
+    @pl.when(at == 0)
     def _():
         query_sum[...] = jnp.zeros_like(query_sum)
         key_sum[...] = jnp.zeros_like(key_sum)
@@ -386,73 +476,147 @@
     for head in range(2):
         back(back_ref[2 * head, 1], 4 + head, key_gain[...], key_sum)
         grad_ref[0, :, (6 + head) * HEAD_DIM : (7 + head) * HEAD_DIM] = back_ref[2 * head + 1, 1]
-
-
-def first_back(returned, pre, cosine, sine, query_gain, key_gain):
-    _, rows, _ = pre.shape
+    all_grads[pl.ds(pl.multiple_of(at * rows, rows), rows), :] = grad_ref[0]
+
+    @pl.when(at == RING - 1)
+    def _():
+        grads = all_grads[...]
+        first_core = core_ref[0] == 0
+        for pair in range(8):
+            inputs = first_ref[:, :, pair * 256 : (pair + 1) * 256].reshape(RING * rows, 256)
+            term = lax.dot_general(
+                inputs, grads, contract_first, preferred_element_type=jnp.float32
+            ).astype(low)
+            keep_ref[pair] = jnp.where(first_core, term[:128], term[128:])
+            give_ref[pair] = jnp.where(first_core, term[128:], term[:128])
+
+
+def first_back(core_at, returned, pre, cosine, sine, query_gain, key_gain, first_in):
+    _, rows, width = first_in.shape
     row = pl.BlockSpec((1, HEAD_DIM), lambda r: (0, 0))
     turn = pl.BlockSpec((1, rows, HEAD_DIM), lambda r: (r, 0, 0))
     wide = pl.BlockSpec((1, rows, 1024), lambda r: (r, 0, 0))
+    half = pl.BlockSpec((8, 128, 1024), lambda r: (0, 0, 0))
     return pl.pallas_call(
         first_back_kernel,
         grid=(RING,),
         in_specs=[
+            pl.BlockSpec(memory_space=pltpu.SMEM),
             pl.BlockSpec((4, 2, rows, HEAD_DIM), lambda r: (r, 0, 0, 0)),
             wide,
             turn,
             turn,
             row,
             row,
+            pl.BlockSpec((RING, rows, width), lambda r: (0, 0, 0)),
         ],
-        out_specs=(wide, row, row),
+        out_specs=(wide, half, half, row, row),
         out_shape=(
             jax.ShapeDtypeStruct((RING, rows, 1024), low),
+            jax.ShapeDtypeStruct((8, 128, 1024), low),
+            jax.ShapeDtypeStruct((8, 128, 1024), low),
             jax.ShapeDtypeStruct((1, HEAD_DIM), jnp.float32),
             jax.ShapeDtypeStruct((1, HEAD_DIM), jnp.float32),
         ),
-        compiler_params=pltpu.CompilerParams(vmem_limit_bytes=40 * 1024 * 1024),
-        cost_estimate=pl.CostEstimate(
-            flops=1024, bytes_accessed=1024, transcendentals=0
-        ),
-    )(returned, pre, cosine, sine, query_gain, key_gain)
-
-
-def last_kernel(grad_ref, weight_ref, hidden_ref, part_ref, gain_ref):
+        scratch_shapes=[pltpu.VMEM((RING * rows, 1024), low)],
+        compiler_params=pltpu.CompilerParams(vmem_limit_bytes=48 * 1024 * 1024),
+        cost_estimate=pl.CostEstimate(flops=1024, bytes_accessed=1024, transcendentals=0),
+    )(core_at[None], returned, pre, cosine, sine, query_gain, key_gain, first_in)
+
+
+def last_kernel(
+    core_ref, grad_ref, weight_ref, hidden_ref, mlp_ref, query_ref, key_ref,
+    own_ref, left_ref, opposite_ref, right_ref, keep_ref, give_ref, gain_acc,
+):
+    at = pl.program_id(0)
+    width = hidden_ref.shape[2]
     part = lax.dot_general(
         grad_ref[0], weight_ref[...], contract_last, preferred_element_type=jnp.float32
     )
-    part_ref[0] = part.astype(low)
+    for r, out in enumerate((own_ref, left_ref, opposite_ref, right_ref)):
+
+        @pl.when(at == r)
+        def _(out=out):
+            out[...] = part.astype(low)
+
     normed = normalize(hidden_ref[0].astype(jnp.float32))
     gain = jnp.sum(part * normed, axis=0, keepdims=True)
 
-    @pl.when(pl.program_id(0) == 0)
-    def _():
-        gain_ref[...] = gain
-
-    @pl.when(pl.program_id(0) > 0)
-    def _():
-        gain_ref[...] += gain
-
-
-def last_part(grads, weights, hidden_all):
+    @pl.when(at == 0)
+    def _():
+        gain_acc[...] = gain
+
+    @pl.when(at > 0)
+    def _():
+        gain_acc[...] += gain
+
+    @pl.when(at == RING - 1)
+    def _():
+        lines = [
+            gain_acc[...],
+            mlp_ref[...],
+            jnp.concatenate([query_ref[...]] * BLOCKS, axis=1),
+            jnp.concatenate([key_ref[...]] * BLOCKS, axis=1),
+            jnp.zeros((HEAD_DIM - 4, width), jnp.float32),
+        ]
+        turned = jnp.concatenate(lines, axis=0).T.astype(low)
+        first_core = core_ref[0] == 0
+        for pair in range(8):
+            first = turned[pair * 256 : pair * 256 + 128]
+            second = turned[pair * 256 + 128 : (pair + 1) * 256]
+            keep_ref[pair] = jnp.where(first_core, first, second)
+            give_ref[pair] = jnp.where(first_core, second, first)
+
+
+def last_part(core_at, grads, weights, hidden_all, mlp_part, query_part, key_part):
     _, rows, width = hidden_all.shape
-    wide = pl.BlockSpec((1, rows, width), lambda r: (r, 0, 0))
+    block = pl.BlockSpec((rows, width), lambda r: (0, 0))
+    row = pl.BlockSpec((1, HEAD_DIM), lambda r: (0, 0))
+    half = pl.BlockSpec((8, 128, HEAD_DIM), lambda r: (0, 0, 0))
     return pl.pallas_call(
         last_kernel,
         grid=(RING,),
         in_specs=[
+            pl.BlockSpec(memory_space=pltpu.SMEM),
             pl.BlockSpec((1, rows, 1024), lambda r: (r, 0, 0)),
             pl.BlockSpec((width, 1024), lambda r: (0, 0)),
-            wide,
+            pl.BlockSpec((1, rows, width), lambda r: (r, 0, 0)),
+            pl.BlockSpec((1, width), lambda r: (0, 0)),
+            row,
+            row,
         ],
-        out_specs=(wide, pl.BlockSpec((1, width), lambda r: (0, 0))),
-        out_shape=(
-            jax.ShapeDtypeStruct((RING, rows, width), low),
-            jax.ShapeDtypeStruct((1, width), jnp.float32),
-        ),
+        out_specs=(block,) * RING + (half, half),
+        out_shape=(jax.ShapeDtypeStruct((rows, width), low),) * RING
+        + (jax.ShapeDtypeStruct((8, 128, HEAD_DIM), low),) * 2,
+        scratch_shapes=[pltpu.VMEM((1, width), jnp.float32)],
         compiler_params=pltpu.CompilerParams(vmem_limit_bytes=40 * 1024 * 1024),
         cost_estimate=pl.CostEstimate(flops=1024, bytes_accessed=1024, transcendentals=0),
-    )(grads, weights, hidden_all)
+    )(core_at[None], grads, weights, hidden_all, mlp_part, query_part, key_part)
+
+
+def arrange_kernel(at_ref, own_ref, other_ref, out_ref):
+    y_at, x_at, core_at = at_ref[0], at_ref[1], at_ref[2]
+    for dy in range(RING):
+        for dx in range(2):
+            first = ((y_at - dy + RING) & 3) * 4 + (x_at ^ dx) * 2
+            own = pl.multiple_of((first + core_at) * 128, 128)
+            other = pl.multiple_of((first + 1 - core_at) * 128, 128)
+            out_ref[pl.ds(own, 128), :] = own_ref[dy, dx]
+            out_ref[pl.ds(other, 128), :] = other_ref[dy, dx]
+
+
+def gather_by_permutes(pair, y_at, x_at, core_at):
+    own = jnp.stack([pair] + [shift(pair, "y", r) for r in range(1, RING)])
+    other = shift(own, "core", 1, 2)
+    whole = pl.BlockSpec(memory_space=pltpu.VMEM)
+    return pl.pallas_call(
+        arrange_kernel,
+        in_specs=[pl.BlockSpec(memory_space=pltpu.SMEM), whole, whole],
+        out_specs=whole,
+        out_shape=jax.ShapeDtypeStruct((BLOCKS * 128, pair.shape[2]), pair.dtype),
+        compiler_params=pltpu.CompilerParams(vmem_limit_bytes=16 * 1024 * 1024),
+        cost_estimate=pl.CostEstimate(flops=1024, bytes_accessed=1024, transcendentals=0),
+    )(jnp.stack([y_at, x_at, core_at]), own, other)
 
 
 def to_heads(send):
@@ -477,48 +641,34 @@
     return lax.optimization_barrier(values)
 
 
-def place_kernel(z_ref, *refs):
-    blocks, outs = refs[:RING], refs[RING:]
-    for r in range(RING):
-        slot = lax.rem(z_ref[0] - r + RING, RING)
-        start = 0
-        for out in outs:
-            if out.shape[1] == HEAD_DIM:
-                columns = blocks[r][:, start : start + HEAD_DIM].astype(jnp.float32)
-                out[...] = columns if r == 0 else out[...] + columns
-                continue
-            part = out.shape[1] // RING
-            at = pl.multiple_of(slot * part, part)
-            out[:, pl.ds(at, part)] = blocks[r][:, start : start + part].astype(jnp.float32)
-            start += part
-
-
-def place(z_at, blocks, widths, summed=False):
-    shapes = [RING * part for part in widths] + [HEAD_DIM] * summed
+def place(z_at, blocks, widths, chunk=None, summed=False):
     rows = blocks[0].shape[0]
     whole = pl.BlockSpec(memory_space=pltpu.VMEM)
+    shapes = [RING * part for part in widths] + [HEAD_DIM] * summed
+
+    def kernel(z_ref, *refs):
+        ins, outs = refs[:RING], refs[RING:]
+        for r in range(RING):
+            slot = (z_ref[0] - r + RING) & 3
+            start = 0
+            for turn in range(widths[0] // chunk if chunk else 1):
+                for out, part in zip(outs, widths):
+                    size = chunk or part
+                    at = pl.multiple_of(slot * part + turn * size, 128)
+                    out[:, pl.ds(at, size)] = ins[r][:, start : start + size].astype(jnp.float32)
+                    start += size
+            if summed:
+                columns = ins[r][:, start : start + HEAD_DIM].astype(jnp.float32)
+                outs[-1][...] = columns if r == 0 else outs[-1][...] + columns
+
     return pl.pallas_call(
-        place_kernel,
+        kernel,
         in_specs=[pl.BlockSpec(memory_space=pltpu.SMEM)] + [whole] * RING,
         out_specs=tuple(whole for _ in shapes),
         out_shape=tuple(jax.ShapeDtypeStruct((rows, part), jnp.float32) for part in shapes),
         compiler_params=pltpu.CompilerParams(vmem_limit_bytes=24 * 1024 * 1024),
-        cost_estimate=pl.CostEstimate(
-            flops=0, bytes_accessed=rows * sum(widths) * 24, transcendentals=0
-        ),
+        cost_estimate=pl.CostEstimate(flops=1024, bytes_accessed=1024, transcendentals=0),
     )(z_at[None], *blocks)
-
-
-def ring_sum(own, left, opposite, right):
-    half = left.shape[0] // 2
-    f32 = jnp.float32
-    top = shift(opposite[:half], "z", 3)
-    bottom = shift(opposite[half:], "z", 1)
-    left_top = (left[:half].astype(f32) + top.astype(f32)).astype(low)
-    right_bottom = (right[half:].astype(f32) + bottom.astype(f32)).astype(low)
-    left = shift(jnp.concatenate([left_top, left[half:]], axis=0), "z", 3)
-    right = shift(jnp.concatenate([right[:half], right_bottom], axis=0), "z", 1)
-    return own, left, right
 
 
 def send_back(block, r):
@@ -547,8 +697,9 @@
     ring_rows = RING * rows
     z_at = lax.axis_index("z")
     y_at = lax.axis_index("y")
+    x_at = lax.axis_index("x_hi")
     core_at = lax.axis_index("core")
-    my_index = (y_at * 2 + lax.axis_index("x_hi")) * 2 + core_at
+    my_index = (y_at * 2 + x_at) * 2 + core_at
 
     def columns(weight):
         part = weight.shape[1] // RING
@@ -572,29 +723,29 @@
     )
     first_weights = gather(
         jnp.concatenate(
-            [
-                columns(query_weight),
-                columns(key_weight),
-                columns(value_weight),
-                columns(out_weight),
-                gains,
-            ],
-            axis=1,
+            [columns(query_weight), columns(key_weight), columns(value_weight), gains], axis=1
         )
     )
-    out_full = first_weights[:, 1024:1536]
-    attn_scale = first_weights[:, 1536].astype(f32)[None]
-    mlp_scale = first_weights[:, 1537].astype(f32)[None]
-    mlp_weights = gather(
-        jnp.concatenate([columns(gate_weight), columns(up_weight), columns(down_weight)], axis=1)
-    )
+    attn_scale = first_weights[:, 1024].astype(f32)[None]
+    mlp_scale = first_weights[:, 1025].astype(f32)[None]
+    out_columns = columns(out_weight)
+    out_come = shift(out_columns, "x_hi", 1, 2)
+    gate_columns, up_columns, down_columns, out_come = together(
+        gate_weight, up_weight, down_weight, out_come
+    )
+    gate_columns, up_columns = columns(gate_columns), columns(up_columns)
+    mlp_columns = []
+    for start in range(0, gate_columns.shape[1], FF_STEP):
+        mlp_columns.append(gate_columns[:, start : start + FF_STEP])
+        mlp_columns.append(up_columns[:, start : start + FF_STEP])
+    mlp_weights = gather(jnp.concatenate(mlp_columns + [columns(down_columns)], axis=1))
     down_full = mlp_weights[:, 3072:]
-    out_all = gather(out_weight.astype(low))
+    out_slice = gather_by_permutes(jnp.stack([out_columns, out_come]), y_at, x_at, core_at)
 
     hidden_blocks = ring_blocks(hidden_in)
-    cot_own = after(cotangent, *hidden_blocks)
-    cot_left = shift(cot_own, "z", 1)
-    cot_right = shift(cot_own, "z", 3)
+    out_slice = after(out_slice, *hidden_blocks)
+    out_left = shift(out_slice, "z", 1)
+    out_right = shift(out_slice, "z", 3)
     frequency = rope_base ** (-2.0 * jnp.arange(HEAD_DIM // 2, dtype=f32) / HEAD_DIM)
     angles = places.astype(f32)[:, :, None] * frequency[None, None, :]
     cosine = jnp.cos(angles)
@@ -608,10 +759,13 @@
     first_in, qkv_pre, send = first_part(
         hidden_all, attn_scale, first_weights, cosine, sine, query_row, key_row
     )
-    arrived, cot_left, cot_right, cot_own = together(
-        to_heads(send), cot_left, cot_right, cot_own
-    )
-    cot_opposite = shift(cot_own, "z", 2)
+    arrived, out_left, out_right, cot_own = together(
+        to_heads(send), out_left, out_right, cotangent
+    )
+    out_top = shift(out_left[: width // 2], "z", 1)
+    out_bottom = shift(out_right[width // 2 :], "z", 3)
+    cot_left = shift(cot_own, "z", 1)
+    cot_right = shift(cot_own, "z", 3)
     head_queries = arrived[:, 0]
     own_pair = arrived[:, 1]
     other_pair = shift(own_pair, "core", 1, 2)
@@ -624,19 +778,27 @@
     def from_heads(values):
         return values.reshape(RING, 4, rows, HEAD_DIM).transpose(0, 2, 1, 3).reshape(ring_rows, 512)
 
-    mixed_arrived, cot_opposite = together(to_heads(head_mixed), cot_opposite)
+    mixed_arrived, out_top, out_bottom, cot_left, cot_right = together(
+        to_heads(head_mixed), out_top, out_bottom, cot_left, cot_right
+    )
+    half = rows // 2
+    cot_top = shift(cot_left[:half], "z", 1)
+    cot_bottom = shift(cot_right[half:], "z", 3)
     mixed = from_heads(mixed_arrived)
-    attn_out = lax.dot_general(mixed, out_full, contract_last, preferred_element_type=f32)
+    mixed_blocks = [mixed_arrived[:4]] + [
+        shift(mixed_arrived[4 * (RING - j) : 4 * (RING - j) + 4], "z", j) for j in range(1, RING)
+    ]
+    out_opposite = jnp.concatenate([out_top, out_bottom], axis=0)
+    out_weights = [out_slice, out_left, out_opposite, out_right]
+    mixed_blocks, out_weights, cot_top, cot_bottom = together(
+        mixed_blocks, out_weights, cot_top, cot_bottom
+    )
+    middle, second_in = middle_part(mixed_blocks, out_weights, hidden_in, mlp_scale)
     hidden = hidden_in.astype(f32)
-    middle = hidden + scatter_z(attn_out)
-    middle_rms = inverse_rms(middle)
-    second_norm = middle * middle_rms
-    second_in = (second_norm * mlp_scale).astype(low)
     left = shift(second_in, "z", 1)
     right = shift(second_in, "z", 3)
     *held, own_part = mlp_block(0, second_in, cot_own, mlp_weights, ())
     held, own_part, left, right = together(held, own_part, left, right)
-    half = rows // 2
     top = shift(left[:half], "z", 1)
     bottom = shift(right[half:], "z", 3)
     *held, left_part = mlp_block(1, left, cot_left, mlp_weights, held)
@@ -645,6 +807,7 @@
     right_back = send_back(right_part, 3)
     held, top, bottom = together(held, top, bottom)
     opposite = jnp.concatenate([top, bottom], axis=0)
+    cot_opposite = jnp.concatenate([cot_top, cot_bottom], axis=0)
     *held, opposite_part = mlp_block(2, opposite, cot_opposite, mlp_weights, held)
     opposite_back = send_back(opposite_part, 2)
     inner = held[0].reshape(ring_rows, 1536)
@@ -686,56 +849,46 @@
     )
     both_share = lax.psum_scatter(both_term, GROUP_AXES, scatter_dimension=0, tiled=True)
 
-    second_grad = (
-        own_part.astype(f32)
-        + left_back.astype(f32)
-        + right_back.astype(f32)
-        + opposite_back.astype(f32)
-    )
-    mlp_gain_part = jnp.sum(second_grad * second_norm, axis=0)
-    scaled_grad = second_grad * mlp_scale
-    middle_grad = cotangent.astype(f32) + middle_rms * (
-        scaled_grad - second_norm * jnp.mean(scaled_grad * second_norm, axis=-1, keepdims=True)
-    )
-    own_low = middle_grad.astype(low)
-    mixed_grad = jnp.dot(own_low, out_all, preferred_element_type=f32).astype(low)
-
-    def heads_of(r):
-        return lax.dynamic_slice_in_dim(mixed_grad, ((z_at + r) & (RING - 1)) * 512, 512, 1)
-
-    grad_blocks = [heads_of(0)] + [shift(heads_of(r), "z", r) for r in range(1, RING)]
+    middle_grad, own_low, mlp_gain_part, *grad_blocks = middle_back(
+        (own_part, left_back, right_back, opposite_back),
+        out_weights,
+        middle,
+        cotangent,
+        mlp_scale,
+    )
+    grad_blocks = [grad_blocks[0]] + [shift(grad_blocks[RING - r], "z", r) for r in range(1, RING)]
     down_term = weight_grad(cot_all, inner)
     grad_blocks, down_term, own_low, mlp_rest = together(grad_blocks, down_term, own_low, mlp_rest)
     down_pair = pair_start(down_term)
-    mixed_grad = jnp.stack(grad_blocks).reshape(RING, rows, 4, HEAD_DIM).transpose(0, 2, 1, 3)
-    head_grads = to_heads(mixed_grad.reshape(BLOCKS, rows, HEAD_DIM))
+    head_grads = to_heads(jnp.concatenate(grad_blocks, axis=0))
     down_sum = pair_sum(*down_pair)
     low_left = shift(own_low, "z", 1)
     low_right = shift(own_low, "z", 3)
     head_grads, down_sum, low_left, low_right, own_low, mlp_rest = together(
         head_grads, down_sum, low_left, low_right, own_low, mlp_rest
     )
-    low_opposite = shift(own_low, "z", 2)
+    low_top = shift(low_left[:half], "z", 1)
+    low_bottom = shift(low_right[half:], "z", 3)
     down_share = to_owners(down_sum)
 
     query_grad, key_grad, value_grad = attention_backward(
         order, head_queries, head_keys, head_values, head_grads, head_mixed_t, head_logs
-    )
-    query_grad, key_grad, value_grad, low_opposite, mlp_rest = together(
-        query_grad, key_grad, value_grad, low_opposite, mlp_rest
     )
     keep = jnp.where(core_at == 0, key_grad, value_grad)
     give = jnp.where(core_at == 0, value_grad, key_grad)
     pair_grad = (keep.astype(f32) + shift(give, "core", 1, 2).astype(f32)).astype(low)
-    returned = to_heads(jnp.stack([query_grad, pair_grad], axis=1))
+    grads_send, low_top, low_bottom, down_share, mlp_rest = together(
+        jnp.stack([query_grad, pair_grad], axis=1), low_top, low_bottom, down_share, mlp_rest
+    )
     down_pair = over_x(down_share)
-    middle_low = jnp.concatenate([own_low, low_left, low_opposite, low_right], axis=0)
+    returned = to_heads(grads_send)
+    middle_low = jnp.concatenate(
+        [own_low, low_left, low_top, low_bottom, low_right], axis=0
+    )
     out_sum = pair_sum(*pair_start(weight_grad(middle_low, mixed)))
     mlp_top = shift(mlp_rest[1][:half], "z", 3)
     mlp_bottom = shift(mlp_rest[1][half:], "z", 1)
-    returned, down_pair, out_sum, mlp_top, mlp_bottom = together(
-        returned, down_pair, out_sum, mlp_top, mlp_bottom
-    )
+    returned, out_sum, mlp_top, mlp_bottom = together(returned, out_sum, mlp_top, mlp_bottom)
     out_share = to_owners(out_sum)
     mlp_left = jnp.concatenate(
         [(mlp_rest[0][:half].astype(f32) + mlp_top.astype(f32)).astype(low), mlp_rest[0][half:]],
@@ -747,41 +900,37 @@
     )
     mlp_left = shift(mlp_left, "z", 3)
     mlp_right = shift(mlp_right, "z", 1)
-    qkv_grad, query_gain_part, key_gain_part = first_back(
-        returned, qkv_pre, cosine, sine, query_row, key_row
-    )
-    qkv_term = weight_grad(
-        first_in.reshape(ring_rows, width), qkv_grad.reshape(ring_rows, 1024)
-    )
-    qkv_pair = pair_start(qkv_term)
-    first_partial, attn_gain_part = last_part(
-        after(qkv_grad, qkv_term), first_weights, hidden_all
-    )
-    first_partial, attn_gain_part, out_share = together(first_partial, attn_gain_part, out_share)
-    gains_part = jnp.stack(
-        [
-            attn_gain_part[0],
-            mlp_gain_part,
-            jnp.tile(query_gain_part[0], BLOCKS),
-            jnp.tile(key_gain_part[0], BLOCKS),
-        ],
-        axis=1,
-    )
-    gains_part = jnp.pad(gains_part.astype(low), ((0, 0), (0, HEAD_DIM - 4)))
-    gains_pair = pair_start(gains_part)
+    qkv_grad, qkv_keep, qkv_give, query_gain_part, key_gain_part = first_back(
+        core_at, returned, qkv_pre, cosine, sine, query_row, key_row, first_in
+    )
+    qkv_come = shift(qkv_give, "core", 1, 2)
+    *first_parts, gains_keep, gains_give = last_part(
+        core_at,
+        qkv_grad,
+        first_weights,
+        hidden_all,
+        mlp_gain_part,
+        query_gain_part,
+        key_gain_part,
+    )
+    first_parts, gains_give, qkv_come, out_share, mlp_left, mlp_right, down_pair, both_share = (
+        together(
+            first_parts, gains_give, qkv_come, out_share, mlp_left, mlp_right, down_pair, both_share
+        )
+    )
+    gains_come = shift(gains_give, "core", 1, 2)
+    first_blocks = [first_parts[0]] + [send_back(first_parts[r], r) for r in range(1, RING)]
+    qkv_share = to_owners(
+        jnp.concatenate([pair_sum(qkv_keep, qkv_come), pair_sum(gains_keep, gains_come)], axis=2)
+    )
+    out_pair = over_x(out_share)
+    both_pair = over_x(both_share)
     down_blocks = over_z(down_pair)
-    qkv_pair, gains_pair, first_partial = together(qkv_pair, gains_pair, first_partial)
-    qkv_share = to_owners(
-        jnp.concatenate([pair_sum(*qkv_pair), pair_sum(*gains_pair)], axis=2)
-    )
-    out_pair = over_x(out_share)
-    first_blocks = ring_sum(*[first_partial[r] for r in range(RING)])
-    both_pair = over_x(both_share)
-    first_blocks, qkv_share, out_pair, both_pair, down_blocks, mlp_left, mlp_right = together(
-        first_blocks, qkv_share, out_pair, both_pair, down_blocks, mlp_left, mlp_right
-    )
+    qkv_share, out_pair, both_pair, down_blocks = together(
+        qkv_share, out_pair, both_pair, down_blocks
+    )
+    both_blocks = over_z(both_pair)
     qkv_pair = over_x(qkv_share)
-    both_blocks = over_z(both_pair)
     output = (
         middle + mlp_own.astype(f32) + mlp_left.astype(f32) + mlp_right.astype(f32)
     ).astype(low)
@@ -796,10 +945,10 @@
     ).astype(low)
 
     (down_grad_out,) = place(z_at, down_blocks, (1536,))
-    gate_grad_out, up_grad_out = place(z_at, both_blocks, (1536, 1536))
+    gate_grad_out, up_grad_out = place(z_at, both_blocks, (1536, 1536), chunk=FF_STEP)
     (out_grad_out,) = place(z_at, over_z(out_pair), (512,))
     query_grad_out, key_grad_out, value_grad_out, gain_sum = place(
-        z_at, over_z(qkv_pair), (512, 256, 256), True
+        z_at, over_z(qkv_pair), (512, 256, 256), summed=True
     )
     gain_sum = gain_sum[:, :4].T
 

time: 752 us -> 766 us (1.019)
  starting transfers between devices: 127 us -> 179 us
  waiting for transfers between devices: 277 us -> 225 us
  Pallas kernels: 147 us -> 176 us
  matrix products: 57.3 us -> 41 us
  local copies, waits for them, and re-layouts: 50.7 us -> 63.7 us
  other arithmetic: 66.9 us -> 55.1 us
    ppermute x56 -> x66, starting transfers between devices: 75.8 us -> 130 us  [shift(): lax.ppermute(values, axis, [(i, (i + by) % size) for i in range(size)])]
    ppermute x56 -> x66, waiting for transfers between devices: 205 us -> 170 us  [shift(): lax.ppermute(values, axis, [(i, (i + by) % size) for i in range(size)])]
    pallas_call x6 -> x9, Pallas kernels: 20.8 us -> 52.3 us  [the longest x1 13.6 us: first_back(): pl.pallas_call(first_back_kernel, grid=(RING,), in_specs=[pl.BlockSpec(me...]
    all_gather x3 -> x2, waiting for transfers between devices: 18.4 us -> 0.02 us  [gather(): return lax.all_gather(block, GROUP_AXES, axis=0, tiled=True)]
    all_to_all x4, waiting for transfers between devices: 44.2 us -> 55.2 us  [to_heads(): return lax.all_to_all(send, GROUP_AXES, 0, 0, tiled=True)]
    dot_general x2 -> x0, matrix products: 10.5 us -> none  [the longest x1 6.18 us: local(): jnp.dot(own_low, out_all, preferred_element_type=f32).astype(low)]
    slice x2 -> x7, local copies, waits for them, and re-layouts: 1.4 us -> 11.9 us  [the longest x1 2.28 us: local(): out_top = shift(out_left[:width // 2], 'z', 1)]
    all_to_all x3, waiting for transfers between devices: 9.8 us -> 0.14 us  [to_owners(): terms = lax.all_to_all(pair, ('y', 'x_hi'), 0, 0, tiled=True)]
  transfers between devices with their start and end apart: 67 -> 76, of which waited for: 24 -> 33; matrix products, arithmetic and copies ran while one was open for 19% -> 17% of each run, Pallas kernels for 19% -> 21%
where the time goes in v3:
time: 766 us; the launch traced here: 755 us
  waiting for transfers between devices  225 us (29%)
  starting transfers between devices  179 us (23%)
  Pallas kernels  176 us (23%)
  local copies, waits for them, and re-layouts  63.7 us (8%)
  other arithmetic  55.1 us (7%)
  matrix products  41 us (5%)
  between operations  14.8 us (2%)
    ppermute x66, waiting for transfers between devices, shift(): lax.ppermute(values, axis, [(i, (i + by) % size) for i in range(size)])  170 us
    ppermute x66, starting transfers between devices, shift(): lax.ppermute(values, axis, [(i, (i + by) % size) for i in range(size)])  130 us
    pallas_call x4, Pallas kernels, mlp_block(): pl.pallas_call(mlp_kernel, grid=(steps,), in_specs=[whole, whole, pl.Bloc...  63 us
    all_to_all x4, waiting for transfers between devices, to_heads(): return lax.all_to_all(send, GROUP_AXES, 0, 0, tiled=True)  55.2 us
    pallas_call x1, Pallas kernels, attention_backward(): pl.pallas_call(backward_kernel, out_shape=(jax.ShapeDtypeStruct((BLOCKS,...  33.3 us
    dot_general x3, matrix products, weight_grad(): lax.dot_general(left, right, contract_first, preferred_element_type=f32)  31.2 us
    unnamed x115, local copies, waits for them, and re-layouts  28.7 us
    all_to_all x4, starting transfers between devices, to_heads(): return lax.all_to_all(send, GROUP_AXES, 0, 0, tiled=True)  28.2 us
  transfers between devices with their start and end apart: 76, of which 33 were waited for; matrix products, arithmetic and copies ran while one was open for 17% of the time, Pallas kernels for 21%

profile of v3, /device:TPU:4, one launch (start us, length us, event | category | flops | bytes accessed | tf_op | source)
XLA Modules:
  0.0 755.4 jit_solution(6617916374355974461)
XLA Ops:
  99.4 16.6 %collective-permute-done.12.refs_5_ = bf16[2048,512]{1,0:T(8,128)(2,1)} collective-permute-done((bf16[2048,512]{1,0:T(8,128)(2,1)}, bf16[2048,512]{1,0:T(8,128)(2,1)}, u32[]{:S(2)}, u32[]{:S(2)}) %collective-permute-start.12) | collective-permute-done | bytes 2097184 | tf_op jit(solution)/shard_map/ppermute | solution.py:38
  116.0 19.3 %all-to-all-done = bf16[16,2,256,128]{3,2,1,0:T(8,128)(2,1)} async-done(((bf16[16,2,256,128]{3,2,1,0:T(8,128)(2,1)}), bf16[16,2,256,128]{3,2,1,0:T(8,128)(2,1)}, u32[]{:S(2)}, u32[]{:S(2)}) %all-to-all-start) | async-done | bytes 2097184 | tf_op jit(solution)/shard_map/all_to_all | solution.py:623
  138.2 15.8 %collective-permute-start.17 = (bf16[256,2048]{1,0:T(8,128)(2,1)}, bf16[256,2048]{1,0:T(8,128)(2,1)}, u32[]{:S(2)}, u32[]{:S(2)}) collective-permute-start(bf16[256,2048]{1,0:T(8,128)(2,1)} %refs_9_.1), channel_id=1, source_target_pairs={{0,16},{16,32},{32,48},{48,0},{1,17},{17,33},{33,49},{49,1},{2,18}... | collective-permute-start | bytes 3145736 | tf_op jit(solution)/shard_map/ppermute | solution.py:38
  166.8 18.4 %shard_map.248 = (bf16[16,256,128]{2,1,0:T(8,128)(2,1)S(1)}, f32[8,128,512]{2,1,0:T(8,128)S(1)}, f32[8,1,512]{2,1,0:T(1,128)S(1)}) custom-call(s32[16]{0:T(128)S(1)} %dynamic-slice_bitcast_fusion.2.order, bf16[16,256,128]{2,1,0:T(8,128)(2,1)S(1)} %copy-done.6, bf16[16,256,128]{2,1,0:T(8,128)(2,1)S(1)} %get-tuple-element.310.k_ref, ...), custom_call_target="tpu_custom_call" | custom-call | flops 1024 | bytes 1024 | tf_op jit(solution)/shard_map/pallas_call | solution.py:88
  193.3 9.8 %collective-permute-done.15 = bf16[1024,512]{1,0:T(8,128)(2,1)} collective-permute-done((bf16[1024,512]{1,0:T(8,128)(2,1)}, bf16[1024,512]{1,0:T(8,128)(2,1)}, u32[]{:S(2)}, u32[]{:S(2)}) %collective-permute-start.15) | collective-permute-done | bytes 1048608 | tf_op jit(solution)/shard_map/ppermute | solution.py:38
  203.1 11.1 %all-to-all-done.1 = bf16[16,256,128]{2,1,0:T(8,128)(2,1)} async-done(((bf16[16,256,128]{2,1,0:T(8,128)(2,1)}), bf16[16,256,128]{2,1,0:T(8,128)(2,1)}, u32[]{:S(2)}, u32[]{:S(2)}) %all-to-all-start.1) | async-done | bytes 1048608 | tf_op jit(solution)/shard_map/all_to_all | solution.py:623
  226.2 15.6 %collective-permute-done.19.refs_1_ = bf16[4,256,128]{2,1,0:T(8,128)(2,1)S(1)} collective-permute-done((bf16[4,256,128]{2,1,0:T(8,128)(2,1)S(1)}, bf16[4,256,128]{2,1,0:T(8,128)(2,1)S(1)}, u32[]{:S(2)}, u32[]{:S(2)}) %collective-permute-start.19) | collective-permute-done | bytes 262176 | tf_op jit(solution)/shard_map/ppermute | solution.py:38
  253.7 15.7 %shard_map.250 = (bf16[4,256,1536]{2,1,0:T(8,128)(2,1)}, bf16[4,256,3072]{2,1,0:T(8,128)(2,1)}, bf16[4,256,2048]{2,1,0:T(8,128)(2,1)}, bf16[4,256,2048]{2,1,0:T(8,128)(2,1)}, bf16[256,2048]{1,0:T(8,128)(2,1)S(1)}) custom-call(bf16[256,2048]{1,0:T(8,128)(2,1)} %get-tuple-element.177.second_ref, bf16[256,2048]{1,0:T(8,128)(2,1)} %refs_9_.1, ...), custom_call_target="tpu_custom_call" | custom-call | flops 8053063680 | bytes 18874368 | tf_op jit(solution)/shard_map/pallas_call | solution.py:265
  277.1 16.0 %shard_map.251 = (bf16[4,256,1536]{2,1,0:T(8,128)(2,1)}, bf16[4,256,3072]{2,1,0:T(8,128)(2,1)}, bf16[4,256,2048]{2,1,0:T(8,128)(2,1)}, bf16[4,256,2048]{2,1,0:T(8,128)(2,1)}, bf16[256,2048]{1,0:T(8,128)(2,1)}) custom-call(bf16[256,2048]{1,0:T(8,128)(2,1)} %collective-permute-done.24.second_re, ...), custom_call_target="tpu_custom_call", output_to_operand_aliasing={{0}: (4, {}), {1}: (5, {}), {2}: (6, {}), {3}: (7, {})} | custom-call | flops 8053063680 | bytes 18874368 | tf_op jit(solution)/shard_map/pallas_call | solution.py:265
  300.5 16.0 %shard_map.252 = (bf16[4,256,1536]{2,1,0:T(8,128)(2,1)}, bf16[4,256,3072]{2,1,0:T(8,128)(2,1)}, bf16[4,256,2048]{2,1,0:T(8,128)(2,1)}, bf16[4,256,2048]{2,1,0:T(8,128)(2,1)}, bf16[256,2048]{1,0:T(8,128)(2,1)}) custom-call(bf16[256,2048]{1,0:T(8,128)(2,1)} %collective-permute-done.25.second_re, ...), custom_call_target="tpu_custom_call", output_to_operand_aliasing={{0}: (4, {}), {1}: (5, {}), {2}: (6, {}), {3}: (7, {})} | custom-call | flops 8053063680 | bytes 18874368 | tf_op jit(solution)/shard_map/pallas_call | solution.py:265
  316.5 11.5 %collective-permute-done.29 = bf16[128,2048]{1,0:T(8,128)(2,1)S(1)} collective-permute-done((bf16[128,2048]{1,0:T(8,128)(2,1)S(1)}, bf16[128,2048]{1,0:T(8,128)(2,1)S(1)}, u32[]{:S(2)}, u32[]{:S(2)}) %collective-permute-start.29) | collective-permute-done | bytes 524320 | tf_op jit(solution)/shard_map/ppermute | solution.py:38
  328.1 15.4 %shard_map.253 = (bf16[4,256,1536]{2,1,0:T(8,128)(2,1)}, bf16[4,256,3072]{2,1,0:T(8,128)(2,1)}, bf16[4,256,2048]{2,1,0:T(8,128)(2,1)}, bf16[4,256,2048]{2,1,0:T(8,128)(2,1)}, bf16[256,2048]{1,0:T(8,128)(2,1)}) custom-call(bf16[256,2048]{1,0:T(8,128)(2,1)S(1)} %pad_maximum_fusion.5.second_ref,, ...), custom_call_target="tpu_custom_call", output_to_operand_aliasing={{0}: (4, {}), {1}: (5, {}), {2}: (6, {}), {3}: (7, {})} | custom-call | flops 8053063680 | bytes 18874368 | tf_op jit(solution)/shard_map/pallas_call | solution.py:265
  346.1 19.3 %bitcast_convert_fusion = bf16[2048,3072]{1,0:T(8,128)(2,1)} fusion(bf16[4,256,2048]{2,1,0:T(8,128)(2,1)} %get-tuple-element.211, bf16[4,256,3072]{2,1,0:T(8,128)(2,1)} %get-tuple-element.212), kind=kOutput, calls=%fused_computation | convolution fusion | flops 12891193344 | bytes 23068672 | tf_op jit(solution)/shard_map/dot_general | solution.py:819
  365.5 9.8 %fusion.3 = bf16[1024,2048]{1,0:T(8,128)(2,1)S(1)} fusion(bf16[1024,1536]{1,0:T(8,128)(2,1)} %bitcast.93, bf16[2048,4608]{1,0:T(8,128)(2,1)} %all-gather.5.cloned.1.call-done.both_weight_ref.down_ref), kind=kOutput, calls=%fused_computation.8 | convolution fusion | flops 6444548096 | bytes 13631488 | tf_op jit(solution)/shard_map/dot_general | solution.py:842
  381.6 10.5 %shard_map.254 = (f32[256,2048]{1,0:T(8,128)S(1)}, bf16[256,2048]{1,0:T(8,128)(2,1)}, f32[1,2048]{1,0:T(1,128)S(1)}, bf16[4,256,128]{2,1,0:T(8,128)(2,1)S(1)}, b...) custom-call(bf16[256,2048]{1,0:T(8,128)(2,1)S(1)} %copy-done.24, ...), custom_call_target="tpu_custom_call" | custom-call | flops 1024 | bytes 1024 | tf_op jit(solution)/shard_map/pallas_call | solution.py:373
  426.3 17.0 %all-to-all-done.2.g_ref = bf16[16,256,128]{2,1,0:T(8,128)(2,1)} async-done(((bf16[16,256,128]{2,1,0:T(8,128)(2,1)}), bf16[16,256,128]{2,1,0:T(8,128)(2,1)}, u32[]{:S(2)}, u32[]{:S(2)}) %all-to-all-start.2) | async-done | bytes 1048608 | tf_op jit(solution)/shard_map/all_to_all | solution.py:623
  443.3 9.9 %all-to-all-start.3 = ((bf16[8,128,1536]{2,1,0:T(8,128)(2,1)}), bf16[8,128,1536]{2,1,0:T(8,128)(2,1)}, u32[]{:S(2)}, u32[]{:S(2)}) async-start(bf16[8,128,1536]{2,1,0:T(8,128)(2,1)} %fusion.2), calls=%async_computation.3 | async-start | bytes 6291456 | tf_op jit(solution)/shard_map/all_to_all | solution.py:831
  453.2 33.3 %shard_map.255 = (bf16[16,256,128]{2,1,0:T(8,128)(2,1)S(1)}, bf16[16,256,128]{2,1,0:T(8,128)(2,1)S(1)}, bf16[16,256,128]{2,1,0:T(8,128)(2,1)S(1)}) custom-call(s32[16]{0:T(128)S(1)} %dynamic-slice_bitcast_fusion.2.order, bf16[16,256,128]{2,1,0:T(8,128)(2,1)S(1)} %copy-done.7, bf16[16,256,128]{2,1,0:T(8,128)(2,1)S(1)} %get-tuple-element.310.k_ref, ...), custom_call_target="tpu_custom_call" | custom-call | flops 1024 | bytes 1024 | tf_op jit(solution)/shard_map/pallas_call | solution.py:192
  532.7 10.9 %collective-permute-done.41 = bf16[128,2048]{1,0:T(8,128)(2,1)} collective-permute-done((bf16[128,2048]{1,0:T(8,128)(2,1)S(1)}, bf16[128,2048]{1,0:T(8,128)(2,1)}, u32[]{:S(2)}, u32[]{:S(2)}) %collective-permute-start.41) | collective-permute-done | bytes 524320 | tf_op jit(solution)/shard_map/ppermute | solution.py:38
  554.4 13.6 %shard_map.256 = (bf16[4,256,1024]{2,1,0:T(8,128)(2,1)S(1)}, bf16[8,128,1024]{2,1,0:T(8,128)(2,1)S(1)}, bf16[8,128,1024]{2,1,0:T(8,128)(2,1)}, f32[1,128]{1,0:T(1,128)S(1)}, f32[1,128]{1,0:T(1,128)S(1)}) custom-call(s32[1]{0:T(128)} %bitcast.11.core_ref, bf16[16,2,256,128]{3,2,1,0:T(8,128)(2,1)} %all-to-all-done.4.back_ref, f32[4,256,1024]{2,1,0:T(8,128)} %copy-done.11, ...), custom_call_target="tpu_custom_call" | custom-call | flops 1024 | bytes 1024 | tf_op jit(solution)/shard_map/pallas_call | solution.py:500
  585.3 11.4 %shard_map.257 = (bf16[256,2048]{1,0:T(8,128)(2,1)S(1)}, bf16[256,2048]{1,0:T(8,128)(2,1)}, bf16[256,2048]{1,0:T(8,128)(2,1)}, bf16[256,2048]{1,0:T(8,128)(2,1)}...) custom-call(s32[1]{0:T(128)} %bitcast.11.core_ref, bf16[4,256,1024]{2,1,0:T(8,128)(2,1)S(1)} %copy-done.15, ...), custom_call_target="tpu_custom_call" | custom-call | flops 1024 | bytes 1024 | tf_op jit(solution)/shard_map/pallas_call | solution.py:576
  627.4 14.8 %collective-permute-done.49 = bf16[256,2048]{1,0:T(8,128)(2,1)S(1)} collective-permute-done((bf16[256,2048]{1,0:T(8,128)(2,1)}, bf16[256,2048]{1,0:T(8,128)(2,1)S(1)}, u32[]{:S(2)}, u32[]{:S(2)}) %collective-permute-start.49) | collective-permute-done | bytes 1048608 | tf_op jit(solution)/shard_map/ppermute | solution.py:38
  642.2 21.8 %collective-permute-start.54 = (bf16[128,1536]{1,0:T(8,128)(2,1)S(1)}, bf16[128,1536]{1,0:T(8,128)(2,1)S(1)}, u32[]{:S(2)}, u32[]{:S(2)}) collective-permute-start(bf16[128,1536]{1,0:T(8,128)(2,1)S(1)} %add_convert_fusion.4.refs_0_), channel_id=1, source_target_pairs={{0,32},{16,48},{32,0},{48,16},{1,33},{17,49},{33,1},{49,17},{2,34}... | collective-permute-start | bytes 1179656 | tf_op jit(solution)/shard_map/ppermute | solution.py:38
  711.6 30.0 %collective-permute-done.58.refs_2_ = bf16[128,1152]{1,0:T(8,128)(2,1)S(1)} collective-permute-done((bf16[128,1152]{1,0:T(8,128)(2,1)S(1)}, bf16[128,1152]{1,0:T(8,128)(2,1)S(1)}, u32[]{:S(2)}, u32[]{:S(2)}) %collective-permute-start.58) | collective-permute-done | bytes 294944 | tf_op jit(solution)/shard_map/ppermute | solution.py:38
  (346 shorter events, 356.9 us)
Async XLA Ops:
  7.2 69.9 %all-gather.3.cloned.1.call-start = ((), (), s32[]{:S(2)}) async-start(), calls=%async_computation.8 | async-start | bytes 5013504 | tf_op jit(solution)/shard_map/all_gather | solution.py:709
  10.9 242.8 %all-gather.5.cloned.1.call-start = ((), (), s32[]{:S(2)}) async-start(), calls=%async_computation.9 | async-start | bytes 20054016 | tf_op jit(solution)/shard_map/all_gather | solution.py:709
  69.9 46.1 %collective-permute-start.12 = (bf16[2048,512]{1,0:T(8,128)(2,1)}, bf16[2048,512]{1,0:T(8,128)(2,1)}, u32[]{:S(2)}, u32[]{:S(2)}) collective-permute-start(bf16[2048,512]{1,0:T(8,128)(2,1)} %shard_map.247.refs_4_), channel_id=1, source_target_pairs={{0,16},{16,32},{32,48},{48,0},{1,17},{17,33},{33,49},{49,1},{2,18}... | collective-permute-start | bytes 6291464 | tf_op jit(solution)/shard_map/ppermute | solution.py:38
  70.3 45.8 %collective-permute-start.13 = (bf16[2048,512]{1,0:T(8,128)(2,1)}, bf16[2048,512]{1,0:T(8,128)(2,1)}, u32[]{:S(2)}, u32[]{:S(2)}) collective-permute-start(bf16[2048,512]{1,0:T(8,128)(2,1)} %shard_map.247.refs_4_), channel_id=1, source_target_pairs={{0,48},{16,0},{32,16},{48,32},{1,49},{17,1},{33,17},{49,33},{2,50}... | collective-permute-start | bytes 6291464 | tf_op jit(solution)/shard_map/ppermute | solution.py:38
  93.5 41.8 %all-to-all-start = ((bf16[16,2,256,128]{3,2,1,0:T(8,128)(2,1)}), bf16[16,2,256,128]{3,2,1,0:T(8,128)(2,1)}, u32[]{:S(2)}, u32[]{:S(2)}) async-start(bf16[16,2,256,128]{3,2,1,0:T(8,128)(2,1)} %copy-done.20), calls=%async_computation | async-start | bytes 4194304 | tf_op jit(solution)/shard_map/all_to_all | solution.py:623
  138.2 64.8 %collective-permute-start.17 = (bf16[256,2048]{1,0:T(8,128)(2,1)}, bf16[256,2048]{1,0:T(8,128)(2,1)}, u32[]{:S(2)}, u32[]{:S(2)}) collective-permute-start(bf16[256,2048]{1,0:T(8,128)(2,1)} %refs_9_.1), channel_id=1, source_target_pairs={{0,16},{16,32},{32,48},{48,0},{1,17},{17,33},{33,49},{49,1},{2,18}... | collective-permute-start | bytes 3145736 | tf_op jit(solution)/shard_map/ppermute | solution.py:38
  154.1 49.0 %collective-permute-start.18 = (bf16[256,2048]{1,0:T(8,128)(2,1)}, bf16[256,2048]{1,0:T(8,128)(2,1)}, u32[]{:S(2)}, u32[]{:S(2)}) collective-permute-start(bf16[256,2048]{1,0:T(8,128)(2,1)} %refs_9_.1), channel_id=1, source_target_pairs={{0,48},{16,0},{32,16},{48,32},{1,49},{17,1},{33,17},{49,33},{2,50}... | collective-permute-start | bytes 3145736 | tf_op jit(solution)/shard_map/ppermute | solution.py:38
  159.2 43.9 %collective-permute-start.15 = (bf16[1024,512]{1,0:T(8,128)(2,1)}, bf16[1024,512]{1,0:T(8,128)(2,1)}, u32[]{:S(2)}, u32[]{:S(2)}) collective-permute-start(bf16[1024,512]{1,0:T(8,128)(2,1)} %slice.169), channel_id=1, source_target_pairs={{0,16},{16,32},{32,48},{48,0},{1,17},{17,33},{33,49},{49,1},{2,18}... | collective-permute-start | bytes 3145736 | tf_op jit(solution)/shard_map/ppermute | solution.py:38
  161.5 41.6 %collective-permute-start.16 = (bf16[1024,512]{1,0:T(8,128)(2,1)}, bf16[1024,512]{1,0:T(8,128)(2,1)}, u32[]{:S(2)}, u32[]{:S(2)}) collective-permute-start(bf16[1024,512]{1,0:T(8,128)(2,1)} %slice.170), channel_id=1, source_target_pairs={{0,48},{16,0},{32,16},{48,32},{1,49},{17,1},{33,17},{49,33},{2,50}... | collective-permute-start | bytes 3145736 | tf_op jit(solution)/shard_map/ppermute | solution.py:38
  193.2 409.0 %reduce-scatter.2.cloned.1.call-start = ((), (), s32[]{:S(2)}) async-start(), calls=%async_computation.10 | async-start | bytes 13369344 | tf_op jit(solution)/shard_map/reduce_scatter | solution.py:850
  293.1 85.0 %collective-permute-start.26 = (bf16[256,2048]{1,0:T(8,128)(2,1)}, bf16[256,2048]{1,0:T(8,128)(2,1)}, u32[]{:S(2)}, u32[]{:S(2)}) collective-permute-start(bf16[256,2048]{1,0:T(8,128)(2,1)} %get-tuple-element.191), channel_id=1, source_target_pairs={{0,48},{16,0},{32,16},{48,32},{1,49},{17,1},{33,17},{49,33},{2,50}... | collective-permute-start | bytes 3145736 | tf_op jit(solution)/shard_map/ppermute | solution.py:38
  316.4 61.7 %collective-permute-start.27 = (bf16[256,2048]{1,0:T(8,128)(2,1)}, bf16[256,2048]{1,0:T(8,128)(2,1)}, u32[]{:S(2)}, u32[]{:S(2)}) collective-permute-start(bf16[256,2048]{1,0:T(8,128)(2,1)} %get-tuple-element.197), channel_id=1, source_target_pairs={{0,16},{16,32},{32,48},{48,0},{1,17},{17,33},{33,49},{49,1},{2,18}... | collective-permute-start | bytes 3145736 | tf_op jit(solution)/shard_map/ppermute | solution.py:38
  443.3 58.9 %all-to-all-start.3 = ((bf16[8,128,1536]{2,1,0:T(8,128)(2,1)}), bf16[8,128,1536]{2,1,0:T(8,128)(2,1)}, u32[]{:S(2)}, u32[]{:S(2)}) async-start(bf16[8,128,1536]{2,1,0:T(8,128)(2,1)} %fusion.2), calls=%async_computation.3 | async-start | bytes 6291456 | tf_op jit(solution)/shard_map/all_to_all | solution.py:831
  507.7 46.6 %all-to-all-start.4 = ((bf16[16,2,256,128]{3,2,1,0:T(8,128)(2,1)}), bf16[16,2,256,128]{3,2,1,0:T(8,128)(2,1)}, u32[]{:S(2)}, u32[]{:S(2)}) async-start(bf16[16,2,256,128]{3,2,1,0:T(8,128)(2,1)} %pad_maximum_fusion.3), calls=%async_computation.4 | async-start | bytes 4194304 | tf_op jit(solution)/shard_map/all_to_all | solution.py:623
  607.2 61.2 %all-to-all-start.6 = ((bf16[8,128,1152]{2,1,0:T(8,128)(2,1)}), bf16[8,128,1152]{2,1,0:T(8,128)(2,1)}, u32[]{:S(2)}, u32[]{:S(2)}) async-start(bf16[8,128,1152]{2,1,0:T(8,128)(2,1)} %pad_maximum_fusion.1), calls=%async_computation.7 | async-start | bytes 4718592 | tf_op jit(solution)/shard_map/all_to_all | solution.py:831
  613.9 51.1 %collective-permute-start.48 = (bf16[256,2048]{1,0:T(8,128)(2,1)}, bf16[256,2048]{1,0:T(8,128)(2,1)S(1)}, u32[]{:S(2)}, u32[]{:S(2)}) collective-permute-start(bf16[256,2048]{1,0:T(8,128)(2,1)} %get-tuple-element.272), channel_id=1, source_target_pairs={{0,32},{16,48},{32,0},{48,16},{1,33},{17,49},{33,1},{49,17},{2,34}... | collective-permute-start | bytes 3145736 | tf_op jit(solution)/shard_map/ppermute | solution.py:38
  618.3 46.7 %collective-permute-start.47 = (bf16[256,2048]{1,0:T(8,128)(2,1)}, bf16[256,2048]{1,0:T(8,128)(2,1)S(1)}, u32[]{:S(2)}, u32[]{:S(2)}) collective-permute-start(bf16[256,2048]{1,0:T(8,128)(2,1)} %get-tuple-element.271), channel_id=1, source_target_pairs={{0,48},{16,0},{32,16},{48,32},{1,49},{17,1},{33,17},{49,33},{2,50}... | collective-permute-start | bytes 3145736 | tf_op jit(solution)/shard_map/ppermute | solution.py:38
  618.3 62.6 %collective-permute-start.52 = (bf16[128,3072]{1,0:T(8,128)(2,1)}, bf16[128,3072]{1,0:T(8,128)(2,1)}, u32[]{:S(2)}, u32[]{:S(2)}) collective-permute-start(bf16[128,3072]{1,0:T(8,128)(2,1)} %reduce-scatter.2.cloned.1.call-done), channel_id=1, source_target_pairs={{0,64},{64,0},{1,65},{65,1},{2,66},{66,2},{3,67},{67,3},{4,68},{68... | collective-permute-start | bytes 2359304 | tf_op jit(solution)/shard_map/ppermute | solution.py:38
  621.8 49.4 %collective-permute-start.53 = (bf16[128,1536]{1,0:T(8,128)(2,1)S(1)}, bf16[128,1536]{1,0:T(8,128)(2,1)S(1)}, u32[]{:S(2)}, u32[]{:S(2)}) collective-permute-start(bf16[128,1536]{1,0:T(8,128)(2,1)S(1)} %add_convert_fusion.4.refs_0_), channel_id=1, source_target_pairs={{0,16},{16,32},{32,48},{48,0},{1,17},{17,33},{33,49},{49,1},{2,18}... | collective-permute-start | bytes 1179656 | tf_op jit(solution)/shard_map/ppermute | solution.py:38
  693.5 52.1 %collective-permute-start.63 = (bf16[128,3072]{1,0:T(8,128)(2,1)S(1)}, bf16[128,3072]{1,0:T(8,128)(2,1)S(1)}, u32[]{:S(2)}, u32[]{:S(2)}) collective-permute-start(bf16[128,3072]{1,0:T(8,128)(2,1)S(1)} %add_convert_fusion.3.refs_0_), channel_id=1, source_target_pairs={{0,16},{16,32},{32,48},{48,0},{1,17},{17,33},{33,49},{49,1},{2,18}... | collective-permute-start | bytes 2359304 | tf_op jit(solution)/shard_map/ppermute | solution.py:38
  693.6 52.0 %collective-permute-start.64 = (bf16[128,3072]{1,0:T(8,128)(2,1)S(1)}, bf16[128,3072]{1,0:T(8,128)(2,1)S(1)}, u32[]{:S(2)}, u32[]{:S(2)}) collective-permute-start(bf16[128,3072]{1,0:T(8,128)(2,1)S(1)} %add_convert_fusion.3.refs_0_), channel_id=1, source_target_pairs={{0,32},{16,48},{32,0},{48,16},{1,33},{17,49},{33,1},{49,17},{2,34}... | collective-permute-start | bytes 2359304 | tf_op jit(solution)/shard_map/ppermute | solution.py:38
  697.1 48.5 %collective-permute-start.65 = (bf16[128,3072]{1,0:T(8,128)(2,1)S(1)}, bf16[128,3072]{1,0:T(8,128)(2,1)S(1)}, u32[]{:S(2)}, u32[]{:S(2)}) collective-permute-start(bf16[128,3072]{1,0:T(8,128)(2,1)S(1)} %add_convert_fusion.3.refs_0_), channel_id=1, source_target_pairs={{0,48},{16,0},{32,16},{48,32},{1,49},{17,1},{33,17},{49,33},{2,50}... | collective-permute-start | bytes 2359304 | tf_op jit(solution)/shard_map/ppermute | solution.py:38
  699.8 41.9 %collective-permute-start.58 = (bf16[128,1152]{1,0:T(8,128)(2,1)S(1)}, bf16[128,1152]{1,0:T(8,128)(2,1)S(1)}, u32[]{:S(2)}, u32[]{:S(2)}) collective-permute-start(bf16[128,1152]{1,0:T(8,128)(2,1)S(1)} %add_convert_fusion.5.refs_0_), channel_id=1, source_target_pairs={{0,32},{16,48},{32,0},{48,16},{1,33},{17,49},{33,1},{49,17},{2,34}... | collective-permute-start | bytes 884744 | tf_op jit(solution)/shard_map/ppermute | solution.py:38
  701.9 41.5 %collective-permute-start.59 = (bf16[128,1152]{1,0:T(8,128)(2,1)S(1)}, bf16[128,1152]{1,0:T(8,128)(2,1)S(1)}, u32[]{:S(2)}, u32[]{:S(2)}) collective-permute-start(bf16[128,1152]{1,0:T(8,128)(2,1)S(1)} %add_convert_fusion.5.refs_0_), channel_id=1, source_target_pairs={{0,48},{16,0},{32,16},{48,32},{1,49},{17,1},{33,17},{49,33},{2,50}... | collective-permute-start | bytes 884744 | tf_op jit(solution)/shard_map/ppermute | solution.py:38
  (104 other events, 1527.1 us)
Sparse Core Ops, SparseCore 0:
  11.1 63.0 all-gather.2
  77.2 146.5 all-gather.4
  379.3 175.9 reduce-scatter.1

commit v4 on v3

--- a/solution.py
+++ b/solution.py
@@ -1,3 +1,5 @@
+import functools
+
 import jax
 import jax.numpy as jnp
 from jax import lax
@@ -14,6 +16,7 @@
 TILES = 8
 PROMPT_TILES = 6
 FF_STEP = 512
+VMEM_LIMIT = 60 * 1024 * 1024
 
 norm_eps = 1e-06
 rope_base = 1000000.0
@@ -44,18 +47,31 @@
     )
 
 
-def forward_kernel(order, q_ref, k_ref, v_ref, mixed_ref, mixed_t_ref, log_ref, k_all, v_t, acc, total):
+def tile_rows(ref, order, tile, *slot):
+    return jnp.concatenate([ref[order[2 * tile + half], *slot] for half in range(2)], axis=0)
+
+
+def forward_kernel(
+    order, core, own_ref, other_ref, mixed_ref, mixed_t_ref, log_ref, k_all, v_t, acc, total
+):
     tile = pl.program_id(0)
 
-    @pl.when(tile == 0)
-    def _():
+    def take(keys_of, values_of):
         for at in range(BLOCKS):
-            k_all[at * BLOCK : (at + 1) * BLOCK, :] = k_ref[order[at]]
+            k_all[at * BLOCK : (at + 1) * BLOCK, :] = keys_of(order[at])
             v_t[at // 2, :, (at % 2) * BLOCK : (at % 2 + 1) * BLOCK] = (
-                v_ref[order[at]].astype(jnp.float32).T.astype(low)
+                values_of(order[at]).astype(jnp.float32).T.astype(low)
             )
 
-    queries = jnp.concatenate([q_ref[order[2 * tile]], q_ref[order[2 * tile + 1]]], axis=0)
+    @pl.when((tile == 0) & (core[0] == 0))
+    def _():
+        take(lambda at: own_ref[at, 1], lambda at: other_ref[at])
+
+    @pl.when((tile == 0) & (core[0] == 1))
+    def _():
+        take(lambda at: other_ref[at], lambda at: own_ref[at, 1])
+
+    queries = tile_rows(own_ref, order, tile, 0)
     acc[...] = jnp.zeros_like(acc)
     total[...] = jnp.zeros_like(total)
 
@@ -83,7 +99,7 @@
     mixed_ref[order[2 * tile + 1]] = mixed[BLOCK:]
 
 
-def attention_forward(order, queries, keys, values):
+def attention_forward(order, core_at, arrived, other):
     whole = pl.BlockSpec(memory_space=pltpu.VMEM)
     return pl.pallas_call(
         forward_kernel,
@@ -93,9 +109,9 @@
             jax.ShapeDtypeStruct((TILES, 1, TILE), jnp.float32),
         ),
         grid_spec=pltpu.PrefetchScalarGridSpec(
-            num_scalar_prefetch=1,
+            num_scalar_prefetch=2,
             grid=(TILES,),
-            in_specs=[whole] * 3,
+            in_specs=[whole] * 2,
             out_specs=(whole, whole, whole),
             scratch_shapes=[
                 pltpu.VMEM((BLOCKS * BLOCK, HEAD_DIM), low),
@@ -104,48 +120,44 @@
                 pltpu.VMEM((1, TILE), jnp.float32),
             ],
         ),
-        compiler_params=pltpu.CompilerParams(vmem_limit_bytes=40 * 1024 * 1024),
+        compiler_params=pltpu.CompilerParams(vmem_limit_bytes=VMEM_LIMIT),
         cost_estimate=pl.CostEstimate(
             flops=1024, bytes_accessed=1024, transcendentals=0
         ),
-    )(order, queries, keys, values)
+    )(order, core_at[None], arrived, other)
 
 
 def backward_kernel(
-    order,
-    q_ref,
-    k_ref,
-    v_ref,
-    g_ref,
-    mixed_t_ref,
-    log_ref,
-    q_out,
-    k_out,
-    v_out,
-    k_all,
-    v_all,
-    k_t,
-    q_acc,
-    k_acc,
-    v_acc,
+    order, core, own_ref, other_ref, g_ref, mixed_t_ref, log_ref, q_out, keep_out, give_out,
+    k_all, v_all, k_t, q_acc, k_acc, v_acc,
 ):
     tile = pl.program_id(0)
 
-    @pl.when(tile == 0)
-    def _():
+    def take(keys_of, values_of):
         for at in range(BLOCKS):
             rows = slice(at * BLOCK, (at + 1) * BLOCK)
-            keys = k_ref[order[at]]
+            keys = keys_of(order[at])
             k_all[rows, :] = keys
-            v_all[rows, :] = v_ref[order[at]]
+            v_all[rows, :] = values_of(order[at])
             k_t[at // 2, :, (at % 2) * BLOCK : (at % 2 + 1) * BLOCK] = (
                 keys.astype(jnp.float32).T.astype(low)
             )
+
+    @pl.when((tile == 0) & (core[0] == 0))
+    def _():
+        take(lambda at: own_ref[at, 1], lambda at: other_ref[at])
+
+    @pl.when((tile == 0) & (core[0] == 1))
+    def _():
+        take(lambda at: other_ref[at], lambda at: own_ref[at, 1])
+
+    @pl.when(tile == 0)
+    def _():
         k_acc[...] = jnp.zeros_like(k_acc)
         v_acc[...] = jnp.zeros_like(v_acc)
 
-    queries = jnp.concatenate([q_ref[order[2 * tile]], q_ref[order[2 * tile + 1]]], axis=0)
-    grads = jnp.concatenate([g_ref[order[2 * tile]], g_ref[order[2 * tile + 1]]], axis=0)
+    queries = tile_rows(own_ref, order, tile, 0)
+    grads = tile_rows(g_ref, order, tile)
     grads_t = grads.astype(jnp.float32).T
     shared = jnp.sum(grads_t * mixed_t_ref[tile], axis=0, keepdims=True)
     logs = log_ref[tile]
@@ -175,27 +187,35 @@
 
     chunk(tile, True)
     query_grad = (q_acc[...] * score_scale).T.astype(low)
-    q_out[order[2 * tile]] = query_grad[:BLOCK]
-    q_out[order[2 * tile + 1]] = query_grad[BLOCK:]
-
-    @pl.when(tile == TILES - 1)
-    def _():
+    q_out[order[2 * tile], 0] = query_grad[:BLOCK]
+    q_out[order[2 * tile + 1], 0] = query_grad[BLOCK:]
+
+    def give(keep_acc, keep_scale, give_acc, give_scale):
         for at in range(BLOCKS):
             rows = slice(at * BLOCK, (at + 1) * BLOCK)
-            k_out[order[at]] = (k_acc[rows, :] * score_scale).astype(low)
-            v_out[order[at]] = v_acc[rows, :].astype(low)
-
-
-def attention_backward(order, queries, keys, values, grads, mixed_t, logs):
+            keep_out[order[at]] = (keep_acc[rows, :] * keep_scale).astype(low)
+            give_out[order[at]] = (give_acc[rows, :] * give_scale).astype(low)
+
+    @pl.when((tile == TILES - 1) & (core[0] == 0))
+    def _():
+        give(k_acc, score_scale, v_acc, 1.0)
+
+    @pl.when((tile == TILES - 1) & (core[0] == 1))
+    def _():
+        give(v_acc, 1.0, k_acc, score_scale)
+
+
+def attention_backward(order, core_at, arrived, other, grads, mixed_t, logs):
     whole = pl.BlockSpec(memory_space=pltpu.VMEM)
     rows = BLOCKS * BLOCK
     return pl.pallas_call(
         backward_kernel,
-        out_shape=(jax.ShapeDtypeStruct((BLOCKS, BLOCK, HEAD_DIM), low),) * 3,
+        out_shape=(jax.ShapeDtypeStruct((BLOCKS, 2, BLOCK, HEAD_DIM), low),)
+        + (jax.ShapeDtypeStruct((BLOCKS, BLOCK, HEAD_DIM), low),) * 2,
         grid_spec=pltpu.PrefetchScalarGridSpec(
-            num_scalar_prefetch=1,
+            num_scalar_prefetch=2,
             grid=(TILES,),
-            in_specs=[whole] * 6,
+            in_specs=[whole] * 5,
             out_specs=(whole, whole, whole),
             scratch_shapes=[
                 pltpu.VMEM((rows, HEAD_DIM), low),
@@ -206,34 +226,47 @@
                 pltpu.VMEM((rows, HEAD_DIM), jnp.float32),
             ],
         ),
-        compiler_params=pltpu.CompilerParams(vmem_limit_bytes=48 * 1024 * 1024),
+        compiler_params=pltpu.CompilerParams(vmem_limit_bytes=VMEM_LIMIT),
         cost_estimate=pl.CostEstimate(
             flops=1024, bytes_accessed=1024, transcendentals=0
         ),
-    )(order, queries, keys, values, grads, mixed_t, logs)
-
-
-def mlp_kernel(second_ref, cot_ref, both_weight_ref, down_ref, *refs):
-    inner_ref, both_ref, second_out, cot_out, grad_ref, acc = refs[-6:]
+    )(order, core_at[None], arrived, other, grads, mixed_t, logs)
+
+
+def mlp_kernel(parts, *refs):
+    second_refs, cot_refs = refs[:parts], refs[parts : 2 * parts]
+    both_weight_ref, down_ref = refs[2 * parts : 2 * parts + 2]
+    count = refs[-1].shape[0] // BLOCK
+    inner_ref, both_ref, second_out, cot_out = refs[-5 - count : -1 - count]
+    grad_refs, acc = refs[-1 - count : -1], refs[-1]
     at = pl.program_id(0)
     step = down_ref.shape[1]
-    second = second_ref[...]
+    rows, width = acc.shape
 
     @pl.when(at == 0)
     def _():
-        second_out[0] = second
-        cot_out[0] = cot_ref[...]
-
+        for ins, out in ((second_refs, second_out), (cot_refs, cot_out)):
+            start = 0
+            for part in ins:
+                size = part.shape[0]
+                out[start // BLOCK, start % BLOCK : start % BLOCK + size, :] = part[...]
+                start += size
+
+    second = second_out[...].reshape(rows, width)
     both_act = jnp.dot(second, both_weight_ref[...], preferred_element_type=jnp.float32)
-    inner_grad = jnp.dot(cot_ref[...], down_ref[...], preferred_element_type=jnp.float32)
+    inner_grad = jnp.dot(
+        cot_out[...].reshape(rows, width), down_ref[...], preferred_element_type=jnp.float32
+    )
     gate_act = both_act[:, :step]
     up_act = both_act[:, step:]
     sigmoid = 1.0 / (1.0 + jnp.exp(-gate_act))
     silu = gate_act * sigmoid
-    inner_ref[0] = (silu * up_act).astype(low)
+    inner_ref[...] = (silu * up_act).astype(low).reshape(inner_ref.shape)
     gate_grad = (inner_grad * up_act * (sigmoid * (1.0 + gate_act * (1.0 - sigmoid)))).astype(low)
     both_grad = jnp.concatenate([gate_grad, (inner_grad * silu).astype(low)], axis=1)
-    both_ref[0, :, pl.ds(pl.multiple_of(at * 2 * step, 2 * step), 2 * step)] = both_grad
+    both_ref[:, :, pl.ds(pl.multiple_of(at * 2 * step, 2 * step), 2 * step)] = both_grad.reshape(
+        count, BLOCK, 2 * step
+    )
     part = lax.dot_general(
         both_grad, both_weight_ref[...], contract_last, preferred_element_type=jnp.float32
     )
@@ -249,46 +282,130 @@
 
     @pl.when(at == last)
     def _():
-        grad_ref[...] = (acc[...] + part).astype(low)
-
-
-def mlp_block(block, second, cot, weights, held):
-    rows, width = second.shape
+        total = (acc[...] + part).astype(low)
+        for block, grad in enumerate(grad_refs):
+            grad[...] = total[block * BLOCK : (block + 1) * BLOCK]
+
+
+def mlp_blocks(place_at, seconds, cots, weights, held):
+    rows = sum(second.shape[0] for second in seconds)
+    width = seconds[0].shape[1]
+    count = rows // BLOCK
     hidden_width = weights.shape[1] // 3
     step = FF_STEP
     steps = hidden_width // step
-    whole = pl.BlockSpec((rows, width), lambda c: (0, 0))
-    kept = pl.BlockSpec((1, rows, step), lambda c: (block, 0, c))
-    kept_both = pl.BlockSpec((1, rows, 2 * hidden_width), lambda c: (block, 0, 0))
-    kept_rows = pl.BlockSpec((1, rows, width), lambda c: (block, 0, 0))
-    rows_shape = jax.ShapeDtypeStruct((RING, rows, width), low)
+    ins = [
+        pl.BlockSpec(value.shape, lambda c: (0, 0), pipeline_mode=pl.Buffered(1))
+        for value in (*seconds, *cots)
+    ]
+    kept = pl.BlockSpec((count, BLOCK, step), lambda c: (place_at, 0, c))
+    kept_both = pl.BlockSpec((count, BLOCK, 2 * hidden_width), lambda c: (place_at, 0, 0))
+    kept_rows = pl.BlockSpec((count, BLOCK, width), lambda c: (place_at, 0, 0))
+    rows_shape = jax.ShapeDtypeStruct((RING, BLOCK, width), low)
     return pl.pallas_call(
-        mlp_kernel,
+        functools.partial(mlp_kernel, len(seconds)),
         grid=(steps,),
-        in_specs=[
-            whole,
-            whole,
+        in_specs=ins
+        + [
             pl.BlockSpec((width, 2 * step), lambda c: (0, c)),
             pl.BlockSpec((width, step), lambda c: (0, 2 * steps + c)),
         ]
         + [pl.BlockSpec(memory_space=pl.ANY)] * len(held),
-        out_specs=(kept, kept_both, kept_rows, kept_rows, whole),
+        out_specs=(kept, kept_both, kept_rows, kept_rows)
+        + (pl.BlockSpec((BLOCK, width), lambda c: (0, 0)),) * count,
         out_shape=(
-            jax.ShapeDtypeStruct((RING, rows, hidden_width), low),
-            jax.ShapeDtypeStruct((RING, rows, 2 * hidden_width), low),
+            jax.ShapeDtypeStruct((RING, BLOCK, hidden_width), low),
+            jax.ShapeDtypeStruct((RING, BLOCK, 2 * hidden_width), low),
             rows_shape,
             rows_shape,
-            jax.ShapeDtypeStruct((rows, width), low),
-        ),
+        )
+        + (jax.ShapeDtypeStruct((BLOCK, width), low),) * count,
         scratch_shapes=[pltpu.VMEM((rows, width), jnp.float32)],
-        input_output_aliases={4 + i: i for i in range(len(held))},
-        compiler_params=pltpu.CompilerParams(vmem_limit_bytes=48 * 1024 * 1024),
+        input_output_aliases={len(ins) + 2 + i: i for i in range(len(held))},
+        compiler_params=pltpu.CompilerParams(vmem_limit_bytes=VMEM_LIMIT),
         cost_estimate=pl.CostEstimate(
             flops=2 * 5 * rows * width * hidden_width,
             bytes_accessed=2 * 3 * width * hidden_width,
             transcendentals=rows * hidden_width,
         ),
-    )(second, cot, weights, weights, *held)
+    )(*seconds, *cots, weights, weights, *held)
+
+
+def mlp_out_kernel(inner_ref, weight_ref, *outs):
+    inner = inner_ref[...].reshape(RING * BLOCK, inner_ref.shape[2])
+    part = lax.dot_general(
+        inner, weight_ref[...], contract_last, preferred_element_type=jnp.float32
+    ).astype(low)
+    for block, out in enumerate(outs):
+        out[...] = part[block * BLOCK : (block + 1) * BLOCK]
+
+
+def mlp_out_part(inner, weights):
+    _, rows, hidden_width = inner.shape
+    width = weights.shape[0]
+    steps = 4
+    return pl.pallas_call(
+        mlp_out_kernel,
+        grid=(steps,),
+        in_specs=[
+            pl.BlockSpec(inner.shape, lambda d: (0, 0, 0)),
+            pl.BlockSpec((width // steps, hidden_width), lambda d: (d, 2)),
+        ],
+        out_specs=(pl.BlockSpec((rows, width // steps), lambda d: (0, d)),) * RING,
+        out_shape=(jax.ShapeDtypeStruct((rows, width), low),) * RING,
+        compiler_params=pltpu.CompilerParams(vmem_limit_bytes=VMEM_LIMIT),
+        cost_estimate=pl.CostEstimate(flops=1024, bytes_accessed=1024, transcendentals=0),
+    )(inner, weights)
+
+
+def pair_grad(core_at, lefts, right, by_heads=False):
+    width = lefts[0].shape[-1]
+    outs = 512 if by_heads else right.shape[2]
+    rows = RING * BLOCK
+
+    def kernel(core_ref, *refs):
+        left_refs = refs[: len(lefts)]
+        right_ref, keep_ref, give_ref = refs[len(lefts) : len(lefts) + 3]
+        if by_heads:
+            all_ref = refs[-1]
+
+            @pl.when(pl.program_id(0) == 0)
+            def _():
+                for r in range(RING):
+                    for head in range(4):
+                        all_ref[
+                            r * BLOCK : (r + 1) * BLOCK, head * HEAD_DIM : (head + 1) * HEAD_DIM
+                        ] = right_ref[4 * r + head]
+
+            values = all_ref[...]
+        else:
+            values = right_ref[...].reshape(rows, outs)
+        inputs = [ref[...].reshape(-1, 256) for ref in left_refs]
+        inputs = inputs[0] if len(inputs) == 1 else jnp.concatenate(inputs, axis=0)
+        term = lax.dot_general(
+            inputs, values, contract_first, preferred_element_type=jnp.float32
+        ).astype(low)
+        first_core = core_ref[0] == 0
+        keep_ref[0] = jnp.where(first_core, term[:128], term[128:])
+        give_ref[0] = jnp.where(first_core, term[128:], term[:128])
+
+    def columns(value):
+        lead = value.shape[:-1]
+        return pl.BlockSpec((*lead, 256), lambda i: (0,) * len(lead) + (i,))
+
+    half = pl.BlockSpec((1, 128, outs), lambda i: (i, 0, 0))
+    return pl.pallas_call(
+        kernel,
+        grid=(width // 256,),
+        in_specs=[pl.BlockSpec(memory_space=pltpu.SMEM)]
+        + [columns(value) for value in lefts]
+        + [pl.BlockSpec(right.shape, lambda i: (0, 0, 0))],
+        out_specs=(half, half),
+        out_shape=(jax.ShapeDtypeStruct((width // 256, 128, outs), low),) * 2,
+        scratch_shapes=[pltpu.VMEM((rows, 512), low)] * by_heads,
+        compiler_params=pltpu.CompilerParams(vmem_limit_bytes=VMEM_LIMIT),
+        cost_estimate=pl.CostEstimate(flops=1024, bytes_accessed=1024, transcendentals=0),
+    )(core_at[None], *lefts, right)
 
 
 def middle_kernel(*refs):
@@ -325,7 +442,7 @@
             jax.ShapeDtypeStruct((rows, width), jnp.float32),
             jax.ShapeDtypeStruct((rows, width), low),
         ),
-        compiler_params=pltpu.CompilerParams(vmem_limit_bytes=32 * 1024 * 1024),
+        compiler_params=pltpu.CompilerParams(vmem_limit_bytes=VMEM_LIMIT),
         cost_estimate=pl.CostEstimate(flops=1024, bytes_accessed=1024, transcendentals=0),
     )(*mixed_blocks, *weights, hidden, gain)
 
@@ -384,7 +501,7 @@
         )
         + (jax.ShapeDtypeStruct((4, rows, HEAD_DIM), low),) * RING,
         scratch_shapes=[pltpu.VMEM((rows, 512), jnp.float32)] * RING,
-        compiler_params=pltpu.CompilerParams(vmem_limit_bytes=40 * 1024 * 1024),
+        compiler_params=pltpu.CompilerParams(vmem_limit_bytes=VMEM_LIMIT),
         cost_estimate=pl.CostEstimate(flops=1024, bytes_accessed=1024, transcendentals=0),
     )(*parts, *weights, middle, cot, gain)
 
@@ -436,7 +553,7 @@
             jax.ShapeDtypeStruct((RING, rows, 1024), jnp.float32),
             jax.ShapeDtypeStruct((BLOCKS, 2, rows, HEAD_DIM), low),
         ),
-        compiler_params=pltpu.CompilerParams(vmem_limit_bytes=40 * 1024 * 1024),
+        compiler_params=pltpu.CompilerParams(vmem_limit_bytes=VMEM_LIMIT),
         cost_estimate=pl.CostEstimate(
             flops=2 * RING * rows * width * 1024,
             bytes_accessed=20 * 1024 * 1024,
@@ -519,25 +636,31 @@
             jax.ShapeDtypeStruct((1, HEAD_DIM), jnp.float32),
         ),
         scratch_shapes=[pltpu.VMEM((RING * rows, 1024), low)],
-        compiler_params=pltpu.CompilerParams(vmem_limit_bytes=48 * 1024 * 1024),
+        compiler_params=pltpu.CompilerParams(vmem_limit_bytes=VMEM_LIMIT),
         cost_estimate=pl.CostEstimate(flops=1024, bytes_accessed=1024, transcendentals=0),
     )(core_at[None], returned, pre, cosine, sine, query_gain, key_gain, first_in)
 
 
 def last_kernel(
     core_ref, grad_ref, weight_ref, hidden_ref, mlp_ref, query_ref, key_ref,
-    own_ref, left_ref, opposite_ref, right_ref, keep_ref, give_ref, gain_acc,
+    own_ref, left_ref, top_ref, bottom_ref, right_ref, keep_ref, give_ref, gain_acc,
 ):
     at = pl.program_id(0)
     width = hidden_ref.shape[2]
     part = lax.dot_general(
         grad_ref[0], weight_ref[...], contract_last, preferred_element_type=jnp.float32
     )
-    for r, out in enumerate((own_ref, left_ref, opposite_ref, right_ref)):
+    half = top_ref.shape[0]
+    for r, out in ((0, own_ref), (1, left_ref), (3, right_ref)):
 
         @pl.when(at == r)
         def _(out=out):
             out[...] = part.astype(low)
+
+    @pl.when(at == 2)
+    def _():
+        top_ref[...] = part[:half].astype(low)
+        bottom_ref[...] = part[half:].astype(low)
 
     normed = normalize(hidden_ref[0].astype(jnp.float32))
     gain = jnp.sum(part * normed, axis=0, keepdims=True)
@@ -571,6 +694,9 @@
 def last_part(core_at, grads, weights, hidden_all, mlp_part, query_part, key_part):
     _, rows, width = hidden_all.shape
     block = pl.BlockSpec((rows, width), lambda r: (0, 0))
+    small = pl.BlockSpec((rows // 2, width), lambda r: (0, 0))
+    whole = jax.ShapeDtypeStruct((rows, width), low)
+    part = jax.ShapeDtypeStruct((rows // 2, width), low)
     row = pl.BlockSpec((1, HEAD_DIM), lambda r: (0, 0))
     half = pl.BlockSpec((8, 128, HEAD_DIM), lambda r: (0, 0, 0))
     return pl.pallas_call(
@@ -585,11 +711,11 @@
             row,
             row,
         ],
-        out_specs=(block,) * RING + (half, half),
-        out_shape=(jax.ShapeDtypeStruct((rows, width), low),) * RING
+        out_specs=(block, block, small, small, block, half, half),
+        out_shape=(whole, whole, part, part, whole)
         + (jax.ShapeDtypeStruct((8, 128, HEAD_DIM), low),) * 2,
         scratch_shapes=[pltpu.VMEM((1, width), jnp.float32)],
-        compiler_params=pltpu.CompilerParams(vmem_limit_bytes=40 * 1024 * 1024),
+        compiler_params=pltpu.CompilerParams(vmem_limit_bytes=VMEM_LIMIT),
         cost_estimate=pl.CostEstimate(flops=1024, bytes_accessed=1024, transcendentals=0),
     )(core_at[None], grads, weights, hidden_all, mlp_part, query_part, key_part)
 
@@ -614,7 +740,7 @@
         in_specs=[pl.BlockSpec(memory_space=pltpu.SMEM), whole, whole],
         out_specs=whole,
         out_shape=jax.ShapeDtypeStruct((BLOCKS * 128, pair.shape[2]), pair.dtype),
-        compiler_params=pltpu.CompilerParams(vmem_limit_bytes=16 * 1024 * 1024),
+        compiler_params=pltpu.CompilerParams(vmem_limit_bytes=VMEM_LIMIT),
         cost_estimate=pl.CostEstimate(flops=1024, bytes_accessed=1024, transcendentals=0),
     )(jnp.stack([y_at, x_at, core_at]), own, other)
 
@@ -666,7 +792,7 @@
         in_specs=[pl.BlockSpec(memory_space=pltpu.SMEM)] + [whole] * RING,
         out_specs=tuple(whole for _ in shapes),
         out_shape=tuple(jax.ShapeDtypeStruct((rows, part), jnp.float32) for part in shapes),
-        compiler_params=pltpu.CompilerParams(vmem_limit_bytes=24 * 1024 * 1024),
+        compiler_params=pltpu.CompilerParams(vmem_limit_bytes=VMEM_LIMIT),
         cost_estimate=pl.CostEstimate(flops=1024, bytes_accessed=1024, transcendentals=0),
     )(z_at[None], *blocks)
 
@@ -739,7 +865,6 @@
         mlp_columns.append(gate_columns[:, start : start + FF_STEP])
         mlp_columns.append(up_columns[:, start : start + FF_STEP])
     mlp_weights = gather(jnp.concatenate(mlp_columns + [columns(down_columns)], axis=1))
-    down_full = mlp_weights[:, 3072:]
     out_slice = gather_by_permutes(jnp.stack([out_columns, out_come]), y_at, x_at, core_at)
 
     hidden_blocks = ring_blocks(hidden_in)
@@ -759,76 +884,54 @@
     first_in, qkv_pre, send = first_part(
         hidden_all, attn_scale, first_weights, cosine, sine, query_row, key_row
     )
-    arrived, out_left, out_right, cot_own = together(
-        to_heads(send), out_left, out_right, cotangent
-    )
     out_top = shift(out_left[: width // 2], "z", 1)
     out_bottom = shift(out_right[width // 2 :], "z", 3)
+    arrived, out_left, out_right, out_top, out_bottom = together(
+        to_heads(send), out_left, out_right, out_top, out_bottom
+    )
+    other_pair = shift(arrived[:, 1], "core", 1, 2)
+    head_mixed, head_mixed_t, head_logs = attention_forward(order, core_at, arrived, other_pair)
+    cot_own = after(cotangent, head_mixed)
     cot_left = shift(cot_own, "z", 1)
     cot_right = shift(cot_own, "z", 3)
-    head_queries = arrived[:, 0]
-    own_pair = arrived[:, 1]
-    other_pair = shift(own_pair, "core", 1, 2)
-    head_keys = jnp.where(core_at == 0, own_pair, other_pair)
-    head_values = jnp.where(core_at == 0, other_pair, own_pair)
-    head_mixed, head_mixed_t, head_logs = attention_forward(
-        order, head_queries, head_keys, head_values
-    )
-
-    def from_heads(values):
-        return values.reshape(RING, 4, rows, HEAD_DIM).transpose(0, 2, 1, 3).reshape(ring_rows, 512)
-
-    mixed_arrived, out_top, out_bottom, cot_left, cot_right = together(
-        to_heads(head_mixed), out_top, out_bottom, cot_left, cot_right
-    )
+
+    mixed_arrived, cot_left, cot_right = together(to_heads(head_mixed), cot_left, cot_right)
     half = rows // 2
-    cot_top = shift(cot_left[:half], "z", 1)
-    cot_bottom = shift(cot_right[half:], "z", 3)
-    mixed = from_heads(mixed_arrived)
     mixed_blocks = [mixed_arrived[:4]] + [
         shift(mixed_arrived[4 * (RING - j) : 4 * (RING - j) + 4], "z", j) for j in range(1, RING)
     ]
     out_opposite = jnp.concatenate([out_top, out_bottom], axis=0)
     out_weights = [out_slice, out_left, out_opposite, out_right]
-    mixed_blocks, out_weights, cot_top, cot_bottom = together(
-        mixed_blocks, out_weights, cot_top, cot_bottom
-    )
+    mixed_blocks, out_weights = together(mixed_blocks, out_weights)
     middle, second_in = middle_part(mixed_blocks, out_weights, hidden_in, mlp_scale)
     hidden = hidden_in.astype(f32)
     left = shift(second_in, "z", 1)
     right = shift(second_in, "z", 3)
-    *held, own_part = mlp_block(0, second_in, cot_own, mlp_weights, ())
-    held, own_part, left, right = together(held, own_part, left, right)
+    *held, own_part = mlp_blocks(0, [second_in], [cot_own], mlp_weights, ())
+    held, own_part, left, right, cot_left, cot_right = together(
+        held, own_part, left, right, cot_left, cot_right
+    )
     top = shift(left[:half], "z", 1)
     bottom = shift(right[half:], "z", 3)
-    *held, left_part = mlp_block(1, left, cot_left, mlp_weights, held)
+    cot_top = shift(cot_left[:half], "z", 1)
+    cot_bottom = shift(cot_right[half:], "z", 3)
+    *held, left_part, right_part = mlp_blocks(
+        1, [left, right], [cot_left, cot_right], mlp_weights, held
+    )
     left_back = send_back(left_part, 1)
-    *held, right_part = mlp_block(3, right, cot_right, mlp_weights, held)
     right_back = send_back(right_part, 3)
-    held, top, bottom = together(held, top, bottom)
-    opposite = jnp.concatenate([top, bottom], axis=0)
-    cot_opposite = jnp.concatenate([cot_top, cot_bottom], axis=0)
-    *held, opposite_part = mlp_block(2, opposite, cot_opposite, mlp_weights, held)
+    held, top, bottom, cot_top, cot_bottom = together(held, top, bottom, cot_top, cot_bottom)
+    *held, opposite_part = mlp_blocks(1, [top, bottom], [cot_top, cot_bottom], mlp_weights, held)
     opposite_back = send_back(opposite_part, 2)
-    inner = held[0].reshape(ring_rows, 1536)
-    both_grad = held[1].reshape(ring_rows, 3072)
-    second_all = held[2].reshape(ring_rows, width)
-    cot_all = held[3].reshape(ring_rows, width)
-
-    def weight_grad(left, right):
-        return lax.dot_general(left, right, contract_first, preferred_element_type=f32).astype(low)
-
-    def pair_start(term):
-        term = term.reshape(8, 2, 128, term.shape[1])
-        keep = lax.dynamic_index_in_dim(term, core_at, 1, keepdims=False)
-        give = lax.dynamic_index_in_dim(term, 1 - core_at, 1, keepdims=False)
-        return keep, shift(give, "core", 1, 2)
+    inner, both_grad, second_all, cot_all = held
 
     def pair_sum(keep, come):
         return (keep.astype(f32) + come.astype(f32)).astype(low)
 
     def to_owners(pair):
-        terms = lax.all_to_all(pair, ("y", "x_hi"), 0, 0, tiled=True)
+        return lax.all_to_all(pair, ("y", "x_hi"), 0, 0, tiled=True)
+
+    def add_up(terms):
         return jnp.sum(terms.astype(f32), axis=0).astype(low)
 
     def over_x(share):
@@ -838,14 +941,14 @@
         share = pair_sum(*pair)
         return [share] + [shift(share, "z", r) for r in range(1, RING)]
 
-    both_term = weight_grad(second_all, both_grad)
-    mlp_out = lax.dot_general(
-        inner, down_full, contract_last, preferred_element_type=f32
-    ).reshape(RING, rows, width)
-    mlp_own = mlp_out[0].astype(low)
-    mlp_rest = mlp_out[1:].astype(low)
-    left_back, right_back, opposite_back, both_term, mlp_own, mlp_rest, inner = together(
-        left_back, right_back, opposite_back, both_term, mlp_own, mlp_rest, inner
+    both_term = lax.dot_general(
+        second_all.reshape(ring_rows, width),
+        both_grad.reshape(ring_rows, 3072),
+        contract_first,
+        preferred_element_type=f32,
+    ).astype(low)
+    left_back, right_back, opposite_back, both_term, inner = together(
+        left_back, right_back, opposite_back, both_term, inner
     )
     both_share = lax.psum_scatter(both_term, GROUP_AXES, scatter_dimension=0, tiled=True)
 
@@ -857,52 +960,46 @@
         mlp_scale,
     )
     grad_blocks = [grad_blocks[0]] + [shift(grad_blocks[RING - r], "z", r) for r in range(1, RING)]
-    down_term = weight_grad(cot_all, inner)
-    grad_blocks, down_term, own_low, mlp_rest = together(grad_blocks, down_term, own_low, mlp_rest)
-    down_pair = pair_start(down_term)
+    down_keep, down_give = pair_grad(core_at, [cot_all], inner)
+    grad_blocks, down_keep, down_give, own_low, inner = together(
+        grad_blocks, down_keep, down_give, own_low, inner
+    )
     head_grads = to_heads(jnp.concatenate(grad_blocks, axis=0))
-    down_sum = pair_sum(*down_pair)
     low_left = shift(own_low, "z", 1)
     low_right = shift(own_low, "z", 3)
-    head_grads, down_sum, low_left, low_right, own_low, mlp_rest = together(
-        head_grads, down_sum, low_left, low_right, own_low, mlp_rest
-    )
-    low_top = shift(low_left[:half], "z", 1)
-    low_bottom = shift(low_right[half:], "z", 3)
-    down_share = to_owners(down_sum)
-
-    query_grad, key_grad, value_grad = attention_backward(
-        order, head_queries, head_keys, head_values, head_grads, head_mixed_t, head_logs
-    )
-    keep = jnp.where(core_at == 0, key_grad, value_grad)
-    give = jnp.where(core_at == 0, value_grad, key_grad)
-    pair_grad = (keep.astype(f32) + shift(give, "core", 1, 2).astype(f32)).astype(low)
-    grads_send, low_top, low_bottom, down_share, mlp_rest = together(
-        jnp.stack([query_grad, pair_grad], axis=1), low_top, low_bottom, down_share, mlp_rest
-    )
-    down_pair = over_x(down_share)
+    down_sum = pair_sum(down_keep, shift(down_give, "core", 1, 2))
+    mlp_own, mlp_opposite, mlp_left, mlp_right = mlp_out_part(inner, mlp_weights)
+    head_grads, down_sum, low_left, low_right, own_low, mlp_opposite, mlp_left, mlp_right = together(
+        head_grads, down_sum, low_left, low_right, own_low, mlp_opposite, mlp_left, mlp_right
+    )
+    mlp_left = send_back(mlp_left, 1)
+    mlp_right = send_back(mlp_right, 3)
+    down_terms = to_owners(down_sum)
+
+    query_grad, grad_keep, grad_give = attention_backward(
+        order, core_at, arrived, other_pair, head_grads, head_mixed_t, head_logs
+    )
+    query_grad, grad_keep, grad_give, mlp_left, mlp_right, own_low, mlp_opposite = together(
+        query_grad, grad_keep, grad_give, mlp_left, mlp_right, own_low, mlp_opposite
+    )
+    low_opposite = shift(own_low, "z", 2)
+    grads_send = lax.dynamic_update_slice_in_dim(
+        query_grad, pair_sum(grad_keep, shift(grad_give, "core", 1, 2))[:, None], 1, 1
+    )
+    grads_send, down_terms = together(grads_send, down_terms)
     returned = to_heads(grads_send)
-    middle_low = jnp.concatenate(
-        [own_low, low_left, low_top, low_bottom, low_right], axis=0
-    )
-    out_sum = pair_sum(*pair_start(weight_grad(middle_low, mixed)))
-    mlp_top = shift(mlp_rest[1][:half], "z", 3)
-    mlp_bottom = shift(mlp_rest[1][half:], "z", 1)
-    returned, out_sum, mlp_top, mlp_bottom = together(returned, out_sum, mlp_top, mlp_bottom)
-    out_share = to_owners(out_sum)
-    mlp_left = jnp.concatenate(
-        [(mlp_rest[0][:half].astype(f32) + mlp_top.astype(f32)).astype(low), mlp_rest[0][half:]],
-        axis=0,
-    )
-    mlp_right = jnp.concatenate(
-        [mlp_rest[2][:half], (mlp_rest[2][half:].astype(f32) + mlp_bottom.astype(f32)).astype(low)],
-        axis=0,
-    )
-    mlp_left = shift(mlp_left, "z", 3)
-    mlp_right = shift(mlp_right, "z", 1)
+    down_pair = over_x(add_up(down_terms))
+    out_keep, out_give = pair_grad(
+        core_at, [own_low, low_left, low_opposite, low_right], mixed_arrived, by_heads=True
+    )
+    out_sum = pair_sum(out_keep, shift(out_give, "core", 1, 2))
+    mlp_opposite = send_back(mlp_opposite, 2)
+    returned, out_sum, mlp_opposite = together(returned, out_sum, mlp_opposite)
+    out_terms = to_owners(out_sum)
     qkv_grad, qkv_keep, qkv_give, query_gain_part, key_gain_part = first_back(
         core_at, returned, qkv_pre, cosine, sine, query_row, key_row, first_in
     )
+    qkv_grad, qkv_give, down_pair = together(qkv_grad, qkv_give, down_pair)
     qkv_come = shift(qkv_give, "core", 1, 2)
     *first_parts, gains_keep, gains_give = last_part(
         core_at,
@@ -913,28 +1010,40 @@
         query_gain_part,
         key_gain_part,
     )
-    first_parts, gains_give, qkv_come, out_share, mlp_left, mlp_right, down_pair, both_share = (
-        together(
-            first_parts, gains_give, qkv_come, out_share, mlp_left, mlp_right, down_pair, both_share
-        )
+    down_blocks = over_z(down_pair)
+    first_parts, gains_give, qkv_come, out_terms, down_blocks, both_share = together(
+        first_parts, gains_give, qkv_come, out_terms, down_blocks, both_share
     )
     gains_come = shift(gains_give, "core", 1, 2)
-    first_blocks = [first_parts[0]] + [send_back(first_parts[r], r) for r in range(1, RING)]
-    qkv_share = to_owners(
+    first_own, first_left, first_top, first_bottom, first_right = first_parts
+    first_top = shift(first_top, "z", 3)
+    first_bottom = shift(first_bottom, "z", 1)
+    qkv_terms = to_owners(
         jnp.concatenate([pair_sum(qkv_keep, qkv_come), pair_sum(gains_keep, gains_come)], axis=2)
     )
-    out_pair = over_x(out_share)
     both_pair = over_x(both_share)
-    down_blocks = over_z(down_pair)
-    qkv_share, out_pair, both_pair, down_blocks = together(
-        qkv_share, out_pair, both_pair, down_blocks
-    )
-    both_blocks = over_z(both_pair)
+    out_pair = over_x(add_up(out_terms))
+    first_left = send_back(
+        jnp.concatenate([pair_sum(first_left[:half], first_top), first_left[half:]], axis=0), 1
+    )
+    first_right = send_back(
+        jnp.concatenate([first_right[:half], pair_sum(first_right[half:], first_bottom)], axis=0), 3
+    )
+    qkv_terms, out_pair, both_pair = together(qkv_terms, out_pair, both_pair)
+    qkv_share = add_up(qkv_terms)
+    both_sum = pair_sum(*both_pair)
+    both_left = shift(both_sum, "z", 1)
+    both_right = shift(both_sum, "z", 3)
+    both_blocks = [both_sum, both_left, shift(both_sum, "z", 2), both_right]
     qkv_pair = over_x(qkv_share)
     output = (
-        middle + mlp_own.astype(f32) + mlp_left.astype(f32) + mlp_right.astype(f32)
+        middle
+        + mlp_own.astype(f32)
+        + mlp_left.astype(f32)
+        + mlp_right.astype(f32)
+        + mlp_opposite.astype(f32)
     ).astype(low)
-    first_grad = sum(block.astype(f32) for block in first_blocks)
+    first_grad = first_own.astype(f32) + first_left.astype(f32) + first_right.astype(f32)
     hidden_rms = inverse_rms(hidden)
     own_norm = hidden * hidden_rms
     scaled_first = first_grad * attn_scale

time: 766 us -> 726 us (0.948)
  starting transfers between devices: 179 us -> 126 us
  Pallas kernels: 176 us -> 224 us
  local copies, waits for them, and re-layouts: 63.7 us -> 34.8 us
  blocking collectives: 0 us -> 28.9 us
  matrix products: 41 us -> 19.3 us
  waiting for transfers between devices: 225 us -> 214 us
    ppermute x66 -> x65, starting transfers between devices: 130 us -> 81.1 us  [shift(): lax.ppermute(values, axis, [(i, (i + by) % size) for i in range(size)])]
    all_to_all x4 -> x3, waiting for transfers between devices: 55.2 us -> 8.06 us  [to_heads(): return lax.all_to_all(send, GROUP_AXES, 0, 0, tiled=True)]
    all_to_all x0 -> x1, blocking collectives: none -> 28.9 us  [to_heads(): return lax.all_to_all(send, GROUP_AXES, 0, 0, tiled=True)]
    ppermute x66 -> x65, waiting for transfers between devices: 170 us -> 197 us  [shift(): lax.ppermute(values, axis, [(i, (i + by) % size) for i in range(size)])]
    pallas_call x4 -> x6, Pallas kernels: 63 us -> 89.9 us  [the longest x3 57.9 us: mlp_blocks(): pl.pallas_call(functools.partial(mlp_kernel, len(seconds)), grid=(steps,)...]
    dot_general x4 -> x1, matrix products: 41 us -> 19.3 us  [local(): lax.dot_general(second_all.reshape(ring_rows, width), both_grad.reshape(r...]
    unnamed x115 -> x123, local copies, waits for them, and re-layouts: 28.7 us -> 10.8 us
    all_to_all x3, waiting for transfers between devices: 0.14 us -> 8.68 us  [to_owners(): return lax.all_to_all(pair, ('y', 'x_hi'), 0, 0, tiled=True)]
  transfers between devices with their start and end apart: 76 -> 74, of which waited for: 33 -> 27; matrix products, arithmetic and copies ran while one was open for 17% -> 13% of each run, Pallas kernels for 21% -> 31%
where the time goes in v4:
time: 726 us; the launch traced here: 716 us
  Pallas kernels  224 us (31%)
  waiting for transfers between devices  214 us (29%)
  starting transfers between devices  126 us (17%)
  other arithmetic  54.6 us (8%)
  local copies, waits for them, and re-layouts  34.8 us (5%)
  blocking collectives  28.9 us (4%)
  matrix products  19.3 us (3%)
  between operations  15 us (2%)
    ppermute x65, waiting for transfers between devices, shift(): lax.ppermute(values, axis, [(i, (i + by) % size) for i in range(size)])  197 us
    ppermute x65, starting transfers between devices, shift(): lax.ppermute(values, axis, [(i, (i + by) % size) for i in range(size)])  81.1 us
    pallas_call x3, Pallas kernels, mlp_blocks(): pl.pallas_call(functools.partial(mlp_kernel, len(seconds)), grid=(steps,)...  57.9 us
    pallas_call x1, Pallas kernels, attention_backward(): pl.pallas_call(backward_kernel, out_shape=(jax.ShapeDtypeStruct((BLOCKS,...  36.6 us
    all_to_all x1, blocking collectives, to_heads(): return lax.all_to_all(send, GROUP_AXES, 0, 0, tiled=True)  28.9 us
    all_to_all x3, starting transfers between devices, to_owners(): return lax.all_to_all(pair, ('y', 'x_hi'), 0, 0, tiled=True)  24.3 us
    pallas_call x1, Pallas kernels, attention_forward(): pl.pallas_call(forward_kernel, out_shape=(jax.ShapeDtypeStruct((BLOCKS, B...  22.2 us
    pallas_call x2, Pallas kernels, pair_grad(): pl.pallas_call(kernel, grid=(width // 256,), in_specs=[pl.BlockSpec(memor...  21.4 us
  transfers between devices with their start and end apart: 74, of which 27 were waited for; matrix products, arithmetic and copies ran while one was open for 13% of the time, Pallas kernels for 31%

profile of v4, /device:TPU:4, one launch (start us, length us, event | category | flops | bytes accessed | tf_op | source)
XLA Modules:
  0.0 715.8 jit_solution(17039495514532484883)
XLA Ops:
  30.5 11.6 %collective-permute-done.10 = bf16[2,128,512]{2,1,0:T(8,128)(2,1)S(1)} collective-permute-done((bf16[2,128,512]{2,1,0:T(8,128)(2,1)S(1)}, bf16[2,128,512]{2,1,0:T(8,128)(2,1)S(1)}, u32[]{:S(2)}, u32[]{:S(2)}) %collective-permute-start.10) | collective-permute-done | bytes 262176 | tf_op jit(solution)/shard_map/ppermute | solution.py:41
  57.5 8.8 %collective-permute-done = s32[1,384]{1,0:T(1,128)S(1)} collective-permute-done((s32[1,384]{1,0:T(1,128)S(1)}, s32[1,384]{1,0:T(1,128)S(1)}, u32[]{:S(2)}, u32[]{:S(2)}) %collective-permute-start) | collective-permute-done | bytes 1568 | tf_op jit(solution)/shard_map/ppermute | solution.py:41
  82.8 10.9 %shard_map.246 = (bf16[4,256,2048]{2,1,0:T(8,128)(2,1)}, f32[4,256,1024]{2,1,0:T(8,128)}, bf16[16,2,256,128]{3,2,1,0:T(8,128)(2,1)}) custom-call(bf16[4,256,2048]{2,1,0:T(8,128)(2,1)} %pad_maximum_fusion.hidden_ref, f32[1,2048]{1,0:T(1,128)} %bitcast.47, bf16[2048,1152]{1,0:T(8,128)(2,1)} %all-gather.3.cloned.1.call-done.weight_ref, ...), custom_call_target="tpu_custom_call" | custom-call | flops 4294967296 | bytes 20971520 | tf_op jit(solution)/shard_map/pallas_call | solution.py:534
  101.0 16.9 %collective-permute-done.12.refs_5_ = bf16[2048,512]{1,0:T(8,128)(2,1)} collective-permute-done((bf16[2048,512]{1,0:T(8,128)(2,1)}, bf16[2048,512]{1,0:T(8,128)(2,1)}, u32[]{:S(2)}, u32[]{:S(2)}) %collective-permute-start.12) | collective-permute-done | bytes 2097184 | tf_op jit(solution)/shard_map/ppermute | solution.py:41
  124.0 18.8 %collective-permute-done.14 = bf16[1024,512]{1,0:T(8,128)(2,1)S(1)} collective-permute-done((bf16[1024,512]{1,0:T(8,128)(2,1)S(1)}, bf16[1024,512]{1,0:T(8,128)(2,1)S(1)}, u32[]{:S(2)}, u32[]{:S(2)}) %collective-permute-start.14) | collective-permute-done | bytes 1048608 | tf_op jit(solution)/shard_map/ppermute | solution.py:41
  150.1 22.2 %shard_map.248 = (bf16[16,256,128]{2,1,0:T(8,128)(2,1)}, f32[8,128,512]{2,1,0:T(8,128)}, f32[8,1,512]{2,1,0:T(1,128)}) custom-call(s32[16]{0:T(128)} %dynamic-slice_bitcast_fusion.order, s32[1]{0:T(128)} %bitcast.1.core.core_ref, bf16[16,2,256,128]{3,2,1,0:T(8,128)(2,1)} %copy-done.4, bf16[16,256,128]{2,1,0:T(8,128)(2,1)} %copy-done.11), custom_call_target="tpu_custom_call" | custom-call | flops 1024 | bytes 1024 | tf_op jit(solution)/shard_map/pallas_call | solution.py:104
  175.5 28.9 %all_to_all.35.refs_4_ = bf16[16,256,128]{2,1,0:T(8,128)(2,1)S(1)} all-to-all(bf16[16,256,128]{2,1,0:T(8,128)(2,1)} %get-tuple-element.171), channel_id=1, replica_groups=mesh['x_lo'=2,'z'=4,'y'=4,'x_hi'=2,'core'=2] {'y','x_hi','core'}, dimensions={0} | all-to-all | bytes 2097152 | tf_op jit(solution)/shard_map/all_to_all | solution.py:749
  233.6 15.7 %shard_map.250 = (bf16[4,256,1536]{2,1,0:T(8,128)(2,1)}, bf16[4,256,3072]{2,1,0:T(8,128)(2,1)}, bf16[4,256,2048]{2,1,0:T(8,128)(2,1)}, bf16[4,256,2048]{2,1,0:T(8,128)(2,1)}, bf16[256,2048]{1,0:T(8,128)(2,1)}) custom-call(bf16[256,2048]{1,0:T(8,128)(2,1)} %get-tuple-element.187.refs_0_, bf16[256,2048]{1,0:T(8,128)(2,1)} %refs_9_.1, ...), custom_call_target="tpu_custom_call" | custom-call | flops 8053063680 | bytes 18874368 | tf_op jit(solution)/shard_map/pallas_call | solution.py:305
  267.7 26.6 %shard_map.251 = (bf16[4,256,1536]{2,1,0:T(8,128)(2,1)}, bf16[4,256,3072]{2,1,0:T(8,128)(2,1)}, bf16[4,256,2048]{2,1,0:T(8,128)(2,1)}, bf16[4,256,2048]{2,1,0:T(...) custom-call(bf16[256,2048]{1,0:T(8,128)(2,1)} %copy-done.16, ...), custom_call_target="tpu_custom_call", output_to_operand_aliasing={{0}: (6, {}), {1}: (7, {}), {2}: (8, {}), {3}: (9, {})} | custom-call | flops 16106127360 | bytes 18874368 | tf_op jit(solution)/shard_map/pallas_call | solution.py:305
  297.3 15.6 %shard_map.252 = (bf16[4,256,1536]{2,1,0:T(8,128)(2,1)}, bf16[4,256,3072]{2,1,0:T(8,128)(2,1)}, bf16[4,256,2048]{2,1,0:T(8,128)(2,1)}, bf16[4,256,2048]{2,1,0:T(8,128)(2,1)}, bf16[256,2048]{1,0:T(8,128)(2,1)}) custom-call(bf16[128,2048]{1,0:T(8,128)(2,1)} %copy-done.39, ...), custom_call_target="tpu_custom_call", output_to_operand_aliasing={{0}: (6, {}), {1}: (7, {}), {2}: (8, {}), {3}: (9, {})} | custom-call | flops 8053063680 | bytes 18874368 | tf_op jit(solution)/shard_map/pallas_call | solution.py:305
  313.9 19.3 %bitcast_convert_fusion = bf16[2048,3072]{1,0:T(8,128)(2,1)} fusion(bf16[4,256,2048]{2,1,0:T(8,128)(2,1)} %get-tuple-element.222, bf16[4,256,3072]{2,1,0:T(8,128)(2,1)} %get-tuple-element.223), kind=kOutput, calls=%fused_computation | convolution fusion | flops 12891193344 | bytes 23068672 | tf_op jit(solution)/shard_map/dot_general | solution.py:944
  342.6 12.2 %shard_map.253 = (f32[256,2048]{1,0:T(8,128)}, bf16[256,2048]{1,0:T(8,128)(2,1)}, f32[1,2048]{1,0:T(1,128)}, bf16[4,256,128]{2,1,0:T(8,128)(2,1)}, bf16[4,256,12...) custom-call(bf16[256,2048]{1,0:T(8,128)(2,1)} %get-tuple-element.198.refs_0_, ...), custom_call_target="tpu_custom_call" | custom-call | flops 1024 | bytes 1024 | tf_op jit(solution)/shard_map/pallas_call | solution.py:490
  359.6 12.9 %shard_map.254 = (bf16[8,128,1536]{2,1,0:T(8,128)(2,1)}, bf16[8,128,1536]{2,1,0:T(8,128)(2,1)}) custom-call(s32[1]{0:T(128)} %bitcast.1.core.core_ref, bf16[4,256,2048]{2,1,0:T(8,128)(2,1)} %get-tuple-element.232.refs_0_, bf16[4,256,1536]{2,1,0:T(8,128)(2,1)} %get-tuple-element.237.refs_1_.inner_ref), custom_call_target="tpu_custom_call" | custom-call | flops 1024 | bytes 1024 | tf_op jit(solution)/shard_map/pallas_call | solution.py:397
  385.2 10.6 %shard_map.255 = (bf16[256,2048]{1,0:T(8,128)(2,1)}, bf16[256,2048]{1,0:T(8,128)(2,1)}, bf16[256,2048]{1,0:T(8,128)(2,1)}, bf16[256,2048]{1,0:T(8,128)(2,1)}) custom-call(bf16[4,256,1536]{2,1,0:T(8,128)(2,1)} %get-tuple-element.237.refs_1_.inner_ref, bf16[2048,4608]{1,0:T(8,128)(2,1)} %all-gather.5.cloned.1.call-done.refs_2_.refs_3_.refs_4_.refs_5_.weight_ref), custom_call_target="tpu_custom_call" | custom-call | flops 1024 | bytes 1024 | tf_op jit(solution)/shard_map/pallas_call | solution.py:347
  410.9 9.9 %all-to-all-start.3 = ((bf16[8,128,1536]{2,1,0:T(8,128)(2,1)}), bf16[8,128,1536]{2,1,0:T(8,128)(2,1)}, u32[]{:S(2)}, u32[]{:S(2)}) async-start(bf16[8,128,1536]{2,1,0:T(8,128)(2,1)} %add_convert_fusion), calls=%async_computation.3 | async-start | bytes 6291456 | tf_op jit(solution)/shard_map/all_to_all | solution.py:932
  422.8 36.6 %shard_map.256 = (bf16[16,2,256,128]{3,2,1,0:T(8,128)(2,1)}, bf16[16,256,128]{2,1,0:T(8,128)(2,1)}, bf16[16,256,128]{2,1,0:T(8,128)(2,1)}) custom-call(s32[16]{0:T(128)} %dynamic-slice_bitcast_fusion.order, s32[1]{0:T(128)} %bitcast.1.core.core_ref, bf16[16,2,256,128]{3,2,1,0:T(8,128)(2,1)} %copy-done.4, bf16[16,256,128]{2,1,0:T(8,128)(2,1)} %copy-done.11, ...), custom_call_target="tpu_custom_call" | custom-call | flops 1024 | bytes 1024 | tf_op jit(solution)/shard_map/pallas_call | solution.py:211
  464.9 8.7 %all-to-all-done.3 = bf16[8,128,1536]{2,1,0:T(8,128)(2,1)} async-done(((bf16[8,128,1536]{2,1,0:T(8,128)(2,1)}), bf16[8,128,1536]{2,1,0:T(8,128)(2,1)}, u32[]{:S(2)}, u32[]{:S(2)}) %all-to-all-start.3) | async-done | bytes 3145760 | tf_op jit(solution)/shard_map/all_to_all | solution.py:932
  486.9 8.5 %shard_map.257 = (bf16[8,128,512]{2,1,0:T(8,128)(2,1)}, bf16[8,128,512]{2,1,0:T(8,128)(2,1)}) custom-call(s32[1]{0:T(128)} %bitcast.1.core.core_ref, bf16[256,2048]{1,0:T(8,128)(2,1)} %get-tuple-element.266.refs_0_, bf16[256,2048]{1,0:T(8,128)(2,1)} %copy-done.33, bf16[256,2048]{1,0:T(8,128)(2,1)} %collective-permute-done.40.refs_2_, ...), custom_call_target="tpu_custom_call" | custom-call | flops 1024 | bytes 1024 | tf_op jit(solution)/shard_map/pallas_call | solution.py:397
  503.6 19.2 %collective-permute-done.42 = bf16[256,2048]{1,0:T(8,128)(2,1)S(1)} collective-permute-done((bf16[256,2048]{1,0:T(8,128)(2,1)}, bf16[256,2048]{1,0:T(8,128)(2,1)S(1)}, u32[]{:S(2)}, u32[]{:S(2)}) %collective-permute-start.42) | collective-permute-done | bytes 1048608 | tf_op jit(solution)/shard_map/ppermute | solution.py:41
  524.1 15.0 %shard_map.258 = (bf16[4,256,1024]{2,1,0:T(8,128)(2,1)}, bf16[8,128,1024]{2,1,0:T(8,128)(2,1)}, bf16[8,128,1024]{2,1,0:T(8,128)(2,1)}, f32[1,128]{1,0:T(1,128)}, f32[1,128]{1,0:T(1,128)}) custom-call(s32[1]{0:T(128)} %bitcast.1.core.core_ref, bf16[16,2,256,128]{3,2,1,0:T(8,128)(2,1)} %copy-done.7, f32[4,256,1024]{2,1,0:T(8,128)} %get-tuple-element.275.pre_ref, ...), custom_call_target="tpu_custom_call" | custom-call | flops 1024 | bytes 1024 | tf_op jit(solution)/shard_map/pallas_call | solution.py:617
  551.3 12.6 %shard_map.259 = (bf16[256,2048]{1,0:T(8,128)(2,1)}, bf16[256,2048]{1,0:T(8,128)(2,1)}, bf16[128,2048]{1,0:T(8,128)(2,1)}, bf16[128,2048]{1,0:T(8,128)(2,1)}, bf...) custom-call(s32[1]{0:T(128)} %bitcast.1.core.core_ref, ...), custom_call_target="tpu_custom_call" | custom-call | flops 1024 | bytes 1024 | tf_op jit(solution)/shard_map/pallas_call | solution.py:702
  606.1 10.9 %collective-permute-done.51 = bf16[256,2048]{1,0:T(8,128)(2,1)} collective-permute-done((bf16[256,2048]{1,0:T(8,128)(2,1)}, bf16[256,2048]{1,0:T(8,128)(2,1)}, u32[]{:S(2)}, u32[]{:S(2)}) %collective-permute-start.51) | collective-permute-done | bytes 1048608 | tf_op jit(solution)/shard_map/ppermute | solution.py:41
  621.2 14.6 %collective-permute-done.53 = bf16[128,512]{1,0:T(8,128)(2,1)S(1)} collective-permute-done((bf16[128,512]{1,0:T(8,128)(2,1)S(1)}, bf16[128,512]{1,0:T(8,128)(2,1)S(1)}, u32[]{:S(2)}, u32[]{:S(2)}) %collective-permute-start.53) | collective-permute-done | bytes 131104 | tf_op jit(solution)/shard_map/ppermute | solution.py:41
  664.6 31.4 %collective-permute-done.57.refs_2_ = bf16[128,1152]{1,0:T(8,128)(2,1)} collective-permute-done((bf16[128,1152]{1,0:T(8,128)(2,1)S(1)}, bf16[128,1152]{1,0:T(8,128)(2,1)}, u32[]{:S(2)}, u32[]{:S(2)}) %collective-permute-start.57) | collective-permute-done | bytes 294944 | tf_op jit(solution)/shard_map/ppermute | solution.py:41
  (339 shorter events, 302.5 us)
Async XLA Ops:
  7.2 73.2 %all-gather.3.cloned.1.call-start = ((), (), s32[]{:S(2)}) async-start(), calls=%async_computation.8 | async-start | bytes 5013504 | tf_op jit(solution)/shard_map/all_gather | solution.py:835
  10.9 222.7 %all-gather.5.cloned.1.call-start = ((), (), s32[]{:S(2)}) async-start(), calls=%async_computation.9 | async-start | bytes 20054016 | tf_op jit(solution)/shard_map/all_gather | solution.py:835
  70.5 47.4 %collective-permute-start.12 = (bf16[2048,512]{1,0:T(8,128)(2,1)}, bf16[2048,512]{1,0:T(8,128)(2,1)}, u32[]{:S(2)}, u32[]{:S(2)}) collective-permute-start(bf16[2048,512]{1,0:T(8,128)(2,1)} %shard_map.247.refs_4_), channel_id=1, source_target_pairs={{0,16},{16,32},{32,48},{48,0},{1,17},{17,33},{33,49},{49,1},{2,18}... | collective-permute-start | bytes 6291464 | tf_op jit(solution)/shard_map/ppermute | solution.py:41
  70.7 48.5 %collective-permute-start.13 = (bf16[2048,512]{1,0:T(8,128)(2,1)}, bf16[2048,512]{1,0:T(8,128)(2,1)}, u32[]{:S(2)}, u32[]{:S(2)}) collective-permute-start(bf16[2048,512]{1,0:T(8,128)(2,1)} %shard_map.247.refs_4_), channel_id=1, source_target_pairs={{0,48},{16,0},{32,16},{48,32},{1,49},{17,1},{33,17},{49,33},{2,50}... | collective-permute-start | bytes 6291464 | tf_op jit(solution)/shard_map/ppermute | solution.py:41
  93.8 50.1 %all-to-all-start = ((bf16[16,2,256,128]{3,2,1,0:T(8,128)(2,1)}), bf16[16,2,256,128]{3,2,1,0:T(8,128)(2,1)S(1)}, u32[]{:S(2)}, u32[]{:S(2)}) async-start(bf16[16,2,256,128]{3,2,1,0:T(8,128)(2,1)} %get-tuple-element.167), calls=%async_computation | async-start | bytes 4194304 | tf_op jit(solution)/shard_map/all_to_all | solution.py:749
  100.9 467.9 %reduce-scatter.2.cloned.1.call-start = ((), (), s32[]{:S(2)}) async-start(), calls=%async_computation.10 | async-start | bytes 13369344 | tf_op jit(solution)/shard_map/reduce_scatter | solution.py:953
  257.4 37.7 %collective-permute-start.26 = (bf16[128,2048]{1,0:T(8,128)(2,1)}, bf16[128,2048]{1,0:T(8,128)(2,1)S(1)}, u32[]{:S(2)}, u32[]{:S(2)}) collective-permute-start(bf16[128,2048]{1,0:T(8,128)(2,1)} %slice.127), channel_id=1, source_target_pairs={{0,16},{16,32},{32,48},{48,0},{1,17},{17,33},{33,49},{49,1},{2,18}... | collective-permute-start | bytes 1572872 | tf_op jit(solution)/shard_map/ppermute | solution.py:41
  260.5 36.0 %collective-permute-start.27 = (bf16[128,2048]{1,0:T(8,128)(2,1)}, bf16[128,2048]{1,0:T(8,128)(2,1)}, u32[]{:S(2)}, u32[]{:S(2)}) collective-permute-start(bf16[128,2048]{1,0:T(8,128)(2,1)} %slice.128), channel_id=1, source_target_pairs={{0,48},{16,0},{32,16},{48,32},{1,49},{17,1},{33,17},{49,33},{2,50}... | collective-permute-start | bytes 1572872 | tf_op jit(solution)/shard_map/ppermute | solution.py:41
  294.3 38.9 %collective-permute-start.24 = (bf16[256,2048]{1,0:T(8,128)(2,1)}, bf16[256,2048]{1,0:T(8,128)(2,1)S(1)}, u32[]{:S(2)}, u32[]{:S(2)}) collective-permute-start(bf16[256,2048]{1,0:T(8,128)(2,1)} %get-tuple-element.207), channel_id=1, source_target_pairs={{0,48},{16,0},{32,16},{48,32},{1,49},{17,1},{33,17},{49,33},{2,50}... | collective-permute-start | bytes 3145736 | tf_op jit(solution)/shard_map/ppermute | solution.py:41
  295.1 46.2 %collective-permute-start.25 = (bf16[256,2048]{1,0:T(8,128)(2,1)}, bf16[256,2048]{1,0:T(8,128)(2,1)S(1)}, u32[]{:S(2)}, u32[]{:S(2)}) collective-permute-start(bf16[256,2048]{1,0:T(8,128)(2,1)} %get-tuple-element.208), channel_id=1, source_target_pairs={{0,16},{16,32},{32,48},{48,0},{1,17},{17,33},{33,49},{49,1},{2,18}... | collective-permute-start | bytes 3145736 | tf_op jit(solution)/shard_map/ppermute | solution.py:41
  372.6 36.7 %collective-permute-start.35 = (bf16[256,2048]{1,0:T(8,128)(2,1)}, bf16[256,2048]{1,0:T(8,128)(2,1)S(1)}, u32[]{:S(2)}, u32[]{:S(2)}) collective-permute-start(bf16[256,2048]{1,0:T(8,128)(2,1)} %get-tuple-element.266.refs_0_), channel_id=1, source_target_pairs={{0,16},{16,32},{32,48},{48,0},{1,17},{17,33},{33,49},{49,1},{2,18}... | collective-permute-start | bytes 3145736 | tf_op jit(solution)/shard_map/ppermute | solution.py:41
  372.7 36.6 %collective-permute-start.36 = (bf16[256,2048]{1,0:T(8,128)(2,1)}, bf16[256,2048]{1,0:T(8,128)(2,1)S(1)}, u32[]{:S(2)}, u32[]{:S(2)}) collective-permute-start(bf16[256,2048]{1,0:T(8,128)(2,1)} %get-tuple-element.266.refs_0_), channel_id=1, source_target_pairs={{0,48},{16,0},{32,16},{48,32},{1,49},{17,1},{33,17},{49,33},{2,50}... | collective-permute-start | bytes 3145736 | tf_op jit(solution)/shard_map/ppermute | solution.py:41
  410.9 62.6 %all-to-all-start.3 = ((bf16[8,128,1536]{2,1,0:T(8,128)(2,1)}), bf16[8,128,1536]{2,1,0:T(8,128)(2,1)}, u32[]{:S(2)}, u32[]{:S(2)}) async-start(bf16[8,128,1536]{2,1,0:T(8,128)(2,1)} %add_convert_fusion), calls=%async_computation.3 | async-start | bytes 6291456 | tf_op jit(solution)/shard_map/all_to_all | solution.py:932
  420.8 38.6 %collective-permute-start.37 = (bf16[256,2048]{1,0:T(8,128)(2,1)}, bf16[256,2048]{1,0:T(8,128)(2,1)S(1)}, u32[]{:S(2)}, u32[]{:S(2)}) collective-permute-start(bf16[256,2048]{1,0:T(8,128)(2,1)} %get-tuple-element.255), channel_id=1, source_target_pairs={{0,48},{16,0},{32,16},{48,32},{1,49},{17,1},{33,17},{49,33},{2,50}... | collective-permute-start | bytes 3145736 | tf_op jit(solution)/shard_map/ppermute | solution.py:41
  421.0 38.5 %collective-permute-start.38 = (bf16[256,2048]{1,0:T(8,128)(2,1)}, bf16[256,2048]{1,0:T(8,128)(2,1)}, u32[]{:S(2)}, u32[]{:S(2)}) collective-permute-start(bf16[256,2048]{1,0:T(8,128)(2,1)} %get-tuple-element.256), channel_id=1, source_target_pairs={{0,16},{16,32},{32,48},{48,0},{1,17},{17,33},{33,49},{49,1},{2,18}... | collective-permute-start | bytes 3145736 | tf_op jit(solution)/shard_map/ppermute | solution.py:41
  473.6 49.2 %all-to-all-start.4 = ((bf16[16,2,256,128]{3,2,1,0:T(8,128)(2,1)}), bf16[16,2,256,128]{3,2,1,0:T(8,128)(2,1)S(1)}, u32[]{:S(2)}, u32[]{:S(2)}) async-start(bf16[16,2,256,128]{3,2,1,0:T(8,128)(2,1)} %fusion.9), calls=%async_computation.4 | async-start | bytes 4194304 | tf_op jit(solution)/shard_map/all_to_all | solution.py:749
  499.2 39.9 %collective-permute-start.43 = (bf16[128,1536]{1,0:T(8,128)(2,1)S(1)}, bf16[128,1536]{1,0:T(8,128)(2,1)}, u32[]{:S(2)}, u32[]{:S(2)}) collective-permute-start(bf16[128,1536]{1,0:T(8,128)(2,1)S(1)} %reduce_sum.65), channel_id=1, source_target_pairs={{0,64},{64,0},{1,65},{65,1},{2,66},{66,2},{3,67},{67,3},{4,68},{68... | collective-permute-start | bytes 1179656 | tf_op jit(solution)/shard_map/ppermute | solution.py:41
  580.4 56.1 %all-to-all-start.6 = ((bf16[8,128,1152]{2,1,0:T(8,128)(2,1)}), bf16[8,128,1152]{2,1,0:T(8,128)(2,1)S(1)}, u32[]{:S(2)}, u32[]{:S(2)}) async-start(bf16[8,128,1152]{2,1,0:T(8,128)(2,1)} %pad_maximum_fusion.1), calls=%async_computation.7 | async-start | bytes 4718592 | tf_op jit(solution)/shard_map/all_to_all | solution.py:932
  596.3 40.2 %collective-permute-start.54 = (bf16[128,3072]{1,0:T(8,128)(2,1)}, bf16[128,3072]{1,0:T(8,128)(2,1)}, u32[]{:S(2)}, u32[]{:S(2)}) collective-permute-start(bf16[128,3072]{1,0:T(8,128)(2,1)} %reduce-scatter.2.cloned.1.call-done), channel_id=1, source_target_pairs={{0,64},{64,0},{1,65},{65,1},{2,66},{66,2},{3,67},{67,3},{4,68},{68... | collective-permute-start | bytes 2359304 | tf_op jit(solution)/shard_map/ppermute | solution.py:41
  649.0 53.8 %collective-permute-start.62 = (bf16[128,3072]{1,0:T(8,128)(2,1)S(1)}, bf16[128,3072]{1,0:T(8,128)(2,1)S(1)}, u32[]{:S(2)}, u32[]{:S(2)}) collective-permute-start(bf16[128,3072]{1,0:T(8,128)(2,1)S(1)} %add_convert_fusion.5.refs_0_), channel_id=1, source_target_pairs={{0,16},{16,32},{32,48},{48,0},{1,17},{17,33},{33,49},{49,1},{2,18}... | collective-permute-start | bytes 2359304 | tf_op jit(solution)/shard_map/ppermute | solution.py:41
  649.8 53.0 %collective-permute-start.63 = (bf16[128,3072]{1,0:T(8,128)(2,1)S(1)}, bf16[128,3072]{1,0:T(8,128)(2,1)S(1)}, u32[]{:S(2)}, u32[]{:S(2)}) collective-permute-start(bf16[128,3072]{1,0:T(8,128)(2,1)S(1)} %add_convert_fusion.5.refs_0_), channel_id=1, source_target_pairs={{0,32},{16,48},{32,0},{48,16},{1,33},{17,49},{33,1},{49,17},{2,34}... | collective-permute-start | bytes 2359304 | tf_op jit(solution)/shard_map/ppermute | solution.py:41
  653.7 49.1 %collective-permute-start.64 = (bf16[128,3072]{1,0:T(8,128)(2,1)S(1)}, bf16[128,3072]{1,0:T(8,128)(2,1)}, u32[]{:S(2)}, u32[]{:S(2)}) collective-permute-start(bf16[128,3072]{1,0:T(8,128)(2,1)S(1)} %add_convert_fusion.5.refs_0_), channel_id=1, source_target_pairs={{0,48},{16,0},{32,16},{48,32},{1,49},{17,1},{33,17},{49,33},{2,50}... | collective-permute-start | bytes 2359304 | tf_op jit(solution)/shard_map/ppermute | solution.py:41
  654.5 41.4 %collective-permute-start.57 = (bf16[128,1152]{1,0:T(8,128)(2,1)S(1)}, bf16[128,1152]{1,0:T(8,128)(2,1)}, u32[]{:S(2)}, u32[]{:S(2)}) collective-permute-start(bf16[128,1152]{1,0:T(8,128)(2,1)S(1)} %add_convert_fusion.9.refs_0_), channel_id=1, source_target_pairs={{0,32},{16,48},{32,0},{48,16},{1,33},{17,49},{33,1},{49,17},{2,34}... | collective-permute-start | bytes 884744 | tf_op jit(solution)/shard_map/ppermute | solution.py:41
  658.5 40.0 %collective-permute-start.58 = (bf16[128,1152]{1,0:T(8,128)(2,1)S(1)}, bf16[128,1152]{1,0:T(8,128)(2,1)}, u32[]{:S(2)}, u32[]{:S(2)}) collective-permute-start(bf16[128,1152]{1,0:T(8,128)(2,1)S(1)} %add_convert_fusion.9.refs_0_), channel_id=1, source_target_pairs={{0,48},{16,0},{32,16},{48,32},{1,49},{17,1},{33,17},{49,33},{2,50}... | collective-permute-start | bytes 884744 | tf_op jit(solution)/shard_map/ppermute | solution.py:41
  (108 other events, 1622.4 us)
Sparse Core Ops, SparseCore 0:
  11.1 63.2 all-gather.2
  76.8 147.2 all-gather.4
  341.5 167.8 reduce-scatter.1

commit v5 on v4

--- a/solution.py
+++ b/solution.py
@@ -47,31 +47,29 @@
     )
 
 
-def tile_rows(ref, order, tile, *slot):
-    return jnp.concatenate([ref[order[2 * tile + half], *slot] for half in range(2)], axis=0)
-
-
 def forward_kernel(
-    order, core, own_ref, other_ref, mixed_ref, mixed_t_ref, log_ref, k_all, v_t, acc, total
+    order, core, own_a, own_b, other_a, other_b, mixed_ref, mixed_t_ref, log_ref, k_all, v_t, acc, total
 ):
     tile = pl.program_id(0)
-
-    def take(keys_of, values_of):
-        for at in range(BLOCKS):
-            k_all[at * BLOCK : (at + 1) * BLOCK, :] = keys_of(order[at])
-            v_t[at // 2, :, (at % 2) * BLOCK : (at % 2 + 1) * BLOCK] = (
-                values_of(order[at]).astype(jnp.float32).T.astype(low)
+    start = tile * TILE
+
+    def take(keys, values):
+        for half in range(2):
+            rows = pl.ds(pl.multiple_of(start + half * BLOCK, BLOCK), BLOCK)
+            k_all[rows, :] = keys[half]
+            v_t[tile, :, half * BLOCK : (half + 1) * BLOCK] = (
+                values[half].astype(jnp.float32).T.astype(low)
             )
 
-    @pl.when((tile == 0) & (core[0] == 0))
-    def _():
-        take(lambda at: own_ref[at, 1], lambda at: other_ref[at])
-
-    @pl.when((tile == 0) & (core[0] == 1))
-    def _():
-        take(lambda at: other_ref[at], lambda at: own_ref[at, 1])
-
-    queries = tile_rows(own_ref, order, tile, 0)
+    @pl.when(core[0] == 0)
+    def _():
+        take((own_a[0, 1], own_b[0, 1]), (other_a[0], other_b[0]))
+
+    @pl.when(core[0] == 1)
+    def _():
+        take((other_a[0], other_b[0]), (own_a[0, 1], own_b[0, 1]))
+
+    queries = jnp.concatenate([own_a[0, 0], own_b[0, 0]], axis=0)
     acc[...] = jnp.zeros_like(acc)
     total[...] = jnp.zeros_like(total)
 
@@ -92,15 +90,30 @@
 
     chunk(tile, True)
     mixed_t = acc[...] / total[...]
-    mixed_t_ref[tile] = mixed_t
-    log_ref[tile] = jnp.log2(total[...])
+    mixed_t_ref[0] = mixed_t
+    log_ref[0] = jnp.log2(total[...])
     mixed = mixed_t.T.astype(low)
     mixed_ref[order[2 * tile]] = mixed[:BLOCK]
     mixed_ref[order[2 * tile + 1]] = mixed[BLOCK:]
 
 
+def tile_specs(lead):
+    return [
+        pl.BlockSpec(
+            (1, *lead, BLOCK, HEAD_DIM),
+            functools.partial(
+                lambda half, tile, order, core: (order[2 * tile + half],) + (0,) * (len(lead) + 2),
+                half,
+            ),
+        )
+        for half in range(2)
+    ]
+
+
 def attention_forward(order, core_at, arrived, other):
     whole = pl.BlockSpec(memory_space=pltpu.VMEM)
+    turned = pl.BlockSpec((1, HEAD_DIM, TILE), lambda tile, order, core: (tile, 0, 0))
+    line = pl.BlockSpec((1, 1, TILE), lambda tile, order, core: (tile, 0, 0))
     return pl.pallas_call(
         forward_kernel,
         out_shape=(
@@ -111,8 +124,8 @@
         grid_spec=pltpu.PrefetchScalarGridSpec(
             num_scalar_prefetch=2,
             grid=(TILES,),
-            in_specs=[whole] * 2,
-            out_specs=(whole, whole, whole),
+            in_specs=tile_specs((2,)) + tile_specs(()),
+            out_specs=(whole, turned, line),
             scratch_shapes=[
                 pltpu.VMEM((BLOCKS * BLOCK, HEAD_DIM), low),
                 pltpu.VMEM((TILES, HEAD_DIM, TILE), low),
@@ -124,43 +137,41 @@
         cost_estimate=pl.CostEstimate(
             flops=1024, bytes_accessed=1024, transcendentals=0
         ),
-    )(order, core_at[None], arrived, other)
+    )(order, core_at[None], arrived, arrived, other, other)
 
 
 def backward_kernel(
-    order, core, own_ref, other_ref, g_ref, mixed_t_ref, log_ref, q_out, keep_out, give_out,
-    k_all, v_all, k_t, q_acc, k_acc, v_acc,
+    order, core, own_a, own_b, other_a, other_b, grad_a, grad_b, mixed_t_ref, log_ref,
+    q_out, keep_out, give_out, k_all, v_all, k_t, q_acc, k_acc, v_acc,
 ):
     tile = pl.program_id(0)
-
-    def take(keys_of, values_of):
-        for at in range(BLOCKS):
-            rows = slice(at * BLOCK, (at + 1) * BLOCK)
-            keys = keys_of(order[at])
-            k_all[rows, :] = keys
-            v_all[rows, :] = values_of(order[at])
-            k_t[at // 2, :, (at % 2) * BLOCK : (at % 2 + 1) * BLOCK] = (
-                keys.astype(jnp.float32).T.astype(low)
+    start = tile * TILE
+
+    def take(keys, values):
+        for half in range(2):
+            rows = pl.ds(pl.multiple_of(start + half * BLOCK, BLOCK), BLOCK)
+            k_all[rows, :] = keys[half]
+            v_all[rows, :] = values[half]
+            k_t[tile, :, half * BLOCK : (half + 1) * BLOCK] = (
+                keys[half].astype(jnp.float32).T.astype(low)
             )
 
-    @pl.when((tile == 0) & (core[0] == 0))
-    def _():
-        take(lambda at: own_ref[at, 1], lambda at: other_ref[at])
-
-    @pl.when((tile == 0) & (core[0] == 1))
-    def _():
-        take(lambda at: other_ref[at], lambda at: own_ref[at, 1])
-
-    @pl.when(tile == 0)
-    def _():
-        k_acc[...] = jnp.zeros_like(k_acc)
-        v_acc[...] = jnp.zeros_like(v_acc)
-
-    queries = tile_rows(own_ref, order, tile, 0)
-    grads = tile_rows(g_ref, order, tile)
+    @pl.when(core[0] == 0)
+    def _():
+        take((own_a[0, 1], own_b[0, 1]), (other_a[0], other_b[0]))
+
+    @pl.when(core[0] == 1)
+    def _():
+        take((other_a[0], other_b[0]), (own_a[0, 1], own_b[0, 1]))
+
+    rows = pl.ds(pl.multiple_of(start, TILE), TILE)
+    k_acc[rows, :] = jnp.zeros((TILE, HEAD_DIM), jnp.float32)
+    v_acc[rows, :] = jnp.zeros((TILE, HEAD_DIM), jnp.float32)
+    queries = jnp.concatenate([own_a[0, 0], own_b[0, 0]], axis=0)
+    grads = jnp.concatenate([grad_a[0], grad_b[0]], axis=0)
     grads_t = grads.astype(jnp.float32).T
-    shared = jnp.sum(grads_t * mixed_t_ref[tile], axis=0, keepdims=True)
-    logs = log_ref[tile]
+    shared = jnp.sum(grads_t * mixed_t_ref[0], axis=0, keepdims=True)
+    logs = log_ref[0]
     q_acc[...] = jnp.zeros_like(q_acc)
 
     def chunk(at, masked):
@@ -208,6 +219,8 @@
 def attention_backward(order, core_at, arrived, other, grads, mixed_t, logs):
     whole = pl.BlockSpec(memory_space=pltpu.VMEM)
     rows = BLOCKS * BLOCK
+    turned = pl.BlockSpec((1, HEAD_DIM, TILE), lambda tile, order, core: (tile, 0, 0))
+    line = pl.BlockSpec((1, 1, TILE), lambda tile, order, core: (tile, 0, 0))
     return pl.pallas_call(
         backward_kernel,
         out_shape=(jax.ShapeDtypeStruct((BLOCKS, 2, BLOCK, HEAD_DIM), low),)
@@ -215,7 +228,7 @@
         grid_spec=pltpu.PrefetchScalarGridSpec(
             num_scalar_prefetch=2,
             grid=(TILES,),
-            in_specs=[whole] * 5,
+            in_specs=tile_specs((2,)) + tile_specs(()) + tile_specs(()) + [turned, line],
             out_specs=(whole, whole, whole),
             scratch_shapes=[
                 pltpu.VMEM((rows, HEAD_DIM), low),
@@ -230,7 +243,7 @@
         cost_estimate=pl.CostEstimate(
             flops=1024, bytes_accessed=1024, transcendentals=0
         ),
-    )(order, core_at[None], arrived, other, grads, mixed_t, logs)
+    )(order, core_at[None], arrived, arrived, other, other, grads, grads, mixed_t, logs)
 
 
 def mlp_kernel(parts, *refs):
@@ -365,7 +378,8 @@
 
     def kernel(core_ref, *refs):
         left_refs = refs[: len(lefts)]
-        right_ref, keep_ref, give_ref = refs[len(lefts) : len(lefts) + 3]
+        right_ref, keep_ref = refs[len(lefts) : len(lefts) + 2]
+        give_ref = refs[-1]
         if by_heads:
             all_ref = refs[-1]
 
@@ -385,6 +399,9 @@
         term = lax.dot_general(
             inputs, values, contract_first, preferred_element_type=jnp.float32
         ).astype(low)
+        if by_heads:
+            keep_ref[...] = term
+            return
         first_core = core_ref[0] == 0
         keep_ref[0] = jnp.where(first_core, term[:128], term[128:])
         give_ref[0] = jnp.where(first_core, term[128:], term[:128])
@@ -400,8 +417,10 @@
         in_specs=[pl.BlockSpec(memory_space=pltpu.SMEM)]
         + [columns(value) for value in lefts]
         + [pl.BlockSpec(right.shape, lambda i: (0, 0, 0))],
-        out_specs=(half, half),
-        out_shape=(jax.ShapeDtypeStruct((width // 256, 128, outs), low),) * 2,
+        out_specs=pl.BlockSpec((256, outs), lambda i: (i, 0)) if by_heads else (half, half),
+        out_shape=jax.ShapeDtypeStruct((width, outs), low)
+        if by_heads
+        else (jax.ShapeDtypeStruct((width // 256, 128, outs), low),) * 2,
         scratch_shapes=[pltpu.VMEM((rows, 512), low)] * by_heads,
         compiler_params=pltpu.CompilerParams(vmem_limit_bytes=VMEM_LIMIT),
         cost_estimate=pl.CostEstimate(flops=1024, bytes_accessed=1024, transcendentals=0),
@@ -442,7 +461,7 @@
             jax.ShapeDtypeStruct((rows, width), jnp.float32),
             jax.ShapeDtypeStruct((rows, width), low),
         ),
-        compiler_params=pltpu.CompilerParams(vmem_limit_bytes=VMEM_LIMIT),
+        compiler_params=pltpu.CompilerParams(vmem_limit_bytes=32 * 1024 * 1024),
         cost_estimate=pl.CostEstimate(flops=1024, bytes_accessed=1024, transcendentals=0),
     )(*mixed_blocks, *weights, hidden, gain)
 
@@ -501,15 +520,37 @@
         )
         + (jax.ShapeDtypeStruct((4, rows, HEAD_DIM), low),) * RING,
         scratch_shapes=[pltpu.VMEM((rows, 512), jnp.float32)] * RING,
-        compiler_params=pltpu.CompilerParams(vmem_limit_bytes=VMEM_LIMIT),
+        compiler_params=pltpu.CompilerParams(vmem_limit_bytes=40 * 1024 * 1024),
         cost_estimate=pl.CostEstimate(flops=1024, bytes_accessed=1024, transcendentals=0),
     )(*parts, *weights, middle, cot, gain)
 
 
 def first_kernel(
-    hidden_ref, gain_ref, weight_ref, cos_ref, sin_ref, query_gain, key_gain, first_ref, pre_ref, send_ref
+    own_ref, left_ref, top_ref, bottom_ref, right_ref, weight_ref, gains_ref, cos_ref, sin_ref,
+    query_gain, key_gain, hidden_ref, first_ref, pre_ref, send_ref, gain_out,
 ):
-    first = (normalize(hidden_ref[0].astype(jnp.float32)) * gain_ref[...]).astype(low)
+    at = pl.program_id(0)
+    half = top_ref.shape[0]
+
+    @pl.when(at == 0)
+    def _():
+        gain_out[...] = gains_ref[...].astype(jnp.float32).T[:8]
+        hidden_ref[0] = own_ref[...]
+
+    @pl.when(at == 1)
+    def _():
+        hidden_ref[0] = left_ref[...]
+
+    @pl.when(at == 2)
+    def _():
+        hidden_ref[0, :half] = top_ref[...]
+        hidden_ref[0, half:] = bottom_ref[...]
+
+    @pl.when(at == 3)
+    def _():
+        hidden_ref[0] = right_ref[...]
+
+    first = (normalize(hidden_ref[0].astype(jnp.float32)) * gain_out[0:1]).astype(low)
     first_ref[0] = first
     pre = jnp.dot(first, weight_ref[...], preferred_element_type=jnp.float32)
     pre_ref[0] = pre
@@ -527,17 +568,17 @@
         send_ref[2 * head + 1, 1] = pre[:, (6 + head) * HEAD_DIM : (7 + head) * HEAD_DIM].astype(low)
 
 
-def first_part(hidden_all, gain, weights, cosine, sine, query_gain, key_gain):
-    _, rows, width = hidden_all.shape
+def first_part(blocks, weights, cosine, sine, query_gain, key_gain):
+    rows, width = blocks[0].shape
     row = pl.BlockSpec((1, HEAD_DIM), lambda r: (0, 0))
     turn = pl.BlockSpec((1, rows, HEAD_DIM), lambda r: (r, 0, 0))
     return pl.pallas_call(
         first_kernel,
         grid=(RING,),
-        in_specs=[
-            pl.BlockSpec((1, rows, width), lambda r: (r, 0, 0)),
-            pl.BlockSpec((1, width), lambda r: (0, 0)),
+        in_specs=[pl.BlockSpec(block.shape, lambda r: (0, 0)) for block in blocks]
+        + [
             pl.BlockSpec((width, 1024), lambda r: (0, 0)),
+            pl.BlockSpec((width, HEAD_DIM), lambda r: (0, 8)),
             turn,
             turn,
             row,
@@ -545,13 +586,17 @@
         ],
         out_specs=(
             pl.BlockSpec((1, rows, width), lambda r: (r, 0, 0)),
+            pl.BlockSpec((1, rows, width), lambda r: (r, 0, 0)),
             pl.BlockSpec((1, rows, 1024), lambda r: (r, 0, 0)),
             pl.BlockSpec((4, 2, rows, HEAD_DIM), lambda r: (r, 0, 0, 0)),
+            pl.BlockSpec((8, width), lambda r: (0, 0)),
         ),
         out_shape=(
             jax.ShapeDtypeStruct((RING, rows, width), low),
+            jax.ShapeDtypeStruct((RING, rows, width), low),
             jax.ShapeDtypeStruct((RING, rows, 1024), jnp.float32),
             jax.ShapeDtypeStruct((BLOCKS, 2, rows, HEAD_DIM), low),
+            jax.ShapeDtypeStruct((8, width), jnp.float32),
         ),
         compiler_params=pltpu.CompilerParams(vmem_limit_bytes=VMEM_LIMIT),
         cost_estimate=pl.CostEstimate(
@@ -559,7 +604,7 @@
             bytes_accessed=20 * 1024 * 1024,
             transcendentals=0,
         ),
-    )(hidden_all, gain, weights, cosine, sine, query_gain, key_gain)
+    )(*blocks, weights, weights, cosine, sine, query_gain, key_gain)
 
 
 def first_back_kernel(
@@ -643,7 +688,7 @@
 
 def last_kernel(
     core_ref, grad_ref, weight_ref, hidden_ref, mlp_ref, query_ref, key_ref,
-    own_ref, left_ref, top_ref, bottom_ref, right_ref, keep_ref, give_ref, gain_acc,
+    own_ref, left_a, left_b, top_ref, bottom_ref, right_a, right_b, keep_ref, give_ref, gain_acc,
 ):
     at = pl.program_id(0)
     width = hidden_ref.shape[2]
@@ -651,16 +696,16 @@
         grad_ref[0], weight_ref[...], contract_last, preferred_element_type=jnp.float32
     )
     half = top_ref.shape[0]
-    for r, out in ((0, own_ref), (1, left_ref), (3, right_ref)):
+    @pl.when(at == 0)
+    def _():
+        own_ref[...] = part.astype(low)
+
+    for r, first, second in ((1, left_a, left_b), (2, top_ref, bottom_ref), (3, right_a, right_b)):
 
         @pl.when(at == r)
-        def _(out=out):
-            out[...] = part.astype(low)
-
-    @pl.when(at == 2)
-    def _():
-        top_ref[...] = part[:half].astype(low)
-        bottom_ref[...] = part[half:].astype(low)
+        def _(first=first, second=second):
+            first[...] = part[:half].astype(low)
+            second[...] = part[half:].astype(low)
 
     normed = normalize(hidden_ref[0].astype(jnp.float32))
     gain = jnp.sum(part * normed, axis=0, keepdims=True)
@@ -711,8 +756,8 @@
             row,
             row,
         ],
-        out_specs=(block, block, small, small, block, half, half),
-        out_shape=(whole, whole, part, part, whole)
+        out_specs=(block,) + (small,) * 6 + (half, half),
+        out_shape=(whole,) + (part,) * 6
         + (jax.ShapeDtypeStruct((8, 128, HEAD_DIM), low),) * 2,
         scratch_shapes=[pltpu.VMEM((1, width), jnp.float32)],
         compiler_params=pltpu.CompilerParams(vmem_limit_bytes=VMEM_LIMIT),
@@ -731,18 +776,40 @@
             out_ref[pl.ds(other, 128), :] = other_ref[dy, dx]
 
 
-def gather_by_permutes(pair, y_at, x_at, core_at):
-    own = jnp.stack([pair] + [shift(pair, "y", r) for r in range(1, RING)])
+def gather_by_permutes(pairs, y_at, x_at, core_at):
+    own = jnp.stack(pairs)
     other = shift(own, "core", 1, 2)
     whole = pl.BlockSpec(memory_space=pltpu.VMEM)
     return pl.pallas_call(
         arrange_kernel,
         in_specs=[pl.BlockSpec(memory_space=pltpu.SMEM), whole, whole],
         out_specs=whole,
-        out_shape=jax.ShapeDtypeStruct((BLOCKS * 128, pair.shape[2]), pair.dtype),
+        out_shape=jax.ShapeDtypeStruct((BLOCKS * 128, own.shape[3]), own.dtype),
         compiler_params=pltpu.CompilerParams(vmem_limit_bytes=VMEM_LIMIT),
         cost_estimate=pl.CostEstimate(flops=1024, bytes_accessed=1024, transcendentals=0),
     )(jnp.stack([y_at, x_at, core_at]), own, other)
+
+
+def pair_sums_kernel(keep_ref, come_ref, gains_keep, gains_come, out_ref):
+    f32 = jnp.float32
+    wide = keep_ref.shape[2]
+    out_ref[0, :, :wide] = (keep_ref[0].astype(f32) + come_ref[0].astype(f32)).astype(low)
+    out_ref[0, :, wide:] = (gains_keep[0].astype(f32) + gains_come[0].astype(f32)).astype(low)
+
+
+def pair_sums(keep, come, gains_keep, gains_come):
+    blocks, rows, wide = keep.shape
+    large = pl.BlockSpec((1, rows, wide), lambda i: (i, 0, 0))
+    small = pl.BlockSpec((1, rows, HEAD_DIM), lambda i: (i, 0, 0))
+    return pl.pallas_call(
+        pair_sums_kernel,
+        grid=(blocks,),
+        in_specs=[large, large, small, small],
+        out_specs=pl.BlockSpec((1, rows, wide + HEAD_DIM), lambda i: (i, 0, 0)),
+        out_shape=jax.ShapeDtypeStruct((blocks, rows, wide + HEAD_DIM), low),
+        compiler_params=pltpu.CompilerParams(vmem_limit_bytes=VMEM_LIMIT),
+        cost_estimate=pl.CostEstimate(flops=1024, bytes_accessed=1024, transcendentals=0),
+    )(keep, come, gains_keep, gains_come)
 
 
 def to_heads(send):
@@ -852,22 +919,32 @@
             [columns(query_weight), columns(key_weight), columns(value_weight), gains], axis=1
         )
     )
-    attn_scale = first_weights[:, 1024].astype(f32)[None]
-    mlp_scale = first_weights[:, 1025].astype(f32)[None]
     out_columns = columns(out_weight)
     out_come = shift(out_columns, "x_hi", 1, 2)
-    gate_columns, up_columns, down_columns, out_come = together(
-        gate_weight, up_weight, down_weight, out_come
-    )
+    out_pairs = jnp.stack([out_columns, out_come])
+    out_pairs = [out_pairs] + [shift(out_pairs, "y", r) for r in range(1, RING)]
+
+    hidden_own = after(hidden_in, notes, out_come)
+    hidden_left = shift(hidden_own, "z", 1)
+    hidden_right = shift(hidden_own, "z", 3)
+    gate_columns, up_columns, down_columns, hidden_left, hidden_right, out_pairs = together(
+        gate_weight, up_weight, down_weight, hidden_left, hidden_right, out_pairs
+    )
+    out_slice = gather_by_permutes(out_pairs, y_at, x_at, core_at)
     gate_columns, up_columns = columns(gate_columns), columns(up_columns)
     mlp_columns = []
     for start in range(0, gate_columns.shape[1], FF_STEP):
         mlp_columns.append(gate_columns[:, start : start + FF_STEP])
         mlp_columns.append(up_columns[:, start : start + FF_STEP])
     mlp_weights = gather(jnp.concatenate(mlp_columns + [columns(down_columns)], axis=1))
-    out_slice = gather_by_permutes(jnp.stack([out_columns, out_come]), y_at, x_at, core_at)
-
-    hidden_blocks = ring_blocks(hidden_in)
+    half = rows // 2
+    hidden_blocks = [
+        hidden_own,
+        hidden_left,
+        shift(hidden_left[:half], "z", 1),
+        shift(hidden_right[half:], "z", 3),
+        hidden_right,
+    ]
     out_slice = after(out_slice, *hidden_blocks)
     out_left = shift(out_slice, "z", 1)
     out_right = shift(out_slice, "z", 3)
@@ -880,10 +957,11 @@
     query_row = query_gain[None]
     key_row = key_gain[None]
 
-    hidden_all = jnp.stack(hidden_blocks)
-    first_in, qkv_pre, send = first_part(
-        hidden_all, attn_scale, first_weights, cosine, sine, query_row, key_row
-    )
+    hidden_all, first_in, qkv_pre, send, gain_rows = first_part(
+        hidden_blocks, first_weights, cosine, sine, query_row, key_row
+    )
+    attn_scale = gain_rows[0:1]
+    mlp_scale = gain_rows[1:2]
     out_top = shift(out_left[: width // 2], "z", 1)
     out_bottom = shift(out_right[width // 2 :], "z", 3)
     arrived, out_left, out_right, out_top, out_bottom = together(
@@ -896,32 +974,28 @@
     cot_right = shift(cot_own, "z", 3)
 
     mixed_arrived, cot_left, cot_right = together(to_heads(head_mixed), cot_left, cot_right)
-    half = rows // 2
     mixed_blocks = [mixed_arrived[:4]] + [
         shift(mixed_arrived[4 * (RING - j) : 4 * (RING - j) + 4], "z", j) for j in range(1, RING)
     ]
     out_opposite = jnp.concatenate([out_top, out_bottom], axis=0)
     out_weights = [out_slice, out_left, out_opposite, out_right]
     mixed_blocks, out_weights = together(mixed_blocks, out_weights)
-    middle, second_in = middle_part(mixed_blocks, out_weights, hidden_in, mlp_scale)
+    middle, second_in, cot_opposite = together(
+        *middle_part(mixed_blocks, out_weights, hidden_in, mlp_scale), shift(cot_own, "z", 2)
+    )
     hidden = hidden_in.astype(f32)
     left = shift(second_in, "z", 1)
     right = shift(second_in, "z", 3)
     *held, own_part = mlp_blocks(0, [second_in], [cot_own], mlp_weights, ())
-    held, own_part, left, right, cot_left, cot_right = together(
-        held, own_part, left, right, cot_left, cot_right
-    )
-    top = shift(left[:half], "z", 1)
-    bottom = shift(right[half:], "z", 3)
-    cot_top = shift(cot_left[:half], "z", 1)
-    cot_bottom = shift(cot_right[half:], "z", 3)
+    held, own_part, left, right, second_in = together(held, own_part, left, right, second_in)
+    opposite = shift(second_in, "z", 2)
     *held, left_part, right_part = mlp_blocks(
         1, [left, right], [cot_left, cot_right], mlp_weights, held
     )
     left_back = send_back(left_part, 1)
     right_back = send_back(right_part, 3)
-    held, top, bottom, cot_top, cot_bottom = together(held, top, bottom, cot_top, cot_bottom)
-    *held, opposite_part = mlp_blocks(1, [top, bottom], [cot_top, cot_bottom], mlp_weights, held)
+    held, opposite = together(held, opposite)
+    *held, opposite_part = mlp_blocks(1, [opposite], [cot_opposite], mlp_weights, held)
     opposite_back = send_back(opposite_part, 2)
     inner, both_grad, second_all, cot_all = held
 
@@ -960,15 +1034,15 @@
         mlp_scale,
     )
     grad_blocks = [grad_blocks[0]] + [shift(grad_blocks[RING - r], "z", r) for r in range(1, RING)]
+    grad_blocks, own_low, inner = together(grad_blocks, own_low, inner)
     down_keep, down_give = pair_grad(core_at, [cot_all], inner)
-    grad_blocks, down_keep, down_give, own_low, inner = together(
-        grad_blocks, down_keep, down_give, own_low, inner
-    )
     head_grads = to_heads(jnp.concatenate(grad_blocks, axis=0))
     low_left = shift(own_low, "z", 1)
     low_right = shift(own_low, "z", 3)
     down_sum = pair_sum(down_keep, shift(down_give, "core", 1, 2))
-    mlp_own, mlp_opposite, mlp_left, mlp_right = mlp_out_part(inner, mlp_weights)
+    mlp_own, mlp_opposite, mlp_left, mlp_right = mlp_out_part(
+        after(inner, down_give), mlp_weights
+    )
     head_grads, down_sum, low_left, low_right, own_low, mlp_opposite, mlp_left, mlp_right = together(
         head_grads, down_sum, low_left, low_right, own_low, mlp_opposite, mlp_left, mlp_right
     )
@@ -989,17 +1063,21 @@
     grads_send, down_terms = together(grads_send, down_terms)
     returned = to_heads(grads_send)
     down_pair = over_x(add_up(down_terms))
-    out_keep, out_give = pair_grad(
+    out_term = pair_grad(
         core_at, [own_low, low_left, low_opposite, low_right], mixed_arrived, by_heads=True
     )
-    out_sum = pair_sum(out_keep, shift(out_give, "core", 1, 2))
     mlp_opposite = send_back(mlp_opposite, 2)
-    returned, out_sum, mlp_opposite = together(returned, out_sum, mlp_opposite)
-    out_terms = to_owners(out_sum)
+    returned, both_share, out_term = together(returned, both_share, out_term)
+    out_share = lax.psum_scatter(out_term, GROUP_AXES, scatter_dimension=0, tiled=True)
+    both_pair = over_x(both_share)
     qkv_grad, qkv_keep, qkv_give, query_gain_part, key_gain_part = first_back(
         core_at, returned, qkv_pre, cosine, sine, query_row, key_row, first_in
     )
-    qkv_grad, qkv_give, down_pair = together(qkv_grad, qkv_give, down_pair)
+    qkv_grad, qkv_give, down_pair, both_pair = together(qkv_grad, qkv_give, down_pair, both_pair)
+    both_sum = pair_sum(*both_pair)
+    both_left = shift(both_sum, "z", 1)
+    both_right = shift(both_sum, "z", 3)
+    down_blocks = over_z(down_pair)
     qkv_come = shift(qkv_give, "core", 1, 2)
     *first_parts, gains_keep, gains_give = last_part(
         core_at,
@@ -1010,31 +1088,21 @@
         query_gain_part,
         key_gain_part,
     )
-    down_blocks = over_z(down_pair)
-    first_parts, gains_give, qkv_come, out_terms, down_blocks, both_share = together(
-        first_parts, gains_give, qkv_come, out_terms, down_blocks, both_share
+    first_parts, gains_give, qkv_come, mlp_opposite, both_left, both_right, both_sum = together(
+        first_parts, gains_give, qkv_come, mlp_opposite, both_left, both_right, both_sum
     )
     gains_come = shift(gains_give, "core", 1, 2)
-    first_own, first_left, first_top, first_bottom, first_right = first_parts
+    first_own, left_a, left_b, first_top, first_bottom, right_a, right_b = first_parts
     first_top = shift(first_top, "z", 3)
     first_bottom = shift(first_bottom, "z", 1)
-    qkv_terms = to_owners(
-        jnp.concatenate([pair_sum(qkv_keep, qkv_come), pair_sum(gains_keep, gains_come)], axis=2)
-    )
-    both_pair = over_x(both_share)
-    out_pair = over_x(add_up(out_terms))
-    first_left = send_back(
-        jnp.concatenate([pair_sum(first_left[:half], first_top), first_left[half:]], axis=0), 1
-    )
-    first_right = send_back(
-        jnp.concatenate([first_right[:half], pair_sum(first_right[half:], first_bottom)], axis=0), 3
-    )
-    qkv_terms, out_pair, both_pair = together(qkv_terms, out_pair, both_pair)
+    qkv_terms = to_owners(pair_sums(qkv_keep, qkv_come, gains_keep, gains_come))
+    first_left = send_back(jnp.concatenate([pair_sum(left_a, first_top), left_b], axis=0), 1)
+    first_right = send_back(jnp.concatenate([right_a, pair_sum(right_b, first_bottom)], axis=0), 3)
+    both_opposite = shift(both_sum, "z", 2)
+    qkv_terms, down_blocks, both_opposite = together(qkv_terms, down_blocks, both_opposite)
+    out_pair = over_x(out_share)
     qkv_share = add_up(qkv_terms)
-    both_sum = pair_sum(*both_pair)
-    both_left = shift(both_sum, "z", 1)
-    both_right = shift(both_sum, "z", 3)
-    both_blocks = [both_sum, both_left, shift(both_sum, "z", 2), both_right]
+    both_blocks = [both_sum, both_left, both_opposite, both_right]
     qkv_pair = over_x(qkv_share)
     output = (
         middle

time: 726 us -> 746 us (1.028)
  waiting for transfers between devices: 214 us -> 272 us
  blocking collectives: 28.9 us -> 0 us
  other arithmetic: 54.6 us -> 40.3 us
  starting transfers between devices: 126 us -> 134 us
    ppermute x65 -> x62, waiting for transfers between devices: 197 us -> 245 us  [shift(): lax.ppermute(values, axis, [(i, (i + by) % size) for i in range(size)])]
    all_to_all x1 -> x0, blocking collectives: 28.9 us -> none  [to_heads(): return lax.all_to_all(send, GROUP_AXES, 0, 0, tiled=True)]
    all_to_all x3 -> x4, waiting for transfers between devices: 8.06 us -> 19.8 us  [to_heads(): return lax.all_to_all(send, GROUP_AXES, 0, 0, tiled=True)]
    slice x8 -> x3, local copies, waits for them, and re-layouts: 11.1 us -> 1 us  [the longest x1 0.93 us: local(): attn_scale = gain_rows[0:1]]
    ppermute x65 -> x62, starting transfers between devices: 81.1 us -> 90.3 us  [shift(): lax.ppermute(values, axis, [(i, (i + by) % size) for i in range(size)])]
    all_to_all x3 -> x2, starting transfers between devices: 24.3 us -> 16.1 us  [to_owners(): return lax.all_to_all(pair, ('y', 'x_hi'), 0, 0, tiled=True)]
    all_to_all x3 -> x4, starting transfers between devices: 20.1 us -> 27.4 us  [to_heads(): return lax.all_to_all(send, GROUP_AXES, 0, 0, tiled=True)]
    pallas_call x1 -> x2, Pallas kernels: 10.9 us -> 18.3 us  [the longest x1 12 us: first_part(): pl.pallas_call(first_kernel, grid=(RING,), in_specs=[pl.BlockSpec(block.s...]
  transfers between devices with their start and end apart: 74 -> 72, of which waited for: 27 -> 31; matrix products, arithmetic and copies ran while one was open for 13% -> 9% of each run, Pallas kernels for 31% -> 30%
where the time goes in v5:
time: 746 us; the launch traced here: 735 us
  waiting for transfers between devices  272 us (36%)
  Pallas kernels  223 us (30%)
  starting transfers between devices  134 us (18%)
  other arithmetic  40.3 us (5%)
  local copies, waits for them, and re-layouts  30.8 us (4%)
  matrix products  19.4 us (3%)
  between operations  14.9 us (2%)
    ppermute x62, waiting for transfers between devices, shift(): lax.ppermute(values, axis, [(i, (i + by) % size) for i in range(size)])  245 us
    ppermute x62, starting transfers between devices, shift(): lax.ppermute(values, axis, [(i, (i + by) % size) for i in range(size)])  90.3 us
    pallas_call x3, Pallas kernels, mlp_blocks(): pl.pallas_call(functools.partial(mlp_kernel, len(seconds)), grid=(steps,)...  57.9 us
    pallas_call x1, Pallas kernels, attention_backward(): pl.pallas_call(backward_kernel, out_shape=(jax.ShapeDtypeStruct((BLOCKS,...  35.5 us
    all_to_all x4, starting transfers between devices, to_heads(): return lax.all_to_all(send, GROUP_AXES, 0, 0, tiled=True)  27.4 us
    pallas_call x1, Pallas kernels, attention_forward(): pl.pallas_call(forward_kernel, out_shape=(jax.ShapeDtypeStruct((BLOCKS, B...  21.5 us
    pallas_call x2, Pallas kernels, pair_grad(): pl.pallas_call(kernel, grid=(width // 256,), in_specs=[pl.BlockSpec(memor...  21 us
    all_to_all x4, waiting for transfers between devices, to_heads(): return lax.all_to_all(send, GROUP_AXES, 0, 0, tiled=True)  19.8 us
  transfers between devices with their start and end apart: 72, of which 31 were waited for; matrix products, arithmetic and copies ran while one was open for 9% of the time, Pallas kernels for 30%

profile of v5, /device:TPU:4, one launch (start us, length us, event | category | flops | bytes accessed | tf_op | source)
XLA Modules:
  0.0 734.7 jit_solution(11824555282001240282)
XLA Ops:
  78.5 12.0 %shard_map.246 = (bf16[4,256,2048]{2,1,0:T(8,128)(2,1)}, bf16[4,256,2048]{2,1,0:T(8,128)(2,1)}, f32[4,256,1024]{2,1,0:T(8,128)}, bf16[16,2,256,128]{3,2,1,0:T(8,128)(2,1)}, f32[8,2048]{1,0:T(8,128)}) custom-call(bf16[256,2048]{1,0:T(8,128)(2,1)} %refs_8_.1, bf16[256,2048]{1,0:T(8,128)(2,1)} %copy-done.42, bf16[128,2048]{1,0:T(8,128)(2,1)} %collective-permute-done.9.top_ref, ...), custom_call_target="tpu_custom_call" | custom-call | flops 4294967296 | bytes 20971520 | tf_op jit(solution)/shard_map/pallas_call | solution.py:575
  98.1 22.3 %collective-permute-done.12.refs_5_ = bf16[2048,512]{1,0:T(8,128)(2,1)S(1)} collective-permute-done((bf16[2048,512]{1,0:T(8,128)(2,1)}, bf16[2048,512]{1,0:T(8,128)(2,1)S(1)}, u32[]{:S(2)}, u32[]{:S(2)}) %collective-permute-start.12) | collective-permute-done | bytes 2097184 | tf_op jit(solution)/shard_map/ppermute | solution.py:41
  125.1 20.2 %collective-permute-done.14 = bf16[1024,512]{1,0:T(8,128)(2,1)S(1)} collective-permute-done((bf16[1024,512]{1,0:T(8,128)(2,1)S(1)}, bf16[1024,512]{1,0:T(8,128)(2,1)S(1)}, u32[]{:S(2)}, u32[]{:S(2)}) %collective-permute-start.14) | collective-permute-done | bytes 1048608 | tf_op jit(solution)/shard_map/ppermute | solution.py:41
  151.6 21.5 %shard_map.248 = (bf16[16,256,128]{2,1,0:T(8,128)(2,1)}, f32[8,128,512]{2,1,0:T(8,128)}, f32[8,1,512]{2,1,0:T(1,128)}) custom-call(s32[16]{0:T(128)} %dynamic-slice_bitcast_fusion.order, s32[1]{0:T(128)} %bitcast.1.core.core_ref, bf16[16,2,256,128]{3,2,1,0:T(8,128)(2,1)} %all-to-all-done.own_a.own_b, bf16[16,2,256,128]{3,2,1,0:T(8,128)(2,1)} %all-to-all-done.own_a.own_b, ...), custom_call_target="tpu_custom_call" | custom-call | flops 1024 | bytes 1024 | tf_op jit(solution)/shard_map/pallas_call | solution.py:117
  186.6 17.4 %all-to-all-done.1.refs_4_ = bf16[16,256,128]{2,1,0:T(8,128)(2,1)S(1)} async-done(((bf16[16,256,128]{2,1,0:T(8,128)(2,1)}), bf16[16,256,128]{2,1,0:T(8,128)(2,1)S(1)}, u32[]{:S(2)}, u32[]{:S(2)}) %all-to-all-start.1) | async-done | bytes 1048608 | tf_op jit(solution)/shard_map/all_to_all | solution.py:816
  204.0 18.2 %collective-permute-done.18.refs_3_ = bf16[256,2048]{1,0:T(8,128)(2,1)S(1)} collective-permute-done((bf16[256,2048]{1,0:T(8,128)(2,1)}, bf16[256,2048]{1,0:T(8,128)(2,1)S(1)}, u32[]{:S(2)}, u32[]{:S(2)}) %collective-permute-start.18) | collective-permute-done | bytes 1048608 | tf_op jit(solution)/shard_map/ppermute | solution.py:41
  248.9 15.7 %shard_map.250 = (bf16[4,256,1536]{2,1,0:T(8,128)(2,1)}, bf16[4,256,3072]{2,1,0:T(8,128)(2,1)}, bf16[4,256,2048]{2,1,0:T(8,128)(2,1)}, bf16[4,256,2048]{2,1,0:T(8,128)(2,1)}, bf16[256,2048]{1,0:T(8,128)(2,1)}) custom-call(bf16[256,2048]{1,0:T(8,128)(2,1)} %get-tuple-element.229.refs_0_, bf16[256,2048]{1,0:T(8,128)(2,1)} %refs_9_.1, ...), custom_call_target="tpu_custom_call" | custom-call | flops 8053063680 | bytes 18874368 | tf_op jit(solution)/shard_map/pallas_call | solution.py:318
  274.6 26.6 %shard_map.251 = (bf16[4,256,1536]{2,1,0:T(8,128)(2,1)}, bf16[4,256,3072]{2,1,0:T(8,128)(2,1)}, bf16[4,256,2048]{2,1,0:T(8,128)(2,1)}, bf16[4,256,2048]{2,1,0:T(...) custom-call(bf16[256,2048]{1,0:T(8,128)(2,1)} %collective-permute-do, ...), custom_call_target="tpu_custom_call", output_to_operand_aliasing={{0}: (6, {}), {1}: (7, {}), {2}: (8, {}), {3}: (9, {})} | custom-call | flops 16106127360 | bytes 18874368 | tf_op jit(solution)/shard_map/pallas_call | solution.py:318
  303.3 15.7 %shard_map.252 = (bf16[4,256,1536]{2,1,0:T(8,128)(2,1)}, bf16[4,256,3072]{2,1,0:T(8,128)(2,1)}, bf16[4,256,2048]{2,1,0:T(8,128)(2,1)}, bf16[4,256,2048]{2,1,0:T(8,128)(2,1)}, bf16[256,2048]{1,0:T(8,128)(2,1)}) custom-call(bf16[256,2048]{1,0:T(8,128)(2,1)} %collective-permute-done.27.refs_0_, ...), custom_call_target="tpu_custom_call", output_to_operand_aliasing={{0}: (4, {}), {1}: (5, {}), {2}: (6, {}), {3}: (7, {})} | custom-call | flops 8053063680 | bytes 18874368 | tf_op jit(solution)/shard_map/pallas_call | solution.py:318
  320.3 19.4 %bitcast_convert_fusion = bf16[2048,3072]{1,0:T(8,128)(2,1)} fusion(bf16[4,256,2048]{2,1,0:T(8,128)(2,1)} %get-tuple-element.237, bf16[4,256,3072]{2,1,0:T(8,128)(2,1)} %get-tuple-element.238), kind=kOutput, calls=%fused_computation | convolution fusion | flops 12891193344 | bytes 23068672 | tf_op jit(solution)/shard_map/dot_general | solution.py:1018
  339.6 10.2 %collective-permute-done.26.refs_2_ = bf16[256,2048]{1,0:T(8,128)(2,1)} collective-permute-done((bf16[256,2048]{1,0:T(8,128)(2,1)}, bf16[256,2048]{1,0:T(8,128)(2,1)}, u32[]{:S(2)}, u32[]{:S(2)}) %collective-permute-start.26) | collective-permute-done | bytes 1048608 | tf_op jit(solution)/shard_map/ppermute | solution.py:41
  352.7 9.0 %shard_map.253 = (f32[256,2048]{1,0:T(8,128)S(1)}, bf16[256,2048]{1,0:T(8,128)(2,1)S(1)}, f32[1,2048]{1,0:T(1,128)S(1)}, bf16[4,256,128]{2,1,0:T(8,128)(2,1)S(1)...) custom-call(bf16[256,2048]{1,0:T(8,128)(2,1)S(1)} %copy-done.12, ...), custom_call_target="tpu_custom_call" | custom-call | flops 1024 | bytes 1024 | tf_op jit(solution)/shard_map/pallas_call | solution.py:509
  367.9 8.1 %collective-permute-done.29 = bf16[4,256,128]{2,1,0:T(8,128)(2,1)S(1)} collective-permute-done((bf16[4,256,128]{2,1,0:T(8,128)(2,1)S(1)}, bf16[4,256,128]{2,1,0:T(8,128)(2,1)S(1)}, u32[]{:S(2)}, u32[]{:S(2)}) %collective-permute-start.29) | collective-permute-done | bytes 262176 | tf_op jit(solution)/shard_map/ppermute | solution.py:41
  376.0 12.5 %shard_map.254 = (bf16[8,128,1536]{2,1,0:T(8,128)(2,1)}, bf16[8,128,1536]{2,1,0:T(8,128)(2,1)}) custom-call(s32[1]{0:T(128)} %bitcast.1.core.core_ref, bf16[4,256,2048]{2,1,0:T(8,128)(2,1)} %get-tuple-element.250.refs_0_, bf16[4,256,1536]{2,1,0:T(8,128)(2,1)} %get-tuple-element.252.refs_1_.inner_ref), custom_call_target="tpu_custom_call" | custom-call | flops 1024 | bytes 1024 | tf_op jit(solution)/shard_map/pallas_call | solution.py:414
  400.6 10.6 %shard_map.255 = (bf16[256,2048]{1,0:T(8,128)(2,1)}, bf16[256,2048]{1,0:T(8,128)(2,1)}, bf16[256,2048]{1,0:T(8,128)(2,1)}, bf16[256,2048]{1,0:T(8,128)(2,1)}) custom-call(bf16[4,256,1536]{2,1,0:T(8,128)(2,1)} %get-tuple-element.252.refs_1_.inner_ref, bf16[2048,4608]{1,0:T(8,128)(2,1)} %all-gather.5.cloned.1.call-done.refs_2_.refs_3_.refs_4_.refs_5_.weight_ref), custom_call_target="tpu_custom_call" | custom-call | flops 1024 | bytes 1024 | tf_op jit(solution)/shard_map/pallas_call | solution.py:360
  420.0 9.0 %all-to-all-start.3 = ((bf16[8,128,1536]{2,1,0:T(8,128)(2,1)}), bf16[8,128,1536]{2,1,0:T(8,128)(2,1)}, u32[]{:S(2)}, u32[]{:S(2)}) async-start(bf16[8,128,1536]{2,1,0:T(8,128)(2,1)} %add_convert_fusion), calls=%async_computation.3 | async-start | bytes 6291456 | tf_op jit(solution)/shard_map/all_to_all | solution.py:1006
  431.9 35.5 %shard_map.256 = (bf16[16,2,256,128]{3,2,1,0:T(8,128)(2,1)}, bf16[16,256,128]{2,1,0:T(8,128)(2,1)}, bf16[16,256,128]{2,1,0:T(8,128)(2,1)}) custom-call(s32[16]{0:T(128)} %dynamic-slice_bitcast_fusion.order, s32[1]{0:T(128)} %bitcast.1.core.core_ref, bf16[16,2,256,128]{3,2,1,0:T(8,128)(2,1)} %all-to-all-done.own_a.own_b, ...), custom_call_target="tpu_custom_call" | custom-call | flops 1024 | bytes 1024 | tf_op jit(solution)/shard_map/pallas_call | solution.py:224
  489.8 23.5 %collective-permute-done.38.refs_2_ = bf16[256,2048]{1,0:T(8,128)(2,1)S(1)} collective-permute-done((bf16[256,2048]{1,0:T(8,128)(2,1)S(1)}, bf16[256,2048]{1,0:T(8,128)(2,1)S(1)}, u32[]{:S(2)}, u32[]{:S(2)}) %collective-permute-start.38) | collective-permute-done | bytes 1048608 | tf_op jit(solution)/shard_map/ppermute | solution.py:41
  514.3 8.5 %shard_map.257 = bf16[2048,512]{1,0:T(8,128)(2,1)} custom-call(s32[1]{0:T(128)} %bitcast.1.core.core_ref, bf16[256,2048]{1,0:T(8,128)(2,1)} %copy-done.13, bf16[256,2048]{1,0:T(8,128)(2,1)} %collective-permute-done.33.refs_1_, bf16[256,2048]{1,0:T(8,128)(2,1)} %copy-done.33, bf16[256,2048]{1,0:T(8,128)(2,1)} %collective-permute-done.34.refs_3_, ...), custom_call_target="tpu_custom_call" | custom-call | flops 1024 | bytes 1024 | tf_op jit(solution)/shard_map/pallas_call | solution.py:414
  527.6 15.1 %shard_map.258 = (bf16[4,256,1024]{2,1,0:T(8,128)(2,1)}, bf16[8,128,1024]{2,1,0:T(8,128)(2,1)}, bf16[8,128,1024]{2,1,0:T(8,128)(2,1)}, f32[1,128]{1,0:T(1,128)}, f32[1,128]{1,0:T(1,128)}) custom-call(s32[1]{0:T(128)} %bitcast.1.core.core_ref, bf16[16,2,256,128]{3,2,1,0:T(8,128)(2,1)} %all-to-all-done.4.back_ref, f32[4,256,1024]{2,1,0:T(8,128)} %get-tuple-element.285.pre_ref, ...), custom_call_target="tpu_custom_call" | custom-call | flops 1024 | bytes 1024 | tf_op jit(solution)/shard_map/pallas_call | solution.py:662
  560.2 12.6 %shard_map.259 = (bf16[256,2048]{1,0:T(8,128)(2,1)}, bf16[128,2048]{1,0:T(8,128)(2,1)}, bf16[128,2048]{1,0:T(8,128)(2,1)}, bf16[128,2048]{1,0:T(8,128)(2,1)}, bf...) custom-call(s32[1]{0:T(128)} %bitcast.1.core.core_ref, ...), custom_call_target="tpu_custom_call" | custom-call | flops 1024 | bytes 1024 | tf_op jit(solution)/shard_map/pallas_call | solution.py:747
  579.3 16.4 %collective-permute-done.43.refs_1_ = bf16[128,3072]{1,0:T(8,128)(2,1)} collective-permute-done((bf16[128,3072]{1,0:T(8,128)(2,1)}, bf16[128,3072]{1,0:T(8,128)(2,1)}, u32[]{:S(2)}, u32[]{:S(2)}) %collective-permute-start.43) | collective-permute-done | bytes 786464 | tf_op jit(solution)/shard_map/ppermute | solution.py:41
  625.7 19.3 %collective-permute-done.58 = bf16[128,512]{1,0:T(8,128)(2,1)S(1)} collective-permute-done((bf16[128,512]{1,0:T(8,128)(2,1)}, bf16[128,512]{1,0:T(8,128)(2,1)S(1)}, u32[]{:S(2)}, u32[]{:S(2)}) %collective-permute-start.58) | collective-permute-done | bytes 131104 | tf_op jit(solution)/shard_map/ppermute | solution.py:41
  650.4 24.0 %collective-permute-done.59.refs_1_ = bf16[128,512]{1,0:T(8,128)(2,1)S(1)} collective-permute-done((bf16[128,512]{1,0:T(8,128)(2,1)S(1)}, bf16[128,512]{1,0:T(8,128)(2,1)S(1)}, u32[]{:S(2)}, u32[]{:S(2)}) %collective-permute-start.59) | collective-permute-done | bytes 131104 | tf_op jit(solution)/shard_map/ppermute | solution.py:41
  (310 shorter events, 316.8 us)
Async XLA Ops:
  7.2 71.3 %all-gather.3.cloned.1.call-start = ((), (), s32[]{:S(2)}) async-start(), calls=%async_computation.8 | async-start | bytes 5013504 | tf_op jit(solution)/shard_map/all_gather | solution.py:902
  10.9 238.0 %all-gather.5.cloned.1.call-start = ((), (), s32[]{:S(2)}) async-start(), calls=%async_computation.9 | async-start | bytes 20054016 | tf_op jit(solution)/shard_map/all_gather | solution.py:902
  72.0 48.3 %collective-permute-start.12 = (bf16[2048,512]{1,0:T(8,128)(2,1)}, bf16[2048,512]{1,0:T(8,128)(2,1)S(1)}, u32[]{:S(2)}, u32[]{:S(2)}) collective-permute-start(bf16[2048,512]{1,0:T(8,128)(2,1)} %shard_map.247.refs_4_), channel_id=1, source_target_pairs={{0,16},{16,32},{32,48},{48,0},{1,17},{17,33},{33,49},{49,1},{2,18}... | collective-permute-start | bytes 6291464 | tf_op jit(solution)/shard_map/ppermute | solution.py:41
  72.0 48.5 %collective-permute-start.13 = (bf16[2048,512]{1,0:T(8,128)(2,1)}, bf16[2048,512]{1,0:T(8,128)(2,1)}, u32[]{:S(2)}, u32[]{:S(2)}) collective-permute-start(bf16[2048,512]{1,0:T(8,128)(2,1)} %shard_map.247.refs_4_), channel_id=1, source_target_pairs={{0,48},{16,0},{32,16},{48,32},{1,49},{17,1},{33,17},{49,33},{2,50}... | collective-permute-start | bytes 6291464 | tf_op jit(solution)/shard_map/ppermute | solution.py:41
  90.5 55.9 %all-to-all-start = ((bf16[16,2,256,128]{3,2,1,0:T(8,128)(2,1)}), bf16[16,2,256,128]{3,2,1,0:T(8,128)(2,1)}, u32[]{:S(2)}, u32[]{:S(2)}) async-start(bf16[16,2,256,128]{3,2,1,0:T(8,128)(2,1)} %get-tuple-element.179), calls=%async_computation | async-start | bytes 4194304 | tf_op jit(solution)/shard_map/all_to_all | solution.py:816
  173.1 49.1 %collective-permute-start.18 = (bf16[256,2048]{1,0:T(8,128)(2,1)}, bf16[256,2048]{1,0:T(8,128)(2,1)S(1)}, u32[]{:S(2)}, u32[]{:S(2)}) collective-permute-start(bf16[256,2048]{1,0:T(8,128)(2,1)} %refs_9_.1), channel_id=1, source_target_pairs={{0,48},{16,0},{32,16},{48,32},{1,49},{17,1},{33,17},{49,33},{2,50}... | collective-permute-start | bytes 3145736 | tf_op jit(solution)/shard_map/ppermute | solution.py:41
  184.2 338.6 %reduce-scatter.3.cloned.1.call-start = ((), (), s32[]{:S(2)}) async-start(), calls=%async_computation.10 | async-start | bytes 13369344 | tf_op jit(solution)/shard_map/reduce_scatter | solution.py:1027
  184.2 61.5 %collective-permute-start.22 = (bf16[256,2048]{1,0:T(8,128)(2,1)}, bf16[256,2048]{1,0:T(8,128)(2,1)}, u32[]{:S(2)}, u32[]{:S(2)}) collective-permute-start(bf16[256,2048]{1,0:T(8,128)(2,1)} %refs_9_.1), channel_id=1, source_target_pairs={{0,32},{16,48},{32,0},{48,16},{1,33},{17,49},{33,1},{49,17},{2,34}... | collective-permute-start | bytes 3145736 | tf_op jit(solution)/shard_map/ppermute | solution.py:41
  271.5 31.8 %collective-permute-start.27 = (bf16[256,2048]{1,0:T(8,128)(2,1)}, bf16[256,2048]{1,0:T(8,128)(2,1)}, u32[]{:S(2)}, u32[]{:S(2)}) collective-permute-start(bf16[256,2048]{1,0:T(8,128)(2,1)} %get-tuple-element.229.refs_0_), channel_id=1, source_target_pairs={{0,32},{16,48},{32,0},{48,16},{1,33},{17,49},{33,1},{49,17},{2,34}... | collective-permute-start | bytes 3145736 | tf_op jit(solution)/shard_map/ppermute | solution.py:41
  301.2 38.5 %collective-permute-start.25 = (bf16[256,2048]{1,0:T(8,128)(2,1)}, bf16[256,2048]{1,0:T(8,128)(2,1)}, u32[]{:S(2)}, u32[]{:S(2)}) collective-permute-start(bf16[256,2048]{1,0:T(8,128)(2,1)} %get-tuple-element.223), channel_id=1, source_target_pairs={{0,48},{16,0},{32,16},{48,32},{1,49},{17,1},{33,17},{49,33},{2,50}... | collective-permute-start | bytes 3145736 | tf_op jit(solution)/shard_map/ppermute | solution.py:41
  302.1 47.7 %collective-permute-start.26 = (bf16[256,2048]{1,0:T(8,128)(2,1)}, bf16[256,2048]{1,0:T(8,128)(2,1)}, u32[]{:S(2)}, u32[]{:S(2)}) collective-permute-start(bf16[256,2048]{1,0:T(8,128)(2,1)} %get-tuple-element.224), channel_id=1, source_target_pairs={{0,16},{16,32},{32,48},{48,0},{1,17},{17,33},{33,49},{49,1},{2,18}... | collective-permute-start | bytes 3145736 | tf_op jit(solution)/shard_map/ppermute | solution.py:41
  420.0 60.2 %all-to-all-start.3 = ((bf16[8,128,1536]{2,1,0:T(8,128)(2,1)}), bf16[8,128,1536]{2,1,0:T(8,128)(2,1)}, u32[]{:S(2)}, u32[]{:S(2)}) async-start(bf16[8,128,1536]{2,1,0:T(8,128)(2,1)} %add_convert_fusion), calls=%async_computation.3 | async-start | bytes 6291456 | tf_op jit(solution)/shard_map/all_to_all | solution.py:1006
  429.0 38.4 %collective-permute-start.35 = (bf16[256,2048]{1,0:T(8,128)(2,1)}, bf16[256,2048]{1,0:T(8,128)(2,1)S(1)}, u32[]{:S(2)}, u32[]{:S(2)}) collective-permute-start(bf16[256,2048]{1,0:T(8,128)(2,1)} %get-tuple-element.269), channel_id=1, source_target_pairs={{0,48},{16,0},{32,16},{48,32},{1,49},{17,1},{33,17},{49,33},{2,50}... | collective-permute-start | bytes 3145736 | tf_op jit(solution)/shard_map/ppermute | solution.py:41
  431.9 35.5 %collective-permute-start.36 = (bf16[256,2048]{1,0:T(8,128)(2,1)}, bf16[256,2048]{1,0:T(8,128)(2,1)}, u32[]{:S(2)}, u32[]{:S(2)}) collective-permute-start(bf16[256,2048]{1,0:T(8,128)(2,1)} %get-tuple-element.270), channel_id=1, source_target_pairs={{0,16},{16,32},{32,48},{48,0},{1,17},{17,33},{33,49},{49,1},{2,18}... | collective-permute-start | bytes 3145736 | tf_op jit(solution)/shard_map/ppermute | solution.py:41
  480.3 42.5 %all-to-all-start.4 = ((bf16[16,2,256,128]{3,2,1,0:T(8,128)(2,1)}), bf16[16,2,256,128]{3,2,1,0:T(8,128)(2,1)}, u32[]{:S(2)}, u32[]{:S(2)}) async-start(bf16[16,2,256,128]{3,2,1,0:T(8,128)(2,1)} %fusion.9), calls=%async_computation.4 | async-start | bytes 4194304 | tf_op jit(solution)/shard_map/all_to_all | solution.py:816
  485.1 128.6 %reduce-scatter.5.cloned.1.call-start = ((), (), s32[]{:S(2)}) async-start(), calls=%async_computation.11 | async-start | bytes 2228224 | tf_op jit(solution)/shard_map/reduce_scatter | solution.py:1071
  551.5 44.3 %collective-permute-start.41 = (bf16[8,128,1024]{2,1,0:T(8,128)(2,1)}, bf16[8,128,1024]{2,1,0:T(8,128)(2,1)S(1)}, u32[]{:S(2)}, u32[]{:S(2)}) collective-permute-start(bf16[8,128,1024]{2,1,0:T(8,128)(2,1)} %get-tuple-element.304), channel_id=1, source_target_pairs={{0,1},{1,0},{2,3},{3,2},{4,5},{5,4},{6,7},{7,6},{8,9},{9,8},{10,11... | collective-permute-start | bytes 6291464 | tf_op jit(solution)/shard_map/ppermute | solution.py:41
  556.9 38.8 %collective-permute-start.43 = (bf16[128,3072]{1,0:T(8,128)(2,1)}, bf16[128,3072]{1,0:T(8,128)(2,1)}, u32[]{:S(2)}, u32[]{:S(2)}) collective-permute-start(bf16[128,3072]{1,0:T(8,128)(2,1)} %add_convert_fusion.3.refs_0_), channel_id=1, source_target_pairs={{0,16},{16,32},{32,48},{48,0},{1,17},{17,33},{33,49},{49,1},{2,18}... | collective-permute-start | bytes 2359304 | tf_op jit(solution)/shard_map/ppermute | solution.py:41
  557.3 38.4 %collective-permute-start.44 = (bf16[128,3072]{1,0:T(8,128)(2,1)}, bf16[128,3072]{1,0:T(8,128)(2,1)}, u32[]{:S(2)}, u32[]{:S(2)}) collective-permute-start(bf16[128,3072]{1,0:T(8,128)(2,1)} %add_convert_fusion.3.refs_0_), channel_id=1, source_target_pairs={{0,48},{16,0},{32,16},{48,32},{1,49},{17,1},{33,17},{49,33},{2,50}... | collective-permute-start | bytes 2359304 | tf_op jit(solution)/shard_map/ppermute | solution.py:41
  599.1 50.5 %collective-permute-start.50 = (bf16[128,1536]{1,0:T(8,128)(2,1)}, bf16[128,1536]{1,0:T(8,128)(2,1)}, u32[]{:S(2)}, u32[]{:S(2)}) collective-permute-start(bf16[128,1536]{1,0:T(8,128)(2,1)} %add_convert_fusion.6.refs_0_), channel_id=1, source_target_pairs={{0,16},{16,32},{32,48},{48,0},{1,17},{17,33},{33,49},{49,1},{2,18}... | collective-permute-start | bytes 1179656 | tf_op jit(solution)/shard_map/ppermute | solution.py:41
  606.5 89.1 %all-to-all-start.5 = ((bf16[8,128,1152]{2,1,0:T(8,128)(2,1)}), bf16[8,128,1152]{2,1,0:T(8,128)(2,1)S(1)}, u32[]{:S(2)}, u32[]{:S(2)}) async-start(bf16[8,128,1152]{2,1,0:T(8,128)(2,1)} %shard_map.260), calls=%async_computation.6 | async-start | bytes 4718592 | tf_op jit(solution)/shard_map/all_to_all | solution.py:1006
  619.0 79.5 %collective-permute-start.46 = (bf16[256,2048]{1,0:T(8,128)(2,1)}, bf16[256,2048]{1,0:T(8,128)(2,1)}, u32[]{:S(2)}, u32[]{:S(2)}) collective-permute-start(bf16[256,2048]{1,0:T(8,128)(2,1)} %pad_maximum_fusion.3), channel_id=1, source_target_pairs={{0,48},{16,0},{32,16},{48,32},{1,49},{17,1},{33,17},{49,33},{2,50}... | collective-permute-start | bytes 3145736 | tf_op jit(solution)/shard_map/ppermute | solution.py:41
  625.7 72.7 %collective-permute-start.48 = (bf16[256,2048]{1,0:T(8,128)(2,1)}, bf16[256,2048]{1,0:T(8,128)(2,1)}, u32[]{:S(2)}, u32[]{:S(2)}) collective-permute-start(bf16[256,2048]{1,0:T(8,128)(2,1)} %pad_maximum_fusion.4), channel_id=1, source_target_pairs={{0,16},{16,32},{32,48},{48,0},{1,17},{17,33},{33,49},{49,1},{2,18}... | collective-permute-start | bytes 3145736 | tf_op jit(solution)/shard_map/ppermute | solution.py:41
  646.8 48.8 %collective-permute-start.53 = (bf16[128,3072]{1,0:T(8,128)(2,1)}, bf16[128,3072]{1,0:T(8,128)(2,1)}, u32[]{:S(2)}, u32[]{:S(2)}) collective-permute-start(bf16[128,3072]{1,0:T(8,128)(2,1)} %add_convert_fusion.3.refs_0_), channel_id=1, source_target_pairs={{0,32},{16,48},{32,0},{48,16},{1,33},{17,49},{33,1},{49,17},{2,34}... | collective-permute-start | bytes 2359304 | tf_op jit(solution)/shard_map/ppermute | solution.py:41
  (100 other events, 1414.7 us)
Sparse Core Ops, SparseCore 0:
  11.1 62.2 all-gather.2
  75.8 142.9 all-gather.4
  350.0 164.8 reduce-scatter.2
  524.5 71.4 reduce-scatter.4

commit v6 on v5

--- a/solution.py
+++ b/solution.py
@@ -246,9 +246,9 @@
     )(order, core_at[None], arrived, arrived, other, other, grads, grads, mixed_t, logs)
 
 
-def mlp_kernel(parts, *refs):
-    second_refs, cot_refs = refs[:parts], refs[parts : 2 * parts]
-    both_weight_ref, down_ref = refs[2 * parts : 2 * parts + 2]
+def mlp_kernel(parts, cot_parts, *refs):
+    second_refs, cot_refs = refs[:parts], refs[parts : parts + cot_parts]
+    both_weight_ref, down_ref = refs[parts + cot_parts : parts + cot_parts + 2]
     count = refs[-1].shape[0] // BLOCK
     inner_ref, both_ref, second_out, cot_out = refs[-5 - count : -1 - count]
     grad_refs, acc = refs[-1 - count : -1], refs[-1]
@@ -316,7 +316,7 @@
     kept_rows = pl.BlockSpec((count, BLOCK, width), lambda c: (place_at, 0, 0))
     rows_shape = jax.ShapeDtypeStruct((RING, BLOCK, width), low)
     return pl.pallas_call(
-        functools.partial(mlp_kernel, len(seconds)),
+        functools.partial(mlp_kernel, len(seconds), len(cots)),
         grid=(steps,),
         in_specs=ins
         + [
@@ -520,7 +520,7 @@
         )
         + (jax.ShapeDtypeStruct((4, rows, HEAD_DIM), low),) * RING,
         scratch_shapes=[pltpu.VMEM((rows, 512), jnp.float32)] * RING,
-        compiler_params=pltpu.CompilerParams(vmem_limit_bytes=40 * 1024 * 1024),
+        compiler_params=pltpu.CompilerParams(vmem_limit_bytes=VMEM_LIMIT),
         cost_estimate=pl.CostEstimate(flops=1024, bytes_accessed=1024, transcendentals=0),
     )(*parts, *weights, middle, cot, gain)
 
@@ -973,16 +973,18 @@
     cot_left = shift(cot_own, "z", 1)
     cot_right = shift(cot_own, "z", 3)
 
-    mixed_arrived, cot_left, cot_right = together(to_heads(head_mixed), cot_left, cot_right)
+    cot_top = shift(cot_left[:half], "z", 1)
+    cot_bottom = shift(cot_right[half:], "z", 3)
+    mixed_arrived, cot_left, cot_right, cot_top, cot_bottom = together(
+        to_heads(head_mixed), cot_left, cot_right, cot_top, cot_bottom
+    )
     mixed_blocks = [mixed_arrived[:4]] + [
         shift(mixed_arrived[4 * (RING - j) : 4 * (RING - j) + 4], "z", j) for j in range(1, RING)
     ]
     out_opposite = jnp.concatenate([out_top, out_bottom], axis=0)
     out_weights = [out_slice, out_left, out_opposite, out_right]
     mixed_blocks, out_weights = together(mixed_blocks, out_weights)
-    middle, second_in, cot_opposite = together(
-        *middle_part(mixed_blocks, out_weights, hidden_in, mlp_scale), shift(cot_own, "z", 2)
-    )
+    middle, second_in = middle_part(mixed_blocks, out_weights, hidden_in, mlp_scale)
     hidden = hidden_in.astype(f32)
     left = shift(second_in, "z", 1)
     right = shift(second_in, "z", 3)
@@ -995,7 +997,9 @@
     left_back = send_back(left_part, 1)
     right_back = send_back(right_part, 3)
     held, opposite = together(held, opposite)
-    *held, opposite_part = mlp_blocks(1, [opposite], [cot_opposite], mlp_weights, held)
+    *held, opposite_part = mlp_blocks(
+        1, [opposite], [cot_top, cot_bottom], mlp_weights, held
+    )
     opposite_back = send_back(opposite_part, 2)
     inner, both_grad, second_all, cot_all = held
 
@@ -1034,29 +1038,30 @@
         mlp_scale,
     )
     grad_blocks = [grad_blocks[0]] + [shift(grad_blocks[RING - r], "z", r) for r in range(1, RING)]
-    grad_blocks, own_low, inner = together(grad_blocks, own_low, inner)
     down_keep, down_give = pair_grad(core_at, [cot_all], inner)
+    grad_blocks, down_keep, down_give, own_low, inner = together(
+        grad_blocks, down_keep, down_give, own_low, inner
+    )
     head_grads = to_heads(jnp.concatenate(grad_blocks, axis=0))
     low_left = shift(own_low, "z", 1)
     low_right = shift(own_low, "z", 3)
     down_sum = pair_sum(down_keep, shift(down_give, "core", 1, 2))
-    mlp_own, mlp_opposite, mlp_left, mlp_right = mlp_out_part(
-        after(inner, down_give), mlp_weights
-    )
+    mlp_own, mlp_opposite, mlp_left, mlp_right = mlp_out_part(inner, mlp_weights)
     head_grads, down_sum, low_left, low_right, own_low, mlp_opposite, mlp_left, mlp_right = together(
         head_grads, down_sum, low_left, low_right, own_low, mlp_opposite, mlp_left, mlp_right
     )
+    low_opposite = shift(own_low, "z", 2)
+    down_terms = to_owners(down_sum)
+
+    query_grad, grad_keep, grad_give = attention_backward(
+        order, core_at, arrived, other_pair, head_grads, head_mixed_t, head_logs
+    )
+    query_grad, grad_keep, grad_give, low_opposite, mlp_opposite, mlp_left, mlp_right = together(
+        query_grad, grad_keep, grad_give, low_opposite, mlp_opposite, mlp_left, mlp_right
+    )
     mlp_left = send_back(mlp_left, 1)
     mlp_right = send_back(mlp_right, 3)
-    down_terms = to_owners(down_sum)
-
-    query_grad, grad_keep, grad_give = attention_backward(
-        order, core_at, arrived, other_pair, head_grads, head_mixed_t, head_logs
-    )
-    query_grad, grad_keep, grad_give, mlp_left, mlp_right, own_low, mlp_opposite = together(
-        query_grad, grad_keep, grad_give, mlp_left, mlp_right, own_low, mlp_opposite
-    )
-    low_opposite = shift(own_low, "z", 2)
+    mlp_opposite = send_back(mlp_opposite, 2)
     grads_send = lax.dynamic_update_slice_in_dim(
         query_grad, pair_sum(grad_keep, shift(grad_give, "core", 1, 2))[:, None], 1, 1
     )
@@ -1066,18 +1071,21 @@
     out_term = pair_grad(
         core_at, [own_low, low_left, low_opposite, low_right], mixed_arrived, by_heads=True
     )
-    mlp_opposite = send_back(mlp_opposite, 2)
-    returned, both_share, out_term = together(returned, both_share, out_term)
+    returned, both_share, out_term, down_pair, mlp_left, mlp_right, mlp_opposite = together(
+        returned, both_share, out_term, down_pair, mlp_left, mlp_right, mlp_opposite
+    )
     out_share = lax.psum_scatter(out_term, GROUP_AXES, scatter_dimension=0, tiled=True)
     both_pair = over_x(both_share)
+    down_blocks = over_z(down_pair)
     qkv_grad, qkv_keep, qkv_give, query_gain_part, key_gain_part = first_back(
         core_at, returned, qkv_pre, cosine, sine, query_row, key_row, first_in
     )
-    qkv_grad, qkv_give, down_pair, both_pair = together(qkv_grad, qkv_give, down_pair, both_pair)
+    qkv_grad, qkv_give, down_blocks, both_pair = together(
+        qkv_grad, qkv_give, down_blocks, both_pair
+    )
     both_sum = pair_sum(*both_pair)
     both_left = shift(both_sum, "z", 1)
     both_right = shift(both_sum, "z", 3)
-    down_blocks = over_z(down_pair)
     qkv_come = shift(qkv_give, "core", 1, 2)
     *first_parts, gains_keep, gains_give = last_part(
         core_at,
@@ -1088,8 +1096,8 @@
         query_gain_part,
         key_gain_part,
     )
-    first_parts, gains_give, qkv_come, mlp_opposite, both_left, both_right, both_sum = together(
-        first_parts, gains_give, qkv_come, mlp_opposite, both_left, both_right, both_sum
+    first_parts, gains_give, qkv_come, both_left, both_right, both_sum = together(
+        first_parts, gains_give, qkv_come, both_left, both_right, both_sum
     )
     gains_come = shift(gains_give, "core", 1, 2)
     first_own, left_a, left_b, first_top, first_bottom, right_a, right_b = first_parts
@@ -1099,11 +1107,13 @@
     first_left = send_back(jnp.concatenate([pair_sum(left_a, first_top), left_b], axis=0), 1)
     first_right = send_back(jnp.concatenate([right_a, pair_sum(right_b, first_bottom)], axis=0), 3)
     both_opposite = shift(both_sum, "z", 2)
-    qkv_terms, down_blocks, both_opposite = together(qkv_terms, down_blocks, both_opposite)
-    out_pair = over_x(out_share)
+    qkv_terms, first_left, first_right, both_opposite = together(
+        qkv_terms, first_left, first_right, both_opposite
+    )
     qkv_share = add_up(qkv_terms)
     both_blocks = [both_sum, both_left, both_opposite, both_right]
-    qkv_pair = over_x(qkv_share)
+    qkv_pair, out_share = together(over_x(qkv_share), out_share)
+    out_pair = over_x(out_share)
     output = (
         middle
         + mlp_own.astype(f32)

time: 746 us -> 709 us (0.950)
  waiting for transfers between devices: 272 us -> 226 us
    ppermute x62 -> x63, waiting for transfers between devices: 245 us -> 201 us  [shift(): lax.ppermute(values, axis, [(i, (i + by) % size) for i in range(size)])]
    all_to_all x4, waiting for transfers between devices: 19.8 us -> 8.07 us  [to_heads(): return lax.all_to_all(send, GROUP_AXES, 0, 0, tiled=True)]
    reduce_scatter x1, waiting for transfers between devices: 0.01 us -> 7.62 us  [local(): lax.psum_scatter(out_term, GROUP_AXES, scatter_dimension=0, tiled=True)]
    ppermute x62 -> x63, starting transfers between devices: 90.3 us -> 90 us  [shift(): lax.ppermute(values, axis, [(i, (i + by) % size) for i in range(size)])]
  transfers between devices with their start and end apart: 72 -> 73, of which waited for: 31 -> 30; matrix products, arithmetic and copies ran while one was open for 9% -> 11% of each run, Pallas kernels for 30% -> 32%
where the time goes in v6:
time: 709 us; the launch traced here: 697 us
  Pallas kernels  227 us (32%)
  waiting for transfers between devices  226 us (32%)
  starting transfers between devices  138 us (19%)
  other arithmetic  42.7 us (6%)
  local copies, waits for them, and re-layouts  28.7 us (4%)
  matrix products  19.3 us (3%)
  between operations  15 us (2%)
    ppermute x63, waiting for transfers between devices, shift(): lax.ppermute(values, axis, [(i, (i + by) % size) for i in range(size)])  201 us
    ppermute x63, starting transfers between devices, shift(): lax.ppermute(values, axis, [(i, (i + by) % size) for i in range(size)])  90 us
    pallas_call x3, Pallas kernels, mlp_blocks(): pl.pallas_call(functools.partial(mlp_kernel, len(seconds), len(cots)), gr...  58 us
    pallas_call x1, Pallas kernels, attention_backward(): pl.pallas_call(backward_kernel, out_shape=(jax.ShapeDtypeStruct((BLOCKS,...  35.4 us
    all_to_all x4, starting transfers between devices, to_heads(): return lax.all_to_all(send, GROUP_AXES, 0, 0, tiled=True)  31.2 us
    pallas_call x1, Pallas kernels, attention_forward(): pl.pallas_call(forward_kernel, out_shape=(jax.ShapeDtypeStruct((BLOCKS, B...  21.5 us
    pallas_call x2, Pallas kernels, pair_grad(): pl.pallas_call(kernel, grid=(width // 256,), in_specs=[pl.BlockSpec(memor...  21.4 us
    dot_general x1, matrix products, local(): lax.dot_general(second_all.reshape(ring_rows, width), both_grad.reshape(r...  19.3 us
  transfers between devices with their start and end apart: 73, of which 30 were waited for; matrix products, arithmetic and copies ran while one was open for 11% of the time, Pallas kernels for 32%

profile of v6, /device:TPU:4, one launch (start us, length us, event | category | flops | bytes accessed | tf_op | source)
XLA Modules:
  0.0 697.4 jit_solution(15328216736005211989)
XLA Ops:
  78.5 12.0 %shard_map.246 = (bf16[4,256,2048]{2,1,0:T(8,128)(2,1)}, bf16[4,256,2048]{2,1,0:T(8,128)(2,1)}, f32[4,256,1024]{2,1,0:T(8,128)}, bf16[16,2,256,128]{3,2,1,0:T(8,128)(2,1)}, f32[8,2048]{1,0:T(8,128)}) custom-call(bf16[256,2048]{1,0:T(8,128)(2,1)} %refs_8_.1, bf16[256,2048]{1,0:T(8,128)(2,1)} %copy-done.40, bf16[128,2048]{1,0:T(8,128)(2,1)} %collective-permute-done.9.top_ref, ...), custom_call_target="tpu_custom_call" | custom-call | flops 4294967296 | bytes 20971520 | tf_op jit(solution)/shard_map/pallas_call | solution.py:575
  98.1 22.3 %collective-permute-done.12.refs_5_ = bf16[2048,512]{1,0:T(8,128)(2,1)S(1)} collective-permute-done((bf16[2048,512]{1,0:T(8,128)(2,1)}, bf16[2048,512]{1,0:T(8,128)(2,1)S(1)}, u32[]{:S(2)}, u32[]{:S(2)}) %collective-permute-start.12) | collective-permute-done | bytes 2097184 | tf_op jit(solution)/shard_map/ppermute | solution.py:41
  125.1 20.2 %collective-permute-done.14 = bf16[1024,512]{1,0:T(8,128)(2,1)S(1)} collective-permute-done((bf16[1024,512]{1,0:T(8,128)(2,1)S(1)}, bf16[1024,512]{1,0:T(8,128)(2,1)S(1)}, u32[]{:S(2)}, u32[]{:S(2)}) %collective-permute-start.14) | collective-permute-done | bytes 1048608 | tf_op jit(solution)/shard_map/ppermute | solution.py:41
  151.6 21.5 %shard_map.248 = (bf16[16,256,128]{2,1,0:T(8,128)(2,1)}, f32[8,128,512]{2,1,0:T(8,128)}, f32[8,1,512]{2,1,0:T(1,128)}) custom-call(s32[16]{0:T(128)} %dynamic-slice_bitcast_fusion.order, s32[1]{0:T(128)} %bitcast.1.core.core_ref, bf16[16,2,256,128]{3,2,1,0:T(8,128)(2,1)} %all-to-all-done.own_a.own_b, bf16[16,2,256,128]{3,2,1,0:T(8,128)(2,1)} %all-to-all-done.own_a.own_b, ...), custom_call_target="tpu_custom_call" | custom-call | flops 1024 | bytes 1024 | tf_op jit(solution)/shard_map/pallas_call | solution.py:117
  184.3 15.9 %collective-permute-done.17.refs_2_ = bf16[256,2048]{1,0:T(8,128)(2,1)S(1)} collective-permute-done((bf16[256,2048]{1,0:T(8,128)(2,1)S(1)}, bf16[256,2048]{1,0:T(8,128)(2,1)S(1)}, u32[]{:S(2)}, u32[]{:S(2)}) %collective-permute-start.17) | collective-permute-done | bytes 1048608 | tf_op jit(solution)/shard_map/ppermute | solution.py:41
  207.4 8.8 %collective-permute-done.19.refs_1_ = bf16[128,2048]{1,0:T(8,128)(2,1)} collective-permute-done((bf16[128,2048]{1,0:T(8,128)(2,1)}, bf16[128,2048]{1,0:T(8,128)(2,1)}, u32[]{:S(2)}, u32[]{:S(2)}) %collective-permute-start.19) | collective-permute-done | bytes 524320 | tf_op jit(solution)/shard_map/ppermute | solution.py:41
  243.5 15.7 %shard_map.250 = (bf16[4,256,1536]{2,1,0:T(8,128)(2,1)}, bf16[4,256,3072]{2,1,0:T(8,128)(2,1)}, bf16[4,256,2048]{2,1,0:T(8,128)(2,1)}, bf16[4,256,2048]{2,1,0:T(8,128)(2,1)}, bf16[256,2048]{1,0:T(8,128)(2,1)}) custom-call(bf16[256,2048]{1,0:T(8,128)(2,1)} %get-tuple-element.234.refs_0_, bf16[256,2048]{1,0:T(8,128)(2,1)} %refs_9_.1, ...), custom_call_target="tpu_custom_call" | custom-call | flops 8053063680 | bytes 18874368 | tf_op jit(solution)/shard_map/pallas_call | solution.py:318
  269.0 26.7 %shard_map.251 = (bf16[4,256,1536]{2,1,0:T(8,128)(2,1)}, bf16[4,256,3072]{2,1,0:T(8,128)(2,1)}, bf16[4,256,2048]{2,1,0:T(8,128)(2,1)}, bf16[4,256,2048]{2,1,0:T(...) custom-call(bf16[256,2048]{1,0:T(8,128)(2,1)} %copy-done.24, ...), custom_call_target="tpu_custom_call", output_to_operand_aliasing={{0}: (6, {}), {1}: (7, {}), {2}: (8, {}), {3}: (9, {})} | custom-call | flops 16106127360 | bytes 18874368 | tf_op jit(solution)/shard_map/pallas_call | solution.py:318
  298.8 15.6 %shard_map.252 = (bf16[4,256,1536]{2,1,0:T(8,128)(2,1)}, bf16[4,256,3072]{2,1,0:T(8,128)(2,1)}, bf16[4,256,2048]{2,1,0:T(8,128)(2,1)}, bf16[4,256,2048]{2,1,0:T(8,128)(2,1)}, bf16[256,2048]{1,0:T(8,128)(2,1)}) custom-call(bf16[256,2048]{1,0:T(8,128)(2,1)} %copy-done.23, ...), custom_call_target="tpu_custom_call", output_to_operand_aliasing={{0}: (5, {}), {1}: (6, {}), {2}: (7, {}), {3}: (8, {})} | custom-call | flops 8053063680 | bytes 18874368 | tf_op jit(solution)/shard_map/pallas_call | solution.py:318
  315.7 19.3 %bitcast_convert_fusion = bf16[2048,3072]{1,0:T(8,128)(2,1)} fusion(bf16[4,256,2048]{2,1,0:T(8,128)(2,1)} %get-tuple-element.243, bf16[4,256,3072]{2,1,0:T(8,128)(2,1)} %get-tuple-element.244), kind=kOutput, calls=%fused_computation | convolution fusion | flops 12891193344 | bytes 23068672 | tf_op jit(solution)/shard_map/dot_general | solution.py:1022
  335.1 9.2 %collective-permute-done.27.refs_2_ = bf16[256,2048]{1,0:T(8,128)(2,1)} collective-permute-done((bf16[256,2048]{1,0:T(8,128)(2,1)}, bf16[256,2048]{1,0:T(8,128)(2,1)}, u32[]{:S(2)}, u32[]{:S(2)}) %collective-permute-start.27) | collective-permute-done | bytes 1048608 | tf_op jit(solution)/shard_map/ppermute | solution.py:41
  344.3 12.5 %shard_map.253 = (f32[256,2048]{1,0:T(8,128)}, bf16[256,2048]{1,0:T(8,128)(2,1)}, f32[1,2048]{1,0:T(1,128)}, bf16[4,256,128]{2,1,0:T(8,128)(2,1)}, bf16[4,256,12...) custom-call(bf16[256,2048]{1,0:T(8,128)(2,1)} %get-tuple-element.219.refs_0_, ...), custom_call_target="tpu_custom_call" | custom-call | flops 1024 | bytes 1024 | tf_op jit(solution)/shard_map/pallas_call | solution.py:509
  360.1 12.9 %shard_map.254 = (bf16[8,128,1536]{2,1,0:T(8,128)(2,1)}, bf16[8,128,1536]{2,1,0:T(8,128)(2,1)}) custom-call(s32[1]{0:T(128)} %bitcast.1.core.core_ref, bf16[4,256,2048]{2,1,0:T(8,128)(2,1)} %get-tuple-element.253.refs_0_, bf16[4,256,1536]{2,1,0:T(8,128)(2,1)} %get-tuple-element.258.refs_1_.inner_ref), custom_call_target="tpu_custom_call" | custom-call | flops 1024 | bytes 1024 | tf_op jit(solution)/shard_map/pallas_call | solution.py:414
  385.6 10.6 %shard_map.255 = (bf16[256,2048]{1,0:T(8,128)(2,1)}, bf16[256,2048]{1,0:T(8,128)(2,1)}, bf16[256,2048]{1,0:T(8,128)(2,1)}, bf16[256,2048]{1,0:T(8,128)(2,1)}) custom-call(bf16[4,256,1536]{2,1,0:T(8,128)(2,1)} %get-tuple-element.258.refs_1_.inner_ref, bf16[2048,4608]{1,0:T(8,128)(2,1)} %all-gather.5.cloned.1.call-done.refs_2_.refs_3_.refs_4_.refs_5_.weight_ref), custom_call_target="tpu_custom_call" | custom-call | flops 1024 | bytes 1024 | tf_op jit(solution)/shard_map/pallas_call | solution.py:360
  410.7 9.9 %all-to-all-start.3 = ((bf16[8,128,1536]{2,1,0:T(8,128)(2,1)}), bf16[8,128,1536]{2,1,0:T(8,128)(2,1)}, u32[]{:S(2)}, u32[]{:S(2)}) async-start(bf16[8,128,1536]{2,1,0:T(8,128)(2,1)} %add_convert_fusion), calls=%async_computation.3 | async-start | bytes 6291456 | tf_op jit(solution)/shard_map/all_to_all | solution.py:1010
  421.6 35.4 %shard_map.256 = (bf16[16,2,256,128]{3,2,1,0:T(8,128)(2,1)}, bf16[16,256,128]{2,1,0:T(8,128)(2,1)}, bf16[16,256,128]{2,1,0:T(8,128)(2,1)}) custom-call(s32[16]{0:T(128)} %dynamic-slice_bitcast_fusion.order, s32[1]{0:T(128)} %bitcast.1.core.core_ref, bf16[16,2,256,128]{3,2,1,0:T(8,128)(2,1)} %all-to-all-done.own_a.own_b, ...), custom_call_target="tpu_custom_call" | custom-call | flops 1024 | bytes 1024 | tf_op jit(solution)/shard_map/pallas_call | solution.py:224
  462.5 9.4 %all-to-all-done.3 = bf16[8,128,1536]{2,1,0:T(8,128)(2,1)} async-done(((bf16[8,128,1536]{2,1,0:T(8,128)(2,1)}), bf16[8,128,1536]{2,1,0:T(8,128)(2,1)}, u32[]{:S(2)}, u32[]{:S(2)}) %all-to-all-start.3) | async-done | bytes 3145760 | tf_op jit(solution)/shard_map/all_to_all | solution.py:1010
  471.9 8.2 %all-to-all-start.4 = ((bf16[16,2,256,128]{3,2,1,0:T(8,128)(2,1)}), bf16[16,2,256,128]{3,2,1,0:T(8,128)(2,1)S(1)}, u32[]{:S(2)}, u32[]{:S(2)}) async-start(bf16[16,2,256,128]{3,2,1,0:T(8,128)(2,1)} %fusion.9), calls=%async_computation.4 | async-start | bytes 4194304 | tf_op jit(solution)/shard_map/all_to_all | solution.py:816
  488.2 8.5 %shard_map.257 = bf16[2048,512]{1,0:T(8,128)(2,1)} custom-call(s32[1]{0:T(128)} %bitcast.1.core.core_ref, bf16[256,2048]{1,0:T(8,128)(2,1)} %get-tuple-element.276.refs_0_, bf16[256,2048]{1,0:T(8,128)(2,1)} %collective-permute-done.34.refs_1_, bf16[256,2048]{1,0:T(8,128)(2,1)} %copy-done.31, bf16[256,2048]{1,0:T(8,128)(2,1)} %collective-permute-done.35.refs_3_, ...), custom_call_target="tpu_custom_call" | custom-call | flops 1024 | bytes 1024 | tf_op jit(solution)/shard_map/pallas_call | solution.py:414
  496.7 9.9 %collective-permute-done.39 = bf16[256,2048]{1,0:T(8,128)(2,1)} collective-permute-done((bf16[256,2048]{1,0:T(8,128)(2,1)}, bf16[256,2048]{1,0:T(8,128)(2,1)}, u32[]{:S(2)}, u32[]{:S(2)}) %collective-permute-start.39) | collective-permute-done | bytes 1048608 | tf_op jit(solution)/shard_map/ppermute | solution.py:41
  508.2 21.4 %collective-permute-done.41 = bf16[256,2048]{1,0:T(8,128)(2,1)} collective-permute-done((bf16[256,2048]{1,0:T(8,128)(2,1)}, bf16[256,2048]{1,0:T(8,128)(2,1)}, u32[]{:S(2)}, u32[]{:S(2)}) %collective-permute-start.41) | collective-permute-done | bytes 1048608 | tf_op jit(solution)/shard_map/ppermute | solution.py:41
  537.8 15.0 %shard_map.258 = (bf16[4,256,1024]{2,1,0:T(8,128)(2,1)}, bf16[8,128,1024]{2,1,0:T(8,128)(2,1)}, bf16[8,128,1024]{2,1,0:T(8,128)(2,1)}, f32[1,128]{1,0:T(1,128)}, f32[1,128]{1,0:T(1,128)}) custom-call(s32[1]{0:T(128)} %bitcast.1.core.core_ref, bf16[16,2,256,128]{3,2,1,0:T(8,128)(2,1)} %copy-done.13, f32[4,256,1024]{2,1,0:T(8,128)} %get-tuple-element.298.pre_ref, ...), custom_call_target="tpu_custom_call" | custom-call | flops 1024 | bytes 1024 | tf_op jit(solution)/shard_map/pallas_call | solution.py:662
  558.6 12.6 %shard_map.259 = (bf16[256,2048]{1,0:T(8,128)(2,1)}, bf16[128,2048]{1,0:T(8,128)(2,1)}, bf16[128,2048]{1,0:T(8,128)(2,1)}, bf16[128,2048]{1,0:T(8,128)(2,1)}, bf...) custom-call(s32[1]{0:T(128)} %bitcast.1.core.core_ref, ...), custom_call_target="tpu_custom_call" | custom-call | flops 1024 | bytes 1024 | tf_op jit(solution)/shard_map/pallas_call | solution.py:747
  612.6 28.7 %collective-permute-done.54.refs_2_ = bf16[128,3072]{1,0:T(8,128)(2,1)} collective-permute-done((bf16[128,3072]{1,0:T(8,128)(2,1)}, bf16[128,3072]{1,0:T(8,128)(2,1)}, u32[]{:S(2)}, u32[]{:S(2)}) %collective-permute-start.54) | collective-permute-done | bytes 786464 | tf_op jit(solution)/shard_map/ppermute | solution.py:41
  (314 shorter events, 300.2 us)
Async XLA Ops:
  7.2 71.3 %all-gather.3.cloned.1.call-start = ((), (), s32[]{:S(2)}) async-start(), calls=%async_computation.8 | async-start | bytes 5013504 | tf_op jit(solution)/shard_map/all_gather | solution.py:902
  10.9 232.6 %all-gather.5.cloned.1.call-start = ((), (), s32[]{:S(2)}) async-start(), calls=%async_computation.9 | async-start | bytes 20054016 | tf_op jit(solution)/shard_map/all_gather | solution.py:902
  72.0 48.3 %collective-permute-start.12 = (bf16[2048,512]{1,0:T(8,128)(2,1)}, bf16[2048,512]{1,0:T(8,128)(2,1)S(1)}, u32[]{:S(2)}, u32[]{:S(2)}) collective-permute-start(bf16[2048,512]{1,0:T(8,128)(2,1)} %shard_map.247.refs_4_), channel_id=1, source_target_pairs={{0,16},{16,32},{32,48},{48,0},{1,17},{17,33},{33,49},{49,1},{2,18}... | collective-permute-start | bytes 6291464 | tf_op jit(solution)/shard_map/ppermute | solution.py:41
  72.0 48.5 %collective-permute-start.13 = (bf16[2048,512]{1,0:T(8,128)(2,1)}, bf16[2048,512]{1,0:T(8,128)(2,1)}, u32[]{:S(2)}, u32[]{:S(2)}) collective-permute-start(bf16[2048,512]{1,0:T(8,128)(2,1)} %shard_map.247.refs_4_), channel_id=1, source_target_pairs={{0,48},{16,0},{32,16},{48,32},{1,49},{17,1},{33,17},{49,33},{2,50}... | collective-permute-start | bytes 6291464 | tf_op jit(solution)/shard_map/ppermute | solution.py:41
  90.5 55.8 %all-to-all-start = ((bf16[16,2,256,128]{3,2,1,0:T(8,128)(2,1)}), bf16[16,2,256,128]{3,2,1,0:T(8,128)(2,1)}, u32[]{:S(2)}, u32[]{:S(2)}) async-start(bf16[16,2,256,128]{3,2,1,0:T(8,128)(2,1)} %get-tuple-element.186), calls=%async_computation | async-start | bytes 4194304 | tf_op jit(solution)/shard_map/all_to_all | solution.py:816
  176.6 30.7 %all-to-all-start.1 = ((bf16[16,256,128]{2,1,0:T(8,128)(2,1)}), bf16[16,256,128]{2,1,0:T(8,128)(2,1)S(1)}, u32[]{:S(2)}, u32[]{:S(2)}) async-start(bf16[16,256,128]{2,1,0:T(8,128)(2,1)} %get-tuple-element.193), calls=%async_computation.1 | async-start | bytes 2097152 | tf_op jit(solution)/shard_map/all_to_all | solution.py:816
  184.2 345.4 %reduce-scatter.3.cloned.1.call-start = ((), (), s32[]{:S(2)}) async-start(), calls=%async_computation.10 | async-start | bytes 13369344 | tf_op jit(solution)/shard_map/reduce_scatter | solution.py:1031
  265.8 32.0 %collective-permute-start.28 = (bf16[256,2048]{1,0:T(8,128)(2,1)}, bf16[256,2048]{1,0:T(8,128)(2,1)S(1)}, u32[]{:S(2)}, u32[]{:S(2)}) collective-permute-start(bf16[256,2048]{1,0:T(8,128)(2,1)} %get-tuple-element.234.refs_0_), channel_id=1, source_target_pairs={{0,32},{16,48},{32,0},{48,16},{1,33},{17,49},{33,1},{49,17},{2,34}... | collective-permute-start | bytes 3145736 | tf_op jit(solution)/shard_map/ppermute | solution.py:41
  295.7 39.4 %collective-permute-start.26 = (bf16[256,2048]{1,0:T(8,128)(2,1)}, bf16[256,2048]{1,0:T(8,128)(2,1)S(1)}, u32[]{:S(2)}, u32[]{:S(2)}) collective-permute-start(bf16[256,2048]{1,0:T(8,128)(2,1)} %get-tuple-element.228), channel_id=1, source_target_pairs={{0,48},{16,0},{32,16},{48,32},{1,49},{17,1},{33,17},{49,33},{2,50}... | collective-permute-start | bytes 3145736 | tf_op jit(solution)/shard_map/ppermute | solution.py:41
  296.7 47.6 %collective-permute-start.27 = (bf16[256,2048]{1,0:T(8,128)(2,1)}, bf16[256,2048]{1,0:T(8,128)(2,1)}, u32[]{:S(2)}, u32[]{:S(2)}) collective-permute-start(bf16[256,2048]{1,0:T(8,128)(2,1)} %get-tuple-element.229), channel_id=1, source_target_pairs={{0,16},{16,32},{32,48},{48,0},{1,17},{17,33},{33,49},{49,1},{2,18}... | collective-permute-start | bytes 3145736 | tf_op jit(solution)/shard_map/ppermute | solution.py:41
  314.4 29.9 %collective-permute-start.29 = (bf16[256,2048]{1,0:T(8,128)(2,1)}, bf16[256,2048]{1,0:T(8,128)(2,1)}, u32[]{:S(2)}, u32[]{:S(2)}) collective-permute-start(bf16[256,2048]{1,0:T(8,128)(2,1)} %get-tuple-element.242), channel_id=1, source_target_pairs={{0,32},{16,48},{32,0},{48,16},{1,33},{17,49},{33,1},{49,17},{2,34}... | collective-permute-start | bytes 3145736 | tf_op jit(solution)/shard_map/ppermute | solution.py:41
  373.2 36.5 %collective-permute-start.34 = (bf16[256,2048]{1,0:T(8,128)(2,1)S(1)}, bf16[256,2048]{1,0:T(8,128)(2,1)}, u32[]{:S(2)}, u32[]{:S(2)}) collective-permute-start(bf16[256,2048]{1,0:T(8,128)(2,1)S(1)} %copy-done.30), channel_id=1, source_target_pairs={{0,16},{16,32},{32,48},{48,0},{1,17},{17,33},{33,49},{49,1},{2,18}... | collective-permute-start | bytes 3145736 | tf_op jit(solution)/shard_map/ppermute | solution.py:41
  374.1 35.6 %collective-permute-start.35 = (bf16[256,2048]{1,0:T(8,128)(2,1)S(1)}, bf16[256,2048]{1,0:T(8,128)(2,1)}, u32[]{:S(2)}, u32[]{:S(2)}) collective-permute-start(bf16[256,2048]{1,0:T(8,128)(2,1)S(1)} %copy-done.30), channel_id=1, source_target_pairs={{0,48},{16,0},{32,16},{48,32},{1,49},{17,1},{33,17},{49,33},{2,50}... | collective-permute-start | bytes 3145736 | tf_op jit(solution)/shard_map/ppermute | solution.py:41
  377.8 31.9 %all-to-all-start.2 = ((bf16[16,256,128]{2,1,0:T(8,128)(2,1)}), bf16[16,256,128]{2,1,0:T(8,128)(2,1)S(1)}, u32[]{:S(2)}, u32[]{:S(2)}) async-start(bf16[16,256,128]{2,1,0:T(8,128)(2,1)} %pad_maximum_fusion.2), calls=%async_computation.2 | async-start | bytes 2097152 | tf_op jit(solution)/shard_map/all_to_all | solution.py:816
  410.7 61.3 %all-to-all-start.3 = ((bf16[8,128,1536]{2,1,0:T(8,128)(2,1)}), bf16[8,128,1536]{2,1,0:T(8,128)(2,1)}, u32[]{:S(2)}, u32[]{:S(2)}) async-start(bf16[8,128,1536]{2,1,0:T(8,128)(2,1)} %add_convert_fusion), calls=%async_computation.3 | async-start | bytes 6291456 | tf_op jit(solution)/shard_map/all_to_all | solution.py:1010
  420.5 36.5 %collective-permute-start.36 = (bf16[256,2048]{1,0:T(8,128)(2,1)S(1)}, bf16[256,2048]{1,0:T(8,128)(2,1)S(1)}, u32[]{:S(2)}, u32[]{:S(2)}) collective-permute-start(bf16[256,2048]{1,0:T(8,128)(2,1)S(1)} %copy-done.30), channel_id=1, source_target_pairs={{0,32},{16,48},{32,0},{48,16},{1,33},{17,49},{33,1},{49,17},{2,34}... | collective-permute-start | bytes 3145736 | tf_op jit(solution)/shard_map/ppermute | solution.py:41
  471.9 57.7 %all-to-all-start.4 = ((bf16[16,2,256,128]{3,2,1,0:T(8,128)(2,1)}), bf16[16,2,256,128]{3,2,1,0:T(8,128)(2,1)S(1)}, u32[]{:S(2)}, u32[]{:S(2)}) async-start(bf16[16,2,256,128]{3,2,1,0:T(8,128)(2,1)} %fusion.9), calls=%async_computation.4 | async-start | bytes 4194304 | tf_op jit(solution)/shard_map/all_to_all | solution.py:816
  480.2 174.7 %reduce-scatter.5.cloned.1.call-start = ((), (), s32[]{:S(2)}) async-start(), calls=%async_computation.11 | async-start | bytes 2228224 | tf_op jit(solution)/shard_map/reduce_scatter | solution.py:1077
  482.3 47.3 %collective-permute-start.41 = (bf16[256,2048]{1,0:T(8,128)(2,1)}, bf16[256,2048]{1,0:T(8,128)(2,1)}, u32[]{:S(2)}, u32[]{:S(2)}) collective-permute-start(bf16[256,2048]{1,0:T(8,128)(2,1)} %get-tuple-element.292), channel_id=1, source_target_pairs={{0,32},{16,48},{32,0},{48,16},{1,33},{17,49},{33,1},{49,17},{2,34}... | collective-permute-start | bytes 3145736 | tf_op jit(solution)/shard_map/ppermute | solution.py:41
  486.4 43.2 %collective-permute-start.38 = (bf16[128,1536]{1,0:T(8,128)(2,1)S(1)}, bf16[128,1536]{1,0:T(8,128)(2,1)}, u32[]{:S(2)}, u32[]{:S(2)}) collective-permute-start(bf16[128,1536]{1,0:T(8,128)(2,1)S(1)} %reduce_sum.52), channel_id=1, source_target_pairs={{0,64},{64,0},{1,65},{65,1},{2,66},{66,2},{3,67},{67,3},{4,68},{68... | collective-permute-start | bytes 1179656 | tf_op jit(solution)/shard_map/ppermute | solution.py:41
  587.3 55.5 %all-to-all-start.5 = ((bf16[8,128,1152]{2,1,0:T(8,128)(2,1)}), bf16[8,128,1152]{2,1,0:T(8,128)(2,1)S(1)}, u32[]{:S(2)}, u32[]{:S(2)}) async-start(bf16[8,128,1152]{2,1,0:T(8,128)(2,1)} %shard_map.260), calls=%async_computation.6 | async-start | bytes 4718592 | tf_op jit(solution)/shard_map/all_to_all | solution.py:1010
  598.3 43.0 %collective-permute-start.53 = (bf16[256,2048]{1,0:T(8,128)(2,1)}, bf16[256,2048]{1,0:T(8,128)(2,1)}, u32[]{:S(2)}, u32[]{:S(2)}) collective-permute-start(bf16[256,2048]{1,0:T(8,128)(2,1)} %pad_maximum_fusion.4), channel_id=1, source_target_pairs={{0,16},{16,32},{32,48},{48,0},{1,17},{17,33},{33,49},{49,1},{2,18}... | collective-permute-start | bytes 3145736 | tf_op jit(solution)/shard_map/ppermute | solution.py:41
  601.5 41.3 %collective-permute-start.51 = (bf16[256,2048]{1,0:T(8,128)(2,1)}, bf16[256,2048]{1,0:T(8,128)(2,1)}, u32[]{:S(2)}, u32[]{:S(2)}) collective-permute-start(bf16[256,2048]{1,0:T(8,128)(2,1)} %pad_maximum_fusion.3), channel_id=1, source_target_pairs={{0,48},{16,0},{32,16},{48,32},{1,49},{17,1},{33,17},{49,33},{2,50}... | collective-permute-start | bytes 3145736 | tf_op jit(solution)/shard_map/ppermute | solution.py:41
  604.1 37.2 %collective-permute-start.54 = (bf16[128,3072]{1,0:T(8,128)(2,1)}, bf16[128,3072]{1,0:T(8,128)(2,1)}, u32[]{:S(2)}, u32[]{:S(2)}) collective-permute-start(bf16[128,3072]{1,0:T(8,128)(2,1)} %add_convert_fusion.3.refs_0_), channel_id=1, source_target_pairs={{0,32},{16,48},{32,0},{48,16},{1,33},{17,49},{33,1},{49,17},{2,34}... | collective-permute-start | bytes 2359304 | tf_op jit(solution)/shard_map/ppermute | solution.py:41
  (101 other events, 1223.5 us)
Sparse Core Ops, SparseCore 0:
  11.1 62.2 all-gather.2
  75.8 142.9 all-gather.4
  344.4 175.2 reduce-scatter.2
  577.7 77.0 reduce-scatter.4

commit v7 on v6

--- a/solution.py
+++ b/solution.py
@@ -378,8 +378,7 @@
 
     def kernel(core_ref, *refs):
         left_refs = refs[: len(lefts)]
-        right_ref, keep_ref = refs[len(lefts) : len(lefts) + 2]
-        give_ref = refs[-1]
+        right_ref, keep_ref, give_ref = refs[len(lefts) : len(lefts) + 3]
         if by_heads:
             all_ref = refs[-1]
 
@@ -399,9 +398,6 @@
         term = lax.dot_general(
             inputs, values, contract_first, preferred_element_type=jnp.float32
         ).astype(low)
-        if by_heads:
-            keep_ref[...] = term
-            return
         first_core = core_ref[0] == 0
         keep_ref[0] = jnp.where(first_core, term[:128], term[128:])
         give_ref[0] = jnp.where(first_core, term[128:], term[:128])
@@ -417,10 +413,8 @@
         in_specs=[pl.BlockSpec(memory_space=pltpu.SMEM)]
         + [columns(value) for value in lefts]
         + [pl.BlockSpec(right.shape, lambda i: (0, 0, 0))],
-        out_specs=pl.BlockSpec((256, outs), lambda i: (i, 0)) if by_heads else (half, half),
-        out_shape=jax.ShapeDtypeStruct((width, outs), low)
-        if by_heads
-        else (jax.ShapeDtypeStruct((width // 256, 128, outs), low),) * 2,
+        out_specs=(half, half),
+        out_shape=(jax.ShapeDtypeStruct((width // 256, 128, outs), low),) * 2,
         scratch_shapes=[pltpu.VMEM((rows, 512), low)] * by_heads,
         compiler_params=pltpu.CompilerParams(vmem_limit_bytes=VMEM_LIMIT),
         cost_estimate=pl.CostEstimate(flops=1024, bytes_accessed=1024, transcendentals=0),
@@ -793,23 +787,24 @@
 def pair_sums_kernel(keep_ref, come_ref, gains_keep, gains_come, out_ref):
     f32 = jnp.float32
     wide = keep_ref.shape[2]
-    out_ref[0, :, :wide] = (keep_ref[0].astype(f32) + come_ref[0].astype(f32)).astype(low)
-    out_ref[0, :, wide:] = (gains_keep[0].astype(f32) + gains_come[0].astype(f32)).astype(low)
-
-
-def pair_sums(keep, come, gains_keep, gains_come):
+    out_ref[:, :, :wide] = (keep_ref[...].astype(f32) + come_ref[...].astype(f32)).astype(low)
+    out_ref[:, :, wide:] = (gains_keep[...].astype(f32) + gains_come[...].astype(f32)).astype(low)
+
+
+def pair_sums(keep, come, more_keep, more_come):
     blocks, rows, wide = keep.shape
-    large = pl.BlockSpec((1, rows, wide), lambda i: (i, 0, 0))
-    small = pl.BlockSpec((1, rows, HEAD_DIM), lambda i: (i, 0, 0))
+    narrow = more_keep.shape[2]
+    large = pl.BlockSpec((4, rows, wide), lambda i: (i, 0, 0))
+    small = pl.BlockSpec((4, rows, narrow), lambda i: (i, 0, 0))
     return pl.pallas_call(
         pair_sums_kernel,
-        grid=(blocks,),
+        grid=(blocks // 4,),
         in_specs=[large, large, small, small],
-        out_specs=pl.BlockSpec((1, rows, wide + HEAD_DIM), lambda i: (i, 0, 0)),
-        out_shape=jax.ShapeDtypeStruct((blocks, rows, wide + HEAD_DIM), low),
+        out_specs=pl.BlockSpec((4, rows, wide + narrow), lambda i: (i, 0, 0)),
+        out_shape=jax.ShapeDtypeStruct((blocks, rows, wide + narrow), low),
         compiler_params=pltpu.CompilerParams(vmem_limit_bytes=VMEM_LIMIT),
         cost_estimate=pl.CostEstimate(flops=1024, bytes_accessed=1024, transcendentals=0),
-    )(keep, come, gains_keep, gains_come)
+    )(keep, come, more_keep, more_come)
 
 
 def to_heads(send):
@@ -962,13 +957,14 @@
     )
     attn_scale = gain_rows[0:1]
     mlp_scale = gain_rows[1:2]
+    arrived, out_left, out_right = together(to_heads(send), out_left, out_right)
+    other_pair = shift(arrived[:, 1], "core", 1, 2)
+    head_mixed, head_mixed_t, head_logs = attention_forward(order, core_at, arrived, other_pair)
     out_top = shift(out_left[: width // 2], "z", 1)
     out_bottom = shift(out_right[width // 2 :], "z", 3)
-    arrived, out_left, out_right, out_top, out_bottom = together(
-        to_heads(send), out_left, out_right, out_top, out_bottom
-    )
-    other_pair = shift(arrived[:, 1], "core", 1, 2)
-    head_mixed, head_mixed_t, head_logs = attention_forward(order, core_at, arrived, other_pair)
+    head_mixed, head_mixed_t, head_logs, out_top, out_bottom = together(
+        head_mixed, head_mixed_t, head_logs, out_top, out_bottom
+    )
     cot_own = after(cotangent, head_mixed)
     cot_left = shift(cot_own, "z", 1)
     cot_right = shift(cot_own, "z", 3)
@@ -1045,43 +1041,42 @@
     head_grads = to_heads(jnp.concatenate(grad_blocks, axis=0))
     low_left = shift(own_low, "z", 1)
     low_right = shift(own_low, "z", 3)
-    down_sum = pair_sum(down_keep, shift(down_give, "core", 1, 2))
     mlp_own, mlp_opposite, mlp_left, mlp_right = mlp_out_part(inner, mlp_weights)
-    head_grads, down_sum, low_left, low_right, own_low, mlp_opposite, mlp_left, mlp_right = together(
-        head_grads, down_sum, low_left, low_right, own_low, mlp_opposite, mlp_left, mlp_right
-    )
-    low_opposite = shift(own_low, "z", 2)
-    down_terms = to_owners(down_sum)
+    head_grads, low_left, low_right, own_low, mlp_opposite, mlp_left, mlp_right = together(
+        head_grads, low_left, low_right, own_low, mlp_opposite, mlp_left, mlp_right
+    )
+    mlp_left = send_back(mlp_left, 1)
+    mlp_right = send_back(mlp_right, 3)
 
     query_grad, grad_keep, grad_give = attention_backward(
         order, core_at, arrived, other_pair, head_grads, head_mixed_t, head_logs
     )
-    query_grad, grad_keep, grad_give, low_opposite, mlp_opposite, mlp_left, mlp_right = together(
-        query_grad, grad_keep, grad_give, low_opposite, mlp_opposite, mlp_left, mlp_right
-    )
-    mlp_left = send_back(mlp_left, 1)
-    mlp_right = send_back(mlp_right, 3)
-    mlp_opposite = send_back(mlp_opposite, 2)
+    query_grad, grad_keep, grad_give, mlp_left, mlp_right, own_low, mlp_opposite, down_give = together(
+        query_grad, grad_keep, grad_give, mlp_left, mlp_right, own_low, mlp_opposite, down_give
+    )
+    low_opposite = shift(own_low, "z", 2)
+    mlp_opposite = send_back(after(mlp_opposite, low_opposite), 2)
     grads_send = lax.dynamic_update_slice_in_dim(
         query_grad, pair_sum(grad_keep, shift(grad_give, "core", 1, 2))[:, None], 1, 1
     )
-    grads_send, down_terms = together(grads_send, down_terms)
     returned = to_heads(grads_send)
-    down_pair = over_x(add_up(down_terms))
-    out_term = pair_grad(
+    out_keep, out_give = pair_grad(
         core_at, [own_low, low_left, low_opposite, low_right], mixed_arrived, by_heads=True
     )
-    returned, both_share, out_term, down_pair, mlp_left, mlp_right, mlp_opposite = together(
-        returned, both_share, out_term, down_pair, mlp_left, mlp_right, mlp_opposite
-    )
-    out_share = lax.psum_scatter(out_term, GROUP_AXES, scatter_dimension=0, tiled=True)
+    down_sum = pair_sums(
+        down_keep,
+        shift(down_give, "core", 1, 2),
+        out_keep,
+        shift(out_give, "core", 1, 2),
+    )
+    returned, both_share, down_sum = together(returned, both_share, down_sum)
     both_pair = over_x(both_share)
-    down_blocks = over_z(down_pair)
+    down_terms = to_owners(down_sum)
     qkv_grad, qkv_keep, qkv_give, query_gain_part, key_gain_part = first_back(
         core_at, returned, qkv_pre, cosine, sine, query_row, key_row, first_in
     )
-    qkv_grad, qkv_give, down_blocks, both_pair = together(
-        qkv_grad, qkv_give, down_blocks, both_pair
+    qkv_grad, qkv_give, both_pair, mlp_opposite = together(
+        qkv_grad, qkv_give, both_pair, mlp_opposite
     )
     both_sum = pair_sum(*both_pair)
     both_left = shift(both_sum, "z", 1)
@@ -1096,9 +1091,10 @@
         query_gain_part,
         key_gain_part,
     )
-    first_parts, gains_give, qkv_come, both_left, both_right, both_sum = together(
-        first_parts, gains_give, qkv_come, both_left, both_right, both_sum
-    )
+    first_parts, gains_give, qkv_come, both_left, both_right, both_sum, down_terms = together(
+        first_parts, gains_give, qkv_come, both_left, both_right, both_sum, down_terms
+    )
+    down_pair = over_x(add_up(down_terms))
     gains_come = shift(gains_give, "core", 1, 2)
     first_own, left_a, left_b, first_top, first_bottom, right_a, right_b = first_parts
     first_top = shift(first_top, "z", 3)
@@ -1107,13 +1103,13 @@
     first_left = send_back(jnp.concatenate([pair_sum(left_a, first_top), left_b], axis=0), 1)
     first_right = send_back(jnp.concatenate([right_a, pair_sum(right_b, first_bottom)], axis=0), 3)
     both_opposite = shift(both_sum, "z", 2)
-    qkv_terms, first_left, first_right, both_opposite = together(
-        qkv_terms, first_left, first_right, both_opposite
-    )
+    qkv_terms, first_left, first_right, both_opposite, down_pair = together(
+        qkv_terms, first_left, first_right, both_opposite, down_pair
+    )
+    down_blocks = over_z(down_pair)
     qkv_share = add_up(qkv_terms)
     both_blocks = [both_sum, both_left, both_opposite, both_right]
-    qkv_pair, out_share = together(over_x(qkv_share), out_share)
-    out_pair = over_x(out_share)
+    qkv_pair = over_x(qkv_share)
     output = (
         middle
         + mlp_own.astype(f32)
@@ -1131,9 +1127,8 @@
         * (scaled_first - own_norm * jnp.mean(scaled_first * own_norm, axis=-1, keepdims=True))
     ).astype(low)
 
-    (down_grad_out,) = place(z_at, down_blocks, (1536,))
+    down_grad_out, out_grad_out = place(z_at, down_blocks, (1536, 512))
     gate_grad_out, up_grad_out = place(z_at, both_blocks, (1536, 1536), chunk=FF_STEP)
-    (out_grad_out,) = place(z_at, over_z(out_pair), (512,))
     query_grad_out, key_grad_out, value_grad_out, gain_sum = place(
         z_at, over_z(qkv_pair), (512, 256, 256), summed=True
     )

time: 709 us -> 702 us (level)
  waiting for transfers between devices: 226 us -> 240 us
  starting transfers between devices: 138 us -> 125 us
    all_to_all x4, waiting for transfers between devices: 8.07 us -> 29.2 us  [to_heads(): return lax.all_to_all(send, GROUP_AXES, 0, 0, tiled=True)]
    all_to_all x2, waiting for transfers between devices: 9.45 us -> 0.01 us  [to_owners(): return lax.all_to_all(pair, ('y', 'x_hi'), 0, 0, tiled=True)]
    ppermute x63 -> x60, waiting for transfers between devices: 201 us -> 210 us  [shift(): lax.ppermute(values, axis, [(i, (i + by) % size) for i in range(size)])]
    reduce_scatter x1 -> x0, waiting for transfers between devices: 7.62 us -> none  [local(): lax.psum_scatter(out_term, GROUP_AXES, scatter_dimension=0, tiled=True)]
    ppermute x63 -> x60, starting transfers between devices: 90 us -> 83.6 us  [shift(): lax.ppermute(values, axis, [(i, (i + by) % size) for i in range(size)])]
  transfers between devices with their start and end apart: 73 -> 69, of which waited for: 30 -> 31; matrix products, arithmetic and copies ran while one was open for 11% -> 10% of each run, Pallas kernels for 32% -> 33%
where the time goes in v7:
time: 702 us; the launch traced here: 691 us
  waiting for transfers between devices  240 us (34%)
  Pallas kernels  228 us (32%)
  starting transfers between devices  125 us (18%)
  other arithmetic  37.3 us (5%)
  local copies, waits for them, and re-layouts  27.7 us (4%)
  matrix products  19.3 us (3%)
  between operations  14.9 us (2%)
    ppermute x60, waiting for transfers between devices, shift(): lax.ppermute(values, axis, [(i, (i + by) % size) for i in range(size)])  210 us
    ppermute x60, starting transfers between devices, shift(): lax.ppermute(values, axis, [(i, (i + by) % size) for i in range(size)])  83.6 us
    pallas_call x3, Pallas kernels, mlp_blocks(): pl.pallas_call(functools.partial(mlp_kernel, len(seconds), len(cots)), gr...  58 us
    pallas_call x1, Pallas kernels, attention_backward(): pl.pallas_call(backward_kernel, out_shape=(jax.ShapeDtypeStruct((BLOCKS,...  35.4 us
    all_to_all x4, waiting for transfers between devices, to_heads(): return lax.all_to_all(send, GROUP_AXES, 0, 0, tiled=True)  29.2 us
    all_to_all x4, starting transfers between devices, to_heads(): return lax.all_to_all(send, GROUP_AXES, 0, 0, tiled=True)  27.3 us
    pallas_call x1, Pallas kernels, attention_forward(): pl.pallas_call(forward_kernel, out_shape=(jax.ShapeDtypeStruct((BLOCKS, B...  21.5 us
    pallas_call x2, Pallas kernels, pair_grad(): pl.pallas_call(kernel, grid=(width // 256,), in_specs=[pl.BlockSpec(memor...  21.5 us
  transfers between devices with their start and end apart: 69, of which 31 were waited for; matrix products, arithmetic and copies ran while one was open for 10% of the time, Pallas kernels for 33%

profile of v7, /device:TPU:4, one launch (start us, length us, event | category | flops | bytes accessed | tf_op | source)
XLA Modules:
  0.0 691.4 jit_solution(5848390853226978980)
XLA Ops:
  75.9 12.0 %shard_map.246 = (bf16[4,256,2048]{2,1,0:T(8,128)(2,1)}, bf16[4,256,2048]{2,1,0:T(8,128)(2,1)}, f32[4,256,1024]{2,1,0:T(8,128)}, bf16[16,2,256,128]{3,2,1,0:T(8,128)(2,1)}, f32[8,2048]{1,0:T(8,128)}) custom-call(bf16[256,2048]{1,0:T(8,128)(2,1)} %refs_8_.1, bf16[256,2048]{1,0:T(8,128)(2,1)} %copy-done.39, bf16[128,2048]{1,0:T(8,128)(2,1)} %collective-permute-done.9.top_ref, ...), custom_call_target="tpu_custom_call" | custom-call | flops 4294967296 | bytes 20971520 | tf_op jit(solution)/shard_map/pallas_call | solution.py:569
  95.4 25.4 %collective-permute-done.12.refs_5_ = bf16[2048,512]{1,0:T(8,128)(2,1)S(1)} collective-permute-done((bf16[2048,512]{1,0:T(8,128)(2,1)}, bf16[2048,512]{1,0:T(8,128)(2,1)S(1)}, u32[]{:S(2)}, u32[]{:S(2)}) %collective-permute-start.12) | collective-permute-done | bytes 2097184 | tf_op jit(solution)/shard_map/ppermute | solution.py:41
  120.8 12.0 %all-to-all-done.own_a.own_b = bf16[16,2,256,128]{3,2,1,0:T(8,128)(2,1)} async-done(((bf16[16,2,256,128]{3,2,1,0:T(8,128)(2,1)}), bf16[16,2,256,128]{3,2,1,0:T(8,128)(2,1)}, u32[]{:S(2)}, u32[]{:S(2)}) %all-to-all-start) | async-done | bytes 2097184 | tf_op jit(solution)/shard_map/all_to_all | solution.py:811
  142.7 21.5 %shard_map.248 = (bf16[16,256,128]{2,1,0:T(8,128)(2,1)}, f32[8,128,512]{2,1,0:T(8,128)}, f32[8,1,512]{2,1,0:T(1,128)}) custom-call(s32[16]{0:T(128)} %dynamic-slice_bitcast_fusion.order, s32[1]{0:T(128)} %bitcast.1.core.core_ref, bf16[16,2,256,128]{3,2,1,0:T(8,128)(2,1)} %all-to-all-done.own_a.own_b, bf16[16,2,256,128]{3,2,1,0:T(8,128)(2,1)} %all-to-all-done.own_a.own_b, ...), custom_call_target="tpu_custom_call" | custom-call | flops 1024 | bytes 1024 | tf_op jit(solution)/shard_map/pallas_call | solution.py:117
  173.4 17.2 %collective-permute-done.17.refs_2_ = bf16[256,2048]{1,0:T(8,128)(2,1)S(1)} collective-permute-done((bf16[256,2048]{1,0:T(8,128)(2,1)S(1)}, bf16[256,2048]{1,0:T(8,128)(2,1)S(1)}, u32[]{:S(2)}, u32[]{:S(2)}) %collective-permute-start.17) | collective-permute-done | bytes 1048608 | tf_op jit(solution)/shard_map/ppermute | solution.py:41
  197.6 8.4 %collective-permute-done.19.refs_1_ = bf16[128,2048]{1,0:T(8,128)(2,1)} collective-permute-done((bf16[128,2048]{1,0:T(8,128)(2,1)}, bf16[128,2048]{1,0:T(8,128)(2,1)}, u32[]{:S(2)}, u32[]{:S(2)}) %collective-permute-start.19) | collective-permute-done | bytes 524320 | tf_op jit(solution)/shard_map/ppermute | solution.py:41
  232.4 15.7 %shard_map.250 = (bf16[4,256,1536]{2,1,0:T(8,128)(2,1)}, bf16[4,256,3072]{2,1,0:T(8,128)(2,1)}, bf16[4,256,2048]{2,1,0:T(8,128)(2,1)}, bf16[4,256,2048]{2,1,0:T(8,128)(2,1)}, bf16[256,2048]{1,0:T(8,128)(2,1)}) custom-call(bf16[256,2048]{1,0:T(8,128)(2,1)} %get-tuple-element.235.refs_0_, bf16[256,2048]{1,0:T(8,128)(2,1)} %refs_9_.1, ...), custom_call_target="tpu_custom_call" | custom-call | flops 8053063680 | bytes 18874368 | tf_op jit(solution)/shard_map/pallas_call | solution.py:318
  257.4 26.7 %shard_map.251 = (bf16[4,256,1536]{2,1,0:T(8,128)(2,1)}, bf16[4,256,3072]{2,1,0:T(8,128)(2,1)}, bf16[4,256,2048]{2,1,0:T(8,128)(2,1)}, bf16[4,256,2048]{2,1,0:T(...) custom-call(bf16[256,2048]{1,0:T(8,128)(2,1)} %copy-done.24, ...), custom_call_target="tpu_custom_call", output_to_operand_aliasing={{0}: (6, {}), {1}: (7, {}), {2}: (8, {}), {3}: (9, {})} | custom-call | flops 16106127360 | bytes 18874368 | tf_op jit(solution)/shard_map/pallas_call | solution.py:318
  287.1 15.6 %shard_map.252 = (bf16[4,256,1536]{2,1,0:T(8,128)(2,1)}, bf16[4,256,3072]{2,1,0:T(8,128)(2,1)}, bf16[4,256,2048]{2,1,0:T(8,128)(2,1)}, bf16[4,256,2048]{2,1,0:T(8,128)(2,1)}, bf16[256,2048]{1,0:T(8,128)(2,1)}) custom-call(bf16[256,2048]{1,0:T(8,128)(2,1)} %copy-done.23, ...), custom_call_target="tpu_custom_call", output_to_operand_aliasing={{0}: (5, {}), {1}: (6, {}), {2}: (7, {}), {3}: (8, {})} | custom-call | flops 8053063680 | bytes 18874368 | tf_op jit(solution)/shard_map/pallas_call | solution.py:318
  304.0 19.3 %bitcast_convert_fusion = bf16[2048,3072]{1,0:T(8,128)(2,1)} fusion(bf16[4,256,2048]{2,1,0:T(8,128)(2,1)} %get-tuple-element.244, bf16[4,256,3072]{2,1,0:T(8,128)(2,1)} %get-tuple-element.245), kind=kOutput, calls=%fused_computation | convolution fusion | flops 12891193344 | bytes 23068672 | tf_op jit(solution)/shard_map/dot_general | solution.py:1018
  323.4 8.5 %collective-permute-done.27.refs_2_ = bf16[256,2048]{1,0:T(8,128)(2,1)} collective-permute-done((bf16[256,2048]{1,0:T(8,128)(2,1)}, bf16[256,2048]{1,0:T(8,128)(2,1)}, u32[]{:S(2)}, u32[]{:S(2)}) %collective-permute-start.27) | collective-permute-done | bytes 1048608 | tf_op jit(solution)/shard_map/ppermute | solution.py:41
  332.0 12.6 %shard_map.253 = (f32[256,2048]{1,0:T(8,128)}, bf16[256,2048]{1,0:T(8,128)(2,1)}, f32[1,2048]{1,0:T(1,128)}, bf16[4,256,128]{2,1,0:T(8,128)(2,1)}, bf16[4,256,12...) custom-call(bf16[256,2048]{1,0:T(8,128)(2,1)} %get-tuple-element.220.refs_0_, ...), custom_call_target="tpu_custom_call" | custom-call | flops 1024 | bytes 1024 | tf_op jit(solution)/shard_map/pallas_call | solution.py:503
  348.3 13.0 %shard_map.254 = (bf16[8,128,1536]{2,1,0:T(8,128)(2,1)}, bf16[8,128,1536]{2,1,0:T(8,128)(2,1)}) custom-call(s32[1]{0:T(128)} %bitcast.1.core.core_ref, bf16[4,256,2048]{2,1,0:T(8,128)(2,1)} %get-tuple-element.254.refs_0_, bf16[4,256,1536]{2,1,0:T(8,128)(2,1)} %get-tuple-element.259.refs_1_.inner_ref), custom_call_target="tpu_custom_call" | custom-call | flops 1024 | bytes 1024 | tf_op jit(solution)/shard_map/pallas_call | solution.py:410
  370.7 10.6 %shard_map.255 = (bf16[256,2048]{1,0:T(8,128)(2,1)}, bf16[256,2048]{1,0:T(8,128)(2,1)}, bf16[256,2048]{1,0:T(8,128)(2,1)}, bf16[256,2048]{1,0:T(8,128)(2,1)}) custom-call(bf16[4,256,1536]{2,1,0:T(8,128)(2,1)} %get-tuple-element.259.refs_1_.inner_ref, bf16[2048,4608]{1,0:T(8,128)(2,1)} %all-gather.5.cloned.1.call-done.refs_2_.refs_3_.refs_4_.refs_5_.weight_ref), custom_call_target="tpu_custom_call" | custom-call | flops 1024 | bytes 1024 | tf_op jit(solution)/shard_map/pallas_call | solution.py:360
  381.3 13.5 %all-to-all-done.2.grad_a.grad_b = bf16[16,256,128]{2,1,0:T(8,128)(2,1)S(1)} async-done(((bf16[16,256,128]{2,1,0:T(8,128)(2,1)}), bf16[16,256,128]{2,1,0:T(8,128)(2,1)S(1)}, u32[]{:S(2)}, u32[]{:S(2)}) %all-to-all-start.2) | async-done | bytes 1048608 | tf_op jit(solution)/shard_map/all_to_all | solution.py:811
  396.9 35.4 %shard_map.256 = (bf16[16,2,256,128]{3,2,1,0:T(8,128)(2,1)}, bf16[16,256,128]{2,1,0:T(8,128)(2,1)}, bf16[16,256,128]{2,1,0:T(8,128)(2,1)}) custom-call(s32[16]{0:T(128)} %dynamic-slice_bitcast_fusion.order, s32[1]{0:T(128)} %bitcast.1.core.core_ref, bf16[16,2,256,128]{3,2,1,0:T(8,128)(2,1)} %all-to-all-done.own_a.own_b, ...), custom_call_target="tpu_custom_call" | custom-call | flops 1024 | bytes 1024 | tf_op jit(solution)/shard_map/pallas_call | solution.py:224
  438.3 9.1 %all-to-all-start.3 = ((bf16[16,2,256,128]{3,2,1,0:T(8,128)(2,1)}), bf16[16,2,256,128]{3,2,1,0:T(8,128)(2,1)S(1)}, u32[]{:S(2)}, u32[]{:S(2)}) async-start(bf16[16,2,256,128]{3,2,1,0:T(8,128)(2,1)} %fusion.9), calls=%async_computation.3 | async-start | bytes 4194304 | tf_op jit(solution)/shard_map/all_to_all | solution.py:811
  447.5 12.4 %collective-permute-done.39.refs_2_ = bf16[256,2048]{1,0:T(8,128)(2,1)} collective-permute-done((bf16[256,2048]{1,0:T(8,128)(2,1)}, bf16[256,2048]{1,0:T(8,128)(2,1)}, u32[]{:S(2)}, u32[]{:S(2)}) %collective-permute-start.39) | collective-permute-done | bytes 1048608 | tf_op jit(solution)/shard_map/ppermute | solution.py:41
  459.9 8.5 %shard_map.257 = (bf16[8,128,512]{2,1,0:T(8,128)(2,1)}, bf16[8,128,512]{2,1,0:T(8,128)(2,1)}) custom-call(s32[1]{0:T(128)} %bitcast.1.core.core_ref, bf16[256,2048]{1,0:T(8,128)(2,1)} %get-tuple-element.288.refs_0_, bf16[256,2048]{1,0:T(8,128)(2,1)} %collective-permute-done.33.refs_1_, bf16[256,2048]{1,0:T(8,128)(2,1)} %collective-permute-done.39.refs_2_, ...), custom_call_target="tpu_custom_call" | custom-call | flops 1024 | bytes 1024 | tf_op jit(solution)/shard_map/pallas_call | solution.py:410
  491.5 15.0 %shard_map.259 = (bf16[4,256,1024]{2,1,0:T(8,128)(2,1)}, bf16[8,128,1024]{2,1,0:T(8,128)(2,1)}, bf16[8,128,1024]{2,1,0:T(8,128)(2,1)}, f32[1,128]{1,0:T(1,128)}, f32[1,128]{1,0:T(1,128)}) custom-call(s32[1]{0:T(128)} %bitcast.1.core.core_ref, bf16[16,2,256,128]{3,2,1,0:T(8,128)(2,1)} %copy-done.13, f32[4,256,1024]{2,1,0:T(8,128)} %get-tuple-element.294.pre_ref, ...), custom_call_target="tpu_custom_call" | custom-call | flops 1024 | bytes 1024 | tf_op jit(solution)/shard_map/pallas_call | solution.py:656
  506.5 8.2 %collective-permute-done.42 = bf16[256,2048]{1,0:T(8,128)(2,1)S(1)} collective-permute-done((bf16[256,2048]{1,0:T(8,128)(2,1)}, bf16[256,2048]{1,0:T(8,128)(2,1)S(1)}, u32[]{:S(2)}, u32[]{:S(2)}) %collective-permute-start.42) | collective-permute-done | bytes 1048608 | tf_op jit(solution)/shard_map/ppermute | solution.py:41
  514.6 38.7 %collective-permute-done.41 = bf16[128,3072]{1,0:T(8,128)(2,1)S(1)} collective-permute-done((bf16[128,3072]{1,0:T(8,128)(2,1)}, bf16[128,3072]{1,0:T(8,128)(2,1)S(1)}, u32[]{:S(2)}, u32[]{:S(2)}) %collective-permute-start.41) | collective-permute-done | bytes 786464 | tf_op jit(solution)/shard_map/ppermute | solution.py:41
  559.9 12.6 %shard_map.260 = (bf16[256,2048]{1,0:T(8,128)(2,1)}, bf16[128,2048]{1,0:T(8,128)(2,1)}, bf16[128,2048]{1,0:T(8,128)(2,1)}, bf16[128,2048]{1,0:T(8,128)(2,1)}, bf...) custom-call(s32[1]{0:T(128)} %bitcast.1.core.core_ref, ...), custom_call_target="tpu_custom_call" | custom-call | flops 1024 | bytes 1024 | tf_op jit(solution)/shard_map/pallas_call | solution.py:741
  611.3 20.1 %collective-permute-done.52 = bf16[128,2048]{1,0:T(8,128)(2,1)} collective-permute-done((bf16[128,2048]{1,0:T(8,128)(2,1)}, bf16[128,2048]{1,0:T(8,128)(2,1)}, u32[]{:S(2)}, u32[]{:S(2)}) %collective-permute-start.52) | collective-permute-done | bytes 524320 | tf_op jit(solution)/shard_map/ppermute | solution.py:41
  (293 shorter events, 284.5 us)
Async XLA Ops:
  7.2 68.7 %all-gather.3.cloned.1.call-start = ((), (), s32[]{:S(2)}) async-start(), calls=%async_computation.7 | async-start | bytes 5013504 | tf_op jit(solution)/shard_map/all_gather | solution.py:897
  10.9 221.5 %all-gather.5.cloned.1.call-start = ((), (), s32[]{:S(2)}) async-start(), calls=%async_computation.8 | async-start | bytes 20054016 | tf_op jit(solution)/shard_map/all_gather | solution.py:897
  72.6 48.2 %collective-permute-start.12 = (bf16[2048,512]{1,0:T(8,128)(2,1)}, bf16[2048,512]{1,0:T(8,128)(2,1)S(1)}, u32[]{:S(2)}, u32[]{:S(2)}) collective-permute-start(bf16[2048,512]{1,0:T(8,128)(2,1)} %shard_map.247.refs_4_), channel_id=1, source_target_pairs={{0,16},{16,32},{32,48},{48,0},{1,17},{17,33},{33,49},{49,1},{2,18}... | collective-permute-start | bytes 6291464 | tf_op jit(solution)/shard_map/ppermute | solution.py:41
  72.6 48.2 %collective-permute-start.13 = (bf16[2048,512]{1,0:T(8,128)(2,1)}, bf16[2048,512]{1,0:T(8,128)(2,1)}, u32[]{:S(2)}, u32[]{:S(2)}) collective-permute-start(bf16[2048,512]{1,0:T(8,128)(2,1)} %shard_map.247.refs_4_), channel_id=1, source_target_pairs={{0,48},{16,0},{32,16},{48,32},{1,49},{17,1},{33,17},{49,33},{2,50}... | collective-permute-start | bytes 6291464 | tf_op jit(solution)/shard_map/ppermute | solution.py:41
  87.8 45.0 %all-to-all-start = ((bf16[16,2,256,128]{3,2,1,0:T(8,128)(2,1)}), bf16[16,2,256,128]{3,2,1,0:T(8,128)(2,1)}, u32[]{:S(2)}, u32[]{:S(2)}) async-start(bf16[16,2,256,128]{3,2,1,0:T(8,128)(2,1)} %get-tuple-element.184), calls=%async_computation | async-start | bytes 4194304 | tf_op jit(solution)/shard_map/all_to_all | solution.py:811
  167.6 30.0 %all-to-all-start.1 = ((bf16[16,256,128]{2,1,0:T(8,128)(2,1)}), bf16[16,256,128]{2,1,0:T(8,128)(2,1)S(1)}, u32[]{:S(2)}, u32[]{:S(2)}) async-start(bf16[16,256,128]{2,1,0:T(8,128)(2,1)} %get-tuple-element.196), calls=%async_computation.1 | async-start | bytes 2097152 | tf_op jit(solution)/shard_map/all_to_all | solution.py:811
  173.4 306.9 %reduce-scatter.2.cloned.1.call-start = ((), (), s32[]{:S(2)}) async-start(), calls=%async_computation.9 | async-start | bytes 13369344 | tf_op jit(solution)/shard_map/reduce_scatter | solution.py:1027
  254.2 32.0 %collective-permute-start.28 = (bf16[256,2048]{1,0:T(8,128)(2,1)}, bf16[256,2048]{1,0:T(8,128)(2,1)S(1)}, u32[]{:S(2)}, u32[]{:S(2)}) collective-permute-start(bf16[256,2048]{1,0:T(8,128)(2,1)} %get-tuple-element.235.refs_0_), channel_id=1, source_target_pairs={{0,32},{16,48},{32,0},{48,16},{1,33},{17,49},{33,1},{49,17},{2,34}... | collective-permute-start | bytes 3145736 | tf_op jit(solution)/shard_map/ppermute | solution.py:41
  284.0 39.4 %collective-permute-start.26 = (bf16[256,2048]{1,0:T(8,128)(2,1)}, bf16[256,2048]{1,0:T(8,128)(2,1)S(1)}, u32[]{:S(2)}, u32[]{:S(2)}) collective-permute-start(bf16[256,2048]{1,0:T(8,128)(2,1)} %get-tuple-element.229), channel_id=1, source_target_pairs={{0,48},{16,0},{32,16},{48,32},{1,49},{17,1},{33,17},{49,33},{2,50}... | collective-permute-start | bytes 3145736 | tf_op jit(solution)/shard_map/ppermute | solution.py:41
  285.0 46.9 %collective-permute-start.27 = (bf16[256,2048]{1,0:T(8,128)(2,1)}, bf16[256,2048]{1,0:T(8,128)(2,1)}, u32[]{:S(2)}, u32[]{:S(2)}) collective-permute-start(bf16[256,2048]{1,0:T(8,128)(2,1)} %get-tuple-element.230), channel_id=1, source_target_pairs={{0,16},{16,32},{32,48},{48,0},{1,17},{17,33},{33,49},{49,1},{2,18}... | collective-permute-start | bytes 3145736 | tf_op jit(solution)/shard_map/ppermute | solution.py:41
  302.7 29.2 %collective-permute-start.29 = (bf16[256,2048]{1,0:T(8,128)(2,1)}, bf16[256,2048]{1,0:T(8,128)(2,1)}, u32[]{:S(2)}, u32[]{:S(2)}) collective-permute-start(bf16[256,2048]{1,0:T(8,128)(2,1)} %get-tuple-element.243), channel_id=1, source_target_pairs={{0,32},{16,48},{32,0},{48,16},{1,33},{17,49},{33,1},{49,17},{2,34}... | collective-permute-start | bytes 3145736 | tf_op jit(solution)/shard_map/ppermute | solution.py:41
  361.3 33.5 %collective-permute-start.33 = (bf16[256,2048]{1,0:T(8,128)(2,1)S(1)}, bf16[256,2048]{1,0:T(8,128)(2,1)}, u32[]{:S(2)}, u32[]{:S(2)}) collective-permute-start(bf16[256,2048]{1,0:T(8,128)(2,1)S(1)} %copy-done.29), channel_id=1, source_target_pairs={{0,16},{16,32},{32,48},{48,0},{1,17},{17,33},{33,49},{49,1},{2,18}... | collective-permute-start | bytes 3145736 | tf_op jit(solution)/shard_map/ppermute | solution.py:41
  361.7 33.1 %collective-permute-start.34 = (bf16[256,2048]{1,0:T(8,128)(2,1)S(1)}, bf16[256,2048]{1,0:T(8,128)(2,1)}, u32[]{:S(2)}, u32[]{:S(2)}) collective-permute-start(bf16[256,2048]{1,0:T(8,128)(2,1)S(1)} %copy-done.29), channel_id=1, source_target_pairs={{0,48},{16,0},{32,16},{48,32},{1,49},{17,1},{33,17},{49,33},{2,50}... | collective-permute-start | bytes 3145736 | tf_op jit(solution)/shard_map/ppermute | solution.py:41
  365.8 28.9 %all-to-all-start.2 = ((bf16[16,256,128]{2,1,0:T(8,128)(2,1)}), bf16[16,256,128]{2,1,0:T(8,128)(2,1)S(1)}, u32[]{:S(2)}, u32[]{:S(2)}) async-start(bf16[16,256,128]{2,1,0:T(8,128)(2,1)} %pad_maximum_fusion.2), calls=%async_computation.2 | async-start | bytes 2097152 | tf_op jit(solution)/shard_map/all_to_all | solution.py:811
  394.8 37.5 %collective-permute-start.35 = (bf16[256,2048]{1,0:T(8,128)(2,1)}, bf16[256,2048]{1,0:T(8,128)(2,1)S(1)}, u32[]{:S(2)}, u32[]{:S(2)}) collective-permute-start(bf16[256,2048]{1,0:T(8,128)(2,1)} %get-tuple-element.275), channel_id=1, source_target_pairs={{0,48},{16,0},{32,16},{48,32},{1,49},{17,1},{33,17},{49,33},{2,50}... | collective-permute-start | bytes 3145736 | tf_op jit(solution)/shard_map/ppermute | solution.py:41
  394.9 37.5 %collective-permute-start.36 = (bf16[256,2048]{1,0:T(8,128)(2,1)}, bf16[256,2048]{1,0:T(8,128)(2,1)}, u32[]{:S(2)}, u32[]{:S(2)}) collective-permute-start(bf16[256,2048]{1,0:T(8,128)(2,1)} %get-tuple-element.276), channel_id=1, source_target_pairs={{0,16},{16,32},{32,48},{48,0},{1,17},{17,33},{33,49},{49,1},{2,18}... | collective-permute-start | bytes 3145736 | tf_op jit(solution)/shard_map/ppermute | solution.py:41
  432.4 39.0 %collective-permute-start.38 = (bf16[8,128,1536]{2,1,0:T(8,128)(2,1)}, bf16[8,128,1536]{2,1,0:T(8,128)(2,1)}, u32[]{:S(2)}, u32[]{:S(2)}) collective-permute-start(bf16[8,128,1536]{2,1,0:T(8,128)(2,1)} %get-tuple-element.287), channel_id=1, source_target_pairs={{0,1},{1,0},{2,3},{3,2},{4,5},{5,4},{6,7},{7,6},{8,9},{9,8},{10,11... | collective-permute-start | bytes 9437192 | tf_op jit(solution)/shard_map/ppermute | solution.py:41
  438.3 42.0 %all-to-all-start.3 = ((bf16[16,2,256,128]{3,2,1,0:T(8,128)(2,1)}), bf16[16,2,256,128]{3,2,1,0:T(8,128)(2,1)S(1)}, u32[]{:S(2)}, u32[]{:S(2)}) async-start(bf16[16,2,256,128]{3,2,1,0:T(8,128)(2,1)} %fusion.9), calls=%async_computation.3 | async-start | bytes 4194304 | tf_op jit(solution)/shard_map/all_to_all | solution.py:811
  481.6 96.6 %all-to-all-start.4 = ((bf16[8,128,2048]{2,1,0:T(8,128)(2,1)}), bf16[8,128,2048]{2,1,0:T(8,128)(2,1)}, u32[]{:S(2)}, u32[]{:S(2)}) async-start(bf16[8,128,2048]{2,1,0:T(8,128)(2,1)} %shard_map.258), calls=%async_computation.5 | async-start | bytes 8388608 | tf_op jit(solution)/shard_map/all_to_all | solution.py:1006
  489.3 64.1 %collective-permute-start.41 = (bf16[128,3072]{1,0:T(8,128)(2,1)}, bf16[128,3072]{1,0:T(8,128)(2,1)S(1)}, u32[]{:S(2)}, u32[]{:S(2)}) collective-permute-start(bf16[128,3072]{1,0:T(8,128)(2,1)} %reduce-scatter.2.cloned.1.call-done), channel_id=1, source_target_pairs={{0,64},{64,0},{1,65},{65,1},{2,66},{66,2},{3,67},{67,3},{4,68},{68... | collective-permute-start | bytes 2359304 | tf_op jit(solution)/shard_map/ppermute | solution.py:41
  585.8 54.1 %all-to-all-start.5 = ((bf16[8,128,1152]{2,1,0:T(8,128)(2,1)}), bf16[8,128,1152]{2,1,0:T(8,128)(2,1)}, u32[]{:S(2)}, u32[]{:S(2)}) async-start(bf16[8,128,1152]{2,1,0:T(8,128)(2,1)} %shard_map.261), calls=%async_computation.6 | async-start | bytes 4718592 | tf_op jit(solution)/shard_map/all_to_all | solution.py:1006
  595.6 42.7 %collective-permute-start.50 = (bf16[256,2048]{1,0:T(8,128)(2,1)}, bf16[256,2048]{1,0:T(8,128)(2,1)}, u32[]{:S(2)}, u32[]{:S(2)}) collective-permute-start(bf16[256,2048]{1,0:T(8,128)(2,1)} %pad_maximum_fusion.4), channel_id=1, source_target_pairs={{0,16},{16,32},{32,48},{48,0},{1,17},{17,33},{33,49},{49,1},{2,18}... | collective-permute-start | bytes 3145736 | tf_op jit(solution)/shard_map/ppermute | solution.py:41
  597.9 42.0 %collective-permute-start.48 = (bf16[256,2048]{1,0:T(8,128)(2,1)}, bf16[256,2048]{1,0:T(8,128)(2,1)}, u32[]{:S(2)}, u32[]{:S(2)}) collective-permute-start(bf16[256,2048]{1,0:T(8,128)(2,1)} %pad_maximum_fusion.3), channel_id=1, source_target_pairs={{0,48},{16,0},{32,16},{48,32},{1,49},{17,1},{33,17},{49,33},{2,50}... | collective-permute-start | bytes 3145736 | tf_op jit(solution)/shard_map/ppermute | solution.py:41
  601.4 36.9 %collective-permute-start.51 = (bf16[128,3072]{1,0:T(8,128)(2,1)}, bf16[128,3072]{1,0:T(8,128)(2,1)}, u32[]{:S(2)}, u32[]{:S(2)}) collective-permute-start(bf16[128,3072]{1,0:T(8,128)(2,1)} %add_convert_fusion.2.refs_0_), channel_id=1, source_target_pairs={{0,32},{16,48},{32,0},{48,16},{1,33},{17,49},{33,1},{49,17},{2,34}... | collective-permute-start | bytes 2359304 | tf_op jit(solution)/shard_map/ppermute | solution.py:41
  (92 other events, 1177.7 us)
Sparse Core Ops, SparseCore 0:
  11.1 62.2 all-gather.2
  75.8 147.3 all-gather.4
  332.1 146.4 reduce-scatter.1

commit v8 on v7

--- a/solution.py
+++ b/solution.py
@@ -1071,7 +1071,9 @@
     )
     returned, both_share, down_sum = together(returned, both_share, down_sum)
     both_pair = over_x(both_share)
-    down_terms = to_owners(down_sum)
+    down_terms = lax.all_to_all(
+        down_sum.reshape(RING, 2, 128, down_sum.shape[2]), "y", 0, 0, tiled=True
+    )
     qkv_grad, qkv_keep, qkv_give, query_gain_part, key_gain_part = first_back(
         core_at, returned, qkv_pre, cosine, sine, query_row, key_row, first_in
     )
@@ -1091,10 +1093,14 @@
         query_gain_part,
         key_gain_part,
     )
-    first_parts, gains_give, qkv_come, both_left, both_right, both_sum, down_terms = together(
-        first_parts, gains_give, qkv_come, both_left, both_right, both_sum, down_terms
-    )
-    down_pair = over_x(add_up(down_terms))
+    first_parts, gains_give, qkv_come, both_left, both_right, both_sum = together(
+        first_parts, gains_give, qkv_come, both_left, both_right, both_sum
+    )
+    down_halves = add_up(down_terms)
+    down_keep = lax.dynamic_index_in_dim(down_halves, x_at, 0, keepdims=False)
+    down_give = lax.dynamic_index_in_dim(down_halves, 1 - x_at, 0, keepdims=False)
+    down_come = lax.ppermute(down_give, ("x_lo", "x_hi"), [(i, 3 - i) for i in range(4)])
+    down_pair = over_x(pair_sum(down_keep, down_come))
     gains_come = shift(gains_give, "core", 1, 2)
     first_own, left_a, left_b, first_top, first_bottom, right_a, right_b = first_parts
     first_top = shift(first_top, "z", 3)

time: 702 us -> 663 us (0.944)
  waiting for transfers between devices: 240 us -> 199 us
    ppermute x60, waiting for transfers between devices: 210 us -> 152 us  [shift(): lax.ppermute(values, axis, [(i, (i + by) % size) for i in range(size)])]
    ppermute x0 -> x1, waiting for transfers between devices: none -> 16.6 us  [local(): lax.ppermute(down_give, ('x_lo', 'x_hi'), [(i, 3 - i) for i in range(4)])]
    all_to_all x2 -> x1, starting transfers between devices: 13.5 us -> 6.39 us  [to_owners(): return lax.all_to_all(pair, ('y', 'x_hi'), 0, 0, tiled=True)]
  transfers between devices with their start and end apart: 69 -> 70, of which waited for: 31 -> 29; matrix products, arithmetic and copies ran while one was open for 10% -> 10% of each run, Pallas kernels for 33% -> 35%
where the time goes in v8:
time: 663 us; the launch traced here: 650 us
  Pallas kernels  228 us (34%)
  waiting for transfers between devices  199 us (30%)
  starting transfers between devices  123 us (19%)
  other arithmetic  36.1 us (5%)
  local copies, waits for them, and re-layouts  29.6 us (4%)
  matrix products  19.4 us (3%)
  between operations  15 us (2%)
    ppermute x60, waiting for transfers between devices, shift(): lax.ppermute(values, axis, [(i, (i + by) % size) for i in range(size)])  152 us
    ppermute x60, starting transfers between devices, shift(): lax.ppermute(values, axis, [(i, (i + by) % size) for i in range(size)])  83.6 us
    pallas_call x3, Pallas kernels, mlp_blocks(): pl.pallas_call(functools.partial(mlp_kernel, len(seconds), len(cots)), gr...  58.1 us
    pallas_call x1, Pallas kernels, attention_backward(): pl.pallas_call(backward_kernel, out_shape=(jax.ShapeDtypeStruct((BLOCKS,...  35.4 us
    all_to_all x4, waiting for transfers between devices, to_heads(): return lax.all_to_all(send, GROUP_AXES, 0, 0, tiled=True)  29.1 us
    all_to_all x4, starting transfers between devices, to_heads(): return lax.all_to_all(send, GROUP_AXES, 0, 0, tiled=True)  27.3 us
    pallas_call x2, Pallas kernels, pair_grad(): pl.pallas_call(kernel, grid=(width // 256,), in_specs=[pl.BlockSpec(memor...  21.6 us
    pallas_call x1, Pallas kernels, attention_forward(): pl.pallas_call(forward_kernel, out_shape=(jax.ShapeDtypeStruct((BLOCKS, B...  21.5 us
  transfers between devices with their start and end apart: 70, of which 29 were waited for; matrix products, arithmetic and copies ran while one was open for 10% of the time, Pallas kernels for 35%

profile of v8, /device:TPU:4, one launch (start us, length us, event | category | flops | bytes accessed | tf_op | source)
XLA Modules:
  0.0 650.2 jit_solution(13303568027814051101)
XLA Ops:
  75.9 12.0 %shard_map.246 = (bf16[4,256,2048]{2,1,0:T(8,128)(2,1)}, bf16[4,256,2048]{2,1,0:T(8,128)(2,1)}, f32[4,256,1024]{2,1,0:T(8,128)}, bf16[16,2,256,128]{3,2,1,0:T(8,128)(2,1)}, f32[8,2048]{1,0:T(8,128)}) custom-call(bf16[256,2048]{1,0:T(8,128)(2,1)} %refs_8_.1, bf16[256,2048]{1,0:T(8,128)(2,1)} %copy-done.43, bf16[128,2048]{1,0:T(8,128)(2,1)} %collective-permute-done.9.top_ref, ...), custom_call_target="tpu_custom_call" | custom-call | flops 4294967296 | bytes 20971520 | tf_op jit(solution)/shard_map/pallas_call | solution.py:569
  95.4 25.4 %collective-permute-done.12.refs_5_ = bf16[2048,512]{1,0:T(8,128)(2,1)S(1)} collective-permute-done((bf16[2048,512]{1,0:T(8,128)(2,1)}, bf16[2048,512]{1,0:T(8,128)(2,1)S(1)}, u32[]{:S(2)}, u32[]{:S(2)}) %collective-permute-start.12) | collective-permute-done | bytes 2097184 | tf_op jit(solution)/shard_map/ppermute | solution.py:41
  120.8 12.0 %all-to-all-done.own_a.own_b = bf16[16,2,256,128]{3,2,1,0:T(8,128)(2,1)} async-done(((bf16[16,2,256,128]{3,2,1,0:T(8,128)(2,1)}), bf16[16,2,256,128]{3,2,1,0:T(8,128)(2,1)}, u32[]{:S(2)}, u32[]{:S(2)}) %all-to-all-start) | async-done | bytes 2097184 | tf_op jit(solution)/shard_map/all_to_all | solution.py:811
  142.7 21.5 %shard_map.248 = (bf16[16,256,128]{2,1,0:T(8,128)(2,1)}, f32[8,128,512]{2,1,0:T(8,128)}, f32[8,1,512]{2,1,0:T(1,128)}) custom-call(s32[16]{0:T(128)} %dynamic-slice_bitcast_fusion.1.order, s32[1]{0:T(128)} %bitcast.1.core.core_ref, bf16[16,2,256,128]{3,2,1,0:T(8,128)(2,1)} %all-to-all-done.own_a.own_b, bf16[16,2,256,128]{3,2,1,0:T(8,128)(2,1)} %all-to-all-done.own_a.own_b, ...), custom_call_target="tpu_custom_call" | custom-call | flops 1024 | bytes 1024 | tf_op jit(solution)/shard_map/pallas_call | solution.py:117
  173.4 17.2 %collective-permute-done.17.refs_2_ = bf16[256,2048]{1,0:T(8,128)(2,1)S(1)} collective-permute-done((bf16[256,2048]{1,0:T(8,128)(2,1)S(1)}, bf16[256,2048]{1,0:T(8,128)(2,1)S(1)}, u32[]{:S(2)}, u32[]{:S(2)}) %collective-permute-start.17) | collective-permute-done | bytes 1048608 | tf_op jit(solution)/shard_map/ppermute | solution.py:41
  197.6 8.4 %collective-permute-done.19.refs_1_ = bf16[128,2048]{1,0:T(8,128)(2,1)} collective-permute-done((bf16[128,2048]{1,0:T(8,128)(2,1)}, bf16[128,2048]{1,0:T(8,128)(2,1)}, u32[]{:S(2)}, u32[]{:S(2)}) %collective-permute-start.19) | collective-permute-done | bytes 524320 | tf_op jit(solution)/shard_map/ppermute | solution.py:41
  232.4 15.7 %shard_map.250 = (bf16[4,256,1536]{2,1,0:T(8,128)(2,1)}, bf16[4,256,3072]{2,1,0:T(8,128)(2,1)}, bf16[4,256,2048]{2,1,0:T(8,128)(2,1)}, bf16[4,256,2048]{2,1,0:T(8,128)(2,1)}, bf16[256,2048]{1,0:T(8,128)(2,1)}) custom-call(bf16[256,2048]{1,0:T(8,128)(2,1)} %get-tuple-element.234.refs_0_, bf16[256,2048]{1,0:T(8,128)(2,1)} %refs_9_.1, ...), custom_call_target="tpu_custom_call" | custom-call | flops 8053063680 | bytes 18874368 | tf_op jit(solution)/shard_map/pallas_call | solution.py:318
  257.4 26.7 %shard_map.251 = (bf16[4,256,1536]{2,1,0:T(8,128)(2,1)}, bf16[4,256,3072]{2,1,0:T(8,128)(2,1)}, bf16[4,256,2048]{2,1,0:T(8,128)(2,1)}, bf16[4,256,2048]{2,1,0:T(...) custom-call(bf16[256,2048]{1,0:T(8,128)(2,1)} %copy-done.27, ...), custom_call_target="tpu_custom_call", output_to_operand_aliasing={{0}: (6, {}), {1}: (7, {}), {2}: (8, {}), {3}: (9, {})} | custom-call | flops 16106127360 | bytes 18874368 | tf_op jit(solution)/shard_map/pallas_call | solution.py:318
  287.2 15.6 %shard_map.252 = (bf16[4,256,1536]{2,1,0:T(8,128)(2,1)}, bf16[4,256,3072]{2,1,0:T(8,128)(2,1)}, bf16[4,256,2048]{2,1,0:T(8,128)(2,1)}, bf16[4,256,2048]{2,1,0:T(8,128)(2,1)}, bf16[256,2048]{1,0:T(8,128)(2,1)}) custom-call(bf16[256,2048]{1,0:T(8,128)(2,1)} %copy-done.26, ...), custom_call_target="tpu_custom_call", output_to_operand_aliasing={{0}: (5, {}), {1}: (6, {}), {2}: (7, {}), {3}: (8, {})} | custom-call | flops 8053063680 | bytes 18874368 | tf_op jit(solution)/shard_map/pallas_call | solution.py:318
  304.1 19.4 %bitcast_convert_fusion = bf16[2048,3072]{1,0:T(8,128)(2,1)} fusion(bf16[4,256,2048]{2,1,0:T(8,128)(2,1)} %get-tuple-element.243, bf16[4,256,3072]{2,1,0:T(8,128)(2,1)} %get-tuple-element.244), kind=kOutput, calls=%fused_computation | convolution fusion | flops 12891193344 | bytes 23068672 | tf_op jit(solution)/shard_map/dot_general | solution.py:1018
  323.5 8.5 %collective-permute-done.27.refs_2_ = bf16[256,2048]{1,0:T(8,128)(2,1)} collective-permute-done((bf16[256,2048]{1,0:T(8,128)(2,1)}, bf16[256,2048]{1,0:T(8,128)(2,1)}, u32[]{:S(2)}, u32[]{:S(2)}) %collective-permute-start.27) | collective-permute-done | bytes 1048608 | tf_op jit(solution)/shard_map/ppermute | solution.py:41
  332.0 12.6 %shard_map.253 = (f32[256,2048]{1,0:T(8,128)}, bf16[256,2048]{1,0:T(8,128)(2,1)}, f32[1,2048]{1,0:T(1,128)}, bf16[4,256,128]{2,1,0:T(8,128)(2,1)}, bf16[4,256,12...) custom-call(bf16[256,2048]{1,0:T(8,128)(2,1)} %get-tuple-element.219.refs_0_, ...), custom_call_target="tpu_custom_call" | custom-call | flops 1024 | bytes 1024 | tf_op jit(solution)/shard_map/pallas_call | solution.py:503
  348.4 13.0 %shard_map.254 = (bf16[8,128,1536]{2,1,0:T(8,128)(2,1)}, bf16[8,128,1536]{2,1,0:T(8,128)(2,1)}) custom-call(s32[1]{0:T(128)} %bitcast.1.core.core_ref, bf16[4,256,2048]{2,1,0:T(8,128)(2,1)} %get-tuple-element.253.refs_0_, bf16[4,256,1536]{2,1,0:T(8,128)(2,1)} %get-tuple-element.258.refs_1_.inner_ref), custom_call_target="tpu_custom_call" | custom-call | flops 1024 | bytes 1024 | tf_op jit(solution)/shard_map/pallas_call | solution.py:410
  370.8 10.6 %shard_map.255 = (bf16[256,2048]{1,0:T(8,128)(2,1)}, bf16[256,2048]{1,0:T(8,128)(2,1)}, bf16[256,2048]{1,0:T(8,128)(2,1)}, bf16[256,2048]{1,0:T(8,128)(2,1)}) custom-call(bf16[4,256,1536]{2,1,0:T(8,128)(2,1)} %get-tuple-element.258.refs_1_.inner_ref, bf16[2048,4608]{1,0:T(8,128)(2,1)} %all-gather.5.cloned.1.call-done.refs_2_.refs_3_.refs_4_.refs_5_.weight_ref), custom_call_target="tpu_custom_call" | custom-call | flops 1024 | bytes 1024 | tf_op jit(solution)/shard_map/pallas_call | solution.py:360
  381.4 13.5 %all-to-all-done.2.grad_a.grad_b = bf16[16,256,128]{2,1,0:T(8,128)(2,1)S(1)} async-done(((bf16[16,256,128]{2,1,0:T(8,128)(2,1)}), bf16[16,256,128]{2,1,0:T(8,128)(2,1)S(1)}, u32[]{:S(2)}, u32[]{:S(2)}) %all-to-all-start.2) | async-done | bytes 1048608 | tf_op jit(solution)/shard_map/all_to_all | solution.py:811
  397.0 35.4 %shard_map.256 = (bf16[16,2,256,128]{3,2,1,0:T(8,128)(2,1)}, bf16[16,256,128]{2,1,0:T(8,128)(2,1)}, bf16[16,256,128]{2,1,0:T(8,128)(2,1)}) custom-call(s32[16]{0:T(128)} %dynamic-slice_bitcast_fusion.1.order, s32[1]{0:T(128)} %bitcast.1.core.core_ref, bf16[16,2,256,128]{3,2,1,0:T(8,128)(2,1)} %all-to-all-done.own_a.own_b, ...), custom_call_target="tpu_custom_call" | custom-call | flops 1024 | bytes 1024 | tf_op jit(solution)/shard_map/pallas_call | solution.py:224
  438.5 9.1 %all-to-all-start.3 = ((bf16[16,2,256,128]{3,2,1,0:T(8,128)(2,1)}), bf16[16,2,256,128]{3,2,1,0:T(8,128)(2,1)S(1)}, u32[]{:S(2)}, u32[]{:S(2)}) async-start(bf16[16,2,256,128]{3,2,1,0:T(8,128)(2,1)} %fusion.9), calls=%async_computation.3 | async-start | bytes 4194304 | tf_op jit(solution)/shard_map/all_to_all | solution.py:811
  447.6 12.4 %collective-permute-done.39.refs_2_ = bf16[256,2048]{1,0:T(8,128)(2,1)} collective-permute-done((bf16[256,2048]{1,0:T(8,128)(2,1)}, bf16[256,2048]{1,0:T(8,128)(2,1)}, u32[]{:S(2)}, u32[]{:S(2)}) %collective-permute-start.39) | collective-permute-done | bytes 1048608 | tf_op jit(solution)/shard_map/ppermute | solution.py:41
  460.1 8.6 %shard_map.257 = (bf16[8,128,512]{2,1,0:T(8,128)(2,1)}, bf16[8,128,512]{2,1,0:T(8,128)(2,1)}) custom-call(s32[1]{0:T(128)} %bitcast.1.core.core_ref, bf16[256,2048]{1,0:T(8,128)(2,1)} %get-tuple-element.287.refs_0_, bf16[256,2048]{1,0:T(8,128)(2,1)} %collective-permute-done.33.refs_1_, bf16[256,2048]{1,0:T(8,128)(2,1)} %collective-permute-done.39.refs_2_, ...), custom_call_target="tpu_custom_call" | custom-call | flops 1024 | bytes 1024 | tf_op jit(solution)/shard_map/pallas_call | solution.py:410
  487.2 15.0 %shard_map.259 = (bf16[4,256,1024]{2,1,0:T(8,128)(2,1)}, bf16[8,128,1024]{2,1,0:T(8,128)(2,1)}, bf16[8,128,1024]{2,1,0:T(8,128)(2,1)}, f32[1,128]{1,0:T(1,128)}, f32[1,128]{1,0:T(1,128)}) custom-call(s32[1]{0:T(128)} %bitcast.1.core.core_ref, bf16[16,2,256,128]{3,2,1,0:T(8,128)(2,1)} %copy-done.13, f32[4,256,1024]{2,1,0:T(8,128)} %get-tuple-element.293.pre_ref, ...), custom_call_target="tpu_custom_call" | custom-call | flops 1024 | bytes 1024 | tf_op jit(solution)/shard_map/pallas_call | solution.py:656
  508.3 12.6 %shard_map.260 = (bf16[256,2048]{1,0:T(8,128)(2,1)}, bf16[128,2048]{1,0:T(8,128)(2,1)}, bf16[128,2048]{1,0:T(8,128)(2,1)}, bf16[128,2048]{1,0:T(8,128)(2,1)}, bf...) custom-call(s32[1]{0:T(128)} %bitcast.1.core.core_ref, ...), custom_call_target="tpu_custom_call" | custom-call | flops 1024 | bytes 1024 | tf_op jit(solution)/shard_map/pallas_call | solution.py:741
  564.1 16.6 %collective-permute-done.52 = bf16[128,2048]{1,0:T(8,128)(2,1)S(1)} collective-permute-done((bf16[128,2048]{1,0:T(8,128)(2,1)S(1)}, bf16[128,2048]{1,0:T(8,128)(2,1)S(1)}, u32[]{:S(2)}, u32[]{:S(2)}) %collective-permute-start.52) | collective-permute-done | bytes 524320 | tf_op jit(solution)/shard_map/ppermute | solution.py:1102
  585.6 9.3 %collective-permute-done.53 = bf16[128,2048]{1,0:T(8,128)(2,1)S(1)} collective-permute-done((bf16[128,2048]{1,0:T(8,128)(2,1)S(1)}, bf16[128,2048]{1,0:T(8,128)(2,1)S(1)}, u32[]{:S(2)}, u32[]{:S(2)}) %collective-permute-start.53) | collective-permute-done | bytes 524320 | tf_op jit(solution)/shard_map/ppermute | solution.py:41
  615.2 10.2 %collective-permute-done.58.refs_1_ = bf16[128,2048]{1,0:T(8,128)(2,1)} collective-permute-done((bf16[128,2048]{1,0:T(8,128)(2,1)}, bf16[128,2048]{1,0:T(8,128)(2,1)}, u32[]{:S(2)}, u32[]{:S(2)}) %collective-permute-start.58) | collective-permute-done | bytes 524320 | tf_op jit(solution)/shard_map/ppermute | solution.py:41
  (305 shorter events, 273.8 us)
Async XLA Ops:
  7.2 68.7 %all-gather.3.cloned.1.call-start = ((), (), s32[]{:S(2)}) async-start(), calls=%async_computation.7 | async-start | bytes 5013504 | tf_op jit(solution)/shard_map/all_gather | solution.py:897
  10.9 221.5 %all-gather.5.cloned.1.call-start = ((), (), s32[]{:S(2)}) async-start(), calls=%async_computation.8 | async-start | bytes 20054016 | tf_op jit(solution)/shard_map/all_gather | solution.py:897
  72.6 48.2 %collective-permute-start.12 = (bf16[2048,512]{1,0:T(8,128)(2,1)}, bf16[2048,512]{1,0:T(8,128)(2,1)S(1)}, u32[]{:S(2)}, u32[]{:S(2)}) collective-permute-start(bf16[2048,512]{1,0:T(8,128)(2,1)} %shard_map.247.refs_4_), channel_id=1, source_target_pairs={{0,16},{16,32},{32,48},{48,0},{1,17},{17,33},{33,49},{49,1},{2,18}... | collective-permute-start | bytes 6291464 | tf_op jit(solution)/shard_map/ppermute | solution.py:41
  72.6 48.2 %collective-permute-start.13 = (bf16[2048,512]{1,0:T(8,128)(2,1)}, bf16[2048,512]{1,0:T(8,128)(2,1)}, u32[]{:S(2)}, u32[]{:S(2)}) collective-permute-start(bf16[2048,512]{1,0:T(8,128)(2,1)} %shard_map.247.refs_4_), channel_id=1, source_target_pairs={{0,48},{16,0},{32,16},{48,32},{1,49},{17,1},{33,17},{49,33},{2,50}... | collective-permute-start | bytes 6291464 | tf_op jit(solution)/shard_map/ppermute | solution.py:41
  87.8 45.0 %all-to-all-start = ((bf16[16,2,256,128]{3,2,1,0:T(8,128)(2,1)}), bf16[16,2,256,128]{3,2,1,0:T(8,128)(2,1)}, u32[]{:S(2)}, u32[]{:S(2)}) async-start(bf16[16,2,256,128]{3,2,1,0:T(8,128)(2,1)} %get-tuple-element.183), calls=%async_computation | async-start | bytes 4194304 | tf_op jit(solution)/shard_map/all_to_all | solution.py:811
  173.4 307.1 %reduce-scatter.2.cloned.1.call-start = ((), (), s32[]{:S(2)}) async-start(), calls=%async_computation.9 | async-start | bytes 13369344 | tf_op jit(solution)/shard_map/reduce_scatter | solution.py:1027
  254.2 32.0 %collective-permute-start.28 = (bf16[256,2048]{1,0:T(8,128)(2,1)}, bf16[256,2048]{1,0:T(8,128)(2,1)S(1)}, u32[]{:S(2)}, u32[]{:S(2)}) collective-permute-start(bf16[256,2048]{1,0:T(8,128)(2,1)} %get-tuple-element.234.refs_0_), channel_id=1, source_target_pairs={{0,32},{16,48},{32,0},{48,16},{1,33},{17,49},{33,1},{49,17},{2,34}... | collective-permute-start | bytes 3145736 | tf_op jit(solution)/shard_map/ppermute | solution.py:41
  284.1 39.4 %collective-permute-start.26 = (bf16[256,2048]{1,0:T(8,128)(2,1)}, bf16[256,2048]{1,0:T(8,128)(2,1)S(1)}, u32[]{:S(2)}, u32[]{:S(2)}) collective-permute-start(bf16[256,2048]{1,0:T(8,128)(2,1)} %get-tuple-element.228), channel_id=1, source_target_pairs={{0,48},{16,0},{32,16},{48,32},{1,49},{17,1},{33,17},{49,33},{2,50}... | collective-permute-start | bytes 3145736 | tf_op jit(solution)/shard_map/ppermute | solution.py:41
  285.1 46.9 %collective-permute-start.27 = (bf16[256,2048]{1,0:T(8,128)(2,1)}, bf16[256,2048]{1,0:T(8,128)(2,1)}, u32[]{:S(2)}, u32[]{:S(2)}) collective-permute-start(bf16[256,2048]{1,0:T(8,128)(2,1)} %get-tuple-element.229), channel_id=1, source_target_pairs={{0,16},{16,32},{32,48},{48,0},{1,17},{17,33},{33,49},{49,1},{2,18}... | collective-permute-start | bytes 3145736 | tf_op jit(solution)/shard_map/ppermute | solution.py:41
  361.4 33.5 %collective-permute-start.33 = (bf16[256,2048]{1,0:T(8,128)(2,1)S(1)}, bf16[256,2048]{1,0:T(8,128)(2,1)}, u32[]{:S(2)}, u32[]{:S(2)}) collective-permute-start(bf16[256,2048]{1,0:T(8,128)(2,1)S(1)} %copy-done.33), channel_id=1, source_target_pairs={{0,16},{16,32},{32,48},{48,0},{1,17},{17,33},{33,49},{49,1},{2,18}... | collective-permute-start | bytes 3145736 | tf_op jit(solution)/shard_map/ppermute | solution.py:41
  361.8 33.1 %collective-permute-start.34 = (bf16[256,2048]{1,0:T(8,128)(2,1)S(1)}, bf16[256,2048]{1,0:T(8,128)(2,1)}, u32[]{:S(2)}, u32[]{:S(2)}) collective-permute-start(bf16[256,2048]{1,0:T(8,128)(2,1)S(1)} %copy-done.33), channel_id=1, source_target_pairs={{0,48},{16,0},{32,16},{48,32},{1,49},{17,1},{33,17},{49,33},{2,50}... | collective-permute-start | bytes 3145736 | tf_op jit(solution)/shard_map/ppermute | solution.py:41
  394.9 37.5 %collective-permute-start.35 = (bf16[256,2048]{1,0:T(8,128)(2,1)}, bf16[256,2048]{1,0:T(8,128)(2,1)S(1)}, u32[]{:S(2)}, u32[]{:S(2)}) collective-permute-start(bf16[256,2048]{1,0:T(8,128)(2,1)} %get-tuple-element.274), channel_id=1, source_target_pairs={{0,48},{16,0},{32,16},{48,32},{1,49},{17,1},{33,17},{49,33},{2,50}... | collective-permute-start | bytes 3145736 | tf_op jit(solution)/shard_map/ppermute | solution.py:41
  395.0 37.5 %collective-permute-start.36 = (bf16[256,2048]{1,0:T(8,128)(2,1)}, bf16[256,2048]{1,0:T(8,128)(2,1)}, u32[]{:S(2)}, u32[]{:S(2)}) collective-permute-start(bf16[256,2048]{1,0:T(8,128)(2,1)} %get-tuple-element.275), channel_id=1, source_target_pairs={{0,16},{16,32},{32,48},{48,0},{1,17},{17,33},{33,49},{49,1},{2,18}... | collective-permute-start | bytes 3145736 | tf_op jit(solution)/shard_map/ppermute | solution.py:41
  432.6 39.0 %collective-permute-start.38 = (bf16[8,128,1536]{2,1,0:T(8,128)(2,1)}, bf16[8,128,1536]{2,1,0:T(8,128)(2,1)}, u32[]{:S(2)}, u32[]{:S(2)}) collective-permute-start(bf16[8,128,1536]{2,1,0:T(8,128)(2,1)} %get-tuple-element.286), channel_id=1, source_target_pairs={{0,1},{1,0},{2,3},{3,2},{4,5},{5,4},{6,7},{7,6},{8,9},{9,8},{10,11... | collective-permute-start | bytes 9437192 | tf_op jit(solution)/shard_map/ppermute | solution.py:41
  438.5 42.0 %all-to-all-start.3 = ((bf16[16,2,256,128]{3,2,1,0:T(8,128)(2,1)}), bf16[16,2,256,128]{3,2,1,0:T(8,128)(2,1)S(1)}, u32[]{:S(2)}, u32[]{:S(2)}) async-start(bf16[16,2,256,128]{3,2,1,0:T(8,128)(2,1)} %fusion.9), calls=%async_computation.3 | async-start | bytes 4194304 | tf_op jit(solution)/shard_map/all_to_all | solution.py:811
  468.6 33.6 %collective-permute-start.42 = (bf16[256,2048]{1,0:T(8,128)(2,1)}, bf16[256,2048]{1,0:T(8,128)(2,1)}, u32[]{:S(2)}, u32[]{:S(2)}) collective-permute-start(bf16[256,2048]{1,0:T(8,128)(2,1)} %get-tuple-element.299), channel_id=1, source_target_pairs={{0,32},{16,48},{32,0},{48,16},{1,33},{17,49},{33,1},{49,17},{2,34}... | collective-permute-start | bytes 3145736 | tf_op jit(solution)/shard_map/ppermute | solution.py:41
  482.1 54.6 %all-to-all-start.5 = ((bf16[4,2,128,2048]{3,2,1,0:T(8,128)(2,1)}), bf16[4,2,128,2048]{3,2,1,0:T(8,128)(2,1)}, u32[]{:S(2)}, u32[]{:S(2)}) async-start(bf16[4,2,128,2048]{3,2,1,0:T(8,128)(2,1)} %bitcast.38), calls=%async_computation.6 | async-start | bytes 8388608 | tf_op jit(solution)/shard_map/all_to_all | solution.py:1074
  529.9 55.7 %collective-permute-start.51 = (bf16[128,3072]{1,0:T(8,128)(2,1)}, bf16[128,3072]{1,0:T(8,128)(2,1)}, u32[]{:S(2)}, u32[]{:S(2)}) collective-permute-start(bf16[128,3072]{1,0:T(8,128)(2,1)} %add_convert_fusion.2.refs_0_), channel_id=1, source_target_pairs={{0,32},{16,48},{32,0},{48,16},{1,33},{17,49},{33,1},{49,17},{2,34}... | collective-permute-start | bytes 2359304 | tf_op jit(solution)/shard_map/ppermute | solution.py:41
  536.8 59.9 %all-to-all-start.4 = ((bf16[8,128,1152]{2,1,0:T(8,128)(2,1)}), bf16[8,128,1152]{2,1,0:T(8,128)(2,1)S(1)}, u32[]{:S(2)}, u32[]{:S(2)}) async-start(bf16[8,128,1152]{2,1,0:T(8,128)(2,1)} %shard_map.261), calls=%async_computation.5 | async-start | bytes 4718592 | tf_op jit(solution)/shard_map/all_to_all | solution.py:1006
  548.6 32.1 %collective-permute-start.52 = (bf16[128,2048]{1,0:T(8,128)(2,1)S(1)}, bf16[128,2048]{1,0:T(8,128)(2,1)S(1)}, u32[]{:S(2)}, u32[]{:S(2)}) collective-permute-start(bf16[128,2048]{1,0:T(8,128)(2,1)S(1)} %dynamic-slice_bitcast_fusion), channel_id=1, source_target_pairs={{0,66},{2,64},{64,2},{66,0},{1,67},{3,65},{65,3},{67,1},{4,70},{6,... | collective-permute-start | bytes 1572872 | tf_op jit(solution)/shard_map/ppermute | solution.py:1102
  550.2 44.7 %collective-permute-start.50 = (bf16[256,2048]{1,0:T(8,128)(2,1)S(1)}, bf16[256,2048]{1,0:T(8,128)(2,1)S(1)}, u32[]{:S(2)}, u32[]{:S(2)}) collective-permute-start(bf16[256,2048]{1,0:T(8,128)(2,1)S(1)} %pad_maximum_fusion.4), channel_id=1, source_target_pairs={{0,16},{16,32},{32,48},{48,0},{1,17},{17,33},{33,49},{49,1},{2,18}... | collective-permute-start | bytes 3145736 | tf_op jit(solution)/shard_map/ppermute | solution.py:41
  560.4 36.3 %collective-permute-start.48 = (bf16[256,2048]{1,0:T(8,128)(2,1)S(1)}, bf16[256,2048]{1,0:T(8,128)(2,1)}, u32[]{:S(2)}, u32[]{:S(2)}) collective-permute-start(bf16[256,2048]{1,0:T(8,128)(2,1)S(1)} %pad_maximum_fusion.3), channel_id=1, source_target_pairs={{0,48},{16,0},{32,16},{48,32},{1,49},{17,1},{33,17},{49,33},{2,50}... | collective-permute-start | bytes 3145736 | tf_op jit(solution)/shard_map/ppermute | solution.py:41
  599.8 33.9 %collective-permute-start.59 = (bf16[128,2048]{1,0:T(8,128)(2,1)}, bf16[128,2048]{1,0:T(8,128)(2,1)}, u32[]{:S(2)}, u32[]{:S(2)}) collective-permute-start(bf16[128,2048]{1,0:T(8,128)(2,1)} %add_convert_fusion.3.refs_0_), channel_id=1, source_target_pairs={{0,32},{16,48},{32,0},{48,16},{1,33},{17,49},{33,1},{49,17},{2,34}... | collective-permute-start | bytes 1572872 | tf_op jit(solution)/shard_map/ppermute | solution.py:41
  601.0 32.7 %collective-permute-start.60 = (bf16[128,2048]{1,0:T(8,128)(2,1)}, bf16[128,2048]{1,0:T(8,128)(2,1)}, u32[]{:S(2)}, u32[]{:S(2)}) collective-permute-start(bf16[128,2048]{1,0:T(8,128)(2,1)} %add_convert_fusion.3.refs_0_), channel_id=1, source_target_pairs={{0,48},{16,0},{32,16},{48,32},{1,49},{17,1},{33,17},{49,33},{2,50}... | collective-permute-start | bytes 1572872 | tf_op jit(solution)/shard_map/ppermute | solution.py:41
  (97 other events, 1283.9 us)
Sparse Core Ops, SparseCore 0:
  11.1 62.2 all-gather.2
  75.8 147.3 all-gather.4
  332.1 146.5 reduce-scatter.1

commit v9 on v7

--- a/solution.py
+++ b/solution.py
@@ -84,11 +84,15 @@
         total[...] += jnp.sum(weights, axis=0, keepdims=True)
         acc[...] += jnp.dot(v_t[at], weights.astype(low), preferred_element_type=jnp.float32)
 
-    @pl.loop(0, jnp.minimum(tile, PROMPT_TILES))
-    def _(at):
-        chunk(at, False)
-
-    chunk(tile, True)
+    full = jnp.minimum(tile, PROMPT_TILES)
+    for count in range(PROMPT_TILES + 1):
+
+        @pl.when(full == count)
+        def _(count=count):
+            for at in range(count):
+                chunk(at, False)
+            chunk(tile, True)
+
     mixed_t = acc[...] / total[...]
     mixed_t_ref[0] = mixed_t
     log_ref[0] = jnp.log2(total[...])
@@ -192,11 +196,15 @@
         k_acc[rows, :] += jnp.dot(score_grads, queries, preferred_element_type=jnp.float32)
         q_acc[...] += jnp.dot(k_t[at], score_grads, preferred_element_type=jnp.float32)
 
-    @pl.loop(0, jnp.minimum(tile, PROMPT_TILES))
-    def _(at):
-        chunk(at, False)
-
-    chunk(tile, True)
+    full = jnp.minimum(tile, PROMPT_TILES)
+    for count in range(PROMPT_TILES + 1):
+
+        @pl.when(full == count)
+        def _(count=count):
+            for at in range(count):
+                chunk(at, False)
+            chunk(tile, True)
+
     query_grad = (q_acc[...] * score_scale).T.astype(low)
     q_out[order[2 * tile], 0] = query_grad[:BLOCK]
     q_out[order[2 * tile + 1], 0] = query_grad[BLOCK:]
@@ -1002,8 +1010,13 @@
     def pair_sum(keep, come):
         return (keep.astype(f32) + come.astype(f32)).astype(low)
 
-    def to_owners(pair):
-        return lax.all_to_all(pair, ("y", "x_hi"), 0, 0, tiled=True)
+    def along_y(pair):
+        return lax.all_to_all(pair.reshape(RING, 2, 128, pair.shape[2]), "y", 0, 0, tiled=True)
+
+    def along_x(halves):
+        keep = lax.dynamic_index_in_dim(halves, x_at, 0, keepdims=False)
+        give = lax.dynamic_index_in_dim(halves, 1 - x_at, 0, keepdims=False)
+        return keep, lax.ppermute(give, ("x_lo", "x_hi"), [(i, 3 - i) for i in range(4)])
 
     def add_up(terms):
         return jnp.sum(terms.astype(f32), axis=0).astype(low)
@@ -1071,7 +1084,7 @@
     )
     returned, both_share, down_sum = together(returned, both_share, down_sum)
     both_pair = over_x(both_share)
-    down_terms = to_owners(down_sum)
+    down_terms = along_y(down_sum)
     qkv_grad, qkv_keep, qkv_give, query_gain_part, key_gain_part = first_back(
         core_at, returned, qkv_pre, cosine, sine, query_row, key_row, first_in
     )
@@ -1091,15 +1104,15 @@
         query_gain_part,
         key_gain_part,
     )
-    first_parts, gains_give, qkv_come, both_left, both_right, both_sum, down_terms = together(
-        first_parts, gains_give, qkv_come, both_left, both_right, both_sum, down_terms
-    )
-    down_pair = over_x(add_up(down_terms))
+    first_parts, gains_give, qkv_come, both_left, both_right, both_sum = together(
+        first_parts, gains_give, qkv_come, both_left, both_right, both_sum
+    )
+    down_pair = over_x(pair_sum(*along_x(add_up(down_terms))))
     gains_come = shift(gains_give, "core", 1, 2)
     first_own, left_a, left_b, first_top, first_bottom, right_a, right_b = first_parts
     first_top = shift(first_top, "z", 3)
     first_bottom = shift(first_bottom, "z", 1)
-    qkv_terms = to_owners(pair_sums(qkv_keep, qkv_come, gains_keep, gains_come))
+    qkv_terms = along_y(pair_sums(qkv_keep, qkv_come, gains_keep, gains_come))
     first_left = send_back(jnp.concatenate([pair_sum(left_a, first_top), left_b], axis=0), 1)
     first_right = send_back(jnp.concatenate([right_a, pair_sum(right_b, first_bottom)], axis=0), 3)
     both_opposite = shift(both_sum, "z", 2)
@@ -1107,7 +1120,7 @@
         qkv_terms, first_left, first_right, both_opposite, down_pair
     )
     down_blocks = over_z(down_pair)
-    qkv_share = add_up(qkv_terms)
+    qkv_share = pair_sum(*along_x(add_up(qkv_terms)))
     both_blocks = [both_sum, both_left, both_opposite, both_right]
     qkv_pair = over_x(qkv_share)
     output = (

time: 702 us -> 653 us (0.930)
  waiting for transfers between devices: 240 us -> 193 us
    ppermute x60, waiting for transfers between devices: 210 us -> 159 us  [shift(): lax.ppermute(values, axis, [(i, (i + by) % size) for i in range(size)])]
  transfers between devices with their start and end apart: 69 -> 71, of which waited for: 31 -> 33; matrix products, arithmetic and copies ran while one was open for 10% -> 11% of each run, Pallas kernels for 33% -> 34%
where the time goes in v9:
time: 653 us; the launch traced here: 640 us
  Pallas kernels  221 us (34%)
  waiting for transfers between devices  193 us (30%)
  starting transfers between devices  125 us (19%)
  other arithmetic  35.2 us (5%)
  local copies, waits for them, and re-layouts  31.1 us (5%)
  matrix products  19.4 us (3%)
  between operations  14.7 us (2%)
    ppermute x60, waiting for transfers between devices, shift(): lax.ppermute(values, axis, [(i, (i + by) % size) for i in range(size)])  159 us
    ppermute x60, starting transfers between devices, shift(): lax.ppermute(values, axis, [(i, (i + by) % size) for i in range(size)])  88.4 us
    pallas_call x3, Pallas kernels, mlp_blocks(): pl.pallas_call(functools.partial(mlp_kernel, len(seconds), len(cots)), gr...  58 us
    pallas_call x1, Pallas kernels, attention_backward(): pl.pallas_call(backward_kernel, out_shape=(jax.ShapeDtypeStruct((BLOCKS,...  32 us
    all_to_all x4, waiting for transfers between devices, to_heads(): return lax.all_to_all(send, GROUP_AXES, 0, 0, tiled=True)  31.6 us
    all_to_all x4, starting transfers between devices, to_heads(): return lax.all_to_all(send, GROUP_AXES, 0, 0, tiled=True)  26.9 us
    pallas_call x2, Pallas kernels, pair_grad(): pl.pallas_call(kernel, grid=(width // 256,), in_specs=[pl.BlockSpec(memor...  21.6 us
    dot_general x1, matrix products, local(): lax.dot_general(second_all.reshape(ring_rows, width), both_grad.reshape(r...  19.4 us
  transfers between devices with their start and end apart: 71, of which 33 were waited for; matrix products, arithmetic and copies ran while one was open for 11% of the time, Pallas kernels for 34%

profile of v9, /device:TPU:4, one launch (start us, length us, event | category | flops | bytes accessed | tf_op | source)
XLA Modules:
  0.0 640.2 jit_solution(3851720561349238734)
XLA Ops:
  75.9 12.0 %shard_map.246 = (bf16[4,256,2048]{2,1,0:T(8,128)(2,1)}, bf16[4,256,2048]{2,1,0:T(8,128)(2,1)}, f32[4,256,1024]{2,1,0:T(8,128)}, bf16[16,2,256,128]{3,2,1,0:T(8,128)(2,1)}, f32[8,2048]{1,0:T(8,128)}) custom-call(bf16[256,2048]{1,0:T(8,128)(2,1)} %refs_8_.1, bf16[256,2048]{1,0:T(8,128)(2,1)} %copy-done.46, bf16[128,2048]{1,0:T(8,128)(2,1)} %collective-permute-done.9.top_ref, ...), custom_call_target="tpu_custom_call" | custom-call | flops 4294967296 | bytes 20971520 | tf_op jit(solution)/shard_map/pallas_call | solution.py:577
  87.9 7.6 %all-to-all-start = ((bf16[16,2,256,128]{3,2,1,0:T(8,128)(2,1)}), bf16[16,2,256,128]{3,2,1,0:T(8,128)(2,1)}, u32[]{:S(2)}, u32[]{:S(2)}) async-start(bf16[16,2,256,128]{3,2,1,0:T(8,128)(2,1)} %get-tuple-element.183), calls=%async_computation | async-start | bytes 4194304 | tf_op jit(solution)/shard_map/all_to_all | solution.py:819
  95.5 25.3 %collective-permute-done.12.refs_5_ = bf16[2048,512]{1,0:T(8,128)(2,1)S(1)} collective-permute-done((bf16[2048,512]{1,0:T(8,128)(2,1)}, bf16[2048,512]{1,0:T(8,128)(2,1)S(1)}, u32[]{:S(2)}, u32[]{:S(2)}) %collective-permute-start.12) | collective-permute-done | bytes 2097184 | tf_op jit(solution)/shard_map/ppermute | solution.py:41
  120.8 12.0 %all-to-all-done.own_a.own_b = bf16[16,2,256,128]{3,2,1,0:T(8,128)(2,1)} async-done(((bf16[16,2,256,128]{3,2,1,0:T(8,128)(2,1)}), bf16[16,2,256,128]{3,2,1,0:T(8,128)(2,1)}, u32[]{:S(2)}, u32[]{:S(2)}) %all-to-all-start) | async-done | bytes 2097184 | tf_op jit(solution)/shard_map/all_to_all | solution.py:819
  142.7 18.0 %shard_map.248 = (bf16[16,256,128]{2,1,0:T(8,128)(2,1)}, f32[8,128,512]{2,1,0:T(8,128)}, f32[8,1,512]{2,1,0:T(1,128)}) custom-call(s32[16]{0:T(128)} %dynamic-slice_bitcast_fusion.2.order, s32[1]{0:T(128)} %bitcast.1.core.core_ref, bf16[16,2,256,128]{3,2,1,0:T(8,128)(2,1)} %all-to-all-done.own_a.own_b, bf16[16,2,256,128]{3,2,1,0:T(8,128)(2,1)} %all-to-all-done.own_a.own_b, ...), custom_call_target="tpu_custom_call" | custom-call | flops 1024 | bytes 1024 | tf_op jit(solution)/shard_map/pallas_call | solution.py:121
  173.0 17.1 %collective-permute-done.17.refs_2_ = bf16[256,2048]{1,0:T(8,128)(2,1)S(1)} collective-permute-done((bf16[256,2048]{1,0:T(8,128)(2,1)S(1)}, bf16[256,2048]{1,0:T(8,128)(2,1)S(1)}, u32[]{:S(2)}, u32[]{:S(2)}) %collective-permute-start.17) | collective-permute-done | bytes 1048608 | tf_op jit(solution)/shard_map/ppermute | solution.py:41
  197.2 7.9 %collective-permute-done.19.refs_1_ = bf16[128,2048]{1,0:T(8,128)(2,1)} collective-permute-done((bf16[128,2048]{1,0:T(8,128)(2,1)}, bf16[128,2048]{1,0:T(8,128)(2,1)}, u32[]{:S(2)}, u32[]{:S(2)}) %collective-permute-start.19) | collective-permute-done | bytes 524320 | tf_op jit(solution)/shard_map/ppermute | solution.py:41
  231.5 15.7 %shard_map.250 = (bf16[4,256,1536]{2,1,0:T(8,128)(2,1)}, bf16[4,256,3072]{2,1,0:T(8,128)(2,1)}, bf16[4,256,2048]{2,1,0:T(8,128)(2,1)}, bf16[4,256,2048]{2,1,0:T(8,128)(2,1)}, bf16[256,2048]{1,0:T(8,128)(2,1)}) custom-call(bf16[256,2048]{1,0:T(8,128)(2,1)} %get-tuple-element.234.refs_0_, bf16[256,2048]{1,0:T(8,128)(2,1)} %refs_9_.1, ...), custom_call_target="tpu_custom_call" | custom-call | flops 8053063680 | bytes 18874368 | tf_op jit(solution)/shard_map/pallas_call | solution.py:326
  255.8 26.6 %shard_map.251 = (bf16[4,256,1536]{2,1,0:T(8,128)(2,1)}, bf16[4,256,3072]{2,1,0:T(8,128)(2,1)}, bf16[4,256,2048]{2,1,0:T(8,128)(2,1)}, bf16[4,256,2048]{2,1,0:T(...) custom-call(bf16[256,2048]{1,0:T(8,128)(2,1)} %copy-done.28, ...), custom_call_target="tpu_custom_call", output_to_operand_aliasing={{0}: (6, {}), {1}: (7, {}), {2}: (8, {}), {3}: (9, {})} | custom-call | flops 16106127360 | bytes 18874368 | tf_op jit(solution)/shard_map/pallas_call | solution.py:326
  285.6 15.6 %shard_map.252 = (bf16[4,256,1536]{2,1,0:T(8,128)(2,1)}, bf16[4,256,3072]{2,1,0:T(8,128)(2,1)}, bf16[4,256,2048]{2,1,0:T(8,128)(2,1)}, bf16[4,256,2048]{2,1,0:T(8,128)(2,1)}, bf16[256,2048]{1,0:T(8,128)(2,1)}) custom-call(bf16[256,2048]{1,0:T(8,128)(2,1)} %copy-done.27, ...), custom_call_target="tpu_custom_call", output_to_operand_aliasing={{0}: (5, {}), {1}: (6, {}), {2}: (7, {}), {3}: (8, {})} | custom-call | flops 8053063680 | bytes 18874368 | tf_op jit(solution)/shard_map/pallas_call | solution.py:326
  302.6 19.4 %bitcast_convert_fusion = bf16[2048,3072]{1,0:T(8,128)(2,1)} fusion(bf16[4,256,2048]{2,1,0:T(8,128)(2,1)} %get-tuple-element.243, bf16[4,256,3072]{2,1,0:T(8,128)(2,1)} %get-tuple-element.244), kind=kOutput, calls=%fused_computation | convolution fusion | flops 12891193344 | bytes 23068672 | tf_op jit(solution)/shard_map/dot_general | solution.py:1031
  322.0 8.0 %collective-permute-done.27.refs_2_ = bf16[256,2048]{1,0:T(8,128)(2,1)} collective-permute-done((bf16[256,2048]{1,0:T(8,128)(2,1)}, bf16[256,2048]{1,0:T(8,128)(2,1)}, u32[]{:S(2)}, u32[]{:S(2)}) %collective-permute-start.27) | collective-permute-done | bytes 1048608 | tf_op jit(solution)/shard_map/ppermute | solution.py:41
  330.0 12.5 %shard_map.253 = (f32[256,2048]{1,0:T(8,128)}, bf16[256,2048]{1,0:T(8,128)(2,1)}, f32[1,2048]{1,0:T(1,128)}, bf16[4,256,128]{2,1,0:T(8,128)(2,1)}, bf16[4,256,12...) custom-call(bf16[256,2048]{1,0:T(8,128)(2,1)} %get-tuple-element.219.refs_0_, ...), custom_call_target="tpu_custom_call" | custom-call | flops 1024 | bytes 1024 | tf_op jit(solution)/shard_map/pallas_call | solution.py:511
  346.4 13.0 %shard_map.254 = (bf16[8,128,1536]{2,1,0:T(8,128)(2,1)}, bf16[8,128,1536]{2,1,0:T(8,128)(2,1)}) custom-call(s32[1]{0:T(128)} %bitcast.1.core.core_ref, bf16[4,256,2048]{2,1,0:T(8,128)(2,1)} %get-tuple-element.253.refs_0_, bf16[4,256,1536]{2,1,0:T(8,128)(2,1)} %get-tuple-element.258.refs_1_.inner_ref), custom_call_target="tpu_custom_call" | custom-call | flops 1024 | bytes 1024 | tf_op jit(solution)/shard_map/pallas_call | solution.py:418
  368.7 10.6 %shard_map.255 = (bf16[256,2048]{1,0:T(8,128)(2,1)}, bf16[256,2048]{1,0:T(8,128)(2,1)}, bf16[256,2048]{1,0:T(8,128)(2,1)}, bf16[256,2048]{1,0:T(8,128)(2,1)}) custom-call(bf16[4,256,1536]{2,1,0:T(8,128)(2,1)} %get-tuple-element.258.refs_1_.inner_ref, bf16[2048,4608]{1,0:T(8,128)(2,1)} %all-gather.5.cloned.1.call-done.refs_2_.refs_3_.refs_4_.refs_5_.weight_ref), custom_call_target="tpu_custom_call" | custom-call | flops 1024 | bytes 1024 | tf_op jit(solution)/shard_map/pallas_call | solution.py:368
  379.3 13.5 %all-to-all-done.2.grad_a.grad_b = bf16[16,256,128]{2,1,0:T(8,128)(2,1)S(1)} async-done(((bf16[16,256,128]{2,1,0:T(8,128)(2,1)}), bf16[16,256,128]{2,1,0:T(8,128)(2,1)S(1)}, u32[]{:S(2)}, u32[]{:S(2)}) %all-to-all-start.2) | async-done | bytes 1048608 | tf_op jit(solution)/shard_map/all_to_all | solution.py:819
  394.9 32.0 %shard_map.256 = (bf16[16,2,256,128]{3,2,1,0:T(8,128)(2,1)}, bf16[16,256,128]{2,1,0:T(8,128)(2,1)}, bf16[16,256,128]{2,1,0:T(8,128)(2,1)}) custom-call(s32[16]{0:T(128)} %dynamic-slice_bitcast_fusion.2.order, s32[1]{0:T(128)} %bitcast.1.core.core_ref, bf16[16,2,256,128]{3,2,1,0:T(8,128)(2,1)} %all-to-all-done.own_a.own_b, ...), custom_call_target="tpu_custom_call" | custom-call | flops 1024 | bytes 1024 | tf_op jit(solution)/shard_map/pallas_call | solution.py:232
  433.0 9.1 %all-to-all-start.3 = ((bf16[16,2,256,128]{3,2,1,0:T(8,128)(2,1)}), bf16[16,2,256,128]{3,2,1,0:T(8,128)(2,1)S(1)}, u32[]{:S(2)}, u32[]{:S(2)}) async-start(bf16[16,2,256,128]{3,2,1,0:T(8,128)(2,1)} %fusion.9), calls=%async_computation.3 | async-start | bytes 4194304 | tf_op jit(solution)/shard_map/all_to_all | solution.py:819
  442.1 12.5 %collective-permute-done.39.refs_2_ = bf16[256,2048]{1,0:T(8,128)(2,1)} collective-permute-done((bf16[256,2048]{1,0:T(8,128)(2,1)}, bf16[256,2048]{1,0:T(8,128)(2,1)}, u32[]{:S(2)}, u32[]{:S(2)}) %collective-permute-start.39) | collective-permute-done | bytes 1048608 | tf_op jit(solution)/shard_map/ppermute | solution.py:41
  454.5 8.5 %shard_map.257 = (bf16[8,128,512]{2,1,0:T(8,128)(2,1)}, bf16[8,128,512]{2,1,0:T(8,128)(2,1)}) custom-call(s32[1]{0:T(128)} %bitcast.1.core.core_ref, bf16[256,2048]{1,0:T(8,128)(2,1)} %get-tuple-element.287.refs_0_, bf16[256,2048]{1,0:T(8,128)(2,1)} %collective-permute-done.33.refs_1_, bf16[256,2048]{1,0:T(8,128)(2,1)} %collective-permute-done.39.refs_2_, ...), custom_call_target="tpu_custom_call" | custom-call | flops 1024 | bytes 1024 | tf_op jit(solution)/shard_map/pallas_call | solution.py:418
  485.4 15.0 %shard_map.259 = (bf16[4,256,1024]{2,1,0:T(8,128)(2,1)}, bf16[8,128,1024]{2,1,0:T(8,128)(2,1)}, bf16[8,128,1024]{2,1,0:T(8,128)(2,1)}, f32[1,128]{1,0:T(1,128)}, f32[1,128]{1,0:T(1,128)}) custom-call(s32[1]{0:T(128)} %bitcast.1.core.core_ref, bf16[16,2,256,128]{3,2,1,0:T(8,128)(2,1)} %copy-done.13, f32[4,256,1024]{2,1,0:T(8,128)} %get-tuple-element.293.pre_ref, ...), custom_call_target="tpu_custom_call" | custom-call | flops 1024 | bytes 1024 | tf_op jit(solution)/shard_map/pallas_call | solution.py:664
  506.2 12.6 %shard_map.260 = (bf16[256,2048]{1,0:T(8,128)(2,1)}, bf16[128,2048]{1,0:T(8,128)(2,1)}, bf16[128,2048]{1,0:T(8,128)(2,1)}, bf16[128,2048]{1,0:T(8,128)(2,1)}, bf...) custom-call(s32[1]{0:T(128)} %bitcast.1.core.core_ref, ...), custom_call_target="tpu_custom_call" | custom-call | flops 1024 | bytes 1024 | tf_op jit(solution)/shard_map/pallas_call | solution.py:749
  546.9 10.4 %collective-permute-done.47 = bf16[128,2048]{1,0:T(8,128)(2,1)} collective-permute-done((bf16[128,2048]{1,0:T(8,128)(2,1)}, bf16[128,2048]{1,0:T(8,128)(2,1)}, u32[]{:S(2)}, u32[]{:S(2)}) %collective-permute-start.47) | collective-permute-done | bytes 524320 | tf_op jit(solution)/shard_map/ppermute | solution.py:41
  566.4 9.6 %collective-permute-done.53 = bf16[128,2048]{1,0:T(8,128)(2,1)S(1)} collective-permute-done((bf16[128,2048]{1,0:T(8,128)(2,1)S(1)}, bf16[128,2048]{1,0:T(8,128)(2,1)S(1)}, u32[]{:S(2)}, u32[]{:S(2)}) %collective-permute-start.53) | collective-permute-done | bytes 524320 | tf_op jit(solution)/shard_map/ppermute | solution.py:41
  (315 shorter events, 280.7 us)
Async XLA Ops:
  7.2 68.7 %all-gather.3.cloned.1.call-start = ((), (), s32[]{:S(2)}) async-start(), calls=%async_computation.7 | async-start | bytes 5013504 | tf_op jit(solution)/shard_map/all_gather | solution.py:905
  10.9 220.6 %all-gather.5.cloned.1.call-start = ((), (), s32[]{:S(2)}) async-start(), calls=%async_computation.8 | async-start | bytes 20054016 | tf_op jit(solution)/shard_map/all_gather | solution.py:905
  72.6 48.2 %collective-permute-start.12 = (bf16[2048,512]{1,0:T(8,128)(2,1)}, bf16[2048,512]{1,0:T(8,128)(2,1)S(1)}, u32[]{:S(2)}, u32[]{:S(2)}) collective-permute-start(bf16[2048,512]{1,0:T(8,128)(2,1)} %shard_map.247.refs_4_), channel_id=1, source_target_pairs={{0,16},{16,32},{32,48},{48,0},{1,17},{17,33},{33,49},{49,1},{2,18}... | collective-permute-start | bytes 6291464 | tf_op jit(solution)/shard_map/ppermute | solution.py:41
  72.6 48.2 %collective-permute-start.13 = (bf16[2048,512]{1,0:T(8,128)(2,1)}, bf16[2048,512]{1,0:T(8,128)(2,1)}, u32[]{:S(2)}, u32[]{:S(2)}) collective-permute-start(bf16[2048,512]{1,0:T(8,128)(2,1)} %shard_map.247.refs_4_), channel_id=1, source_target_pairs={{0,48},{16,0},{32,16},{48,32},{1,49},{17,1},{33,17},{49,33},{2,50}... | collective-permute-start | bytes 6291464 | tf_op jit(solution)/shard_map/ppermute | solution.py:41
  87.9 45.0 %all-to-all-start = ((bf16[16,2,256,128]{3,2,1,0:T(8,128)(2,1)}), bf16[16,2,256,128]{3,2,1,0:T(8,128)(2,1)}, u32[]{:S(2)}, u32[]{:S(2)}) async-start(bf16[16,2,256,128]{3,2,1,0:T(8,128)(2,1)} %get-tuple-element.183), calls=%async_computation | async-start | bytes 4194304 | tf_op jit(solution)/shard_map/all_to_all | solution.py:819
  167.6 29.6 %all-to-all-start.1 = ((bf16[16,256,128]{2,1,0:T(8,128)(2,1)}), bf16[16,256,128]{2,1,0:T(8,128)(2,1)S(1)}, u32[]{:S(2)}, u32[]{:S(2)}) async-start(bf16[16,256,128]{2,1,0:T(8,128)(2,1)} %get-tuple-element.195), calls=%async_computation.1 | async-start | bytes 2097152 | tf_op jit(solution)/shard_map/all_to_all | solution.py:819
  173.0 305.9 %reduce-scatter.2.cloned.1.call-start = ((), (), s32[]{:S(2)}) async-start(), calls=%async_computation.9 | async-start | bytes 13369344 | tf_op jit(solution)/shard_map/reduce_scatter | solution.py:1040
  252.4 32.3 %collective-permute-start.28 = (bf16[256,2048]{1,0:T(8,128)(2,1)}, bf16[256,2048]{1,0:T(8,128)(2,1)S(1)}, u32[]{:S(2)}, u32[]{:S(2)}) collective-permute-start(bf16[256,2048]{1,0:T(8,128)(2,1)} %get-tuple-element.234.refs_0_), channel_id=1, source_target_pairs={{0,32},{16,48},{32,0},{48,16},{1,33},{17,49},{33,1},{49,17},{2,34}... | collective-permute-start | bytes 3145736 | tf_op jit(solution)/shard_map/ppermute | solution.py:41
  282.4 39.5 %collective-permute-start.26 = (bf16[256,2048]{1,0:T(8,128)(2,1)}, bf16[256,2048]{1,0:T(8,128)(2,1)S(1)}, u32[]{:S(2)}, u32[]{:S(2)}) collective-permute-start(bf16[256,2048]{1,0:T(8,128)(2,1)} %get-tuple-element.228), channel_id=1, source_target_pairs={{0,48},{16,0},{32,16},{48,32},{1,49},{17,1},{33,17},{49,33},{2,50}... | collective-permute-start | bytes 3145736 | tf_op jit(solution)/shard_map/ppermute | solution.py:41
  283.4 46.6 %collective-permute-start.27 = (bf16[256,2048]{1,0:T(8,128)(2,1)}, bf16[256,2048]{1,0:T(8,128)(2,1)}, u32[]{:S(2)}, u32[]{:S(2)}) collective-permute-start(bf16[256,2048]{1,0:T(8,128)(2,1)} %get-tuple-element.229), channel_id=1, source_target_pairs={{0,16},{16,32},{32,48},{48,0},{1,17},{17,33},{33,49},{49,1},{2,18}... | collective-permute-start | bytes 3145736 | tf_op jit(solution)/shard_map/ppermute | solution.py:41
  359.5 33.4 %collective-permute-start.33 = (bf16[256,2048]{1,0:T(8,128)(2,1)S(1)}, bf16[256,2048]{1,0:T(8,128)(2,1)}, u32[]{:S(2)}, u32[]{:S(2)}) collective-permute-start(bf16[256,2048]{1,0:T(8,128)(2,1)S(1)} %copy-done.34), channel_id=1, source_target_pairs={{0,16},{16,32},{32,48},{48,0},{1,17},{17,33},{33,49},{49,1},{2,18}... | collective-permute-start | bytes 3145736 | tf_op jit(solution)/shard_map/ppermute | solution.py:41
  359.8 33.0 %collective-permute-start.34 = (bf16[256,2048]{1,0:T(8,128)(2,1)S(1)}, bf16[256,2048]{1,0:T(8,128)(2,1)}, u32[]{:S(2)}, u32[]{:S(2)}) collective-permute-start(bf16[256,2048]{1,0:T(8,128)(2,1)S(1)} %copy-done.34), channel_id=1, source_target_pairs={{0,48},{16,0},{32,16},{48,32},{1,49},{17,1},{33,17},{49,33},{2,50}... | collective-permute-start | bytes 3145736 | tf_op jit(solution)/shard_map/ppermute | solution.py:41
  363.9 28.9 %all-to-all-start.2 = ((bf16[16,256,128]{2,1,0:T(8,128)(2,1)}), bf16[16,256,128]{2,1,0:T(8,128)(2,1)S(1)}, u32[]{:S(2)}, u32[]{:S(2)}) async-start(bf16[16,256,128]{2,1,0:T(8,128)(2,1)} %pad_maximum_fusion.2), calls=%async_computation.2 | async-start | bytes 2097152 | tf_op jit(solution)/shard_map/all_to_all | solution.py:819
  392.8 34.1 %collective-permute-start.35 = (bf16[256,2048]{1,0:T(8,128)(2,1)}, bf16[256,2048]{1,0:T(8,128)(2,1)S(1)}, u32[]{:S(2)}, u32[]{:S(2)}) collective-permute-start(bf16[256,2048]{1,0:T(8,128)(2,1)} %get-tuple-element.274), channel_id=1, source_target_pairs={{0,48},{16,0},{32,16},{48,32},{1,49},{17,1},{33,17},{49,33},{2,50}... | collective-permute-start | bytes 3145736 | tf_op jit(solution)/shard_map/ppermute | solution.py:41
  392.9 34.1 %collective-permute-start.36 = (bf16[256,2048]{1,0:T(8,128)(2,1)}, bf16[256,2048]{1,0:T(8,128)(2,1)}, u32[]{:S(2)}, u32[]{:S(2)}) collective-permute-start(bf16[256,2048]{1,0:T(8,128)(2,1)} %get-tuple-element.275), channel_id=1, source_target_pairs={{0,16},{16,32},{32,48},{48,0},{1,17},{17,33},{33,49},{49,1},{2,18}... | collective-permute-start | bytes 3145736 | tf_op jit(solution)/shard_map/ppermute | solution.py:41
  427.1 39.0 %collective-permute-start.38 = (bf16[8,128,1536]{2,1,0:T(8,128)(2,1)}, bf16[8,128,1536]{2,1,0:T(8,128)(2,1)}, u32[]{:S(2)}, u32[]{:S(2)}) collective-permute-start(bf16[8,128,1536]{2,1,0:T(8,128)(2,1)} %get-tuple-element.286), channel_id=1, source_target_pairs={{0,1},{1,0},{2,3},{3,2},{4,5},{5,4},{6,7},{7,6},{8,9},{9,8},{10,11... | collective-permute-start | bytes 9437192 | tf_op jit(solution)/shard_map/ppermute | solution.py:41
  433.0 44.3 %all-to-all-start.3 = ((bf16[16,2,256,128]{3,2,1,0:T(8,128)(2,1)}), bf16[16,2,256,128]{3,2,1,0:T(8,128)(2,1)S(1)}, u32[]{:S(2)}, u32[]{:S(2)}) async-start(bf16[16,2,256,128]{3,2,1,0:T(8,128)(2,1)} %fusion.9), calls=%async_computation.3 | async-start | bytes 4194304 | tf_op jit(solution)/shard_map/all_to_all | solution.py:819
  463.1 37.4 %collective-permute-start.42 = (bf16[256,2048]{1,0:T(8,128)(2,1)}, bf16[256,2048]{1,0:T(8,128)(2,1)}, u32[]{:S(2)}, u32[]{:S(2)}) collective-permute-start(bf16[256,2048]{1,0:T(8,128)(2,1)} %get-tuple-element.299), channel_id=1, source_target_pairs={{0,32},{16,48},{32,0},{48,16},{1,33},{17,49},{33,1},{49,17},{2,34}... | collective-permute-start | bytes 3145736 | tf_op jit(solution)/shard_map/ppermute | solution.py:41
  480.6 53.2 %all-to-all-start.5 = ((bf16[4,2,128,2048]{3,2,1,0:T(8,128)(2,1)}), bf16[4,2,128,2048]{3,2,1,0:T(8,128)(2,1)}, u32[]{:S(2)}, u32[]{:S(2)}) async-start(bf16[4,2,128,2048]{3,2,1,0:T(8,128)(2,1)} %bitcast.44), calls=%async_computation.6 | async-start | bytes 8388608 | tf_op jit(solution)/shard_map/all_to_all | solution.py:1014
  525.5 31.9 %collective-permute-start.47 = (bf16[128,2048]{1,0:T(8,128)(2,1)}, bf16[128,2048]{1,0:T(8,128)(2,1)}, u32[]{:S(2)}, u32[]{:S(2)}) collective-permute-start(bf16[128,2048]{1,0:T(8,128)(2,1)} %get-tuple-element.324), channel_id=1, source_target_pairs={{0,48},{16,0},{32,16},{48,32},{1,49},{17,1},{33,17},{49,33},{2,50}... | collective-permute-start | bytes 1572872 | tf_op jit(solution)/shard_map/ppermute | solution.py:41
  528.3 38.1 %collective-permute-start.51 = (bf16[128,3072]{1,0:T(8,128)(2,1)}, bf16[128,3072]{1,0:T(8,128)(2,1)}, u32[]{:S(2)}, u32[]{:S(2)}) collective-permute-start(bf16[128,3072]{1,0:T(8,128)(2,1)} %add_convert_fusion.2.refs_0_), channel_id=1, source_target_pairs={{0,32},{16,48},{32,0},{48,16},{1,33},{17,49},{33,1},{49,17},{2,34}... | collective-permute-start | bytes 2359304 | tf_op jit(solution)/shard_map/ppermute | solution.py:41
  533.8 51.0 %all-to-all-start.4 = ((bf16[4,2,128,1152]{3,2,1,0:T(8,128)(2,1)}), bf16[4,2,128,1152]{3,2,1,0:T(8,128)(2,1)S(1)}, u32[]{:S(2)}, u32[]{:S(2)}) async-start(bf16[4,2,128,1152]{3,2,1,0:T(8,128)(2,1)} %bitcast.45), calls=%async_computation.5 | async-start | bytes 4718592 | tf_op jit(solution)/shard_map/all_to_all | solution.py:1014
  545.5 34.2 %collective-permute-start.50 = (bf16[256,2048]{1,0:T(8,128)(2,1)S(1)}, bf16[256,2048]{1,0:T(8,128)(2,1)S(1)}, u32[]{:S(2)}, u32[]{:S(2)}) collective-permute-start(bf16[256,2048]{1,0:T(8,128)(2,1)S(1)} %pad_maximum_fusion.4), channel_id=1, source_target_pairs={{0,16},{16,32},{32,48},{48,0},{1,17},{17,33},{33,49},{49,1},{2,18}... | collective-permute-start | bytes 3145736 | tf_op jit(solution)/shard_map/ppermute | solution.py:41
  588.8 29.4 %collective-permute-start.60 = (bf16[128,2048]{1,0:T(8,128)(2,1)S(1)}, bf16[128,2048]{1,0:T(8,128)(2,1)S(1)}, u32[]{:S(2)}, u32[]{:S(2)}) collective-permute-start(bf16[128,2048]{1,0:T(8,128)(2,1)S(1)} %add_convert_fusion.3.refs_0_), channel_id=1, source_target_pairs={{0,32},{16,48},{32,0},{48,16},{1,33},{17,49},{33,1},{49,17},{2,34}... | collective-permute-start | bytes 1572872 | tf_op jit(solution)/shard_map/ppermute | solution.py:41
  (101 other events, 1194.6 us)
Sparse Core Ops, SparseCore 0:
  11.1 62.2 all-gather.2
  75.8 147.3 all-gather.4
  330.1 148.6 reduce-scatter.1

commit v10 on v9

--- a/solution.py
+++ b/solution.py
@@ -1116,16 +1116,13 @@
     first_left = send_back(jnp.concatenate([pair_sum(left_a, first_top), left_b], axis=0), 1)
     first_right = send_back(jnp.concatenate([right_a, pair_sum(right_b, first_bottom)], axis=0), 3)
     both_opposite = shift(both_sum, "z", 2)
-    qkv_terms, first_left, first_right, both_opposite, down_pair = together(
-        qkv_terms, first_left, first_right, both_opposite, down_pair
-    )
     down_blocks = over_z(down_pair)
     qkv_share = pair_sum(*along_x(add_up(qkv_terms)))
     both_blocks = [both_sum, both_left, both_opposite, both_right]
-    qkv_pair = over_x(qkv_share)
+    qkv_pair, down_blocks = together(over_x(qkv_share), down_blocks)
     output = (
         middle
-        + mlp_own.astype(f32)
+        + after(mlp_own, first_top).astype(f32)
         + mlp_left.astype(f32)
         + mlp_right.astype(f32)
         + mlp_opposite.astype(f32)

time: 653 us -> 649 us (level)
  transfers between devices with their start and end apart: 71 -> 71, of which waited for: 33 -> 35; matrix products, arithmetic and copies ran while one was open for 11% -> 11% of each run, Pallas kernels for 34% -> 34%
where the time goes in v10:
time: 649 us; the launch traced here: 638 us
  Pallas kernels  221 us (34%)
  waiting for transfers between devices  198 us (31%)
  starting transfers between devices  121 us (19%)
  other arithmetic  34.6 us (5%)
  local copies, waits for them, and re-layouts  29.8 us (5%)
  matrix products  19.3 us (3%)
  between operations  14.7 us (2%)
    ppermute x60, waiting for transfers between devices, shift(): lax.ppermute(values, axis, [(i, (i + by) % size) for i in range(size)])  163 us
    ppermute x60, starting transfers between devices, shift(): lax.ppermute(values, axis, [(i, (i + by) % size) for i in range(size)])  83.9 us
    pallas_call x3, Pallas kernels, mlp_blocks(): pl.pallas_call(functools.partial(mlp_kernel, len(seconds), len(cots)), gr...  58 us
    pallas_call x1, Pallas kernels, attention_backward(): pl.pallas_call(backward_kernel, out_shape=(jax.ShapeDtypeStruct((BLOCKS,...  32.1 us
    all_to_all x4, waiting for transfers between devices, to_heads(): return lax.all_to_all(send, GROUP_AXES, 0, 0, tiled=True)  31.3 us
    all_to_all x4, starting transfers between devices, to_heads(): return lax.all_to_all(send, GROUP_AXES, 0, 0, tiled=True)  27.5 us
    pallas_call x2, Pallas kernels, pair_grad(): pl.pallas_call(kernel, grid=(width // 256,), in_specs=[pl.BlockSpec(memor...  21.4 us
    dot_general x1, matrix products, local(): lax.dot_general(second_all.reshape(ring_rows, width), both_grad.reshape(r...  19.3 us
  transfers between devices with their start and end apart: 71, of which 35 were waited for; matrix products, arithmetic and copies ran while one was open for 11% of the time, Pallas kernels for 34%

profile of v10, /device:TPU:4, one launch (start us, length us, event | category | flops | bytes accessed | tf_op | source)
XLA Modules:
  0.0 638.5 jit_solution(4478080971043234071)
XLA Ops:
  75.9 12.0 %shard_map.246 = (bf16[4,256,2048]{2,1,0:T(8,128)(2,1)}, bf16[4,256,2048]{2,1,0:T(8,128)(2,1)}, f32[4,256,1024]{2,1,0:T(8,128)}, bf16[16,2,256,128]{3,2,1,0:T(8,128)(2,1)}, f32[8,2048]{1,0:T(8,128)}) custom-call(bf16[256,2048]{1,0:T(8,128)(2,1)} %refs_8_.1, bf16[256,2048]{1,0:T(8,128)(2,1)} %copy-done.50, bf16[128,2048]{1,0:T(8,128)(2,1)} %collective-permute-done.9.top_ref, ...), custom_call_target="tpu_custom_call" | custom-call | flops 4294967296 | bytes 20971520 | tf_op jit(solution)/shard_map/pallas_call | solution.py:577
  95.4 25.4 %collective-permute-done.12.refs_5_ = bf16[2048,512]{1,0:T(8,128)(2,1)S(1)} collective-permute-done((bf16[2048,512]{1,0:T(8,128)(2,1)}, bf16[2048,512]{1,0:T(8,128)(2,1)S(1)}, u32[]{:S(2)}, u32[]{:S(2)}) %collective-permute-start.12) | collective-permute-done | bytes 2097184 | tf_op jit(solution)/shard_map/ppermute | solution.py:41
  120.8 12.0 %all-to-all-done.own_a.own_b = bf16[16,2,256,128]{3,2,1,0:T(8,128)(2,1)} async-done(((bf16[16,2,256,128]{3,2,1,0:T(8,128)(2,1)}), bf16[16,2,256,128]{3,2,1,0:T(8,128)(2,1)}, u32[]{:S(2)}, u32[]{:S(2)}) %all-to-all-start) | async-done | bytes 2097184 | tf_op jit(solution)/shard_map/all_to_all | solution.py:819
  142.7 18.0 %shard_map.248 = (bf16[16,256,128]{2,1,0:T(8,128)(2,1)}, f32[8,128,512]{2,1,0:T(8,128)}, f32[8,1,512]{2,1,0:T(1,128)}) custom-call(s32[16]{0:T(128)} %dynamic-slice_bitcast_fusion.2.order, s32[1]{0:T(128)} %bitcast.1.core.core_ref, bf16[16,2,256,128]{3,2,1,0:T(8,128)(2,1)} %all-to-all-done.own_a.own_b, bf16[16,2,256,128]{3,2,1,0:T(8,128)(2,1)} %all-to-all-done.own_a.own_b, ...), custom_call_target="tpu_custom_call" | custom-call | flops 1024 | bytes 1024 | tf_op jit(solution)/shard_map/pallas_call | solution.py:121
  173.0 17.2 %collective-permute-done.17.refs_2_ = bf16[256,2048]{1,0:T(8,128)(2,1)S(1)} collective-permute-done((bf16[256,2048]{1,0:T(8,128)(2,1)S(1)}, bf16[256,2048]{1,0:T(8,128)(2,1)S(1)}, u32[]{:S(2)}, u32[]{:S(2)}) %collective-permute-start.17) | collective-permute-done | bytes 1048608 | tf_op jit(solution)/shard_map/ppermute | solution.py:41
  197.1 8.1 %collective-permute-done.19.refs_1_ = bf16[128,2048]{1,0:T(8,128)(2,1)} collective-permute-done((bf16[128,2048]{1,0:T(8,128)(2,1)}, bf16[128,2048]{1,0:T(8,128)(2,1)}, u32[]{:S(2)}, u32[]{:S(2)}) %collective-permute-start.19) | collective-permute-done | bytes 524320 | tf_op jit(solution)/shard_map/ppermute | solution.py:41
  230.5 15.7 %shard_map.250 = (bf16[4,256,1536]{2,1,0:T(8,128)(2,1)}, bf16[4,256,3072]{2,1,0:T(8,128)(2,1)}, bf16[4,256,2048]{2,1,0:T(8,128)(2,1)}, bf16[4,256,2048]{2,1,0:T(8,128)(2,1)}, bf16[256,2048]{1,0:T(8,128)(2,1)}) custom-call(bf16[256,2048]{1,0:T(8,128)(2,1)} %get-tuple-element.235.refs_0_, bf16[256,2048]{1,0:T(8,128)(2,1)} %refs_9_.1, ...), custom_call_target="tpu_custom_call" | custom-call | flops 8053063680 | bytes 18874368 | tf_op jit(solution)/shard_map/pallas_call | solution.py:326
  255.8 26.6 %shard_map.251 = (bf16[4,256,1536]{2,1,0:T(8,128)(2,1)}, bf16[4,256,3072]{2,1,0:T(8,128)(2,1)}, bf16[4,256,2048]{2,1,0:T(8,128)(2,1)}, bf16[4,256,2048]{2,1,0:T(...) custom-call(bf16[256,2048]{1,0:T(8,128)(2,1)} %copy-done.26, ...), custom_call_target="tpu_custom_call", output_to_operand_aliasing={{0}: (6, {}), {1}: (7, {}), {2}: (8, {}), {3}: (9, {})} | custom-call | flops 16106127360 | bytes 18874368 | tf_op jit(solution)/shard_map/pallas_call | solution.py:326
  285.7 15.6 %shard_map.252 = (bf16[4,256,1536]{2,1,0:T(8,128)(2,1)}, bf16[4,256,3072]{2,1,0:T(8,128)(2,1)}, bf16[4,256,2048]{2,1,0:T(8,128)(2,1)}, bf16[4,256,2048]{2,1,0:T(8,128)(2,1)}, bf16[256,2048]{1,0:T(8,128)(2,1)}) custom-call(bf16[256,2048]{1,0:T(8,128)(2,1)} %copy-done.25, ...), custom_call_target="tpu_custom_call", output_to_operand_aliasing={{0}: (5, {}), {1}: (6, {}), {2}: (7, {}), {3}: (8, {})} | custom-call | flops 8053063680 | bytes 18874368 | tf_op jit(solution)/shard_map/pallas_call | solution.py:326
  302.7 19.3 %bitcast_convert_fusion = bf16[2048,3072]{1,0:T(8,128)(2,1)} fusion(bf16[4,256,2048]{2,1,0:T(8,128)(2,1)} %get-tuple-element.244, bf16[4,256,3072]{2,1,0:T(8,128)(2,1)} %get-tuple-element.245), kind=kOutput, calls=%fused_computation | convolution fusion | flops 12891193344 | bytes 23068672 | tf_op jit(solution)/shard_map/dot_general | solution.py:1031
  322.0 8.1 %collective-permute-done.27.refs_2_ = bf16[256,2048]{1,0:T(8,128)(2,1)} collective-permute-done((bf16[256,2048]{1,0:T(8,128)(2,1)}, bf16[256,2048]{1,0:T(8,128)(2,1)}, u32[]{:S(2)}, u32[]{:S(2)}) %collective-permute-start.27) | collective-permute-done | bytes 1048608 | tf_op jit(solution)/shard_map/ppermute | solution.py:41
  331.0 12.6 %shard_map.253 = (f32[256,2048]{1,0:T(8,128)}, bf16[256,2048]{1,0:T(8,128)(2,1)}, f32[1,2048]{1,0:T(1,128)}, bf16[4,256,128]{2,1,0:T(8,128)(2,1)}, bf16[4,256,12...) custom-call(bf16[256,2048]{1,0:T(8,128)(2,1)} %get-tuple-element.220.refs_0_, ...), custom_call_target="tpu_custom_call" | custom-call | flops 1024 | bytes 1024 | tf_op jit(solution)/shard_map/pallas_call | solution.py:511
  346.9 12.9 %shard_map.254 = (bf16[8,128,1536]{2,1,0:T(8,128)(2,1)}, bf16[8,128,1536]{2,1,0:T(8,128)(2,1)}) custom-call(s32[1]{0:T(128)} %bitcast.1.core.core_ref, bf16[4,256,2048]{2,1,0:T(8,128)(2,1)} %get-tuple-element.254.refs_0_, bf16[4,256,1536]{2,1,0:T(8,128)(2,1)} %get-tuple-element.259.refs_1_.inner_ref), custom_call_target="tpu_custom_call" | custom-call | flops 1024 | bytes 1024 | tf_op jit(solution)/shard_map/pallas_call | solution.py:418
  369.0 10.6 %shard_map.255 = (bf16[256,2048]{1,0:T(8,128)(2,1)}, bf16[256,2048]{1,0:T(8,128)(2,1)}, bf16[256,2048]{1,0:T(8,128)(2,1)}, bf16[256,2048]{1,0:T(8,128)(2,1)}) custom-call(bf16[4,256,1536]{2,1,0:T(8,128)(2,1)} %get-tuple-element.259.refs_1_.inner_ref, bf16[2048,4608]{1,0:T(8,128)(2,1)} %all-gather.5.cloned.1.call-done.refs_2_.refs_3_.refs_4_.refs_5_.weight_ref), custom_call_target="tpu_custom_call" | custom-call | flops 1024 | bytes 1024 | tf_op jit(solution)/shard_map/pallas_call | solution.py:368
  379.6 13.6 %all-to-all-done.2.grad_a.grad_b = bf16[16,256,128]{2,1,0:T(8,128)(2,1)S(1)} async-done(((bf16[16,256,128]{2,1,0:T(8,128)(2,1)}), bf16[16,256,128]{2,1,0:T(8,128)(2,1)S(1)}, u32[]{:S(2)}, u32[]{:S(2)}) %all-to-all-start.2) | async-done | bytes 1048608 | tf_op jit(solution)/shard_map/all_to_all | solution.py:819
  395.3 32.1 %shard_map.256 = (bf16[16,2,256,128]{3,2,1,0:T(8,128)(2,1)}, bf16[16,256,128]{2,1,0:T(8,128)(2,1)}, bf16[16,256,128]{2,1,0:T(8,128)(2,1)}) custom-call(s32[16]{0:T(128)} %dynamic-slice_bitcast_fusion.2.order, s32[1]{0:T(128)} %bitcast.1.core.core_ref, bf16[16,2,256,128]{3,2,1,0:T(8,128)(2,1)} %all-to-all-done.own_a.own_b, ...), custom_call_target="tpu_custom_call" | custom-call | flops 1024 | bytes 1024 | tf_op jit(solution)/shard_map/pallas_call | solution.py:232
  433.4 9.8 %all-to-all-start.3 = ((bf16[16,2,256,128]{3,2,1,0:T(8,128)(2,1)}), bf16[16,2,256,128]{3,2,1,0:T(8,128)(2,1)}, u32[]{:S(2)}, u32[]{:S(2)}) async-start(bf16[16,2,256,128]{3,2,1,0:T(8,128)(2,1)} %fusion.9), calls=%async_computation.3 | async-start | bytes 4194304 | tf_op jit(solution)/shard_map/all_to_all | solution.py:819
  443.2 11.8 %collective-permute-done.39.refs_2_ = bf16[256,2048]{1,0:T(8,128)(2,1)} collective-permute-done((bf16[256,2048]{1,0:T(8,128)(2,1)}, bf16[256,2048]{1,0:T(8,128)(2,1)}, u32[]{:S(2)}, u32[]{:S(2)}) %collective-permute-start.39) | collective-permute-done | bytes 1048608 | tf_op jit(solution)/shard_map/ppermute | solution.py:41
  455.0 8.5 %shard_map.257 = (bf16[8,128,512]{2,1,0:T(8,128)(2,1)}, bf16[8,128,512]{2,1,0:T(8,128)(2,1)}) custom-call(s32[1]{0:T(128)} %bitcast.1.core.core_ref, bf16[256,2048]{1,0:T(8,128)(2,1)} %get-tuple-element.286.refs_0_, bf16[256,2048]{1,0:T(8,128)(2,1)} %collective-permute-done.33.refs_1_, bf16[256,2048]{1,0:T(8,128)(2,1)} %collective-permute-done.39.refs_2_, ...), custom_call_target="tpu_custom_call" | custom-call | flops 1024 | bytes 1024 | tf_op jit(solution)/shard_map/pallas_call | solution.py:418
  484.8 15.1 %shard_map.259 = (bf16[4,256,1024]{2,1,0:T(8,128)(2,1)}, bf16[8,128,1024]{2,1,0:T(8,128)(2,1)}, bf16[8,128,1024]{2,1,0:T(8,128)(2,1)}, f32[1,128]{1,0:T(1,128)}, f32[1,128]{1,0:T(1,128)}) custom-call(s32[1]{0:T(128)} %bitcast.1.core.core_ref, bf16[16,2,256,128]{3,2,1,0:T(8,128)(2,1)} %all-to-all-done.3.back_ref, f32[4,256,1024]{2,1,0:T(8,128)} %get-tuple-element.292.pre_ref, ...), custom_call_target="tpu_custom_call" | custom-call | flops 1024 | bytes 1024 | tf_op jit(solution)/shard_map/pallas_call | solution.py:664
  506.3 12.6 %shard_map.260 = (bf16[256,2048]{1,0:T(8,128)(2,1)}, bf16[128,2048]{1,0:T(8,128)(2,1)}, bf16[128,2048]{1,0:T(8,128)(2,1)}, bf16[128,2048]{1,0:T(8,128)(2,1)}, bf...) custom-call(s32[1]{0:T(128)} %bitcast.1.core.core_ref, ...), custom_call_target="tpu_custom_call" | custom-call | flops 1024 | bytes 1024 | tf_op jit(solution)/shard_map/pallas_call | solution.py:749
  541.9 14.8 %collective-permute-done.46 = bf16[128,2048]{1,0:T(8,128)(2,1)S(1)} collective-permute-done((bf16[128,2048]{1,0:T(8,128)(2,1)}, bf16[128,2048]{1,0:T(8,128)(2,1)S(1)}, u32[]{:S(2)}, u32[]{:S(2)}) %collective-permute-start.46) | collective-permute-done | bytes 524320 | tf_op jit(solution)/shard_map/ppermute | solution.py:41
  588.8 7.8 %collective-permute-done.47 = bf16[256,2048]{1,0:T(8,128)(2,1)S(1)} collective-permute-done((bf16[256,2048]{1,0:T(8,128)(2,1)}, bf16[256,2048]{1,0:T(8,128)(2,1)S(1)}, u32[]{:S(2)}, u32[]{:S(2)}) %collective-permute-start.47) | collective-permute-done | bytes 1048608 | tf_op jit(solution)/shard_map/ppermute | solution.py:41
  597.7 14.9 %collective-permute-done.55.refs_1_ = bf16[128,2048]{1,0:T(8,128)(2,1)S(1)} collective-permute-done((bf16[128,2048]{1,0:T(8,128)(2,1)S(1)}, bf16[128,2048]{1,0:T(8,128)(2,1)S(1)}, u32[]{:S(2)}, u32[]{:S(2)}) %collective-permute-start.55) | collective-permute-done | bytes 524320 | tf_op jit(solution)/shard_map/ppermute | solution.py:41
  (323 shorter events, 268.8 us)
Async XLA Ops:
  7.2 68.7 %all-gather.3.cloned.1.call-start = ((), (), s32[]{:S(2)}) async-start(), calls=%async_computation.7 | async-start | bytes 5013504 | tf_op jit(solution)/shard_map/all_gather | solution.py:905
  10.9 219.6 %all-gather.5.cloned.1.call-start = ((), (), s32[]{:S(2)}) async-start(), calls=%async_computation.8 | async-start | bytes 20054016 | tf_op jit(solution)/shard_map/all_gather | solution.py:905
  72.6 48.2 %collective-permute-start.12 = (bf16[2048,512]{1,0:T(8,128)(2,1)}, bf16[2048,512]{1,0:T(8,128)(2,1)S(1)}, u32[]{:S(2)}, u32[]{:S(2)}) collective-permute-start(bf16[2048,512]{1,0:T(8,128)(2,1)} %shard_map.247.refs_4_), channel_id=1, source_target_pairs={{0,16},{16,32},{32,48},{48,0},{1,17},{17,33},{33,49},{49,1},{2,18}... | collective-permute-start | bytes 6291464 | tf_op jit(solution)/shard_map/ppermute | solution.py:41
  72.6 48.2 %collective-permute-start.13 = (bf16[2048,512]{1,0:T(8,128)(2,1)}, bf16[2048,512]{1,0:T(8,128)(2,1)}, u32[]{:S(2)}, u32[]{:S(2)}) collective-permute-start(bf16[2048,512]{1,0:T(8,128)(2,1)} %shard_map.247.refs_4_), channel_id=1, source_target_pairs={{0,48},{16,0},{32,16},{48,32},{1,49},{17,1},{33,17},{49,33},{2,50}... | collective-permute-start | bytes 6291464 | tf_op jit(solution)/shard_map/ppermute | solution.py:41
  87.8 45.0 %all-to-all-start = ((bf16[16,2,256,128]{3,2,1,0:T(8,128)(2,1)}), bf16[16,2,256,128]{3,2,1,0:T(8,128)(2,1)}, u32[]{:S(2)}, u32[]{:S(2)}) async-start(bf16[16,2,256,128]{3,2,1,0:T(8,128)(2,1)} %get-tuple-element.184), calls=%async_computation | async-start | bytes 4194304 | tf_op jit(solution)/shard_map/all_to_all | solution.py:819
  173.0 306.2 %reduce-scatter.2.cloned.1.call-start = ((), (), s32[]{:S(2)}) async-start(), calls=%async_computation.9 | async-start | bytes 13369344 | tf_op jit(solution)/shard_map/reduce_scatter | solution.py:1040
  282.5 39.5 %collective-permute-start.26 = (bf16[256,2048]{1,0:T(8,128)(2,1)}, bf16[256,2048]{1,0:T(8,128)(2,1)S(1)}, u32[]{:S(2)}, u32[]{:S(2)}) collective-permute-start(bf16[256,2048]{1,0:T(8,128)(2,1)} %get-tuple-element.229), channel_id=1, source_target_pairs={{0,48},{16,0},{32,16},{48,32},{1,49},{17,1},{33,17},{49,33},{2,50}... | collective-permute-start | bytes 3145736 | tf_op jit(solution)/shard_map/ppermute | solution.py:41
  283.4 46.6 %collective-permute-start.27 = (bf16[256,2048]{1,0:T(8,128)(2,1)}, bf16[256,2048]{1,0:T(8,128)(2,1)}, u32[]{:S(2)}, u32[]{:S(2)}) collective-permute-start(bf16[256,2048]{1,0:T(8,128)(2,1)} %get-tuple-element.230), channel_id=1, source_target_pairs={{0,16},{16,32},{32,48},{48,0},{1,17},{17,33},{33,49},{49,1},{2,18}... | collective-permute-start | bytes 3145736 | tf_op jit(solution)/shard_map/ppermute | solution.py:41
  359.8 33.4 %collective-permute-start.33 = (bf16[256,2048]{1,0:T(8,128)(2,1)S(1)}, bf16[256,2048]{1,0:T(8,128)(2,1)}, u32[]{:S(2)}, u32[]{:S(2)}) collective-permute-start(bf16[256,2048]{1,0:T(8,128)(2,1)S(1)} %copy-done.37), channel_id=1, source_target_pairs={{0,16},{16,32},{32,48},{48,0},{1,17},{17,33},{33,49},{49,1},{2,18}... | collective-permute-start | bytes 3145736 | tf_op jit(solution)/shard_map/ppermute | solution.py:41
  360.7 32.5 %collective-permute-start.34 = (bf16[256,2048]{1,0:T(8,128)(2,1)S(1)}, bf16[256,2048]{1,0:T(8,128)(2,1)}, u32[]{:S(2)}, u32[]{:S(2)}) collective-permute-start(bf16[256,2048]{1,0:T(8,128)(2,1)S(1)} %copy-done.37), channel_id=1, source_target_pairs={{0,48},{16,0},{32,16},{48,32},{1,49},{17,1},{33,17},{49,33},{2,50}... | collective-permute-start | bytes 3145736 | tf_op jit(solution)/shard_map/ppermute | solution.py:41
  393.2 34.2 %collective-permute-start.35 = (bf16[256,2048]{1,0:T(8,128)(2,1)}, bf16[256,2048]{1,0:T(8,128)(2,1)S(1)}, u32[]{:S(2)}, u32[]{:S(2)}) collective-permute-start(bf16[256,2048]{1,0:T(8,128)(2,1)} %get-tuple-element.275), channel_id=1, source_target_pairs={{0,48},{16,0},{32,16},{48,32},{1,49},{17,1},{33,17},{49,33},{2,50}... | collective-permute-start | bytes 3145736 | tf_op jit(solution)/shard_map/ppermute | solution.py:41
  393.5 34.0 %collective-permute-start.36 = (bf16[256,2048]{1,0:T(8,128)(2,1)}, bf16[256,2048]{1,0:T(8,128)(2,1)}, u32[]{:S(2)}, u32[]{:S(2)}) collective-permute-start(bf16[256,2048]{1,0:T(8,128)(2,1)} %get-tuple-element.276), channel_id=1, source_target_pairs={{0,16},{16,32},{32,48},{48,0},{1,17},{17,33},{33,49},{49,1},{2,18}... | collective-permute-start | bytes 3145736 | tf_op jit(solution)/shard_map/ppermute | solution.py:41
  427.5 38.8 %collective-permute-start.38 = (bf16[8,128,1536]{2,1,0:T(8,128)(2,1)}, bf16[8,128,1536]{2,1,0:T(8,128)(2,1)}, u32[]{:S(2)}, u32[]{:S(2)}) collective-permute-start(bf16[8,128,1536]{2,1,0:T(8,128)(2,1)} %get-tuple-element.285), channel_id=1, source_target_pairs={{0,1},{1,0},{2,3},{3,2},{4,5},{5,4},{6,7},{7,6},{8,9},{9,8},{10,11... | collective-permute-start | bytes 9437192 | tf_op jit(solution)/shard_map/ppermute | solution.py:41
  433.4 44.3 %all-to-all-start.3 = ((bf16[16,2,256,128]{3,2,1,0:T(8,128)(2,1)}), bf16[16,2,256,128]{3,2,1,0:T(8,128)(2,1)}, u32[]{:S(2)}, u32[]{:S(2)}) async-start(bf16[16,2,256,128]{3,2,1,0:T(8,128)(2,1)} %fusion.9), calls=%async_computation.3 | async-start | bytes 4194304 | tf_op jit(solution)/shard_map/all_to_all | solution.py:819
  463.5 36.4 %collective-permute-start.42 = (bf16[256,2048]{1,0:T(8,128)(2,1)}, bf16[256,2048]{1,0:T(8,128)(2,1)S(1)}, u32[]{:S(2)}, u32[]{:S(2)}) collective-permute-start(bf16[256,2048]{1,0:T(8,128)(2,1)} %get-tuple-element.298), channel_id=1, source_target_pairs={{0,32},{16,48},{32,0},{48,16},{1,33},{17,49},{33,1},{49,17},{2,34}... | collective-permute-start | bytes 3145736 | tf_op jit(solution)/shard_map/ppermute | solution.py:41
  479.9 54.1 %all-to-all-start.5 = ((bf16[4,2,128,2048]{3,2,1,0:T(8,128)(2,1)}), bf16[4,2,128,2048]{3,2,1,0:T(8,128)(2,1)}, u32[]{:S(2)}, u32[]{:S(2)}) async-start(bf16[4,2,128,2048]{3,2,1,0:T(8,128)(2,1)} %bitcast.44), calls=%async_computation.6 | async-start | bytes 8388608 | tf_op jit(solution)/shard_map/all_to_all | solution.py:1014
  524.6 32.2 %collective-permute-start.46 = (bf16[128,2048]{1,0:T(8,128)(2,1)}, bf16[128,2048]{1,0:T(8,128)(2,1)S(1)}, u32[]{:S(2)}, u32[]{:S(2)}) collective-permute-start(bf16[128,2048]{1,0:T(8,128)(2,1)} %get-tuple-element.315), channel_id=1, source_target_pairs={{0,48},{16,0},{32,16},{48,32},{1,49},{17,1},{33,17},{49,33},{2,50}... | collective-permute-start | bytes 1572872 | tf_op jit(solution)/shard_map/ppermute | solution.py:41
  528.0 40.4 %collective-permute-start.61 = (bf16[128,3072]{1,0:T(8,128)(2,1)}, bf16[128,3072]{1,0:T(8,128)(2,1)}, u32[]{:S(2)}, u32[]{:S(2)}) collective-permute-start(bf16[128,3072]{1,0:T(8,128)(2,1)} %add_convert_fusion.2.refs_0_), channel_id=1, source_target_pairs={{0,32},{16,48},{32,0},{48,16},{1,33},{17,49},{33,1},{49,17},{2,34}... | collective-permute-start | bytes 2359304 | tf_op jit(solution)/shard_map/ppermute | solution.py:41
  528.6 33.0 %collective-permute-start.48 = (bf16[128,2048]{1,0:T(8,128)(2,1)}, bf16[128,2048]{1,0:T(8,128)(2,1)}, u32[]{:S(2)}, u32[]{:S(2)}) collective-permute-start(bf16[128,2048]{1,0:T(8,128)(2,1)} %get-tuple-element.326), channel_id=1, source_target_pairs={{0,16},{16,32},{32,48},{48,0},{1,17},{17,33},{33,49},{49,1},{2,18}... | collective-permute-start | bytes 1572872 | tf_op jit(solution)/shard_map/ppermute | solution.py:41
  534.0 39.4 %all-to-all-start.4 = ((bf16[4,2,128,1152]{3,2,1,0:T(8,128)(2,1)}), bf16[4,2,128,1152]{3,2,1,0:T(8,128)(2,1)}, u32[]{:S(2)}, u32[]{:S(2)}) async-start(bf16[4,2,128,1152]{3,2,1,0:T(8,128)(2,1)} %bitcast.45), calls=%async_computation.5 | async-start | bytes 4718592 | tf_op jit(solution)/shard_map/all_to_all | solution.py:1014
  558.0 38.6 %collective-permute-start.47 = (bf16[256,2048]{1,0:T(8,128)(2,1)}, bf16[256,2048]{1,0:T(8,128)(2,1)S(1)}, u32[]{:S(2)}, u32[]{:S(2)}) collective-permute-start(bf16[256,2048]{1,0:T(8,128)(2,1)} %pad_maximum_fusion.3), channel_id=1, source_target_pairs={{0,48},{16,0},{32,16},{48,32},{1,49},{17,1},{33,17},{49,33},{2,50}... | collective-permute-start | bytes 3145736 | tf_op jit(solution)/shard_map/ppermute | solution.py:41
  564.1 32.6 %collective-permute-start.49 = (bf16[256,2048]{1,0:T(8,128)(2,1)}, bf16[256,2048]{1,0:T(8,128)(2,1)S(1)}, u32[]{:S(2)}, u32[]{:S(2)}) collective-permute-start(bf16[256,2048]{1,0:T(8,128)(2,1)} %pad_maximum_fusion.4), channel_id=1, source_target_pairs={{0,16},{16,32},{32,48},{48,0},{1,17},{17,33},{33,49},{49,1},{2,18}... | collective-permute-start | bytes 3145736 | tf_op jit(solution)/shard_map/ppermute | solution.py:41
  580.1 32.5 %collective-permute-start.55 = (bf16[128,2048]{1,0:T(8,128)(2,1)S(1)}, bf16[128,2048]{1,0:T(8,128)(2,1)S(1)}, u32[]{:S(2)}, u32[]{:S(2)}) collective-permute-start(bf16[128,2048]{1,0:T(8,128)(2,1)S(1)} %add_convert_fusion.3.refs_0_), channel_id=1, source_target_pairs={{0,16},{16,32},{32,48},{48,0},{1,17},{17,33},{33,49},{49,1},{2,18}... | collective-permute-start | bytes 1572872 | tf_op jit(solution)/shard_map/ppermute | solution.py:41
  580.2 32.4 %collective-permute-start.56 = (bf16[128,2048]{1,0:T(8,128)(2,1)S(1)}, bf16[128,2048]{1,0:T(8,128)(2,1)S(1)}, u32[]{:S(2)}, u32[]{:S(2)}) collective-permute-start(bf16[128,2048]{1,0:T(8,128)(2,1)S(1)} %add_convert_fusion.3.refs_0_), channel_id=1, source_target_pairs={{0,32},{16,48},{32,0},{48,16},{1,33},{17,49},{33,1},{49,17},{2,34}... | collective-permute-start | bytes 1572872 | tf_op jit(solution)/shard_map/ppermute | solution.py:41
  (105 other events, 1274.0 us)
Sparse Core Ops, SparseCore 0:
  11.1 62.2 all-gather.2
  75.8 147.3 all-gather.4
  330.2 148.8 reduce-scatter.1

commit v11 on v10

--- a/solution.py
+++ b/solution.py
@@ -425,7 +425,9 @@
         out_shape=(jax.ShapeDtypeStruct((width // 256, 128, outs), low),) * 2,
         scratch_shapes=[pltpu.VMEM((rows, 512), low)] * by_heads,
         compiler_params=pltpu.CompilerParams(vmem_limit_bytes=VMEM_LIMIT),
-        cost_estimate=pl.CostEstimate(flops=1024, bytes_accessed=1024, transcendentals=0),
+        cost_estimate=pl.CostEstimate(
+            flops=0 if by_heads else 2 * rows * width * outs, bytes_accessed=1024, transcendentals=0
+        ),
     )(core_at[None], *lefts, right)
 
 
@@ -1047,16 +1049,14 @@
         mlp_scale,
     )
     grad_blocks = [grad_blocks[0]] + [shift(grad_blocks[RING - r], "z", r) for r in range(1, RING)]
+    grad_blocks, own_low, inner = together(grad_blocks, own_low, inner)
     down_keep, down_give = pair_grad(core_at, [cot_all], inner)
-    grad_blocks, down_keep, down_give, own_low, inner = together(
-        grad_blocks, down_keep, down_give, own_low, inner
-    )
     head_grads = to_heads(jnp.concatenate(grad_blocks, axis=0))
     low_left = shift(own_low, "z", 1)
     low_right = shift(own_low, "z", 3)
     mlp_own, mlp_opposite, mlp_left, mlp_right = mlp_out_part(inner, mlp_weights)
-    head_grads, low_left, low_right, own_low, mlp_opposite, mlp_left, mlp_right = together(
-        head_grads, low_left, low_right, own_low, mlp_opposite, mlp_left, mlp_right
+    head_grads, low_left, low_right, own_low, mlp_opposite, mlp_left, mlp_right, down_give = together(
+        head_grads, low_left, low_right, own_low, mlp_opposite, mlp_left, mlp_right, down_give
     )
     mlp_left = send_back(mlp_left, 1)
     mlp_right = send_back(mlp_right, 3)
@@ -1119,7 +1119,7 @@
     down_blocks = over_z(down_pair)
     qkv_share = pair_sum(*along_x(add_up(qkv_terms)))
     both_blocks = [both_sum, both_left, both_opposite, both_right]
-    qkv_pair, down_blocks = together(over_x(qkv_share), down_blocks)
+    qkv_pair = over_x(qkv_share)
     output = (
         middle
         + after(mlp_own, first_top).astype(f32)

time: 649 us -> 646 us (level)
  waiting for transfers between devices: 198 us -> 191 us
    all_to_all x4, waiting for transfers between devices: 31.3 us -> 18.2 us  [to_heads(): return lax.all_to_all(send, GROUP_AXES, 0, 0, tiled=True)]
  transfers between devices with their start and end apart: 71 -> 71, of which waited for: 35 -> 37; matrix products, arithmetic and copies ran while one was open for 11% -> 11% of each run, Pallas kernels for 34% -> 34%
where the time goes in v11:
time: 646 us; the launch traced here: 635 us
  Pallas kernels  221 us (34%)
  waiting for transfers between devices  191 us (30%)
  starting transfers between devices  122 us (19%)
  other arithmetic  35.6 us (6%)
  local copies, waits for them, and re-layouts  31.6 us (5%)
  matrix products  19.3 us (3%)
  between operations  14.7 us (2%)
    ppermute x60, waiting for transfers between devices, shift(): lax.ppermute(values, axis, [(i, (i + by) % size) for i in range(size)])  170 us
    ppermute x60, starting transfers between devices, shift(): lax.ppermute(values, axis, [(i, (i + by) % size) for i in range(size)])  84.3 us
    pallas_call x3, Pallas kernels, mlp_blocks(): pl.pallas_call(functools.partial(mlp_kernel, len(seconds), len(cots)), gr...  58 us
    pallas_call x1, Pallas kernels, attention_backward(): pl.pallas_call(backward_kernel, out_shape=(jax.ShapeDtypeStruct((BLOCKS,...  32 us
    all_to_all x4, starting transfers between devices, to_heads(): return lax.all_to_all(send, GROUP_AXES, 0, 0, tiled=True)  27.6 us
    pallas_call x2, Pallas kernels, pair_grad(): pl.pallas_call(kernel, grid=(width // 256,), in_specs=[pl.BlockSpec(memor...  20.7 us
    dot_general x1, matrix products, local(): lax.dot_general(second_all.reshape(ring_rows, width), both_grad.reshape(r...  19.3 us
    all_to_all x4, waiting for transfers between devices, to_heads(): return lax.all_to_all(send, GROUP_AXES, 0, 0, tiled=True)  18.2 us
  transfers between devices with their start and end apart: 71, of which 37 were waited for; matrix products, arithmetic and copies ran while one was open for 11% of the time, Pallas kernels for 34%

profile of v11, /device:TPU:4, one launch (start us, length us, event | category | flops | bytes accessed | tf_op | source)
XLA Modules:
  0.0 634.7 jit_solution(7405480141847723551)
XLA Ops:
  75.9 12.0 %shard_map.246 = (bf16[4,256,2048]{2,1,0:T(8,128)(2,1)}, bf16[4,256,2048]{2,1,0:T(8,128)(2,1)}, f32[4,256,1024]{2,1,0:T(8,128)}, bf16[16,2,256,128]{3,2,1,0:T(8,128)(2,1)}, f32[8,2048]{1,0:T(8,128)}) custom-call(bf16[256,2048]{1,0:T(8,128)(2,1)} %refs_8_.1, bf16[256,2048]{1,0:T(8,128)(2,1)} %copy-done.48, bf16[128,2048]{1,0:T(8,128)(2,1)} %collective-permute-done.9.top_ref, ...), custom_call_target="tpu_custom_call" | custom-call | flops 4294967296 | bytes 20971520 | tf_op jit(solution)/shard_map/pallas_call | solution.py:579
  87.8 7.6 %all-to-all-start = ((bf16[16,2,256,128]{3,2,1,0:T(8,128)(2,1)}), bf16[16,2,256,128]{3,2,1,0:T(8,128)(2,1)}, u32[]{:S(2)}, u32[]{:S(2)}) async-start(bf16[16,2,256,128]{3,2,1,0:T(8,128)(2,1)} %get-tuple-element.177), calls=%async_computation | async-start | bytes 4194304 | tf_op jit(solution)/shard_map/all_to_all | solution.py:821
  95.4 25.4 %collective-permute-done.12.refs_5_ = bf16[2048,512]{1,0:T(8,128)(2,1)S(1)} collective-permute-done((bf16[2048,512]{1,0:T(8,128)(2,1)}, bf16[2048,512]{1,0:T(8,128)(2,1)S(1)}, u32[]{:S(2)}, u32[]{:S(2)}) %collective-permute-start.12) | collective-permute-done | bytes 2097184 | tf_op jit(solution)/shard_map/ppermute | solution.py:41
  120.8 12.0 %all-to-all-done.own_a.own_b = bf16[16,2,256,128]{3,2,1,0:T(8,128)(2,1)} async-done(((bf16[16,2,256,128]{3,2,1,0:T(8,128)(2,1)}), bf16[16,2,256,128]{3,2,1,0:T(8,128)(2,1)}, u32[]{:S(2)}, u32[]{:S(2)}) %all-to-all-start) | async-done | bytes 2097184 | tf_op jit(solution)/shard_map/all_to_all | solution.py:821
  142.7 18.0 %shard_map.248 = (bf16[16,256,128]{2,1,0:T(8,128)(2,1)}, f32[8,128,512]{2,1,0:T(8,128)}, f32[8,1,512]{2,1,0:T(1,128)}) custom-call(s32[16]{0:T(128)} %dynamic-slice_bitcast_fusion.2.order, s32[1]{0:T(128)} %bitcast.1.core.core_ref, bf16[16,2,256,128]{3,2,1,0:T(8,128)(2,1)} %all-to-all-done.own_a.own_b, bf16[16,2,256,128]{3,2,1,0:T(8,128)(2,1)} %all-to-all-done.own_a.own_b, ...), custom_call_target="tpu_custom_call" | custom-call | flops 1024 | bytes 1024 | tf_op jit(solution)/shard_map/pallas_call | solution.py:121
  173.0 17.2 %collective-permute-done.17.refs_2_ = bf16[256,2048]{1,0:T(8,128)(2,1)S(1)} collective-permute-done((bf16[256,2048]{1,0:T(8,128)(2,1)S(1)}, bf16[256,2048]{1,0:T(8,128)(2,1)S(1)}, u32[]{:S(2)}, u32[]{:S(2)}) %collective-permute-start.17) | collective-permute-done | bytes 1048608 | tf_op jit(solution)/shard_map/ppermute | solution.py:41
  197.1 8.0 %collective-permute-done.19.refs_1_ = bf16[128,2048]{1,0:T(8,128)(2,1)} collective-permute-done((bf16[128,2048]{1,0:T(8,128)(2,1)}, bf16[128,2048]{1,0:T(8,128)(2,1)}, u32[]{:S(2)}, u32[]{:S(2)}) %collective-permute-start.19) | collective-permute-done | bytes 524320 | tf_op jit(solution)/shard_map/ppermute | solution.py:41
  230.5 15.7 %shard_map.250 = (bf16[4,256,1536]{2,1,0:T(8,128)(2,1)}, bf16[4,256,3072]{2,1,0:T(8,128)(2,1)}, bf16[4,256,2048]{2,1,0:T(8,128)(2,1)}, bf16[4,256,2048]{2,1,0:T(8,128)(2,1)}, bf16[256,2048]{1,0:T(8,128)(2,1)}) custom-call(bf16[256,2048]{1,0:T(8,128)(2,1)} %get-tuple-element.228.refs_0_, bf16[256,2048]{1,0:T(8,128)(2,1)} %refs_9_.1, ...), custom_call_target="tpu_custom_call" | custom-call | flops 8053063680 | bytes 18874368 | tf_op jit(solution)/shard_map/pallas_call | solution.py:326
  255.8 26.6 %shard_map.251 = (bf16[4,256,1536]{2,1,0:T(8,128)(2,1)}, bf16[4,256,3072]{2,1,0:T(8,128)(2,1)}, bf16[4,256,2048]{2,1,0:T(8,128)(2,1)}, bf16[4,256,2048]{2,1,0:T(...) custom-call(bf16[256,2048]{1,0:T(8,128)(2,1)} %copy-done.26, ...), custom_call_target="tpu_custom_call", output_to_operand_aliasing={{0}: (6, {}), {1}: (7, {}), {2}: (8, {}), {3}: (9, {})} | custom-call | flops 16106127360 | bytes 18874368 | tf_op jit(solution)/shard_map/pallas_call | solution.py:326
  285.7 15.6 %shard_map.252 = (bf16[4,256,1536]{2,1,0:T(8,128)(2,1)}, bf16[4,256,3072]{2,1,0:T(8,128)(2,1)}, bf16[4,256,2048]{2,1,0:T(8,128)(2,1)}, bf16[4,256,2048]{2,1,0:T(8,128)(2,1)}, bf16[256,2048]{1,0:T(8,128)(2,1)}) custom-call(bf16[256,2048]{1,0:T(8,128)(2,1)} %copy-done.25, ...), custom_call_target="tpu_custom_call", output_to_operand_aliasing={{0}: (5, {}), {1}: (6, {}), {2}: (7, {}), {3}: (8, {})} | custom-call | flops 8053063680 | bytes 18874368 | tf_op jit(solution)/shard_map/pallas_call | solution.py:326
  302.7 19.3 %bitcast_convert_fusion = bf16[2048,3072]{1,0:T(8,128)(2,1)} fusion(bf16[4,256,2048]{2,1,0:T(8,128)(2,1)} %get-tuple-element.237, bf16[4,256,3072]{2,1,0:T(8,128)(2,1)} %get-tuple-element.238), kind=kOutput, calls=%fused_computation | convolution fusion | flops 12891193344 | bytes 23068672 | tf_op jit(solution)/shard_map/dot_general | solution.py:1033
  322.0 8.1 %collective-permute-done.27.refs_2_ = bf16[256,2048]{1,0:T(8,128)(2,1)} collective-permute-done((bf16[256,2048]{1,0:T(8,128)(2,1)}, bf16[256,2048]{1,0:T(8,128)(2,1)}, u32[]{:S(2)}, u32[]{:S(2)}) %collective-permute-start.27) | collective-permute-done | bytes 1048608 | tf_op jit(solution)/shard_map/ppermute | solution.py:41
  331.1 12.6 %shard_map.253 = (f32[256,2048]{1,0:T(8,128)}, bf16[256,2048]{1,0:T(8,128)(2,1)}, f32[1,2048]{1,0:T(1,128)}, bf16[4,256,128]{2,1,0:T(8,128)(2,1)}, bf16[4,256,12...) custom-call(bf16[256,2048]{1,0:T(8,128)(2,1)} %get-tuple-element.213.refs_0_, ...), custom_call_target="tpu_custom_call" | custom-call | flops 1024 | bytes 1024 | tf_op jit(solution)/shard_map/pallas_call | solution.py:513
  346.9 8.6 %collective-permute-done.30 = bf16[4,256,128]{2,1,0:T(8,128)(2,1)S(1)} collective-permute-done((bf16[4,256,128]{2,1,0:T(8,128)(2,1)}, bf16[4,256,128]{2,1,0:T(8,128)(2,1)S(1)}, u32[]{:S(2)}, u32[]{:S(2)}) %collective-permute-start.30) | collective-permute-done | bytes 262176 | tf_op jit(solution)/shard_map/ppermute | solution.py:41
  367.2 11.2 %shard_map.254 = (bf16[256,2048]{1,0:T(8,128)(2,1)}, bf16[256,2048]{1,0:T(8,128)(2,1)}, bf16[256,2048]{1,0:T(8,128)(2,1)}, bf16[256,2048]{1,0:T(8,128)(2,1)}) custom-call(bf16[4,256,1536]{2,1,0:T(8,128)(2,1)} %get-tuple-element.249.inner_ref.refs_1_, bf16[2048,4608]{1,0:T(8,128)(2,1)} %all-gather.5.cloned.1.call-done.refs_2_.refs_3_.refs_4_.refs_5_.weight_ref), custom_call_target="tpu_custom_call" | custom-call | flops 1024 | bytes 1024 | tf_op jit(solution)/shard_map/pallas_call | solution.py:368
  378.5 12.2 %shard_map.255 = (bf16[8,128,1536]{2,1,0:T(8,128)(2,1)}, bf16[8,128,1536]{2,1,0:T(8,128)(2,1)}) custom-call(s32[1]{0:T(128)} %bitcast.1.core.core_ref, bf16[4,256,2048]{2,1,0:T(8,128)(2,1)} %get-tuple-element.259.refs_0_, bf16[4,256,1536]{2,1,0:T(8,128)(2,1)} %get-tuple-element.249.inner_ref.refs_1_), custom_call_target="tpu_custom_call" | custom-call | flops 6442450944 | bytes 1024 | tf_op jit(solution)/shard_map/pallas_call | solution.py:418
  393.9 32.0 %shard_map.256 = (bf16[16,2,256,128]{3,2,1,0:T(8,128)(2,1)}, bf16[16,256,128]{2,1,0:T(8,128)(2,1)}, bf16[16,256,128]{2,1,0:T(8,128)(2,1)}) custom-call(s32[16]{0:T(128)} %dynamic-slice_bitcast_fusion.2.order, s32[1]{0:T(128)} %bitcast.1.core.core_ref, bf16[16,2,256,128]{3,2,1,0:T(8,128)(2,1)} %all-to-all-done.own_a.own_b, ...), custom_call_target="tpu_custom_call" | custom-call | flops 1024 | bytes 1024 | tf_op jit(solution)/shard_map/pallas_call | solution.py:232
  432.0 9.8 %all-to-all-start.3 = ((bf16[16,2,256,128]{3,2,1,0:T(8,128)(2,1)}), bf16[16,2,256,128]{3,2,1,0:T(8,128)(2,1)}, u32[]{:S(2)}, u32[]{:S(2)}) async-start(bf16[16,2,256,128]{3,2,1,0:T(8,128)(2,1)} %fusion.9), calls=%async_computation.3 | async-start | bytes 4194304 | tf_op jit(solution)/shard_map/all_to_all | solution.py:821
  441.8 11.8 %collective-permute-done.39.refs_2_ = bf16[256,2048]{1,0:T(8,128)(2,1)} collective-permute-done((bf16[256,2048]{1,0:T(8,128)(2,1)}, bf16[256,2048]{1,0:T(8,128)(2,1)}, u32[]{:S(2)}, u32[]{:S(2)}) %collective-permute-start.39) | collective-permute-done | bytes 1048608 | tf_op jit(solution)/shard_map/ppermute | solution.py:41
  453.6 8.5 %shard_map.257 = (bf16[8,128,512]{2,1,0:T(8,128)(2,1)}, bf16[8,128,512]{2,1,0:T(8,128)(2,1)}) custom-call(s32[1]{0:T(128)} %bitcast.1.core.core_ref, bf16[256,2048]{1,0:T(8,128)(2,1)} %get-tuple-element.278.refs_0_, bf16[256,2048]{1,0:T(8,128)(2,1)} %copy-done.37, bf16[256,2048]{1,0:T(8,128)(2,1)} %collective-permute-done.39.refs_2_, ...), custom_call_target="tpu_custom_call" | custom-call | bytes 1024 | tf_op jit(solution)/shard_map/pallas_call | solution.py:418
  483.2 15.1 %shard_map.259 = (bf16[4,256,1024]{2,1,0:T(8,128)(2,1)}, bf16[8,128,1024]{2,1,0:T(8,128)(2,1)}, bf16[8,128,1024]{2,1,0:T(8,128)(2,1)}, f32[1,128]{1,0:T(1,128)}, f32[1,128]{1,0:T(1,128)}) custom-call(s32[1]{0:T(128)} %bitcast.1.core.core_ref, bf16[16,2,256,128]{3,2,1,0:T(8,128)(2,1)} %all-to-all-done.3.back_ref, f32[4,256,1024]{2,1,0:T(8,128)} %get-tuple-element.284.pre_ref, ...), custom_call_target="tpu_custom_call" | custom-call | flops 1024 | bytes 1024 | tf_op jit(solution)/shard_map/pallas_call | solution.py:666
  504.8 12.6 %shard_map.260 = (bf16[256,2048]{1,0:T(8,128)(2,1)}, bf16[128,2048]{1,0:T(8,128)(2,1)}, bf16[128,2048]{1,0:T(8,128)(2,1)}, bf16[128,2048]{1,0:T(8,128)(2,1)}, bf...) custom-call(s32[1]{0:T(128)} %bitcast.1.core.core_ref, ...), custom_call_target="tpu_custom_call" | custom-call | flops 1024 | bytes 1024 | tf_op jit(solution)/shard_map/pallas_call | solution.py:751
  540.5 14.7 %collective-permute-done.46 = bf16[128,2048]{1,0:T(8,128)(2,1)S(1)} collective-permute-done((bf16[128,2048]{1,0:T(8,128)(2,1)}, bf16[128,2048]{1,0:T(8,128)(2,1)S(1)}, u32[]{:S(2)}, u32[]{:S(2)}) %collective-permute-start.46) | collective-permute-done | bytes 524320 | tf_op jit(solution)/shard_map/ppermute | solution.py:41
  587.4 7.7 %collective-permute-done.47 = bf16[256,2048]{1,0:T(8,128)(2,1)S(1)} collective-permute-done((bf16[256,2048]{1,0:T(8,128)(2,1)}, bf16[256,2048]{1,0:T(8,128)(2,1)S(1)}, u32[]{:S(2)}, u32[]{:S(2)}) %collective-permute-start.47) | collective-permute-done | bytes 1048608 | tf_op jit(solution)/shard_map/ppermute | solution.py:41
  (317 shorter events, 277.8 us)
Async XLA Ops:
  7.2 68.7 %all-gather.3.cloned.1.call-start = ((), (), s32[]{:S(2)}) async-start(), calls=%async_computation.7 | async-start | bytes 5013504 | tf_op jit(solution)/shard_map/all_gather | solution.py:907
  10.9 219.6 %all-gather.5.cloned.1.call-start = ((), (), s32[]{:S(2)}) async-start(), calls=%async_computation.8 | async-start | bytes 20054016 | tf_op jit(solution)/shard_map/all_gather | solution.py:907
  72.6 48.2 %collective-permute-start.12 = (bf16[2048,512]{1,0:T(8,128)(2,1)}, bf16[2048,512]{1,0:T(8,128)(2,1)S(1)}, u32[]{:S(2)}, u32[]{:S(2)}) collective-permute-start(bf16[2048,512]{1,0:T(8,128)(2,1)} %shard_map.247.refs_4_), channel_id=1, source_target_pairs={{0,16},{16,32},{32,48},{48,0},{1,17},{17,33},{33,49},{49,1},{2,18}... | collective-permute-start | bytes 6291464 | tf_op jit(solution)/shard_map/ppermute | solution.py:41
  72.6 48.2 %collective-permute-start.13 = (bf16[2048,512]{1,0:T(8,128)(2,1)}, bf16[2048,512]{1,0:T(8,128)(2,1)}, u32[]{:S(2)}, u32[]{:S(2)}) collective-permute-start(bf16[2048,512]{1,0:T(8,128)(2,1)} %shard_map.247.refs_4_), channel_id=1, source_target_pairs={{0,48},{16,0},{32,16},{48,32},{1,49},{17,1},{33,17},{49,33},{2,50}... | collective-permute-start | bytes 6291464 | tf_op jit(solution)/shard_map/ppermute | solution.py:41
  87.8 45.0 %all-to-all-start = ((bf16[16,2,256,128]{3,2,1,0:T(8,128)(2,1)}), bf16[16,2,256,128]{3,2,1,0:T(8,128)(2,1)}, u32[]{:S(2)}, u32[]{:S(2)}) async-start(bf16[16,2,256,128]{3,2,1,0:T(8,128)(2,1)} %get-tuple-element.177), calls=%async_computation | async-start | bytes 4194304 | tf_op jit(solution)/shard_map/all_to_all | solution.py:821
  173.0 304.8 %reduce-scatter.2.cloned.1.call-start = ((), (), s32[]{:S(2)}) async-start(), calls=%async_computation.9 | async-start | bytes 13369344 | tf_op jit(solution)/shard_map/reduce_scatter | solution.py:1042
  282.5 39.5 %collective-permute-start.26 = (bf16[256,2048]{1,0:T(8,128)(2,1)}, bf16[256,2048]{1,0:T(8,128)(2,1)S(1)}, u32[]{:S(2)}, u32[]{:S(2)}) collective-permute-start(bf16[256,2048]{1,0:T(8,128)(2,1)} %get-tuple-element.222), channel_id=1, source_target_pairs={{0,48},{16,0},{32,16},{48,32},{1,49},{17,1},{33,17},{49,33},{2,50}... | collective-permute-start | bytes 3145736 | tf_op jit(solution)/shard_map/ppermute | solution.py:41
  283.4 46.7 %collective-permute-start.27 = (bf16[256,2048]{1,0:T(8,128)(2,1)}, bf16[256,2048]{1,0:T(8,128)(2,1)}, u32[]{:S(2)}, u32[]{:S(2)}) collective-permute-start(bf16[256,2048]{1,0:T(8,128)(2,1)} %get-tuple-element.223), channel_id=1, source_target_pairs={{0,16},{16,32},{32,48},{48,0},{1,17},{17,33},{33,49},{49,1},{2,18}... | collective-permute-start | bytes 3145736 | tf_op jit(solution)/shard_map/ppermute | solution.py:41
  357.1 33.8 %collective-permute-start.33 = (bf16[256,2048]{1,0:T(8,128)(2,1)}, bf16[256,2048]{1,0:T(8,128)(2,1)S(1)}, u32[]{:S(2)}, u32[]{:S(2)}) collective-permute-start(bf16[256,2048]{1,0:T(8,128)(2,1)} %get-tuple-element.278.refs_0_), channel_id=1, source_target_pairs={{0,16},{16,32},{32,48},{48,0},{1,17},{17,33},{33,49},{49,1},{2,18}... | collective-permute-start | bytes 3145736 | tf_op jit(solution)/shard_map/ppermute | solution.py:41
  357.5 33.4 %collective-permute-start.34 = (bf16[256,2048]{1,0:T(8,128)(2,1)}, bf16[256,2048]{1,0:T(8,128)(2,1)}, u32[]{:S(2)}, u32[]{:S(2)}) collective-permute-start(bf16[256,2048]{1,0:T(8,128)(2,1)} %get-tuple-element.278.refs_0_), channel_id=1, source_target_pairs={{0,48},{16,0},{32,16},{48,32},{1,49},{17,1},{33,17},{49,33},{2,50}... | collective-permute-start | bytes 3145736 | tf_op jit(solution)/shard_map/ppermute | solution.py:41
  391.9 34.0 %collective-permute-start.35 = (bf16[256,2048]{1,0:T(8,128)(2,1)}, bf16[256,2048]{1,0:T(8,128)(2,1)S(1)}, u32[]{:S(2)}, u32[]{:S(2)}) collective-permute-start(bf16[256,2048]{1,0:T(8,128)(2,1)} %get-tuple-element.267), channel_id=1, source_target_pairs={{0,48},{16,0},{32,16},{48,32},{1,49},{17,1},{33,17},{49,33},{2,50}... | collective-permute-start | bytes 3145736 | tf_op jit(solution)/shard_map/ppermute | solution.py:41
  391.9 34.1 %collective-permute-start.36 = (bf16[256,2048]{1,0:T(8,128)(2,1)}, bf16[256,2048]{1,0:T(8,128)(2,1)}, u32[]{:S(2)}, u32[]{:S(2)}) collective-permute-start(bf16[256,2048]{1,0:T(8,128)(2,1)} %get-tuple-element.268), channel_id=1, source_target_pairs={{0,16},{16,32},{32,48},{48,0},{1,17},{17,33},{33,49},{49,1},{2,18}... | collective-permute-start | bytes 3145736 | tf_op jit(solution)/shard_map/ppermute | solution.py:41
  426.1 38.8 %collective-permute-start.38 = (bf16[8,128,1536]{2,1,0:T(8,128)(2,1)}, bf16[8,128,1536]{2,1,0:T(8,128)(2,1)}, u32[]{:S(2)}, u32[]{:S(2)}) collective-permute-start(bf16[8,128,1536]{2,1,0:T(8,128)(2,1)} %get-tuple-element.277), channel_id=1, source_target_pairs={{0,1},{1,0},{2,3},{3,2},{4,5},{5,4},{6,7},{7,6},{8,9},{9,8},{10,11... | collective-permute-start | bytes 9437192 | tf_op jit(solution)/shard_map/ppermute | solution.py:41
  432.0 44.4 %all-to-all-start.3 = ((bf16[16,2,256,128]{3,2,1,0:T(8,128)(2,1)}), bf16[16,2,256,128]{3,2,1,0:T(8,128)(2,1)}, u32[]{:S(2)}, u32[]{:S(2)}) async-start(bf16[16,2,256,128]{3,2,1,0:T(8,128)(2,1)} %fusion.9), calls=%async_computation.3 | async-start | bytes 4194304 | tf_op jit(solution)/shard_map/all_to_all | solution.py:821
  462.0 36.2 %collective-permute-start.42 = (bf16[256,2048]{1,0:T(8,128)(2,1)}, bf16[256,2048]{1,0:T(8,128)(2,1)S(1)}, u32[]{:S(2)}, u32[]{:S(2)}) collective-permute-start(bf16[256,2048]{1,0:T(8,128)(2,1)} %get-tuple-element.290), channel_id=1, source_target_pairs={{0,32},{16,48},{32,0},{48,16},{1,33},{17,49},{33,1},{49,17},{2,34}... | collective-permute-start | bytes 3145736 | tf_op jit(solution)/shard_map/ppermute | solution.py:41
  478.3 54.1 %all-to-all-start.5 = ((bf16[4,2,128,2048]{3,2,1,0:T(8,128)(2,1)}), bf16[4,2,128,2048]{3,2,1,0:T(8,128)(2,1)}, u32[]{:S(2)}, u32[]{:S(2)}) async-start(bf16[4,2,128,2048]{3,2,1,0:T(8,128)(2,1)} %bitcast.44), calls=%async_computation.6 | async-start | bytes 8388608 | tf_op jit(solution)/shard_map/all_to_all | solution.py:1016
  526.5 40.6 %collective-permute-start.61 = (bf16[128,3072]{1,0:T(8,128)(2,1)}, bf16[128,3072]{1,0:T(8,128)(2,1)}, u32[]{:S(2)}, u32[]{:S(2)}) collective-permute-start(bf16[128,3072]{1,0:T(8,128)(2,1)} %add_convert_fusion.2.refs_0_), channel_id=1, source_target_pairs={{0,32},{16,48},{32,0},{48,16},{1,33},{17,49},{33,1},{49,17},{2,34}... | collective-permute-start | bytes 2359304 | tf_op jit(solution)/shard_map/ppermute | solution.py:41
  526.8 33.3 %collective-permute-start.48 = (bf16[128,2048]{1,0:T(8,128)(2,1)}, bf16[128,2048]{1,0:T(8,128)(2,1)}, u32[]{:S(2)}, u32[]{:S(2)}) collective-permute-start(bf16[128,2048]{1,0:T(8,128)(2,1)} %get-tuple-element.318), channel_id=1, source_target_pairs={{0,16},{16,32},{32,48},{48,0},{1,17},{17,33},{33,49},{49,1},{2,18}... | collective-permute-start | bytes 1572872 | tf_op jit(solution)/shard_map/ppermute | solution.py:41
  532.5 39.5 %all-to-all-start.4 = ((bf16[4,2,128,1152]{3,2,1,0:T(8,128)(2,1)}), bf16[4,2,128,1152]{3,2,1,0:T(8,128)(2,1)}, u32[]{:S(2)}, u32[]{:S(2)}) async-start(bf16[4,2,128,1152]{3,2,1,0:T(8,128)(2,1)} %bitcast.45), calls=%async_computation.5 | async-start | bytes 4718592 | tf_op jit(solution)/shard_map/all_to_all | solution.py:1016
  556.5 38.6 %collective-permute-start.47 = (bf16[256,2048]{1,0:T(8,128)(2,1)}, bf16[256,2048]{1,0:T(8,128)(2,1)S(1)}, u32[]{:S(2)}, u32[]{:S(2)}) collective-permute-start(bf16[256,2048]{1,0:T(8,128)(2,1)} %pad_maximum_fusion.3), channel_id=1, source_target_pairs={{0,48},{16,0},{32,16},{48,32},{1,49},{17,1},{33,17},{49,33},{2,50}... | collective-permute-start | bytes 3145736 | tf_op jit(solution)/shard_map/ppermute | solution.py:41
  562.5 33.0 %collective-permute-start.49 = (bf16[256,2048]{1,0:T(8,128)(2,1)}, bf16[256,2048]{1,0:T(8,128)(2,1)S(1)}, u32[]{:S(2)}, u32[]{:S(2)}) collective-permute-start(bf16[256,2048]{1,0:T(8,128)(2,1)} %pad_maximum_fusion.4), channel_id=1, source_target_pairs={{0,16},{16,32},{32,48},{48,0},{1,17},{17,33},{33,49},{49,1},{2,18}... | collective-permute-start | bytes 3145736 | tf_op jit(solution)/shard_map/ppermute | solution.py:41
  578.6 33.8 %collective-permute-start.58 = (bf16[128,2048]{1,0:T(8,128)(2,1)S(1)}, bf16[128,2048]{1,0:T(8,128)(2,1)S(1)}, u32[]{:S(2)}, u32[]{:S(2)}) collective-permute-start(bf16[128,2048]{1,0:T(8,128)(2,1)S(1)} %add_convert_fusion.3.refs_0_), channel_id=1, source_target_pairs={{0,16},{16,32},{32,48},{48,0},{1,17},{17,33},{33,49},{49,1},{2,18}... | collective-permute-start | bytes 1572872 | tf_op jit(solution)/shard_map/ppermute | solution.py:41
  578.6 37.9 %collective-permute-start.59 = (bf16[128,2048]{1,0:T(8,128)(2,1)S(1)}, bf16[128,2048]{1,0:T(8,128)(2,1)S(1)}, u32[]{:S(2)}, u32[]{:S(2)}) collective-permute-start(bf16[128,2048]{1,0:T(8,128)(2,1)S(1)} %add_convert_fusion.3.refs_0_), channel_id=1, source_target_pairs={{0,32},{16,48},{32,0},{48,16},{1,33},{17,49},{33,1},{49,17},{2,34}... | collective-permute-start | bytes 1572872 | tf_op jit(solution)/shard_map/ppermute | solution.py:41
  584.4 32.9 %collective-permute-start.60 = (bf16[128,2048]{1,0:T(8,128)(2,1)S(1)}, bf16[128,2048]{1,0:T(8,128)(2,1)}, u32[]{:S(2)}, u32[]{:S(2)}) collective-permute-start(bf16[128,2048]{1,0:T(8,128)(2,1)S(1)} %add_convert_fusion.3.refs_0_), channel_id=1, source_target_pairs={{0,48},{16,0},{32,16},{48,32},{1,49},{17,1},{33,17},{49,33},{2,50}... | collective-permute-start | bytes 1572872 | tf_op jit(solution)/shard_map/ppermute | solution.py:41
  (102 other events, 1245.9 us)
Sparse Core Ops, SparseCore 0:
  11.1 62.2 all-gather.2
  75.8 147.3 all-gather.4
  330.2 147.4 reduce-scatter.1
